TPU v7x, 32 devices: a whole 2x2x4 slice. The times are simulated.
32 devices in a mesh: groups: 2 (over y), graph: 4 (over z), edge: 4 (over x, core).
Axes of the slice: x: 2, y: 2, z: 4, core: 2. Of those that a mesh axis runs over, the one named last changes fastest.
Arguments:
- atom_embed: bfloat16 [256, 49, 64], P(('groups', 'graph')), parts along dimension 0, may hold values from -6 to 6
- out_cotangent: bfloat16 [256, 49, 64], P(('groups', 'graph')), parts along dimension 0, may hold values from -6 to 6
- send_rows: int32 [8, 4, 4, 4], P(('groups', 'graph'), None, 'edge'), parts along dimension 0, may hold values from 0 to 31, as said below
- recv_rows: int32 [8, 4, 4, 4], P(('groups', 'graph'), None, 'edge'), parts along dimension 0, may hold values from 0 to 31, as said below
- source_slot: int32 [8192], P(('groups', 'graph', 'edge')), parts along dimension 0, may hold values from 0 to 15, as said below
- target_slot: int32 [8192], P(('groups', 'graph', 'edge')), parts along dimension 0, may hold values from 0 to 15, as said below
- rotation: bfloat16 [8192, 235], P(('groups', 'graph', 'edge')), parts along dimension 0, may hold values from -2 to 2
- edge_feats: bfloat16 [8192, 128], P(('groups', 'graph', 'edge')), parts along dimension 0, may hold values from -6 to 6
- edge_bias: float32 [8192, 4], P(('groups', 'graph', 'edge')), parts along dimension 0, may hold values from -4 to 350
- conv_zero: bfloat16 [448, 448], replicated, may hold values from -0.25 to 0.25
- conv_one: bfloat16 [2, 384, 384], replicated, may hold values from -0.21875 to 0.21875
- conv_two: bfloat16 [2, 320, 320], replicated, may hold values from -0.25 to 0.25
- alpha_in: bfloat16 [64, 256], replicated, may hold values from -0.75 to 0.75
- alpha_edge: bfloat16 [128, 256], replicated, may hold values from -0.5 to 0.5
- alpha_dot: bfloat16 [256], replicated, may hold values from -1.5 to 1.5
- out_proj: bfloat16 [7, 64, 64], replicated, may hold values from -0.75 to 0.75
Outputs:
- output: bfloat16 [256, 49, 64], P(('groups', 'graph')), parts along dimension 0
- grad_atom_embed: bfloat16 [256, 49, 64], P(('groups', 'graph')), parts along dimension 0
- grad_conv_zero: bfloat16 [896, 448], P('groups'), parts along dimension 0
- grad_conv_one: bfloat16 [4, 384, 384], P('groups'), parts along dimension 0
- grad_conv_two: bfloat16 [4, 320, 320], P('groups'), parts along dimension 0
- grad_alpha_in: bfloat16 [128, 256], P('groups'), parts along dimension 0
- grad_alpha_edge: bfloat16 [256, 256], P('groups'), parts along dimension 0
- grad_alpha_dot: bfloat16 [512], P('groups'), parts along dimension 0
- grad_out_proj: bfloat16 [14, 64, 64], P('groups'), parts along dimension 0
There are 2 independent parts, one for each index of `groups`. A program takes and returns all parts, laid end to end along the dimension named above; an argument that names none is the same for every part. Nothing has to cross between parts.
Inputs may be any that keep to these rules, and one draw needn't show every extreme that they name: send_rows[p, g, e] lists n distinct atoms of owner p in its entries 0 .. n-1, with n from 2 to 4; later entries hold 0. In every block (g, e) the list of some owner has n = 4. recv_rows[q, g, e] is built as send_rows; every atom is listed in some block. source_slot[f] = p * 4 + c names a listed entry c < n of send_rows[p, g, e] for the edge's block; every listed entry is named by some edge of the block. target_slot[f] = q * 4 + c names a listed entry of recv_rows[q, g, e] for the edge's block; every listed entry is named by some edge of the block, so every atom is the target of some edge.
All inputs are finite; a program needn't handle non-finite values.
Results may differ from a plain program's by a relative error of at most 0.002.
The roundings to bfloat16 on the way count: a program that leaves them out, or rounds other values in their place, can miss the bound.
Values may be sent and summed in bfloat16 or wider, within the bound.
No kernel may reach another device: no remote copies, remote signals or barrier semaphores. Data moves between devices by JAX's collectives and lax.ppermute only.
A program may use at most 128 MiB of HBM per device.

v0:
```python
import jax
import jax.numpy as jnp
import numpy as np
from jax import lax
from jax.experimental import pallas as pl
from jax.experimental.pallas import tpu as pltpu
from jax.sharding import PartitionSpec as P

LMAX = 6
MMAX = 2
CH = 64
HEADS = 4
VAL = 16
ALPHA = 64
COEFFS = (LMAX + 1) * (LMAX + 1)
FLAT = COEFFS * CH
LANES = 128
BLOCKS = (FLAT + LANES - 1) // LANES
COLS = BLOCKS * LANES
WIDE = COLS + LANES
DIM0 = (LMAX + 1) * CH
DIM1 = LMAX * CH
DIM2 = (LMAX - 1) * CH
PANEL = 256

leak_slope = 0.2
floor_value = -1e30
bf16 = jnp.bfloat16
f32 = jnp.float32

VMEM_LIMIT = 56 * 1024 * 1024


def degree_blocks():
    result = []
    offset = 0
    for degree in range(LMAX + 1):
        centre = min(degree, MMAX)
        row_total = 2 * centre + 1
        col_total = 2 * degree + 1
        result.append((degree, centre, row_total, col_total, offset))
        offset += row_total * col_total
    return result


def degree_of(coeff):
    return int(np.sqrt(coeff))


def dot_nn(left, right):
    return jnp.dot(left, right, preferred_element_type=f32)


def dot_nt(left, right):
    return lax.dot_general(left, right, (((1,), (1,)), ((), ())), preferred_element_type=f32)


def dot_tn(left, right):
    return lax.dot_general(left, right, (((0,), (0,)), ((), ())), preferred_element_type=f32)


def iota(shape, dim):
    return lax.broadcasted_iota(jnp.int32, shape, dim)


def split_two(value):
    high = value.astype(bf16)
    return high, (value - high.astype(f32)).astype(bf16)


def to_frame(source, rot, edges, emit):
    def body(half, carry):
        lanes = pl.ds(pl.multiple_of(half * LANES, LANES), LANES)
        for degree, centre, row_total, col_total, offset in degree_blocks():
            sums = [None] * row_total
            for j in range(col_total):
                column = source[pl.ds((degree * degree + j) * CH, CH), lanes]
                for i in range(row_total):
                    term = rot[pl.ds(offset + i * col_total + j, 1), lanes] * column
                    sums[i] = term if j == 0 else sums[i] + term
            for i in range(row_total):
                emit(degree, i - centre, half, sums[i])
        return carry

    lax.fori_loop(0, edges // LANES, body, 0)


def from_frame(load, rot, edges, emit):
    def body(half, carry):
        lanes = pl.ds(pl.multiple_of(half * LANES, LANES), LANES)
        for degree, centre, row_total, col_total, offset in degree_blocks():
            rows = [load(degree, i - centre, half) for i in range(row_total)]
            for j in range(col_total):
                total = None
                for i in range(row_total):
                    term = rot[pl.ds(offset + i * col_total + j, 1), lanes] * rows[i]
                    total = term if i == 0 else total + term
                emit(degree * degree + j, half, total)
        return carry

    lax.fori_loop(0, edges // LANES, body, 0)


def lane_at(half, edges, second):
    return pl.ds(pl.multiple_of(half * LANES + (edges if second else 0), LANES), LANES)


def frame_place(degree, order, refs):
    if order == 0:
        return refs[0], degree * CH, False
    which = abs(order)
    return refs[which], (degree - which) * CH, order < 0


def spread_heads(rows):
    return jnp.concatenate(
        [jnp.broadcast_to(row, (VAL, row.shape[1])) for row in rows], axis=0
    )


def one_hot_rows(slot_ref, slots):
    edges = slot_ref.shape[1]
    return iota((slots, edges), 0) == slot_ref[...]


def mask_to(mask, dtype):
    return jnp.where(mask, 1.0, 0.0).astype(dtype)


def stack_table(table_ref, rows_ref):
    peers, cap, width = table_ref.shape
    for start in range(0, peers * cap, 8):
        parts = [table_ref[g].astype(f32) for g in range(start // cap, (start + 8) // cap)]
        rows_ref[pl.ds(start, 8), :] = jnp.concatenate(parts, axis=0)


def put_rows(out_ref, cols, value):
    peers, cap = out_ref.shape[0], out_ref.shape[1]
    for g in range(peers):
        out_ref[g, :, cols] = value[g * cap : (g + 1) * cap].astype(out_ref.dtype)


def slot_sums(terms, one_hot, out_ref):
    both = jnp.concatenate([one_hot, one_hot], axis=1)
    for start in range(0, COLS, PANEL):
        size = min(PANEL, COLS - start)
        put_rows(out_ref, pl.ds(start, size), dot_nt(both, terms[pl.ds(start, size), :]))


def store_terms(terms, edges):
    def emit(coeff, half, value):
        high, low = split_two(value)
        rows = pl.ds(coeff * CH, CH)
        terms[rows, lane_at(half, edges, False)] = high
        terms[rows, lane_at(half, edges, True)] = low

    return emit


def forward_kernel(
    table, source_slot, target_slot, rot, feats, bias, wzero, wone, wtwo, ain, aedge, adot,
    sums_out, x0, x1, x2, v0, v1, v2, pre_out, logit_out,
    rows, gathered, neg1, neg2, weights, terms,
):
    edges = source_slot.shape[1]
    slots = table.shape[0] * table.shape[1]
    stack_table(table, rows)
    picked = mask_to(one_hot_rows(source_slot, slots), bf16)
    gathered[...] = dot_tn(rows[...].astype(bf16), picked)

    def emit(degree, order, half, value):
        ref, row, second = frame_place(degree, order, (x0, x1, x2))
        value = value.astype(bf16)
        ref[pl.ds(row, CH), lane_at(half, edges, second)] = value
        if order != 0:
            neg = (None, neg1, neg2)[abs(order)]
            swapped = value if order > 0 else -value
            neg[pl.ds(row, CH), lane_at(half, edges, not second)] = swapped

    to_frame(gathered, rot, edges, emit)

    pre = dot_nn(ain[...], x0[pl.ds(0, CH), :]) + dot_nt(aedge[...], feats[...])
    pre_out[...] = pre
    hidden = jnp.where(pre > 0, pre, leak_slope * pre) * adot[...]
    aims = one_hot_rows(target_slot, slots)
    lane = iota((slots, LANES), 1)
    side = jnp.zeros((slots, LANES), f32)
    for h in range(HEADS):
        logit = jnp.sum(hidden[h * ALPHA : (h + 1) * ALPHA], axis=0, keepdims=True)
        logit = logit + bias[pl.ds(h, 1), :]
        logit_out[pl.ds(h, 1), :] = logit
        peak = jnp.max(jnp.where(aims, logit, floor_value), axis=1, keepdims=True)
        of_edge = jnp.sum(jnp.where(aims, peak, 0.0), axis=0, keepdims=True)
        weight = jnp.exp(logit - of_edge)
        weights[pl.ds(h, 1), :] = weight
        den = jnp.sum(jnp.where(aims, weight, 0.0), axis=1, keepdims=True)
        side = jnp.where(lane == h, den, jnp.where(lane == HEADS + h, peak, side))
    put_rows(sums_out, pl.ds(COLS, LANES), side)

    v0[...] = dot_nn(wzero[...], x0[...])
    v1[...] = dot_nn(wone[0], x1[...]) + dot_nn(wone[1], neg1[...])
    v2[...] = dot_nn(wtwo[0], x2[...]) + dot_nn(wtwo[1], neg2[...])

    def load(degree, order, half):
        ref, row, second = frame_place(degree, order, (v0, v1, v2))
        return ref[pl.ds(row, CH), lane_at(half, edges, second)]

    store = store_terms(terms, edges)

    def weigh(coeff, half, value):
        lanes = lane_at(half, edges, False)
        spread = spread_heads([weights[pl.ds(h, 1), lanes] for h in range(HEADS)])
        store(coeff, half, value * spread)

    terms[pl.ds(FLAT, COLS - FLAT), :] = jnp.zeros((COLS - FLAT, 2 * edges), bf16)
    from_frame(load, rot, edges, weigh)
    slot_sums(terms, mask_to(aims, bf16), sums_out)


def lane_heads(values, shape):
    head = (iota(shape, 1) % CH) // VAL
    result = jnp.broadcast_to(values[0], shape)
    for h in range(1, HEADS):
        result = jnp.where(head == h, values[h], result)
    return result


def collect_rows(place, arrivals, rows_ref):
    for k, arrival in enumerate(arrivals):
        peers, cap, width = arrival.shape
        base = (place[0] ^ k) * (peers * cap)
        for start in range(0, peers * cap, 8):
            parts = [arrival[g] for g in range(start // cap, (start + 8) // cap)]
            at = pl.ds(pl.multiple_of(base + start, 8), 8)
            rows_ref[at, :] = jnp.concatenate(parts, axis=0)


def make_finish(lanes_total):
    def finish_kernel(place, index_row, index_col, own_col, cot, pairs, *rest):
        arrivals = rest[:lanes_total]
        out, back, proj, rows, num, num_grad = rest[lanes_total:]
        atoms = cot.shape[0]
        total = index_row.shape[1]
        slots = own_col.shape[0]
        collect_rows(place, arrivals, rows)
        side = rows[:, pl.ds(COLS, LANES)]
        names = iota((total, atoms), 1) == index_col[...]
        picked = mask_to(iota((atoms, total), 0) == index_row[...], bf16)
        own = iota((slots, atoms), 1) == own_col[...]
        eye = iota((atoms, atoms), 0) == iota((atoms, atoms), 1)
        scales, dens, own_peaks = [], [], []
        for h in range(HEADS):
            peak_rows = side[:, HEADS + h : HEADS + h + 1]
            peak = jnp.max(jnp.where(names, peak_rows, floor_value), axis=0, keepdims=True)
            of_row = jnp.sum(jnp.where(names, peak, 0.0), axis=1, keepdims=True)
            scale = jnp.exp(peak_rows - of_row)
            scaled_den = side[:, h : h + 1] * scale
            den = jnp.sum(jnp.where(names, scaled_den, 0.0), axis=0, keepdims=True)
            scales.append(scale)
            dens.append(jnp.sum(jnp.where(eye, den, 0.0), axis=1, keepdims=True))
            own_peaks.append(jnp.sum(jnp.where(own, peak, 0.0), axis=1, keepdims=True))
        scale_full = lane_heads(scales, (total, LANES))
        den_full = lane_heads(dens, (atoms, LANES))
        twice = jnp.concatenate([picked, picked], axis=1)

        def gather_block(block, carry):
            cols = pl.ds(pl.multiple_of(block * LANES, LANES), LANES)
            high, low = split_two(rows[:, cols] * scale_full)
            num[:, cols] = dot_nn(twice, jnp.concatenate([high, low], axis=0))
            return carry

        lax.fori_loop(0, BLOCKS, gather_block, 0)

        den_sum = jnp.zeros((atoms, LANES), f32)
        tops = [None] * (LMAX + 1)
        lows = [None] * (LMAX + 1)
        for block in range(BLOCKS):
            cols = pl.ds(block * LANES, LANES)
            agg = num[:, cols] / den_full
            agg_low = agg.astype(bf16)
            cot_block = cot[:, cols]
            weight = pairs[block]
            out[:, cols] = dot_nn(agg_low, weight).astype(bf16)
            agg_grad = dot_nt(cot_block, weight)
            num_grad[:, cols] = (agg_grad / den_full).astype(bf16)
            den_sum = den_sum + agg_grad * agg
            outer = dot_tn(agg_low, cot_block)
            first = degree_of(2 * block)
            tops[first] = outer[:CH] if tops[first] is None else tops[first] + outer[:CH]
            if 2 * block + 1 < COEFFS:
                second = degree_of(2 * block + 1)
                lows[second] = outer[CH:] if lows[second] is None else lows[second] + outer[CH:]
        for degree in range(LMAX + 1):
            piece = jnp.zeros((CH, CH), f32)
            if tops[degree] is not None:
                piece = piece + tops[degree][:, :CH]
            if lows[degree] is not None:
                piece = piece + lows[degree][:, CH:]
            proj[pl.ds(degree * CH, CH), :] = piece * (1.0 / lanes_total)

        own_low = mask_to(own, bf16)
        put_rows(back, pl.ds(0, COLS), dot_nn(own_low, num_grad[...]))
        head = (iota((atoms, LANES), 1) % CH) // VAL
        lane = iota((slots, LANES), 1)
        extra = jnp.zeros((slots, LANES), f32)
        for h in range(HEADS):
            summed = jnp.sum(jnp.where(head == h, den_sum, 0.0), axis=1, keepdims=True)
            den_grad = (-summed / dens[h]).astype(bf16).astype(f32)
            as_row = jnp.sum(jnp.where(eye, den_grad, 0.0), axis=0, keepdims=True)
            of_row = jnp.sum(jnp.where(own, as_row, 0.0), axis=1, keepdims=True)
            high = own_peaks[h].astype(bf16).astype(f32)
            rest_one = own_peaks[h] - high
            mid = rest_one.astype(bf16).astype(f32)
            for n, value in enumerate((of_row, high, mid, rest_one - mid)):
                extra = jnp.where(lane == n * HEADS + h, value, extra)
        put_rows(back, pl.ds(COLS, LANES), extra)

    return finish_kernel


def gradient_kernel(
    table, target_slot, rot, feats, x0, x1, x2, v0, v1, v2, pre, logits, adot, proj,
    packed, g0, g1, g2, pre_grad_out,
    rows, spread_grad, weights,
):
    edges = target_slot.shape[1]
    slots = table.shape[0] * table.shape[1]
    stack_table(table, rows)
    picked = mask_to(one_hot_rows(target_slot, slots), bf16)
    low_rows = rows[...].astype(bf16)
    spread_grad[...] = dot_tn(low_rows[:, :COLS], picked)
    side = dot_tn(low_rows[:, COLS:], picked)
    for h in range(HEADS):
        peak = (side[HEADS + h : HEADS + h + 1] + side[2 * HEADS + h : 2 * HEADS + h + 1]) + side[
            3 * HEADS + h : 3 * HEADS + h + 1
        ]
        weights[pl.ds(h, 1), :] = jnp.exp(logits[pl.ds(h, 1), :] - peak)

    state = {}

    def emit(degree, order, half, value):
        lanes = lane_at(half, edges, False)
        ref, row, second = frame_place(degree, order, (v0, v1, v2))
        product = value * ref[pl.ds(row, CH), lane_at(half, edges, second)]
        if degree == 0:
            state["sum"] = product
            state["spread"] = spread_heads([weights[pl.ds(h, 1), lanes] for h in range(HEADS)])
        else:
            state["sum"] = state["sum"] + product
        grad = (value * state["spread"]).astype(bf16)
        ref, row, second = frame_place(degree, order, (g0, g1, g2))
        ref[pl.ds(row, CH), lane_at(half, edges, second)] = grad
        if order != 0:
            swapped = grad if order < 0 else -grad
            below = row + (DIM1 if abs(order) == 1 else DIM2)
            ref[pl.ds(below, CH), lane_at(half, edges, not second)] = swapped
        if degree == LMAX and order == MMAX:
            for h in range(HEADS):
                part = state["sum"][h * VAL : (h + 1) * VAL]
                weights[pl.ds(HEADS + h, 1), lanes] = jnp.sum(part, axis=0, keepdims=True)

    to_frame(spread_grad, rot, edges, emit)

    hidden = jnp.where(pre[...] > 0, pre[...], leak_slope * pre[...])
    logit_grads = [
        weights[pl.ds(h, 1), :] * (weights[pl.ds(HEADS + h, 1), :] + side[h : h + 1])
        for h in range(HEADS)
    ]
    tall = jnp.concatenate(
        [jnp.broadcast_to(row, (ALPHA, edges)) for row in logit_grads], axis=0
    )
    slope = jnp.where(pre[...] > 0, 1.0, leak_slope)
    pre_grad = (tall * adot[...] * slope).astype(bf16)
    pre_grad_out[...] = pre_grad
    dot_grad = jnp.sum(tall * hidden, axis=1, keepdims=True)

    row = 0
    for start in range(0, DIM0, PANEL):
        size = min(PANEL, DIM0 - start)
        packed[pl.ds(row, DIM0), pl.ds(0, size)] = dot_nt(x0[...], g0[pl.ds(start, size), :])
        if size < PANEL:
            packed[pl.ds(row, DIM0), pl.ds(size, CH)] = proj[...]
        row += DIM0
    for left, right, dim in ((x1, g1, DIM1), (x2, g2, DIM2)):
        for start in range(0, 2 * dim, PANEL):
            size = min(PANEL, 2 * dim - start)
            packed[pl.ds(row, dim), pl.ds(0, size)] = dot_nt(left[...], right[pl.ds(start, size), :])
            row += dim
    row -= DIM2
    half = pl.ds(LANES, LANES)
    edge_ch = feats.shape[1]
    edge_grad = lax.dot_general(
        feats[...], pre_grad, (((0,), (1,)), ((), ())), preferred_element_type=f32
    )
    packed[pl.ds(row, edge_ch), half] = edge_grad[:, :LANES]
    packed[pl.ds(row + edge_ch, edge_ch), half] = edge_grad[:, LANES:]
    wide_dot = jnp.transpose(jnp.broadcast_to(dot_grad, (HEADS * ALPHA, LANES)))
    spare = DIM2 - 2 * edge_ch
    tail = iota((spare, LANES), 0)
    first = jnp.broadcast_to(wide_dot[:1, :LANES], (spare, LANES))
    second = jnp.broadcast_to(wide_dot[:1, LANES:], (spare, LANES))
    packed[pl.ds(row + 2 * edge_ch, spare), half] = jnp.where(
        tail == 0, first, jnp.where(tail == 1, second, 0.0)
    )
    row += DIM2
    packed[pl.ds(row, CH), :] = dot_nt(x0[pl.ds(0, CH), :], pre_grad)


PACKED_ROWS = 2 * DIM0 + 3 * DIM1 + 3 * DIM2 + CH


def unpack(packed, edge_ch):
    row = 0
    panels = []
    for dim, count in ((DIM0, 2), (DIM1, 3), (DIM2, 3)):
        for _ in range(count):
            panels.append(packed[row : row + dim])
            row += dim
    rest = DIM0 - PANEL
    zero = jnp.concatenate([panels[0], panels[1][:, :rest]], axis=1)
    proj = panels[1][:, rest:].reshape(LMAX + 1, CH, CH)
    one = jnp.concatenate(panels[2:5], axis=1)
    one = jnp.stack([one[:, :DIM1], one[:, DIM1:]])
    two = jnp.concatenate(panels[5:7] + [panels[7][:, :LANES]], axis=1)
    two = jnp.stack([two[:, :DIM2], two[:, DIM2:]])
    half = panels[7][:, LANES:]
    alpha_edge = jnp.concatenate([half[:edge_ch], half[edge_ch : 2 * edge_ch]], axis=1)
    alpha_dot = half[2 * edge_ch : 2 * edge_ch + 2].reshape(-1)
    alpha_in = packed[row : row + CH]
    return zero, one, two, alpha_in, alpha_edge, alpha_dot, proj


def source_kernel(
    source_slot, rot, g0, g1, g2, pre_grad, wzero, wone, wtwo, ain,
    sums_out, d0, d1, d2, terms,
):
    edges = source_slot.shape[1]
    slots = sums_out.shape[0] * sums_out.shape[1]
    d0[...] = dot_nn(wzero[...], g0[...])
    d0[pl.ds(0, CH), :] += dot_nn(ain[...], pre_grad[...])
    d1[...] = dot_nn(wone[0], g1[pl.ds(0, DIM1), :]) + dot_nn(wone[1], g1[pl.ds(DIM1, DIM1), :])
    d2[...] = dot_nn(wtwo[0], g2[pl.ds(0, DIM2), :]) + dot_nn(wtwo[1], g2[pl.ds(DIM2, DIM2), :])

    def load(degree, order, half):
        ref, row, second = frame_place(degree, order, (d0, d1, d2))
        return ref[pl.ds(row, CH), lane_at(half, edges, second)]

    terms[pl.ds(FLAT, COLS - FLAT), :] = jnp.zeros((COLS - FLAT, 2 * edges), bf16)
    from_frame(load, rot, edges, store_terms(terms, edges))
    slot_sums(terms, mask_to(one_hot_rows(source_slot, slots), bf16), sums_out)


def make_collect(lanes_total):
    def collect_kernel(place, index_row, *rest):
        arrivals = rest[:lanes_total]
        out, rows = rest[lanes_total:]
        atoms = out.shape[0]
        total = index_row.shape[1]
        collect_rows(place, arrivals, rows)
        picked = mask_to(iota((atoms, total), 0) == index_row[...], bf16)
        twice = jnp.concatenate([picked, picked], axis=1)

        def gather_block(block, carry):
            cols = pl.ds(pl.multiple_of(block * LANES, LANES), LANES)
            high, low = split_two(rows[:, cols])
            out[:, cols] = dot_nn(twice, jnp.concatenate([high, low], axis=0)).astype(bf16)
            return carry

        lax.fori_loop(0, BLOCKS, gather_block, 0)

    return collect_kernel


vmem = pl.BlockSpec(memory_space=pltpu.VMEM)
smem = pl.BlockSpec(memory_space=pltpu.SMEM)


def call(kernel, outs, scratch, *args, scalar=False):
    specs = [smem if scalar and n == 0 else vmem for n in range(len(args))]
    return pl.pallas_call(
        kernel,
        out_shape=[jax.ShapeDtypeStruct(shape, kind) for shape, kind in outs],
        in_specs=specs,
        out_specs=[vmem] * len(outs),
        scratch_shapes=[pltpu.VMEM(shape, kind) for shape, kind in scratch],
        compiler_params=pltpu.CompilerParams(vmem_limit_bytes=VMEM_LIMIT),
    )(*args)


def swap(value, axis, bit):
    size = lax.axis_size(axis)
    return lax.ppermute(value, axis, [(i, i ^ (1 << bit)) for i in range(size)])


def bits_of(axis):
    return (lax.axis_size(axis) - 1).bit_length()


def gather_lanes(value):
    held = {0: value}
    for bit in reversed(range(bits_of("edge"))):
        held.update({k | (1 << bit): swap(v, "edge", bit) for k, v in list(held.items())})
    return [held[k] for k in range(len(held))]


def own_bit(axis, bit):
    return (lax.axis_index(axis) >> bit) & 1


def sum_all(packed):
    steps = [("edge", n) for n in range(bits_of("edge"))]
    steps += [("graph", n) for n in range(bits_of("graph"))]
    current = packed
    for axis, bit in steps:
        mine = own_bit(axis, bit)
        parts = current.reshape(2, current.shape[0] // 2, -1)
        sent = swap(lax.dynamic_index_in_dim(parts, 1 - mine, 0, False), axis, bit)
        current = lax.dynamic_index_in_dim(parts, mine, 0, False) + sent
    current = current.astype(bf16)
    for axis, bit in reversed(steps):
        mine = own_bit(axis, bit)
        other = swap(current, axis, bit)
        current = jnp.concatenate(
            [jnp.where(mine == 0, current, other), jnp.where(mine == 0, other, current)], axis=0
        )
    return current


def shards(
    atom_embed, out_cotangent, send_rows, recv_rows, source_slot, target_slot, rotation,
    edge_feats, edge_bias, conv_zero, conv_one, conv_two, alpha_in, alpha_edge, alpha_dot,
    out_proj,
):
    peers = lax.axis_size("graph")
    lanes_total = lax.axis_size("edge")
    atoms = atom_embed.shape[0]
    edges = rotation.shape[0]
    send_list = send_rows.reshape(peers, -1)
    recv_list = recv_rows.reshape(peers, -1)
    cap = send_list.shape[1]
    slots = peers * cap

    def exchange(value):
        return lax.all_to_all(value, "graph", split_axis=0, concat_axis=0, tiled=True)

    outgoing = atom_embed[send_list].reshape(peers, cap, FLAT)
    table = exchange(outgoing)

    source_row = source_slot.reshape(1, edges)
    target_row = target_slot.reshape(1, edges)
    rot = rotation.T.astype(f32)
    bias = edge_bias.T
    adot = alpha_dot.astype(f32).reshape(-1, 1)
    cot = jnp.pad(out_cotangent.reshape(atoms, FLAT), ((0, 0), (0, COLS - FLAT)))
    degrees = np.array([degree_of(k) for k in range(COEFFS)] + [LMAX], np.int32)
    blank = jnp.zeros((BLOCKS, CH, CH), bf16)
    pairs = jnp.concatenate(
        [
            jnp.concatenate([out_proj[degrees[0::2]], blank], axis=2),
            jnp.concatenate([blank, out_proj[degrees[1::2]]], axis=2),
        ],
        axis=1,
    )
    lists = lax.all_gather(jnp.stack([send_list.reshape(-1), recv_list.reshape(-1)]), "edge")
    send_all = lists[:, 0].reshape(-1)
    recv_all = lists[:, 1].reshape(-1)
    place = lax.axis_index("edge").astype(jnp.int32).reshape(1)

    sums, x0, x1, x2, v0, v1, v2, pre, logits = call(
        forward_kernel,
        [
            ((peers, cap, WIDE), f32),
            ((DIM0, edges), bf16),
            ((DIM1, 2 * edges), bf16),
            ((DIM2, 2 * edges), bf16),
            ((DIM0, edges), f32),
            ((DIM1, 2 * edges), f32),
            ((DIM2, 2 * edges), f32),
            ((HEADS * ALPHA, edges), f32),
            ((8, edges), f32),
        ],
        [
            ((slots, FLAT), f32),
            ((FLAT, edges), f32),
            ((DIM1, 2 * edges), bf16),
            ((DIM2, 2 * edges), bf16),
            ((8, edges), f32),
            ((COLS, 2 * edges), bf16),
        ],
        table, source_row, target_row, rot, edge_feats, bias,
        conv_zero.T, jnp.swapaxes(conv_one, 1, 2), jnp.swapaxes(conv_two, 1, 2),
        alpha_in.T, alpha_edge.T, adot,
    )

    arrivals = gather_lanes(exchange(sums))
    total = lanes_total * slots
    out, back, proj = call(
        make_finish(lanes_total),
        [((atoms, COLS), bf16), ((peers, cap, WIDE), bf16), (((LMAX + 1) * CH, CH), f32)],
        [((total, WIDE), f32), ((atoms, COLS), f32), ((atoms, COLS), bf16)],
        place, recv_all.reshape(1, -1), recv_all.reshape(-1, 1), recv_list.reshape(-1, 1),
        cot, pairs, *arrivals,
        scalar=True,
    )

    packed, g0, g1, g2, pre_grad = call(
        gradient_kernel,
        [
            ((PACKED_ROWS, PANEL), f32),
            ((DIM0, edges), bf16),
            ((2 * DIM1, 2 * edges), bf16),
            ((2 * DIM2, 2 * edges), bf16),
            ((HEADS * ALPHA, edges), bf16),
        ],
        [((slots, WIDE), f32), ((COLS, edges), f32), ((8, edges), f32)],
        exchange(back), target_row, rot, edge_feats, x0, x1, x2, v0, v1, v2, pre, logits, adot,
        proj,
    )
    grads = sum_all(packed)

    (source_sums,) = call(
        source_kernel,
        [((peers, cap, COLS), f32)],
        [
            ((DIM0, edges), f32),
            ((DIM1, 2 * edges), f32),
            ((DIM2, 2 * edges), f32),
            ((COLS, 2 * edges), bf16),
        ],
        source_row, rot, g0, g1, g2, pre_grad, conv_zero, conv_one, conv_two, alpha_in,
    )
    (embed,) = call(
        make_collect(lanes_total),
        [((atoms, COLS), bf16)],
        [((total, COLS), f32)],
        place, send_all.reshape(1, -1), *gather_lanes(exchange(source_sums)),
        scalar=True,
    )

    def shaped(rows):
        return rows[:, :FLAT].reshape(atoms, COEFFS, CH)

    return (shaped(out), shaped(embed)) + unpack(grads, edge_feats.shape[1])


def solution(mesh):
    in_specs = (
        P(("groups", "graph"), None, None),
        P(("groups", "graph"), None, None),
        P(("groups", "graph"), None, "edge", None),
        P(("groups", "graph"), None, "edge", None),
        P(("groups", "graph", "edge")),
        P(("groups", "graph", "edge")),
        P(("groups", "graph", "edge"), None),
        P(("groups", "graph", "edge"), None),
        P(("groups", "graph", "edge"), None),
        P(),
        P(),
        P(),
        P(),
        P(),
        P(),
        P(),
    )
    out_specs = (
        P(("groups", "graph"), None, None),
        P(("groups", "graph"), None, None),
        P("groups", None),
        P("groups", None, None),
        P("groups", None, None),
        P("groups", None),
        P("groups", None),
        P("groups"),
        P("groups", None, None),
    )
    return jax.shard_map(shards, mesh=mesh, in_specs=in_specs, out_specs=out_specs, check_vma=False)
```

profile of v0, /device:TPU:0, one launch (start us, length us, event | category | flops | bytes accessed | tf_op | source)
XLA Modules:
  0.0 188.2 jit_solution(14435731897756394063)
XLA Ops:
  0.7 0.7 compare_select_fusion
  1.7 1.1 gather_fusion.2
  2.9 0.8 reshape.96
  3.7 6.3 %all-to-all-start = ((bf16[4,4,3136]{2,1,0:T(4,128)(2,1)}), bf16[4,4,3136]{2,1,0:T(4,128)(2,1)S(1)}, u32[]{:S(2)}, u32[]{:S(2)}) async-start(bf16[4,4,3136]{2,1,0:T(4,128)(2,1)} %reshape.96), calls=%async_computation | async-start | bytes 204800 | tf_op jit(solution)/shard_map/all_to_all | solution.py:544
  10.0 0.8 copy.60.adot
  10.8 1.1 copy.56
  11.9 1.0 copy.57
  12.9 1.0 copy.55
  13.9 0.7 copy.58
  14.6 0.7 copy.59
  15.4 0.7 convert_bitcast_fusion.rot
  16.1 0.6 copy-done.8
  16.7 8.6 %shard_map.259 = (f32[4,4,3328]{2,1,0:T(4,128)}, bf16[448,256]{1,0:T(8,128)(2,1)}, bf16[384,512]{1,0:T(8,128)(2,1)}, bf16[320,512]{1,0:T(8,128)(2,1)}, f32[448,2...) custom-call(bf16[4,4,3136]{2,1,0:T(4,128)(2,1)} %copy-done.8, ...), custom_call_target="tpu_custom_call" | custom-call | tf_op jit(solution)/shard_map/pallas_call | solution.py:480
  25.4 5.2 %all-to-all-start.1 = ((f32[4,4,3328]{2,1,0:T(4,128)}), f32[4,4,3328]{2,1,0:T(4,128)S(1)}, u32[]{:S(2)}, u32[]{:S(2)}) async-start(f32[4,4,3328]{2,1,0:T(4,128)} %get-tuple-element.26), calls=%async_computation.1 | async-start | bytes 425984 | tf_op jit(solution)/shard_map/all_to_all | solution.py:544
  30.6 0.5 broadcast.70
  31.1 0.7 reduce.19
  31.9 0.7 reduce.18
  32.6 5.1 %all-gather.1 = s32[4,2,16]{2,1,0:T(2,128)S(1)} all-gather(s32[1,2,16]{2,1,0:T(2,128)S(1)} %add_bitcast_fusion), channel_id=2, replica_groups=mesh['groups'=2,'graph'=4,'edge'=4] {'edge'}, dimensions={0}, use_global_device_ids=true | all-gather | bytes 640 | tf_op jit(solution)/shard_map/all_gather | solution.py:564
  37.7 0.4 all-to-all-done.1.rest_0_
  38.1 1.5 collective-permute-start.1
  39.6 0.7 reshape_reshape_squeeze.12.index_col
  40.3 0.6 reshape_reshape_squeeze.9.index_row
  41.0 0.6 gather_fusion
  41.7 3.5 %collective-permute-done.1.rest_2_ = f32[4,4,3328]{2,1,0:T(4,128)S(1)} collective-permute-done((f32[4,4,3328]{2,1,0:T(4,128)S(1)}, f32[4,4,3328]{2,1,0:T(4,128)S(1)}, u32[]{:S(2)}, u32[]{:S(2)}) %collective-permute-start.1) | collective-permute-done | bytes 213024 | tf_op jit(solution)/shard_map/ppermute | solution.py:492
  45.2 0.6 gather_fusion.1
  46.3 0.7 reshape_reshape.4.own_col
  47.0 0.7 pad.6.cot
  47.7 1.2 fusion.2.pairs
  48.8 0.7 copy-done.11
  49.6 7.9 %shard_map.260 = (bf16[32,3200]{1,0:T(8,128)(2,1)}, bf16[4,4,3328]{2,1,0:T(4,128)(2,1)}, f32[448,64]{1,0:T(8,128)}) custom-call(s32[1]{0:T(128)} %bitcast.place, s32[1,64]{1,0:T(1,128)} %reshape_reshape_squeeze.9.index_row, s32[64,1]{1,0:T(8,128)} %reshape_reshape_squeeze.12.index_col, s32[16,1]{1,0:T(8,128)} %reshape_reshape.4.own_col, ...), custom_call_target="tpu_custom_call" | custom-call | tf_op jit(solution)/shard_map/pallas_call | solution.py:480
  57.4 5.1 %all-to-all-start.2 = ((bf16[4,4,3328]{2,1,0:T(4,128)(2,1)}), bf16[4,4,3328]{2,1,0:T(4,128)(2,1)S(1)}, u32[]{:S(2)}, u32[]{:S(2)}) async-start(bf16[4,4,3328]{2,1,0:T(4,128)(2,1)} %get-tuple-element.28), calls=%async_computation.2 | async-start | bytes 212992 | tf_op jit(solution)/shard_map/all_to_all | solution.py:544
  62.5 6.1 %all-to-all-done.2.table = bf16[4,4,3328]{2,1,0:T(4,128)(2,1)S(1)} async-done(((bf16[4,4,3328]{2,1,0:T(4,128)(2,1)}), bf16[4,4,3328]{2,1,0:T(4,128)(2,1)S(1)}, u32[]{:S(2)}, u32[]{:S(2)}) %all-to-all-start.2) | async-done | bytes 106528 | tf_op jit(solution)/shard_map/all_to_all | solution.py:544
  68.6 0.6 copy-done.7
  69.2 7.6 %shard_map.261 = (f32[3072,256]{1,0:T(8,128)}, bf16[448,256]{1,0:T(8,128)(2,1)}, bf16[768,512]{1,0:T(8,128)(2,1)}, bf16[640,512]{1,0:T(8,128)(2,1)}, bf16[256,256]{1,0:T(8,128)(2,1)}) custom-call(bf16[4,4,3328]{2,1,0:T(4,128)(2,1)} %copy-done.7, s32[1,256]{1,0:T(1,128)} %bitcast.74, f32[235,256]{1,0:T(8,128)} %convert_bitcast_fusion.rot, ...), custom_call_target="tpu_custom_call" | custom-call | tf_op jit(solution)/shard_map/pallas_call | solution.py:480
  76.9 1.5 dynamic-slice_bitcast_fusion
  78.5 3.4 %collective-permute-done.6 = f32[1536,256]{1,0:T(8,128)S(1)} collective-permute-done((f32[1536,256]{1,0:T(8,128)S(1)}, f32[1536,256]{1,0:T(8,128)S(1)}, u32[]{:S(2)}, u32[]{:S(2)}) %collective-permute-start.6) | collective-permute-done | bytes 1572896 | tf_op jit(solution)/shard_map/ppermute | solution.py:492
  81.9 1.8 bitcast_add_fusion
  83.8 1.6 collective-permute-start.7
  85.3 18.1 %collective-permute-done.7 = f32[768,256]{1,0:T(8,128)S(1)} collective-permute-done((f32[768,256]{1,0:T(8,128)S(1)}, f32[768,256]{1,0:T(8,128)S(1)}, u32[]{:S(2)}, u32[]{:S(2)}) %collective-permute-start.7) | collective-permute-done | bytes 786464 | tf_op jit(solution)/shard_map/ppermute | solution.py:492
  103.6 1.1 collective-permute-start.8
  104.6 9.3 %collective-permute-done.8 = f32[384,256]{1,0:T(8,128)S(1)} collective-permute-done((f32[384,256]{1,0:T(8,128)S(1)}, f32[384,256]{1,0:T(8,128)S(1)}, u32[]{:S(2)}, u32[]{:S(2)}) %collective-permute-start.8) | collective-permute-done | bytes 393248 | tf_op jit(solution)/shard_map/ppermute | solution.py:492
  114.0 0.8 collective-permute-start.9
  114.8 9.6 %collective-permute-done.9 = f32[192,256]{1,0:T(8,128)S(1)} collective-permute-done((f32[192,256]{1,0:T(8,128)S(1)}, f32[192,256]{1,0:T(8,128)S(1)}, u32[]{:S(2)}, u32[]{:S(2)}) %collective-permute-start.9) | collective-permute-done | bytes 196640 | tf_op jit(solution)/shard_map/ppermute | solution.py:492
  124.5 6.2 %collective-permute-done.10 = bf16[192,256]{1,0:T(8,128)(2,1)S(1)} collective-permute-done((bf16[192,256]{1,0:T(8,128)(2,1)S(1)}, bf16[192,256]{1,0:T(8,128)(2,1)S(1)}, u32[]{:S(2)}, u32[]{:S(2)}) %collective-permute-start.10) | collective-permute-done | bytes 98336 | tf_op jit(solution)/shard_map/ppermute | solution.py:492
  130.8 6.5 %collective-permute-done.11 = bf16[384,256]{1,0:T(8,128)(2,1)S(1)} collective-permute-done((bf16[384,256]{1,0:T(8,128)(2,1)S(1)}, bf16[384,256]{1,0:T(8,128)(2,1)S(1)}, u32[]{:S(2)}, u32[]{:S(2)}) %collective-permute-start.11) | collective-permute-done | bytes 196640 | tf_op jit(solution)/shard_map/ppermute | solution.py:492
  137.4 1.6 collective-permute-start.12
  139.0 8.3 %collective-permute-done.12 = bf16[768,256]{1,0:T(8,128)(2,1)S(1)} collective-permute-done((bf16[768,256]{1,0:T(8,128)(2,1)S(1)}, bf16[768,256]{1,0:T(8,128)(2,1)S(1)}, u32[]{:S(2)}, u32[]{:S(2)}) %collective-permute-start.12) | collective-permute-done | bytes 393248 | tf_op jit(solution)/shard_map/ppermute | solution.py:492
  147.6 6.4 %shard_map.262 = f32[4,4,3200]{2,1,0:T(4,128)} custom-call(s32[1,256]{1,0:T(1,128)} %bitcast.76, f32[235,256]{1,0:T(8,128)} %convert_bitcast_fusion.rot, bf16[448,256]{1,0:T(8,128)(2,1)} %get-tuple-element.38.g0, bf16[768,512]{1,0:T(8,128)(2,1)} %get-tuple-element.39.g1, bf16[640,512]{1,0:T(8,128)(2,1)} %get-tuple-element.40.g2, ...), custom_call_target="tpu_custom_call" | custom-call | tf_op jit(solution)/shard_map/pallas_call | solution.py:480
  154.0 12.4 %all_to_all.20.rest_0_ = f32[4,4,3200]{2,1,0:T(4,128)S(1)} all-to-all(f32[4,4,3200]{2,1,0:T(4,128)} %shard_map.262), channel_id=1, replica_groups=mesh['groups'=2,'graph'=4,'edge'=4] {'graph'}, dimensions={0} | all-to-all | bytes 409600 | tf_op jit(solution)/shard_map/all_to_all | solution.py:544
  166.4 1.5 collective-permute-start.4
  167.9 4.4 %collective-permute-done.4.rest_2_ = f32[4,4,3200]{2,1,0:T(4,128)} collective-permute-done((f32[4,4,3200]{2,1,0:T(4,128)S(1)}, f32[4,4,3200]{2,1,0:T(4,128)}, u32[]{:S(2)}, u32[]{:S(2)}) %collective-permute-start.4) | collective-permute-done | bytes 204832 | tf_op jit(solution)/shard_map/ppermute | solution.py:492
  172.3 0.6 reshape_reshape_squeeze.11.index_row
  172.9 1.2 reshape.101
  174.1 0.8 copy.64
  174.9 5.4 %shard_map.263 = bf16[32,3200]{1,0:T(8,128)(2,1)} custom-call(s32[1]{0:T(128)} %bitcast.place, s32[1,64]{1,0:T(1,128)} %reshape_reshape_squeeze.11.index_row, f32[4,4,3200]{2,1,0:T(4,128)} %copy-done.6, f32[4,4,3200]{2,1,0:T(4,128)} %collective-permute-done.3.rest_1_, f32[4,4,3200]{2,1,0:T(4,128)} %collective-permute-done.4.rest_2_, ...), custom_call_target="tpu_custom_call" | custom-call | tf_op jit(solution)/shard_map/pallas_call | solution.py:480
  180.3 1.2 reshape.102
  181.5 0.8 copy.65
  182.8 0.7 slice.118
  183.6 0.6 slice.114
  184.2 0.5 slice_bitcast_fusion
  184.7 0.6 pad_maximum_fusion.11
  185.5 0.9 pad_maximum_fusion.2
  186.5 0.9 pad_maximum_fusion.1
  187.3 0.8 pad_maximum_fusion.3
  (86 shorter events, 2.8 us)
Async XLA Ops:
  0.6 1.0 copy-start
  0.7 9.4 %copy-start.20 = (bf16[256]{0:T(256)(128)(2,1)S(1)}, bf16[256]{0:T(256)(128)(2,1)}, u32[]{:S(2)}) copy-start(bf16[256]{0:T(256)(128)(2,1)} %param.34) | copy-start | bytes 1540
  1.7 9.2 %copy-start.2 = (bf16[2,384,384]{2,1,0:T(8,128)(2,1)S(1)}, bf16[2,384,384]{2,1,0:T(8,128)(2,1)}, u32[]{:S(2)}) copy-start(bf16[2,384,384]{2,1,0:T(8,128)(2,1)} %wone.1) | copy-start | bytes 1769476
  2.8 9.1 %copy-start.3 = (bf16[2,320,320]{2,1,0:T(8,128)(2,1)S(1)}, bf16[2,320,320]{2,1,0:T(8,128)(2,1)}, u32[]{:S(2)}) copy-start(bf16[2,320,320]{2,1,0:T(8,128)(2,1)} %wtwo.1) | copy-start | bytes 1228804
  2.8 10.1 %copy-start.4 = (bf16[448,448]{1,0:T(8,128)(2,1)S(1)}, bf16[448,448]{1,0:T(8,128)(2,1)}, u32[]{:S(2)}) copy-start(bf16[448,448]{1,0:T(8,128)(2,1)} %wzero.1) | copy-start | bytes 1204228
  3.7 12.4 %all-to-all-start = ((bf16[4,4,3136]{2,1,0:T(4,128)(2,1)}), bf16[4,4,3136]{2,1,0:T(4,128)(2,1)S(1)}, u32[]{:S(2)}, u32[]{:S(2)}) async-start(bf16[4,4,3136]{2,1,0:T(4,128)(2,1)} %reshape.96), calls=%async_computation | async-start | bytes 204800 | tf_op jit(solution)/shard_map/all_to_all | solution.py:544
  10.8 3.1 %copy-start.13 = (bf16[64,256]{1,0:T(8,128)(2,1)S(1)}, bf16[64,256]{1,0:T(8,128)(2,1)}, u32[]{:S(2)}) copy-start(bf16[64,256]{1,0:T(8,128)(2,1)} %ain.1) | copy-start | bytes 98308
  10.8 3.8 %copy-start.15 = (bf16[128,256]{1,0:T(8,128)(2,1)S(1)}, bf16[128,256]{1,0:T(8,128)(2,1)}, u32[]{:S(2)}) copy-start(bf16[128,256]{1,0:T(8,128)(2,1)} %param.33) | copy-start | bytes 196612
  10.8 4.5 %copy-start.14 = (bf16[256,235]{0,1:T(8,128)(2,1)S(1)}, bf16[256,235]{0,1:T(8,128)(2,1)}, u32[]{:S(2)}) copy-start(bf16[256,235]{0,1:T(8,128)(2,1)} %param.26) | copy-start | bytes 360964
  14.6 16.5 %copy-start.17 = (s32[1,4,1,4]{3,2,1,0:T(1,128)S(1)}, s32[1,4,1,4]{3,2,1,0:T(1,128)}, u32[]{:S(2)}) copy-start(s32[1,4,1,4]{3,2,1,0:T(1,128)} %param.22) | copy-start | bytes 196
  14.6 17.2 %copy-start.16 = (s32[1,4,1,4]{3,2,1,0:T(1,128)S(1)}, s32[1,4,1,4]{3,2,1,0:T(1,128)}, u32[]{:S(2)}) copy-start(s32[1,4,1,4]{3,2,1,0:T(1,128)} %param.23) | copy-start | bytes 196
  15.3 25.6 %copy-start.19 = (s32[25]{0:T(128)S(1)}, s32[25]{0:T(128)}, u32[]{:S(2)}) copy-start(s32[25]{0:T(128)} %constant.68) | copy-start | bytes 304
  15.4 25.6 %copy-start.1 = (bf16[7,64,64]{2,1,0:T(8,128)(2,1)S(1)}, bf16[7,64,64]{2,1,0:T(8,128)(2,1)}, u32[]{:S(2)}) copy-start(bf16[7,64,64]{2,1,0:T(8,128)(2,1)} %param.35) | copy-start | bytes 172036
  16.1 0.6 copy-start.8
  16.7 28.5 %copy-start.18 = (s32[25]{0:T(128)S(1)}, s32[25]{0:T(128)}, u32[]{:S(2)}) copy-start(s32[25]{0:T(128)} %constant.69) | copy-start | bytes 304
  25.3 20.5 %copy-start.9 = (bf16[32,49,64]{2,0,1:T(8,128)(2,1)S(1)}, bf16[32,49,64]{2,0,1:T(8,128)(2,1)}, u32[]{:S(2)}) copy-start(bf16[32,49,64]{2,0,1:T(8,128)(2,1)} %param.21) | copy-start | bytes 602116
  25.4 12.8 %all-to-all-start.1 = ((f32[4,4,3328]{2,1,0:T(4,128)}), f32[4,4,3328]{2,1,0:T(4,128)S(1)}, u32[]{:S(2)}, u32[]{:S(2)}) async-start(f32[4,4,3328]{2,1,0:T(4,128)} %get-tuple-element.26), calls=%async_computation.1 | async-start | bytes 425984 | tf_op jit(solution)/shard_map/all_to_all | solution.py:544
  38.1 8.2 %copy-start.5 = (f32[4,4,3328]{2,1,0:T(4,128)}, f32[4,4,3328]{2,1,0:T(4,128)S(1)}, u32[]{:S(2)}) copy-start(f32[4,4,3328]{2,1,0:T(4,128)S(1)} %all-to-all-done.1.rest_0_) | copy-start | bytes 638980
  38.1 7.1 %collective-permute-start.1 = (f32[4,4,3328]{2,1,0:T(4,128)S(1)}, f32[4,4,3328]{2,1,0:T(4,128)S(1)}, u32[]{:S(2)}, u32[]{:S(2)}) collective-permute-start(f32[4,4,3328]{2,1,0:T(4,128)S(1)} %all-to-all-done.1.rest_0_), channel_id=1, source_target_pairs={{0,2},{1,3},{2,0},{3,1},{4,6},{5,7},{6,4},{7,5},{8,10},{9,11},{10,... | collective-permute-start | bytes 638984 | tf_op jit(solution)/shard_map/ppermute | solution.py:492
  41.6 7.2 %collective-permute-start = (f32[4,4,3328]{2,1,0:T(4,128)S(1)}, f32[4,4,3328]{2,1,0:T(4,128)S(1)}, u32[]{:S(2)}, u32[]{:S(2)}) collective-permute-start(f32[4,4,3328]{2,1,0:T(4,128)S(1)} %all-to-all-done.1.rest_0_), channel_id=1, source_target_pairs={{0,1},{1,0},{2,3},{3,2},{4,5},{5,4},{6,7},{7,6},{8,9},{9,8},{10,11... | collective-permute-start | bytes 638984 | tf_op jit(solution)/shard_map/ppermute | solution.py:492
  45.2 3.6 %copy-start.10 = (f32[4,4,3328]{2,1,0:T(4,128)}, f32[4,4,3328]{2,1,0:T(4,128)S(1)}, u32[]{:S(2)}) copy-start(f32[4,4,3328]{2,1,0:T(4,128)S(1)} %collective-permute-done.1.rest_2_) | copy-start | bytes 638980
  45.2 3.7 %collective-permute-start.2 = (f32[4,4,3328]{2,1,0:T(4,128)S(1)}, f32[4,4,3328]{2,1,0:T(4,128)S(1)}, u32[]{:S(2)}, u32[]{:S(2)}) collective-permute-start(f32[4,4,3328]{2,1,0:T(4,128)S(1)} %collective-permute-done.1.rest_2_), channel_id=1, source_target_pairs={{0,1},{1,0},{2,3},{3,2},{4,5},{5,4},{6,7},{7,6},{8,9},{9,8},{10,11... | collective-permute-start | bytes 638984 | tf_op jit(solution)/shard_map/ppermute | solution.py:492
  48.8 0.7 copy-start.11
  48.8 0.7 copy-start.12
  57.4 11.2 %all-to-all-start.2 = ((bf16[4,4,3328]{2,1,0:T(4,128)(2,1)}), bf16[4,4,3328]{2,1,0:T(4,128)(2,1)S(1)}, u32[]{:S(2)}, u32[]{:S(2)}) async-start(bf16[4,4,3328]{2,1,0:T(4,128)(2,1)} %get-tuple-element.28), calls=%async_computation.2 | async-start | bytes 212992 | tf_op jit(solution)/shard_map/all_to_all | solution.py:544
  68.6 0.6 copy-start.7
  78.4 3.5 %collective-permute-start.6 = (f32[1536,256]{1,0:T(8,128)S(1)}, f32[1536,256]{1,0:T(8,128)S(1)}, u32[]{:S(2)}, u32[]{:S(2)}) collective-permute-start(f32[1536,256]{1,0:T(8,128)S(1)} %dynamic-slice_bitcast_fusion), channel_id=1, source_target_pairs={{0,1},{1,0},{2,3},{3,2},{4,5},{5,4},{6,7},{7,6},{8,9},{9,8},{10,11... | collective-permute-start | bytes 4718600 | tf_op jit(solution)/shard_map/ppermute | solution.py:492
  83.8 19.6 %collective-permute-start.7 = (f32[768,256]{1,0:T(8,128)S(1)}, f32[768,256]{1,0:T(8,128)S(1)}, u32[]{:S(2)}, u32[]{:S(2)}) collective-permute-start(f32[768,256]{1,0:T(8,128)S(1)} %dynamic-slice_bitcast_fusion.1), channel_id=1, source_target_pairs={{0,2},{1,3},{2,0},{3,1},{4,6},{5,7},{6,4},{7,5},{8,10},{9,11},{10,... | collective-permute-start | bytes 2359304 | tf_op jit(solution)/shard_map/ppermute | solution.py:492
  103.6 10.4 %collective-permute-start.8 = (f32[384,256]{1,0:T(8,128)S(1)}, f32[384,256]{1,0:T(8,128)S(1)}, u32[]{:S(2)}, u32[]{:S(2)}) collective-permute-start(f32[384,256]{1,0:T(8,128)S(1)} %dynamic-slice_bitcast_fusion.2), channel_id=1, source_target_pairs={{0,4},{4,0},{8,12},{12,8},{1,5},{5,1},{9,13},{13,9},{2,6},{6,2},{1... | collective-permute-start | bytes 1179656 | tf_op jit(solution)/shard_map/ppermute | solution.py:492
  114.0 10.4 %collective-permute-start.9 = (f32[192,256]{1,0:T(8,128)S(1)}, f32[192,256]{1,0:T(8,128)S(1)}, u32[]{:S(2)}, u32[]{:S(2)}) collective-permute-start(f32[192,256]{1,0:T(8,128)S(1)} %dynamic-slice_bitcast_fusion.3), channel_id=1, source_target_pairs={{0,8},{4,12},{8,0},{12,4},{1,9},{5,13},{9,1},{13,5},{2,10},{6,14},... | collective-permute-start | bytes 589832 | tf_op jit(solution)/shard_map/ppermute | solution.py:492
  124.4 6.3 %collective-permute-start.10 = (bf16[192,256]{1,0:T(8,128)(2,1)S(1)}, bf16[192,256]{1,0:T(8,128)(2,1)S(1)}, u32[]{:S(2)}, u32[]{:S(2)}) collective-permute-start(bf16[192,256]{1,0:T(8,128)(2,1)S(1)} %fusion.7), channel_id=1, source_target_pairs={{0,8},{4,12},{8,0},{12,4},{1,9},{5,13},{9,1},{13,5},{2,10},{6,14},... | collective-permute-start | bytes 294920 | tf_op jit(solution)/shard_map/ppermute | solution.py:492
  130.8 6.6 %collective-permute-start.11 = (bf16[384,256]{1,0:T(8,128)(2,1)S(1)}, bf16[384,256]{1,0:T(8,128)(2,1)S(1)}, u32[]{:S(2)}, u32[]{:S(2)}) collective-permute-start(bf16[384,256]{1,0:T(8,128)(2,1)S(1)} %pad_maximum_fusion.10), channel_id=1, source_target_pairs={{0,4},{4,0},{8,12},{12,8},{1,5},{5,1},{9,13},{13,9},{2,6},{6,2},{1... | collective-permute-start | bytes 589832 | tf_op jit(solution)/shard_map/ppermute | solution.py:492
  137.4 9.9 %collective-permute-start.12 = (bf16[768,256]{1,0:T(8,128)(2,1)S(1)}, bf16[768,256]{1,0:T(8,128)(2,1)S(1)}, u32[]{:S(2)}, u32[]{:S(2)}) collective-permute-start(bf16[768,256]{1,0:T(8,128)(2,1)S(1)} %pad_maximum_fusion.4), channel_id=1, source_target_pairs={{0,2},{1,3},{2,0},{3,1},{4,6},{5,7},{6,4},{7,5},{8,10},{9,11},{10,... | collective-permute-start | bytes 1179656 | tf_op jit(solution)/shard_map/ppermute | solution.py:492
  147.5 34.8 %collective-permute-start.13 = (bf16[1536,256]{1,0:T(8,128)(2,1)S(1)}, bf16[1536,256]{1,0:T(8,128)(2,1)S(1)}, u32[]{:S(2)}, u32[]{:S(2)}) collective-permute-start(bf16[1536,256]{1,0:T(8,128)(2,1)S(1)} %pad_maximum_fusion), channel_id=1, source_target_pairs={{0,1},{1,0},{2,3},{3,2},{4,5},{5,4},{6,7},{7,6},{8,9},{9,8},{10,11... | collective-permute-start | bytes 2359304 | tf_op jit(solution)/shard_map/ppermute | solution.py:492
  166.4 8.5 %copy-start.6 = (f32[4,4,3200]{2,1,0:T(4,128)}, f32[4,4,3200]{2,1,0:T(4,128)S(1)}, u32[]{:S(2)}) copy-start(f32[4,4,3200]{2,1,0:T(4,128)S(1)} %all_to_all.20.rest_0_) | copy-start | bytes 614404
  166.4 5.9 %collective-permute-start.4 = (f32[4,4,3200]{2,1,0:T(4,128)S(1)}, f32[4,4,3200]{2,1,0:T(4,128)}, u32[]{:S(2)}, u32[]{:S(2)}) collective-permute-start(f32[4,4,3200]{2,1,0:T(4,128)S(1)} %all_to_all.20.rest_0_), channel_id=1, source_target_pairs={{0,2},{1,3},{2,0},{3,1},{4,6},{5,7},{6,4},{7,5},{8,10},{9,11},{10,... | collective-permute-start | bytes 614408 | tf_op jit(solution)/shard_map/ppermute | solution.py:492
  167.9 7.0 %collective-permute-start.3 = (f32[4,4,3200]{2,1,0:T(4,128)S(1)}, f32[4,4,3200]{2,1,0:T(4,128)}, u32[]{:S(2)}, u32[]{:S(2)}) collective-permute-start(f32[4,4,3200]{2,1,0:T(4,128)S(1)} %all_to_all.20.rest_0_), channel_id=1, source_target_pairs={{0,1},{1,0},{2,3},{3,2},{4,5},{5,4},{6,7},{7,6},{8,9},{9,8},{10,11... | collective-permute-start | bytes 614408 | tf_op jit(solution)/shard_map/ppermute | solution.py:492
  172.3 2.6 %collective-permute-start.5 = (f32[4,4,3200]{2,1,0:T(4,128)}, f32[4,4,3200]{2,1,0:T(4,128)}, u32[]{:S(2)}, u32[]{:S(2)}) collective-permute-start(f32[4,4,3200]{2,1,0:T(4,128)} %collective-permute-done.4.rest_2_), channel_id=1, source_target_pairs={{0,1},{1,0},{2,3},{3,2},{4,5},{5,4},{6,7},{7,6},{8,9},{9,8},{10,11... | collective-permute-start | bytes 614408 | tf_op jit(solution)/shard_map/ppermute | solution.py:492
where the time goes:
time: 189 us; the launch traced here: 188 us
  waiting for transfers between devices  75.7 us (40%)
  Pallas kernels  35.9 us (19%)
  starting transfers between devices  25 us (13%)
  local copies, waits for them, and re-layouts  22.9 us (12%)
  blocking collectives  17.5 us (9%)
  other arithmetic  10.1 us (5%)
    ppermute x14, waiting for transfers between devices, swap(): return lax.ppermute(value, axis, [(i, i ^ 1 << bit) for i in range(size)])  69.2 us
    pallas_call x5, Pallas kernels, call(): pl.pallas_call(kernel, out_shape=[jax.ShapeDtypeStruct(shape, kind) for s...  35.9 us
    all_to_all x3, starting transfers between devices, exchange(): lax.all_to_all(value, 'graph', split_axis=0, concat_axis=0, tiled=True)  16.6 us
    all_to_all x1, blocking collectives, exchange(): lax.all_to_all(value, 'graph', split_axis=0, concat_axis=0, tiled=True)  12.4 us
    unnamed x51, local copies, waits for them, and re-layouts  9.05 us
    ppermute x14, starting transfers between devices, swap(): return lax.ppermute(value, axis, [(i, i ^ 1 << bit) for i in range(size)])  8.32 us
    all_to_all x3, waiting for transfers between devices, exchange(): lax.all_to_all(value, 'graph', split_axis=0, concat_axis=0, tiled=True)  6.52 us
    all_gather x1, blocking collectives, shards(): lax.all_gather(jnp.stack([send_list.reshape(-1), recv_list.reshape(-1)]),...  5.07 us
  transfers between devices with their start and end apart: 17, of which 11 were waited for; matrix products, arithmetic and copies ran while one was open for 10% of the time, Pallas kernels for 6%

commit v1 on v0

--- a/solution.py
+++ b/solution.py
@@ -157,25 +157,48 @@
     return emit
 
 
+def listed_rows(list_ref, shape):
+    peers, cap = list_ref.shape[1], list_ref.shape[3]
+    row = iota(shape, 0)
+    result = jnp.zeros(shape, jnp.int32)
+    for slot in range(peers * cap):
+        result = jnp.where(row == slot, list_ref[0, slot // cap, 0, slot % cap], result)
+    return result
+
+
+def outgoing_kernel(send, recv, embed, out):
+    atoms = embed.shape[0]
+    slots = out.shape[0] * out.shape[1]
+    sent = listed_rows(send, (slots, LANES))
+    received = listed_rows(recv, (slots, LANES))
+    picked = mask_to(iota((slots, atoms), 1) == sent[:, :atoms], bf16)
+    put_rows(out, pl.ds(0, FLAT), dot_nn(picked, embed[...]))
+    lane = iota((slots, LANES), 1)
+    put_rows(out, pl.ds(FLAT, COLS - FLAT), jnp.zeros((slots, COLS - FLAT), f32))
+    side = jnp.where(lane == 0, received, jnp.where(lane == 1, sent, 0))
+    put_rows(out, pl.ds(COLS, LANES), side.astype(f32))
+
+
+def swapped_halves(value, edges):
+    return jnp.concatenate([-value[:, edges:], value[:, :edges]], axis=1)
+
+
 def forward_kernel(
     table, source_slot, target_slot, rot, feats, bias, wzero, wone, wtwo, ain, aedge, adot,
-    sums_out, x0, x1, x2, v0, v1, v2, pre_out, logit_out,
-    rows, gathered, neg1, neg2, weights, terms,
+    sums_out, x0, x1, x2, v0, v1, v2, pre_out, logit_out, lists_out,
+    rows, gathered, weights, terms,
 ):
     edges = source_slot.shape[1]
     slots = table.shape[0] * table.shape[1]
     stack_table(table, rows)
     picked = mask_to(one_hot_rows(source_slot, slots), bf16)
-    gathered[...] = dot_tn(rows[...].astype(bf16), picked)
+    gathered[...] = dot_tn(rows[:, pl.ds(0, FLAT)].astype(bf16), picked)
+    lists = rows[:, pl.ds(COLS, LANES)]
+    lists_out[...] = lists
 
     def emit(degree, order, half, value):
         ref, row, second = frame_place(degree, order, (x0, x1, x2))
-        value = value.astype(bf16)
-        ref[pl.ds(row, CH), lane_at(half, edges, second)] = value
-        if order != 0:
-            neg = (None, neg1, neg2)[abs(order)]
-            swapped = value if order > 0 else -value
-            neg[pl.ds(row, CH), lane_at(half, edges, not second)] = swapped
+        ref[pl.ds(row, CH), lane_at(half, edges, second)] = value.astype(bf16)
 
     to_frame(gathered, rot, edges, emit)
 
@@ -184,7 +207,7 @@
     hidden = jnp.where(pre > 0, pre, leak_slope * pre) * adot[...]
     aims = one_hot_rows(target_slot, slots)
     lane = iota((slots, LANES), 1)
-    side = jnp.zeros((slots, LANES), f32)
+    side = jnp.where(lane == 2 * HEADS, lists[:, :1], 0.0)
     for h in range(HEADS):
         logit = jnp.sum(hidden[h * ALPHA : (h + 1) * ALPHA], axis=0, keepdims=True)
         logit = logit + bias[pl.ds(h, 1), :]
@@ -198,8 +221,8 @@
     put_rows(sums_out, pl.ds(COLS, LANES), side)
 
     v0[...] = dot_nn(wzero[...], x0[...])
-    v1[...] = dot_nn(wone[0], x1[...]) + dot_nn(wone[1], neg1[...])
-    v2[...] = dot_nn(wtwo[0], x2[...]) + dot_nn(wtwo[1], neg2[...])
+    for out, weight, value in ((v1, wone, x1[...]), (v2, wtwo, x2[...])):
+        out[...] = dot_nn(weight[0], value) + swapped_halves(dot_nn(weight[1], value), edges)
 
     def load(degree, order, half):
         ref, row, second = frame_place(degree, order, (v0, v1, v2))
@@ -235,18 +258,38 @@
             rows_ref[at, :] = jnp.concatenate(parts, axis=0)
 
 
+def pair_weight(out_proj, block):
+    first = out_proj[degree_of(2 * block)]
+    if 2 * block + 1 >= COEFFS:
+        return first
+    second = out_proj[degree_of(2 * block + 1)]
+    blank = jnp.zeros((CH, CH), f32)
+    top = jnp.concatenate([first.astype(f32), blank], axis=1)
+    low = jnp.concatenate([blank, second.astype(f32)], axis=1)
+    return jnp.concatenate([top, low], axis=0).astype(bf16)
+
+
+def pair_key(block):
+    return degree_of(2 * block), min(degree_of(min(2 * block + 1, COEFFS)), LMAX)
+
+
+def block_cols(block):
+    return pl.ds(block * LANES, min(LANES, FLAT - block * LANES))
+
+
 def make_finish(lanes_total):
-    def finish_kernel(place, index_row, index_col, own_col, cot, pairs, *rest):
+    def finish_kernel(place, cot, out_proj, *rest):
         arrivals = rest[:lanes_total]
-        out, back, proj, rows, num, num_grad = rest[lanes_total:]
+        agg_out, back, rows, terms, num_grad = rest[lanes_total:]
         atoms = cot.shape[0]
-        total = index_row.shape[1]
-        slots = own_col.shape[0]
+        slots = back.shape[0] * back.shape[1]
+        total = lanes_total * slots
         collect_rows(place, arrivals, rows)
         side = rows[:, pl.ds(COLS, LANES)]
-        names = iota((total, atoms), 1) == index_col[...]
-        picked = mask_to(iota((atoms, total), 0) == index_row[...], bf16)
-        own = iota((slots, atoms), 1) == own_col[...]
+        at_atom = iota((total, atoms), 1).astype(f32)
+        names = at_atom == side[:, 2 * HEADS : 2 * HEADS + 1]
+        own_side = jnp.concatenate([arrivals[0][g][:, COLS:] for g in range(back.shape[0])], axis=0)
+        own = at_atom[:slots] == own_side[:, 2 * HEADS : 2 * HEADS + 1]
         eye = iota((atoms, atoms), 0) == iota((atoms, atoms), 1)
         scales, dens, own_peaks = [], [], []
         for h in range(HEADS):
@@ -261,45 +304,35 @@
             own_peaks.append(jnp.sum(jnp.where(own, peak, 0.0), axis=1, keepdims=True))
         scale_full = lane_heads(scales, (total, LANES))
         den_full = lane_heads(dens, (atoms, LANES))
-        twice = jnp.concatenate([picked, picked], axis=1)
-
-        def gather_block(block, carry):
-            cols = pl.ds(pl.multiple_of(block * LANES, LANES), LANES)
-            high, low = split_two(rows[:, cols] * scale_full)
-            num[:, cols] = dot_nn(twice, jnp.concatenate([high, low], axis=0))
-            return carry
-
-        lax.fori_loop(0, BLOCKS, gather_block, 0)
-
-        den_sum = jnp.zeros((atoms, LANES), f32)
-        tops = [None] * (LMAX + 1)
-        lows = [None] * (LMAX + 1)
+        picked = mask_to(names, bf16)
+        twice = jnp.concatenate([picked, picked], axis=0)
         for block in range(BLOCKS):
             cols = pl.ds(block * LANES, LANES)
-            agg = num[:, cols] / den_full
-            agg_low = agg.astype(bf16)
-            cot_block = cot[:, cols]
-            weight = pairs[block]
-            out[:, cols] = dot_nn(agg_low, weight).astype(bf16)
-            agg_grad = dot_nt(cot_block, weight)
-            num_grad[:, cols] = (agg_grad / den_full).astype(bf16)
-            den_sum = den_sum + agg_grad * agg
-            outer = dot_tn(agg_low, cot_block)
-            first = degree_of(2 * block)
-            tops[first] = outer[:CH] if tops[first] is None else tops[first] + outer[:CH]
-            if 2 * block + 1 < COEFFS:
-                second = degree_of(2 * block + 1)
-                lows[second] = outer[CH:] if lows[second] is None else lows[second] + outer[CH:]
-        for degree in range(LMAX + 1):
-            piece = jnp.zeros((CH, CH), f32)
-            if tops[degree] is not None:
-                piece = piece + tops[degree][:, :CH]
-            if lows[degree] is not None:
-                piece = piece + lows[degree][:, CH:]
-            proj[pl.ds(degree * CH, CH), :] = piece * (1.0 / lanes_total)
+            high, low = split_two(rows[:, cols] * scale_full)
+            terms[pl.ds(0, total), cols] = high
+            terms[pl.ds(total, total), cols] = low
+
+        den_sum = jnp.zeros((atoms, LANES), f32)
+        weights = {}
+        for block in range(BLOCKS):
+            cols = block_cols(block)
+            width = cols.size
+            agg = dot_tn(twice, terms[:, cols]) / den_full[:, :width]
+            agg_out[:, cols] = agg.astype(bf16)
+            key = pair_key(block)
+            if key not in weights:
+                weights = {key: pair_weight(out_proj, block)}
+            weight = weights[key] if width == LANES else out_proj[LMAX]
+            agg_grad = dot_nt(cot[:, cols], weight)
+            num_grad[:, cols] = (agg_grad / den_full[:, :width]).astype(bf16)
+            product = agg_grad * agg
+            if width < LANES:
+                product = jnp.concatenate([product, jnp.zeros_like(product)], axis=1)
+            den_sum = den_sum + product
 
         own_low = mask_to(own, bf16)
-        put_rows(back, pl.ds(0, COLS), dot_nn(own_low, num_grad[...]))
+        put_rows(back, pl.ds(0, FLAT), dot_nn(own_low, num_grad[...]))
+        put_rows(back, pl.ds(FLAT, COLS - FLAT), jnp.zeros((slots, COLS - FLAT), f32))
         head = (iota((atoms, LANES), 1) % CH) // VAL
         lane = iota((slots, LANES), 1)
         extra = jnp.zeros((slots, LANES), f32)
@@ -318,10 +351,43 @@
     return finish_kernel
 
 
+def make_project(lanes_total):
+    def project_kernel(agg_low, cot, out_proj, out, proj):
+        tops = [None] * (LMAX + 1)
+        lows = [None] * (LMAX + 1)
+        weights = {}
+        for block in range(BLOCKS):
+            cols = block_cols(block)
+            width = cols.size
+            left, right = agg_low[:, cols], cot[:, cols]
+            key = pair_key(block)
+            if key not in weights:
+                weights = {key: pair_weight(out_proj, block)}
+            weight = weights[key] if width == LANES else out_proj[LMAX]
+            out[:, cols] = dot_nn(left, weight).astype(bf16)
+            outer = dot_tn(left, right)
+            first = degree_of(2 * block)
+            top = outer[:CH, :CH]
+            tops[first] = top if tops[first] is None else tops[first] + top
+            if width == LANES:
+                second = degree_of(2 * block + 1)
+                low = outer[CH:]
+                lows[second] = low if lows[second] is None else lows[second] + low
+        for degree in range(LMAX + 1):
+            piece = jnp.zeros((CH, CH), f32)
+            if tops[degree] is not None:
+                piece = piece + tops[degree]
+            if lows[degree] is not None:
+                piece = piece + lows[degree][:, CH:]
+            proj[pl.ds(degree * CH, CH), :] = piece * (1.0 / lanes_total)
+
+    return project_kernel
+
+
 def gradient_kernel(
-    table, target_slot, rot, feats, x0, x1, x2, v0, v1, v2, pre, logits, adot, proj,
-    packed, g0, g1, g2, pre_grad_out,
-    rows, spread_grad, weights,
+    place, table, target_slot, rot, feats, x0, x1, x2, v0, v1, v2, pre, logits, adot, proj,
+    g0, top1, top2, pre_grad_out, kept0, sent0, kept1, sent1, kept2, sent2,
+    rows, spread_grad, weights, g1, g2, packed, semaphores,
 ):
     edges = target_slot.shape[1]
     slots = table.shape[0] * table.shape[1]
@@ -374,72 +440,124 @@
     pre_grad_out[...] = pre_grad
     dot_grad = jnp.sum(tall * hidden, axis=1, keepdims=True)
 
+    top1[...] = g1[pl.ds(0, DIM1), :]
+    top2[...] = g2[pl.ds(0, DIM2), :]
+    mine = place[0] & 1
+    copies = []
+
+    def put(row, value, at=0):
+        for side in range(2):
+            low, high = max(at, side * LANES), min(at + value.shape[1], (side + 1) * LANES)
+            if low < high:
+                piece = value[:, low - at : high - at]
+                cols = pl.ds(low - side * LANES, high - low)
+                packed[side, pl.ds(row, value.shape[0]), cols] = piece
+
+    def send(chunk, kept, sent):
+        start, size = CHUNKS[chunk]
+        rows_of = pl.ds(start, size)
+        for n, (side, out) in enumerate(((mine, kept), (1 - mine, sent))):
+            copy = pltpu.make_async_copy(
+                packed.at[side, rows_of, :], out, semaphores.at[2 * chunk + n]
+            )
+            copy.start()
+            copies.append(copy)
+
+    row = CHUNKS[1][0]
+    for start in range(0, 2 * DIM1, PANEL):
+        put(row, dot_nt(x1[...], g1[pl.ds(start, PANEL), :]))
+        row += DIM1
+    send(1, kept1, sent1)
+
     row = 0
     for start in range(0, DIM0, PANEL):
         size = min(PANEL, DIM0 - start)
-        packed[pl.ds(row, DIM0), pl.ds(0, size)] = dot_nt(x0[...], g0[pl.ds(start, size), :])
+        put(row, dot_nt(x0[...], g0[pl.ds(start, size), :]))
         if size < PANEL:
-            packed[pl.ds(row, DIM0), pl.ds(size, CH)] = proj[...]
+            put(row, proj[...], size)
         row += DIM0
-    for left, right, dim in ((x1, g1, DIM1), (x2, g2, DIM2)):
-        for start in range(0, 2 * dim, PANEL):
-            size = min(PANEL, 2 * dim - start)
-            packed[pl.ds(row, dim), pl.ds(0, size)] = dot_nt(left[...], right[pl.ds(start, size), :])
-            row += dim
+    send(0, kept0, sent0)
+
+    row = CHUNKS[2][0]
+    for start in range(0, 2 * DIM2, PANEL):
+        size = min(PANEL, 2 * DIM2 - start)
+        put(row, dot_nt(x2[...], g2[pl.ds(start, size), :]))
+        row += DIM2
     row -= DIM2
-    half = pl.ds(LANES, LANES)
     edge_ch = feats.shape[1]
     edge_grad = lax.dot_general(
         feats[...], pre_grad, (((0,), (1,)), ((), ())), preferred_element_type=f32
     )
-    packed[pl.ds(row, edge_ch), half] = edge_grad[:, :LANES]
-    packed[pl.ds(row + edge_ch, edge_ch), half] = edge_grad[:, LANES:]
+    put(row, edge_grad[:, :LANES], LANES)
+    put(row + edge_ch, edge_grad[:, LANES:], LANES)
     wide_dot = jnp.transpose(jnp.broadcast_to(dot_grad, (HEADS * ALPHA, LANES)))
     spare = DIM2 - 2 * edge_ch
     tail = iota((spare, LANES), 0)
     first = jnp.broadcast_to(wide_dot[:1, :LANES], (spare, LANES))
     second = jnp.broadcast_to(wide_dot[:1, LANES:], (spare, LANES))
-    packed[pl.ds(row + 2 * edge_ch, spare), half] = jnp.where(
-        tail == 0, first, jnp.where(tail == 1, second, 0.0)
-    )
+    put(row + 2 * edge_ch, jnp.where(tail == 0, first, jnp.where(tail == 1, second, 0.0)), LANES)
     row += DIM2
-    packed[pl.ds(row, CH), :] = dot_nt(x0[pl.ds(0, CH), :], pre_grad)
-
-
-PACKED_ROWS = 2 * DIM0 + 3 * DIM1 + 3 * DIM2 + CH
-
-
-def unpack(packed, edge_ch):
-    row = 0
-    panels = []
-    for dim, count in ((DIM0, 2), (DIM1, 3), (DIM2, 3)):
-        for _ in range(count):
-            panels.append(packed[row : row + dim])
-            row += dim
-    rest = DIM0 - PANEL
-    zero = jnp.concatenate([panels[0], panels[1][:, :rest]], axis=1)
-    proj = panels[1][:, rest:].reshape(LMAX + 1, CH, CH)
-    one = jnp.concatenate(panels[2:5], axis=1)
-    one = jnp.stack([one[:, :DIM1], one[:, DIM1:]])
-    two = jnp.concatenate(panels[5:7] + [panels[7][:, :LANES]], axis=1)
-    two = jnp.stack([two[:, :DIM2], two[:, DIM2:]])
-    half = panels[7][:, LANES:]
-    alpha_edge = jnp.concatenate([half[:edge_ch], half[edge_ch : 2 * edge_ch]], axis=1)
-    alpha_dot = half[2 * edge_ch : 2 * edge_ch + 2].reshape(-1)
-    alpha_in = packed[row : row + CH]
-    return zero, one, two, alpha_in, alpha_edge, alpha_dot, proj
+    put(row, dot_nt(x0[pl.ds(0, CH), :], pre_grad))
+    send(2, kept2, sent2)
+    for copy in copies:
+        copy.wait()
+
+
+CHUNKS = ((0, 2 * DIM0), (2 * DIM0, 3 * DIM1), (2 * DIM0 + 3 * DIM1, 3 * DIM2 + CH))
+PACKED_ROWS = sum(size for start, size in CHUNKS)
+
+
+def halves_of(place, mine, other):
+    first = (place[0] & 1) == 0
+    left, right = mine[...].astype(f32), other[...].astype(f32)
+    return jnp.where(first, left, right), jnp.where(first, right, left)
+
+
+def unpack_zero_kernel(place, mine, other, zero, proj):
+    left, right = halves_of(place, mine, other)
+    zero[:, pl.ds(0, LANES)] = left[:DIM0].astype(bf16)
+    zero[:, pl.ds(LANES, LANES)] = right[:DIM0].astype(bf16)
+    zero[:, pl.ds(2 * LANES, LANES)] = left[DIM0:].astype(bf16)
+    zero[:, pl.ds(3 * LANES, DIM0 - 3 * LANES)] = right[DIM0:, : DIM0 - 3 * LANES].astype(bf16)
+    for degree in range(LMAX + 1):
+        start = DIM0 + degree * CH
+        proj[degree] = right[start : start + CH, DIM0 - 3 * LANES :].astype(bf16)
+
+
+def unpack_one_kernel(place, mine, other, one):
+    left, right = halves_of(place, mine, other)
+    for n in range(2 * DIM1 // LANES):
+        panel = (left, right)[n % 2][(n // 2) * DIM1 : (n // 2 + 1) * DIM1]
+        per = DIM1 // LANES
+        one[n // per, :, pl.ds((n % per) * LANES, LANES)] = panel.astype(bf16)
+
+
+def unpack_two_kernel(place, mine, other, two, alpha_in, alpha_edge, alpha_dot):
+    left, right = halves_of(place, mine, other)
+    panels = [(left, right)[n % 2][(n // 2) * DIM2 : (n // 2 + 1) * DIM2] for n in range(5)]
+    whole = jnp.concatenate(panels, axis=1)
+    two[0] = whole[:, :DIM2].astype(bf16)
+    two[1] = whole[:, DIM2:].astype(bf16)
+    edge_ch = alpha_edge.shape[0]
+    rest = right[2 * DIM2 : 3 * DIM2]
+    alpha_edge[:, pl.ds(0, LANES)] = rest[:edge_ch].astype(bf16)
+    alpha_edge[:, pl.ds(LANES, LANES)] = rest[edge_ch : 2 * edge_ch].astype(bf16)
+    alpha_dot[...] = rest[2 * edge_ch : 2 * edge_ch + 2].astype(bf16)
+    alpha_in[:, pl.ds(0, LANES)] = left[3 * DIM2 :].astype(bf16)
+    alpha_in[:, pl.ds(LANES, LANES)] = right[3 * DIM2 :].astype(bf16)
 
 
 def source_kernel(
-    source_slot, rot, g0, g1, g2, pre_grad, wzero, wone, wtwo, ain,
-    sums_out, d0, d1, d2, terms,
+    source_slot, lists, rot, g0, g1, g2, pre_grad, wzero, wone, wtwo, ain,
+    *rest,
 ):
+    sums_out, d0, d1, d2, terms = rest[-5:]
     edges = source_slot.shape[1]
     slots = sums_out.shape[0] * sums_out.shape[1]
     d0[...] = dot_nn(wzero[...], g0[...])
     d0[pl.ds(0, CH), :] += dot_nn(ain[...], pre_grad[...])
-    d1[...] = dot_nn(wone[0], g1[pl.ds(0, DIM1), :]) + dot_nn(wone[1], g1[pl.ds(DIM1, DIM1), :])
-    d2[...] = dot_nn(wtwo[0], g2[pl.ds(0, DIM2), :]) + dot_nn(wtwo[1], g2[pl.ds(DIM2, DIM2), :])
+    for out, weight, value in ((d1, wone, g1[...]), (d2, wtwo, g2[...])):
+        out[...] = dot_nn(weight[0], value) - swapped_halves(dot_nn(weight[1], value), edges)
 
     def load(degree, order, half):
         ref, row, second = frame_place(degree, order, (d0, d1, d2))
@@ -448,43 +566,48 @@
     terms[pl.ds(FLAT, COLS - FLAT), :] = jnp.zeros((COLS - FLAT, 2 * edges), bf16)
     from_frame(load, rot, edges, store_terms(terms, edges))
     slot_sums(terms, mask_to(one_hot_rows(source_slot, slots), bf16), sums_out)
+    put_rows(sums_out, pl.ds(COLS, LANES), lists[...])
 
 
 def make_collect(lanes_total):
-    def collect_kernel(place, index_row, *rest):
+    def collect_kernel(place, *rest):
         arrivals = rest[:lanes_total]
         out, rows = rest[lanes_total:]
         atoms = out.shape[0]
-        total = index_row.shape[1]
+        total = rows.shape[0]
         collect_rows(place, arrivals, rows)
-        picked = mask_to(iota((atoms, total), 0) == index_row[...], bf16)
-        twice = jnp.concatenate([picked, picked], axis=1)
-
-        def gather_block(block, carry):
-            cols = pl.ds(pl.multiple_of(block * LANES, LANES), LANES)
+        index = rows[:, pl.ds(COLS, LANES)][:, 1:2]
+        picked = mask_to(iota((total, atoms), 1).astype(f32) == index, bf16)
+        twice = jnp.concatenate([picked, picked], axis=0)
+        for block in range(BLOCKS):
+            cols = block_cols(block)
             high, low = split_two(rows[:, cols])
-            out[:, cols] = dot_nn(twice, jnp.concatenate([high, low], axis=0)).astype(bf16)
-            return carry
-
-        lax.fori_loop(0, BLOCKS, gather_block, 0)
+            out[:, cols] = dot_tn(twice, jnp.concatenate([high, low], axis=0)).astype(bf16)
 
     return collect_kernel
 
 
 vmem = pl.BlockSpec(memory_space=pltpu.VMEM)
 smem = pl.BlockSpec(memory_space=pltpu.SMEM)
-
-
-def call(kernel, outs, scratch, *args, scalar=False):
-    specs = [smem if scalar and n == 0 else vmem for n in range(len(args))]
+anywhere = pl.BlockSpec(memory_space=pl.ANY)
+
+
+def call(kernel, outs, scratch, *args, scalars=0, apart=0, after=(), work=4):
+    specs = [smem if n < scalars else vmem for n in range(len(args))] + [anywhere] * len(after)
+    out_specs = [vmem if n < len(outs) - apart else anywhere for n in range(len(outs))]
+    shapes = [pltpu.VMEM(*entry) if isinstance(entry, tuple) else entry for entry in scratch]
+    moved = sum(int(np.prod(a.shape)) * a.dtype.itemsize for a in args)
     return pl.pallas_call(
         kernel,
         out_shape=[jax.ShapeDtypeStruct(shape, kind) for shape, kind in outs],
         in_specs=specs,
-        out_specs=[vmem] * len(outs),
-        scratch_shapes=[pltpu.VMEM(shape, kind) for shape, kind in scratch],
+        out_specs=out_specs,
+        scratch_shapes=shapes,
         compiler_params=pltpu.CompilerParams(vmem_limit_bytes=VMEM_LIMIT),
-    )(*args)
+        cost_estimate=pl.CostEstimate(
+            flops=work * 10**9, bytes_accessed=moved, transcendentals=0
+        ),
+    )(*args, *after)
 
 
 def swap(value, axis, bit):
@@ -507,15 +630,14 @@
     return (lax.axis_index(axis) >> bit) & 1
 
 
-def sum_all(packed):
-    steps = [("edge", n) for n in range(bits_of("edge"))]
+def sum_all(current):
+    steps = [("edge", n) for n in range(1, bits_of("edge"))]
     steps += [("graph", n) for n in range(bits_of("graph"))]
-    current = packed
     for axis, bit in steps:
         mine = own_bit(axis, bit)
         parts = current.reshape(2, current.shape[0] // 2, -1)
-        sent = swap(lax.dynamic_index_in_dim(parts, 1 - mine, 0, False), axis, bit)
-        current = lax.dynamic_index_in_dim(parts, mine, 0, False) + sent
+        other = swap(lax.dynamic_index_in_dim(parts, 1 - mine, 0, False), axis, bit)
+        current = lax.dynamic_index_in_dim(parts, mine, 0, False) + other
     current = current.astype(bf16)
     for axis, bit in reversed(steps):
         mine = own_bit(axis, bit)
@@ -523,7 +645,7 @@
         current = jnp.concatenate(
             [jnp.where(mine == 0, current, other), jnp.where(mine == 0, other, current)], axis=0
         )
-    return current
+    return current, swap(current, "edge", 0)
 
 
 def shards(
@@ -535,15 +657,18 @@
     lanes_total = lax.axis_size("edge")
     atoms = atom_embed.shape[0]
     edges = rotation.shape[0]
-    send_list = send_rows.reshape(peers, -1)
-    recv_list = recv_rows.reshape(peers, -1)
-    cap = send_list.shape[1]
+    cap = send_rows.shape[3]
     slots = peers * cap
+    place = lax.axis_index("edge").astype(jnp.int32).reshape(1)
 
     def exchange(value):
         return lax.all_to_all(value, "graph", split_axis=0, concat_axis=0, tiled=True)
 
-    outgoing = atom_embed[send_list].reshape(peers, cap, FLAT)
+    (outgoing,) = call(
+        outgoing_kernel, [((peers, cap, WIDE), bf16)], [],
+        send_rows, recv_rows, atom_embed.reshape(atoms, FLAT),
+        scalars=2, work=1,
+    )
     table = exchange(outgoing)
 
     source_row = source_slot.reshape(1, edges)
@@ -551,22 +676,9 @@
     rot = rotation.T.astype(f32)
     bias = edge_bias.T
     adot = alpha_dot.astype(f32).reshape(-1, 1)
-    cot = jnp.pad(out_cotangent.reshape(atoms, FLAT), ((0, 0), (0, COLS - FLAT)))
-    degrees = np.array([degree_of(k) for k in range(COEFFS)] + [LMAX], np.int32)
-    blank = jnp.zeros((BLOCKS, CH, CH), bf16)
-    pairs = jnp.concatenate(
-        [
-            jnp.concatenate([out_proj[degrees[0::2]], blank], axis=2),
-            jnp.concatenate([blank, out_proj[degrees[1::2]]], axis=2),
-        ],
-        axis=1,
-    )
-    lists = lax.all_gather(jnp.stack([send_list.reshape(-1), recv_list.reshape(-1)]), "edge")
-    send_all = lists[:, 0].reshape(-1)
-    recv_all = lists[:, 1].reshape(-1)
-    place = lax.axis_index("edge").astype(jnp.int32).reshape(1)
-
-    sums, x0, x1, x2, v0, v1, v2, pre, logits = call(
+    cot = out_cotangent.reshape(atoms, FLAT)
+
+    sums, x0, x1, x2, v0, v1, v2, pre, logits, lists = call(
         forward_kernel,
         [
             ((peers, cap, WIDE), f32),
@@ -578,69 +690,109 @@
             ((DIM2, 2 * edges), f32),
             ((HEADS * ALPHA, edges), f32),
             ((8, edges), f32),
+            ((slots, LANES), f32),
         ],
         [
-            ((slots, FLAT), f32),
+            ((slots, WIDE), f32),
             ((FLAT, edges), f32),
-            ((DIM1, 2 * edges), bf16),
-            ((DIM2, 2 * edges), bf16),
             ((8, edges), f32),
             ((COLS, 2 * edges), bf16),
         ],
         table, source_row, target_row, rot, edge_feats, bias,
         conv_zero.T, jnp.swapaxes(conv_one, 1, 2), jnp.swapaxes(conv_two, 1, 2),
         alpha_in.T, alpha_edge.T, adot,
+        work=8,
     )
 
     arrivals = gather_lanes(exchange(sums))
     total = lanes_total * slots
-    out, back, proj = call(
+    agg_low, back = call(
         make_finish(lanes_total),
-        [((atoms, COLS), bf16), ((peers, cap, WIDE), bf16), (((LMAX + 1) * CH, CH), f32)],
-        [((total, WIDE), f32), ((atoms, COLS), f32), ((atoms, COLS), bf16)],
-        place, recv_all.reshape(1, -1), recv_all.reshape(-1, 1), recv_list.reshape(-1, 1),
-        cot, pairs, *arrivals,
-        scalar=True,
-    )
-
-    packed, g0, g1, g2, pre_grad = call(
+        [((atoms, FLAT), bf16), ((peers, cap, WIDE), bf16)],
+        [((total, WIDE), f32), ((2 * total, COLS), bf16), ((atoms, FLAT), bf16)],
+        place, cot, out_proj, *arrivals,
+        scalars=1,
+    )
+    out, proj = call(
+        make_project(lanes_total),
+        [((atoms, FLAT), bf16), (((LMAX + 1) * CH, CH), f32)],
+        [],
+        agg_low, cot, out_proj,
+    )
+
+    halves = [((size, LANES), f32) for start, size in CHUNKS for _ in range(2)]
+    g0, g1, g2, pre_grad, *halves = call(
         gradient_kernel,
         [
-            ((PACKED_ROWS, PANEL), f32),
             ((DIM0, edges), bf16),
+            ((DIM1, 2 * edges), bf16),
+            ((DIM2, 2 * edges), bf16),
+            ((HEADS * ALPHA, edges), bf16),
+        ]
+        + halves,
+        [
+            ((slots, WIDE), f32),
+            ((COLS, edges), f32),
+            ((8, edges), f32),
             ((2 * DIM1, 2 * edges), bf16),
             ((2 * DIM2, 2 * edges), bf16),
-            ((HEADS * ALPHA, edges), bf16),
+            ((2, PACKED_ROWS, LANES), f32),
+            pltpu.SemaphoreType.DMA((len(halves),)),
         ],
-        [((slots, WIDE), f32), ((COLS, edges), f32), ((8, edges), f32)],
-        exchange(back), target_row, rot, edge_feats, x0, x1, x2, v0, v1, v2, pre, logits, adot,
-        proj,
-    )
-    grads = sum_all(packed)
-
+        place, exchange(back), target_row, rot, edge_feats,
+        x0, x1, x2, v0, v1, v2, pre, logits, adot, proj,
+        scalars=1, apart=len(halves), work=8,
+    )
+    currents = [
+        halves[2 * n] + swap(halves[2 * n + 1], "edge", 0) for n in range(len(CHUNKS))
+    ]
     (source_sums,) = call(
         source_kernel,
-        [((peers, cap, COLS), f32)],
+        [((peers, cap, WIDE), f32)],
         [
             ((DIM0, edges), f32),
             ((DIM1, 2 * edges), f32),
             ((DIM2, 2 * edges), f32),
             ((COLS, 2 * edges), bf16),
         ],
-        source_row, rot, g0, g1, g2, pre_grad, conv_zero, conv_one, conv_two, alpha_in,
+        source_row, lists, rot, g0, g1, g2, pre_grad, conv_zero, conv_one, conv_two, alpha_in,
+        after=currents, work=6,
     )
     (embed,) = call(
         make_collect(lanes_total),
-        [((atoms, COLS), bf16)],
-        [((total, COLS), f32)],
-        place, send_all.reshape(1, -1), *gather_lanes(exchange(source_sums)),
-        scalar=True,
+        [((atoms, FLAT), bf16)],
+        [((total, WIDE), f32)],
+        place, *gather_lanes(exchange(source_sums)),
+        scalars=1,
+    )
+
+    pairs = [sum_all(current) for current in currents]
+    zero, proj_grad = call(
+        unpack_zero_kernel,
+        [((DIM0, DIM0), bf16), ((LMAX + 1, CH, CH), bf16)],
+        [], place, *pairs[0], scalars=1, work=1,
+    )
+    (one,) = call(
+        unpack_one_kernel, [((2, DIM1, DIM1), bf16)], [], place, *pairs[1], scalars=1, work=1
+    )
+    two, grad_in, grad_edge, grad_dot = call(
+        unpack_two_kernel,
+        [
+            ((2, DIM2, DIM2), bf16),
+            (alpha_in.shape, bf16),
+            (alpha_edge.shape, bf16),
+            ((2, LANES), bf16),
+        ],
+        [], place, *pairs[2], scalars=1, work=1,
     )
 
     def shaped(rows):
-        return rows[:, :FLAT].reshape(atoms, COEFFS, CH)
-
-    return (shaped(out), shaped(embed)) + unpack(grads, edge_feats.shape[1])
+        return rows.reshape(atoms, COEFFS, CH)
+
+    return (
+        shaped(out), shaped(embed), zero, one, two, grad_in, grad_edge, grad_dot.reshape(-1),
+        proj_grad,
+    )
 
 
 def solution(mesh):

time: 189 us -> 151 us (0.80)
  waiting for transfers between devices: 75.7 us -> 34.8 us
  starting transfers between devices: 25 us -> 42.4 us
  other arithmetic: 10.1 us -> 1.45 us
  local copies, waits for them, and re-layouts: 22.9 us -> 17.9 us
  blocking collectives: 17.5 us -> 12.6 us
  Pallas kernels: 35.9 us -> 39.3 us
    ppermute x14 -> x30, waiting for transfers between devices: 69.2 us -> 31.4 us  [swap(): return lax.ppermute(value, axis, [(i, i ^ 1 << bit) for i in range(size)])]
    ppermute x14 -> x30, starting transfers between devices: 8.32 us -> 29.1 us  [swap(): return lax.ppermute(value, axis, [(i, i ^ 1 << bit) for i in range(size)])]
    all_gather x1 -> x0, blocking collectives: 5.07 us -> none  [shards(): lax.all_gather(jnp.stack([send_list.reshape(-1), recv_list.reshape(-1)]),...]
    unnamed x51 -> x77, local copies, waits for them, and re-layouts: 9.05 us -> 13.5 us
    pallas_call x5 -> x10, Pallas kernels: 35.9 us -> 39.3 us  [call(): pl.pallas_call(kernel, out_shape=[jax.ShapeDtypeStruct(shape, kind) for s...]
    all_to_all x3, starting transfers between devices: 16.6 us -> 13.3 us  [exchange(): lax.all_to_all(value, 'graph', split_axis=0, concat_axis=0, tiled=True)]
    all_to_all x3, waiting for transfers between devices: 6.52 us -> 3.36 us  [exchange(): lax.all_to_all(value, 'graph', split_axis=0, concat_axis=0, tiled=True)]
    another operation x6 -> x0, local copies, waits for them, and re-layouts: 2.79 us -> none  [the longest x1 0.7 us: shards(): recv_all.reshape(-1, 1)]
  transfers between devices with their start and end apart: 17 -> 33, of which waited for: 11 -> 15; matrix products, arithmetic and copies ran while one was open for 10% -> 7% of each run, Pallas kernels for 6% -> 10%
where the time goes in v1:
time: 151 us; the launch traced here: 150 us
  starting transfers between devices  42.4 us (28%)
  Pallas kernels  39.3 us (26%)
  waiting for transfers between devices  34.8 us (23%)
  local copies, waits for them, and re-layouts  17.9 us (12%)
  blocking collectives  12.6 us (8%)
    pallas_call x10, Pallas kernels, call(): pl.pallas_call(kernel, out_shape=[jax.ShapeDtypeStruct(shape, kind) for s...  39.3 us
    ppermute x30, waiting for transfers between devices, swap(): return lax.ppermute(value, axis, [(i, i ^ 1 << bit) for i in range(size)])  31.4 us
    ppermute x30, starting transfers between devices, swap(): return lax.ppermute(value, axis, [(i, i ^ 1 << bit) for i in range(size)])  29.1 us
    unnamed x77, local copies, waits for them, and re-layouts  13.5 us
    all_to_all x3, starting transfers between devices, exchange(): lax.all_to_all(value, 'graph', split_axis=0, concat_axis=0, tiled=True)  13.3 us
    all_to_all x1, blocking collectives, exchange(): lax.all_to_all(value, 'graph', split_axis=0, concat_axis=0, tiled=True)  12.6 us
    all_to_all x3, waiting for transfers between devices, exchange(): lax.all_to_all(value, 'graph', split_axis=0, concat_axis=0, tiled=True)  3.36 us
  transfers between devices with their start and end apart: 33, of which 15 were waited for; matrix products, arithmetic and copies ran while one was open for 7% of the time, Pallas kernels for 10%

profile of v1, /device:TPU:0, one launch (start us, length us, event | category | flops | bytes accessed | tf_op | source)
XLA Modules:
  0.0 149.6 jit_solution(13720354380226681131)
XLA Ops:
  0.6 1.2 copy.35
  1.8 1.0 reshape.76.embed
  2.8 1.8 %shard_map.223 = bf16[4,4,3328]{2,1,0:T(4,128)(2,1)} custom-call(s32[1,4,1,4]{3,2,1,0:T(1,128)} %send.1, s32[1,4,1,4]{3,2,1,0:T(1,128)} %recv.1, bf16[32,3136]{1,0:T(8,128)(2,1)} %reshape.76.embed), custom_call_target="tpu_custom_call" | custom-call | flops 1000000000 | bytes 200832 | tf_op jit(solution)/shard_map/pallas_call | solution.py:600
  4.6 6.4 %all-to-all-start = ((bf16[4,4,3328]{2,1,0:T(4,128)(2,1)}), bf16[4,4,3328]{2,1,0:T(4,128)(2,1)S(1)}, u32[]{:S(2)}, u32[]{:S(2)}) async-start(bf16[4,4,3328]{2,1,0:T(4,128)(2,1)} %shard_map.223), calls=%async_computation | async-start | bytes 212992 | tf_op jit(solution)/shard_map/all_to_all | solution.py:665
  11.0 0.8 copy.41.adot
  11.8 1.1 copy.37
  12.9 1.0 copy.38
  13.9 1.0 copy.36
  14.9 0.7 copy.39
  15.6 0.7 copy.40
  16.4 0.7 convert_bitcast_fusion.rot
  17.1 0.6 copy-done.21
  17.7 8.5 %shard_map.224 = (f32[4,4,3328]{2,1,0:T(4,128)}, bf16[448,256]{1,0:T(8,128)(2,1)}, bf16[384,512]{1,0:T(8,128)(2,1)}, bf16[320,512]{1,0:T(8,128)(2,1)}, f32[448,2...) custom-call(bf16[4,4,3328]{2,1,0:T(4,128)(2,1)} %copy-done.21, ...), custom_call_target="tpu_custom_call" | custom-call | flops 8000000000 | bytes 1918976 | tf_op jit(solution)/shard_map/pallas_call | solution.py:600
  26.3 12.6 %all_to_all.20.rest_0_ = f32[4,4,3328]{2,1,0:T(4,128)S(1)} all-to-all(f32[4,4,3328]{2,1,0:T(4,128)} %get-tuple-element.39), channel_id=1, replica_groups=mesh['groups'=2,'graph'=4,'edge'=4] {'graph'}, dimensions={0} | all-to-all | bytes 425984 | tf_op jit(solution)/shard_map/all_to_all | solution.py:665
  38.9 1.5 collective-permute-start.1
  40.4 4.4 %collective-permute-done.1.rest_2_ = f32[4,4,3328]{2,1,0:T(4,128)S(1)} collective-permute-done((f32[4,4,3328]{2,1,0:T(4,128)S(1)}, f32[4,4,3328]{2,1,0:T(4,128)S(1)}, u32[]{:S(2)}, u32[]{:S(2)}) %collective-permute-start.1) | collective-permute-done | bytes 213024 | tf_op jit(solution)/shard_map/ppermute | solution.py:615
  45.4 1.0 reshape.75.cot
  46.4 0.7 copy-done.31
  47.1 3.4 %shard_map.225 = (bf16[32,3136]{1,0:T(8,128)(2,1)}, bf16[4,4,3328]{2,1,0:T(4,128)(2,1)}) custom-call(s32[1]{0:T(128)} %bitcast.place, bf16[32,3136]{1,0:T(8,128)(2,1)} %reshape.75.cot, bf16[7,64,64]{2,1,0:T(8,128)(2,1)} %out_proj.3, f32[4,4,3328]{2,1,0:T(4,128)} %copy-done.17, f32[4,4,3328]{2,1,0:T(4,128)} %copy-done.31, f32[4,4,3328]{2,1,0:T(4,128)} %copy-done.30, ...), custom_call_target="tpu_custom_call" | custom-call | flops 4000000000 | bytes 1110020 | tf_op jit(solution)/shard_map/pallas_call | solution.py:600
  50.5 3.5 %all-to-all-start.2 = ((bf16[4,4,3328]{2,1,0:T(4,128)(2,1)}), bf16[4,4,3328]{2,1,0:T(4,128)(2,1)S(1)}, u32[]{:S(2)}, u32[]{:S(2)}) async-start(bf16[4,4,3328]{2,1,0:T(4,128)(2,1)} %get-tuple-element.43), calls=%async_computation.2 | async-start | bytes 212992 | tf_op jit(solution)/shard_map/all_to_all | solution.py:665
  54.0 2.5 %shard_map.226 = (bf16[32,3136]{1,0:T(8,128)(2,1)}, f32[448,64]{1,0:T(8,128)}) custom-call(bf16[32,3136]{1,0:T(8,128)(2,1)} %get-tuple-element.40.agg_low, bf16[32,3136]{1,0:T(8,128)(2,1)} %reshape.75.cot, bf16[7,64,64]{2,1,0:T(8,128)(2,1)} %out_proj.3), custom_call_target="tpu_custom_call" | custom-call | flops 4000000000 | bytes 458752 | tf_op jit(solution)/shard_map/pallas_call | solution.py:600
  56.5 3.4 %all-to-all-done.2.table = bf16[4,4,3328]{2,1,0:T(4,128)(2,1)S(1)} async-done(((bf16[4,4,3328]{2,1,0:T(4,128)(2,1)}), bf16[4,4,3328]{2,1,0:T(4,128)(2,1)S(1)}, u32[]{:S(2)}, u32[]{:S(2)}) %all-to-all-start.2) | async-done | bytes 106528 | tf_op jit(solution)/shard_map/all_to_all | solution.py:665
  59.8 0.6 copy-done.20
  60.5 8.2 %shard_map.227 = (bf16[448,256]{1,0:T(8,128)(2,1)}, bf16[384,512]{1,0:T(8,128)(2,1)}, bf16[320,512]{1,0:T(8,128)(2,1)}, bf16[256,256]{1,0:T(8,128)(2,1)}, f32[89...) custom-call(s32[1]{0:T(128)} %bitcast.place, ...), custom_call_target="tpu_custom_call" | custom-call | flops 8000000000 | bytes 3650564 | tf_op jit(solution)/shard_map/pallas_call | solution.py:600
  69.6 0.8 copy.43
  70.9 1.6 %collective-permute-start.9 = (f32[448,128]{1,0:T(8,128)S(1)}, f32[448,128]{1,0:T(8,128)S(1)}, u32[]{:S(2)}, u32[]{:S(2)}) collective-permute-start(f32[448,128]{1,0:T(8,128)S(1)} %dynamic-slice_bitcast_fusion.2), channel_id=1, source_target_pairs={{0,2},{1,3},{2,0},{3,1},{4,6},{5,7},{6,4},{7,5},{8,10},{9,11},{10,... | collective-permute-start | bytes 688136 | tf_op jit(solution)/shard_map/ppermute | solution.py:615
  72.6 1.1 collective-permute-start.23
  73.9 1.1 collective-permute-start.16
  75.0 6.4 %shard_map.228 = f32[4,4,3328]{2,1,0:T(4,128)} custom-call(s32[1,256]{1,0:T(1,128)} %bitcast.92, f32[16,128]{1,0:T(8,128)} %get-tuple-element.42.lists, f32[235,256]{1,0:T(8,128)} %convert_bitcast_fusion.rot, bf16[448,256]{1,0:T(8,128)(2,1)} %get-tuple-element.53.g0, bf16[384,512]{1,0:T(8,128)(2,1)} %get-tuple-element.54.g1, ...), custom_call_target="tpu_custom_call" | custom-call | flops 6000000000 | bytes 2764800 | tf_op jit(solution)/shard_map/pallas_call | solution.py:600
  81.4 3.4 %all-to-all-start.3 = ((f32[4,4,3328]{2,1,0:T(4,128)}), f32[4,4,3328]{2,1,0:T(4,128)S(1)}, u32[]{:S(2)}, u32[]{:S(2)}) async-start(f32[4,4,3328]{2,1,0:T(4,128)} %shard_map.228), calls=%async_computation.3 | async-start | bytes 425984 | tf_op jit(solution)/shard_map/all_to_all | solution.py:665
  84.8 2.0 %collective-permute-start.10 = (f32[224,128]{1,0:T(8,128)S(1)}, f32[224,128]{1,0:T(8,128)S(1)}, u32[]{:S(2)}, u32[]{:S(2)}) collective-permute-start(f32[224,128]{1,0:T(8,128)S(1)} %dynamic-slice_bitcast_fusion.5), channel_id=1, source_target_pairs={{0,4},{4,0},{8,12},{12,8},{1,5},{5,1},{9,13},{13,9},{2,6},{6,2},{1... | collective-permute-start | bytes 344072 | tf_op jit(solution)/shard_map/ppermute | solution.py:615
  86.9 6.5 %collective-permute-done.10 = f32[224,128]{1,0:T(8,128)S(1)} collective-permute-done((f32[224,128]{1,0:T(8,128)S(1)}, f32[224,128]{1,0:T(8,128)S(1)}, u32[]{:S(2)}, u32[]{:S(2)}) %collective-permute-start.10) | collective-permute-done | bytes 114720 | tf_op jit(solution)/shard_map/ppermute | solution.py:615
  93.5 2.4 %collective-permute-start.11 = (f32[112,128]{1,0:T(8,128)S(1)}, f32[112,128]{1,0:T(8,128)S(1)}, u32[]{:S(2)}, u32[]{:S(2)}) collective-permute-start(f32[112,128]{1,0:T(8,128)S(1)} %dynamic-slice_bitcast_fusion.8), channel_id=1, source_target_pairs={{0,8},{4,12},{8,0},{12,4},{1,9},{5,13},{9,1},{13,5},{2,10},{6,14},... | collective-permute-start | bytes 172040 | tf_op jit(solution)/shard_map/ppermute | solution.py:615
  96.6 2.7 %collective-permute-done.11 = f32[112,128]{1,0:T(8,128)S(1)} collective-permute-done((f32[112,128]{1,0:T(8,128)S(1)}, f32[112,128]{1,0:T(8,128)S(1)}, u32[]{:S(2)}, u32[]{:S(2)}) %collective-permute-start.11) | collective-permute-done | bytes 57376 | tf_op jit(solution)/shard_map/ppermute | solution.py:615
  99.3 2.2 %collective-permute-start.12 = (bf16[112,128]{1,0:T(8,128)(2,1)S(1)}, bf16[112,128]{1,0:T(8,128)(2,1)S(1)}, u32[]{:S(2)}, u32[]{:S(2)}) collective-permute-start(bf16[112,128]{1,0:T(8,128)(2,1)S(1)} %fusion.2), channel_id=1, source_target_pairs={{0,8},{4,12},{8,0},{12,4},{1,9},{5,13},{9,1},{13,5},{2,10},{6,14},... | collective-permute-start | bytes 86024 | tf_op jit(solution)/shard_map/ppermute | solution.py:615
  101.9 2.5 %collective-permute-done.12 = bf16[112,128]{1,0:T(8,128)(2,1)S(1)} collective-permute-done((bf16[112,128]{1,0:T(8,128)(2,1)S(1)}, bf16[112,128]{1,0:T(8,128)(2,1)S(1)}, u32[]{:S(2)}, u32[]{:S(2)}) %collective-permute-start.12) | collective-permute-done | bytes 28704 | tf_op jit(solution)/shard_map/ppermute | solution.py:615
  104.9 1.0 collective-permute-start.7
  105.9 1.8 %collective-permute-start.25 = (f32[128,128]{1,0:T(8,128)S(1)}, f32[128,128]{1,0:T(8,128)S(1)}, u32[]{:S(2)}, u32[]{:S(2)}) collective-permute-start(f32[128,128]{1,0:T(8,128)S(1)} %dynamic-slice_bitcast_fusion.7), channel_id=1, source_target_pairs={{0,8},{4,12},{8,0},{12,4},{1,9},{5,13},{9,1},{13,5},{2,10},{6,14},... | collective-permute-start | bytes 196616 | tf_op jit(solution)/shard_map/ppermute | solution.py:615
  107.8 0.9 collective-permute-done.13
  108.7 4.1 %collective-permute-done.25 = f32[128,128]{1,0:T(8,128)S(1)} collective-permute-done((f32[128,128]{1,0:T(8,128)S(1)}, f32[128,128]{1,0:T(8,128)S(1)}, u32[]{:S(2)}, u32[]{:S(2)}) %collective-permute-start.25) | collective-permute-done | bytes 65568 | tf_op jit(solution)/shard_map/ppermute | solution.py:615
  113.4 1.1 collective-permute-start.14
  114.5 3.3 %collective-permute-done.26 = bf16[128,128]{1,0:T(8,128)(2,1)S(1)} collective-permute-done((bf16[128,128]{1,0:T(8,128)(2,1)S(1)}, bf16[128,128]{1,0:T(8,128)(2,1)S(1)}, u32[]{:S(2)}, u32[]{:S(2)}) %collective-permute-start.26) | collective-permute-done | bytes 32800 | tf_op jit(solution)/shard_map/ppermute | solution.py:615
  118.2 3.0 %collective-permute-start.18 = (f32[144,128]{1,0:T(8,128)S(1)}, f32[144,128]{1,0:T(8,128)S(1)}, u32[]{:S(2)}, u32[]{:S(2)}) collective-permute-start(f32[144,128]{1,0:T(8,128)S(1)} %dynamic-slice_bitcast_fusion.6), channel_id=1, source_target_pairs={{0,8},{4,12},{8,0},{12,4},{1,9},{5,13},{9,1},{13,5},{2,10},{6,14},... | collective-permute-start | bytes 221192 | tf_op jit(solution)/shard_map/ppermute | solution.py:615
  121.3 1.2 collective-permute-done.27
  122.6 0.9 collective-permute-done.18
  123.5 3.0 %collective-permute-start.19 = (bf16[144,128]{1,0:T(8,128)(2,1)S(1)}, bf16[144,128]{1,0:T(8,128)(2,1)S(1)}, u32[]{:S(2)}, u32[]{:S(2)}) collective-permute-start(bf16[144,128]{1,0:T(8,128)(2,1)S(1)} %fusion), channel_id=1, source_target_pairs={{0,8},{4,12},{8,0},{12,4},{1,9},{5,13},{9,1},{13,5},{2,10},{6,14},... | collective-permute-start | bytes 110600 | tf_op jit(solution)/shard_map/ppermute | solution.py:615
  126.5 1.1 collective-permute-start.28
  127.6 0.8 collective-permute-done.19
  128.4 1.9 %collective-permute-start.20 = (bf16[288,128]{1,0:T(8,128)(2,1)S(1)}, bf16[288,128]{1,0:T(8,128)(2,1)S(1)}, u32[]{:S(2)}, u32[]{:S(2)}) collective-permute-start(bf16[288,128]{1,0:T(8,128)(2,1)S(1)} %pad_maximum_fusion.6), channel_id=1, source_target_pairs={{0,4},{4,0},{8,12},{12,8},{1,5},{5,1},{9,13},{13,9},{2,6},{6,2},{1... | collective-permute-start | bytes 221192 | tf_op jit(solution)/shard_map/ppermute | solution.py:615
  130.3 1.2 collective-permute-done.28
  131.6 1.3 collective-permute-done.20
  132.9 1.1 collective-permute-start.21
  134.2 0.7 copy-done.26
  134.8 2.0 %shard_map.230 = (bf16[448,448]{1,0:T(8,128)(2,1)}, bf16[7,64,64]{2,1,0:T(8,128)(2,1)}) custom-call(s32[1]{0:T(128)} %bitcast.place, bf16[896,128]{1,0:T(8,128)(2,1)} %copy-done.15, bf16[896,128]{1,0:T(8,128)(2,1)} %copy-done.26), custom_call_target="tpu_custom_call" | custom-call | flops 1000000000 | bytes 458756 | tf_op jit(solution)/shard_map/pallas_call | solution.py:600
  136.9 1.3 collective-permute-done.21
  138.4 0.7 copy-done.28
  139.0 0.7 copy-done.29
  139.7 2.5 %shard_map.229 = bf16[32,3136]{1,0:T(8,128)(2,1)} custom-call(s32[1]{0:T(128)} %bitcast.place, f32[4,4,3328]{2,1,0:T(4,128)} %copy-done.16, f32[4,4,3328]{2,1,0:T(4,128)} %copy-done.28, f32[4,4,3328]{2,1,0:T(4,128)} %copy-done.27, f32[4,4,3328]{2,1,0:T(4,128)} %copy-done.29), custom_call_target="tpu_custom_call" | custom-call | flops 4000000000 | bytes 851972 | tf_op jit(solution)/shard_map/pallas_call | solution.py:600
  142.2 1.2 reshape.82
  143.4 0.8 copy.44
  144.2 0.7 copy-done.25
  144.9 2.0 %shard_map.232 = (bf16[2,320,320]{2,1,0:T(8,128)(2,1)}, bf16[64,256]{1,0:T(8,128)(2,1)}, bf16[128,256]{1,0:T(8,128)(2,1)}, bf16[2,128]{1,0:T(2,128)(2,1)}) custom-call(s32[1]{0:T(128)} %bitcast.place, bf16[1024,128]{1,0:T(8,128)(2,1)} %copy-done.14, bf16[1024,128]{1,0:T(8,128)(2,1)} %copy-done.25), custom_call_target="tpu_custom_call" | custom-call | flops 1000000000 | bytes 524292 | tf_op jit(solution)/shard_map/pallas_call | solution.py:600
  146.9 0.7 copy-done.24
  147.6 2.0 %shard_map.231 = bf16[2,384,384]{2,1,0:T(8,128)(2,1)} custom-call(s32[1]{0:T(128)} %bitcast.place, bf16[1152,128]{1,0:T(8,128)(2,1)} %copy-done.13, bf16[1152,128]{1,0:T(8,128)(2,1)} %copy-done.24), custom_call_target="tpu_custom_call" | custom-call | flops 1000000000 | bytes 589828 | tf_op jit(solution)/shard_map/pallas_call | solution.py:600
  (136 shorter events, 5.6 us)
Async XLA Ops:
  2.8 9.1 %copy-start.7 = (bf16[2,384,384]{2,1,0:T(8,128)(2,1)S(1)}, bf16[2,384,384]{2,1,0:T(8,128)(2,1)}, u32[]{:S(2)}) copy-start(bf16[2,384,384]{2,1,0:T(8,128)(2,1)} %wone.1) | copy-start | bytes 1769476
  4.6 6.5 %copy-start.33 = (bf16[256]{0:T(256)(128)(2,1)S(1)}, bf16[256]{0:T(256)(128)(2,1)}, u32[]{:S(2)}) copy-start(bf16[256]{0:T(256)(128)(2,1)} %param.30) | copy-start | bytes 1540
  4.6 12.5 %all-to-all-start = ((bf16[4,4,3328]{2,1,0:T(4,128)(2,1)}), bf16[4,4,3328]{2,1,0:T(4,128)(2,1)S(1)}, u32[]{:S(2)}, u32[]{:S(2)}) async-start(bf16[4,4,3328]{2,1,0:T(4,128)(2,1)} %shard_map.223), calls=%async_computation | async-start | bytes 212992 | tf_op jit(solution)/shard_map/all_to_all | solution.py:665
  11.8 1.1 copy-start.9
  12.9 1.0 copy-start.10
  13.9 1.0 copy-start.23
  13.9 1.7 %copy-start.22 = (bf16[128,256]{1,0:T(8,128)(2,1)S(1)}, bf16[128,256]{1,0:T(8,128)(2,1)}, u32[]{:S(2)}) copy-start(bf16[128,256]{1,0:T(8,128)(2,1)} %param.29) | copy-start | bytes 196612
  14.9 1.5 copy-start.19
  26.3 18.5 %copy-start.12 = (bf16[32,49,64]{2,0,1:T(8,128)(2,1)S(1)}, bf16[32,49,64]{2,0,1:T(8,128)(2,1)}, u32[]{:S(2)}) copy-start(bf16[32,49,64]{2,0,1:T(8,128)(2,1)} %param.17) | copy-start | bytes 602116
  38.9 6.0 %copy-start.17 = (f32[4,4,3328]{2,1,0:T(4,128)}, f32[4,4,3328]{2,1,0:T(4,128)S(1)}, u32[]{:S(2)}) copy-start(f32[4,4,3328]{2,1,0:T(4,128)S(1)} %all_to_all.20.rest_0_) | copy-start | bytes 638980
  38.9 5.8 %collective-permute-start.1 = (f32[4,4,3328]{2,1,0:T(4,128)S(1)}, f32[4,4,3328]{2,1,0:T(4,128)S(1)}, u32[]{:S(2)}, u32[]{:S(2)}) collective-permute-start(f32[4,4,3328]{2,1,0:T(4,128)S(1)} %all_to_all.20.rest_0_), channel_id=1, source_target_pairs={{0,2},{1,3},{2,0},{3,1},{4,6},{5,7},{6,4},{7,5},{8,10},{9,11},{10,... | collective-permute-start | bytes 638984 | tf_op jit(solution)/shard_map/ppermute | solution.py:615
  40.4 6.0 %collective-permute-start = (f32[4,4,3328]{2,1,0:T(4,128)S(1)}, f32[4,4,3328]{2,1,0:T(4,128)S(1)}, u32[]{:S(2)}, u32[]{:S(2)}) collective-permute-start(f32[4,4,3328]{2,1,0:T(4,128)S(1)} %all_to_all.20.rest_0_), channel_id=1, source_target_pairs={{0,1},{1,0},{2,3},{3,2},{4,5},{5,4},{6,7},{7,6},{8,9},{9,8},{10,11... | collective-permute-start | bytes 638984 | tf_op jit(solution)/shard_map/ppermute | solution.py:615
  44.7 0.7 copy-start.30
  44.7 1.7 %collective-permute-start.2 = (f32[4,4,3328]{2,1,0:T(4,128)S(1)}, f32[4,4,3328]{2,1,0:T(4,128)S(1)}, u32[]{:S(2)}, u32[]{:S(2)}) collective-permute-start(f32[4,4,3328]{2,1,0:T(4,128)S(1)} %collective-permute-done.1.rest_2_), channel_id=1, source_target_pairs={{0,1},{1,0},{2,3},{3,2},{4,5},{5,4},{6,7},{7,6},{8,9},{9,8},{10,11... | collective-permute-start | bytes 638984 | tf_op jit(solution)/shard_map/ppermute | solution.py:615
  46.4 0.7 copy-start.31
  46.4 0.7 copy-start.32
  50.5 9.3 %all-to-all-start.2 = ((bf16[4,4,3328]{2,1,0:T(4,128)(2,1)}), bf16[4,4,3328]{2,1,0:T(4,128)(2,1)S(1)}, u32[]{:S(2)}, u32[]{:S(2)}) async-start(bf16[4,4,3328]{2,1,0:T(4,128)(2,1)} %get-tuple-element.43), calls=%async_computation.2 | async-start | bytes 212992 | tf_op jit(solution)/shard_map/all_to_all | solution.py:665
  60.5 8.9 %copy-start.18 = (bf16[32,3136]{1,0:T(8,128)(2,1)S(1)}, bf16[32,3136]{1,0:T(8,128)(2,1)}, u32[]{:S(2)}) copy-start(bf16[32,3136]{1,0:T(8,128)(2,1)} %get-tuple-element.41) | copy-start | bytes 602116
  68.7 2.1 %collective-permute-start.3 = (f32[896,128]{1,0:T(8,128)}, f32[896,128]{1,0:T(8,128)S(1)}, u32[]{:S(2)}, u32[]{:S(2)}) collective-permute-start(f32[896,128]{1,0:T(8,128)} %get-tuple-element.58), channel_id=1, source_target_pairs={{0,1},{1,0},{2,3},{3,2},{4,5},{5,4},{6,7},{7,6},{8,9},{9,8},{10,11... | collective-permute-start | bytes 1376264 | tf_op jit(solution)/shard_map/ppermute | solution.py:615
  68.8 3.7 %collective-permute-start.5 = (f32[1024,128]{1,0:T(8,128)}, f32[1024,128]{1,0:T(8,128)S(1)}, u32[]{:S(2)}, u32[]{:S(2)}) collective-permute-start(f32[1024,128]{1,0:T(8,128)} %get-tuple-element.62), channel_id=1, source_target_pairs={{0,1},{1,0},{2,3},{3,2},{4,5},{5,4},{6,7},{7,6},{8,9},{9,8},{10,11... | collective-permute-start | bytes 1572872 | tf_op jit(solution)/shard_map/ppermute | solution.py:615
  69.3 4.4 %collective-permute-start.4 = (f32[1152,128]{1,0:T(8,128)}, f32[1152,128]{1,0:T(8,128)S(1)}, u32[]{:S(2)}, u32[]{:S(2)}) collective-permute-start(f32[1152,128]{1,0:T(8,128)} %get-tuple-element.60), channel_id=1, source_target_pairs={{0,1},{1,0},{2,3},{3,2},{4,5},{5,4},{6,7},{7,6},{8,9},{9,8},{10,11... | collective-permute-start | bytes 1769480 | tf_op jit(solution)/shard_map/ppermute | solution.py:615
  69.6 1.2 copy-start.11
  70.8 1.7 %copy-start.8 = (f32[1024,128]{1,0:T(8,128)S(1)}, f32[1024,128]{1,0:T(8,128)}, u32[]{:S(2)}) copy-start(f32[1024,128]{1,0:T(8,128)} %get-tuple-element.61) | copy-start | bytes 1572868
  70.9 1.7 %copy-start.4 = (f32[896,128]{1,0:T(8,128)}, f32[896,128]{1,0:T(8,128)S(1)}, u32[]{:S(2)}) copy-start(f32[896,128]{1,0:T(8,128)S(1)} %add.78.rest_0_) | copy-start | bytes 1376260
  70.9 13.9 %collective-permute-start.9 = (f32[448,128]{1,0:T(8,128)S(1)}, f32[448,128]{1,0:T(8,128)S(1)}, u32[]{:S(2)}, u32[]{:S(2)}) collective-permute-start(f32[448,128]{1,0:T(8,128)S(1)} %dynamic-slice_bitcast_fusion.2), channel_id=1, source_target_pairs={{0,2},{1,3},{2,0},{3,1},{4,6},{5,7},{6,4},{7,5},{8,10},{9,11},{10,... | collective-permute-start | bytes 688136 | tf_op jit(solution)/shard_map/ppermute | solution.py:615
  72.5 1.3 copy-start.6
  72.6 1.2 copy-start.2
  72.6 14.3 %collective-permute-start.23 = (f32[512,128]{1,0:T(8,128)S(1)}, f32[512,128]{1,0:T(8,128)S(1)}, u32[]{:S(2)}, u32[]{:S(2)}) collective-permute-start(f32[512,128]{1,0:T(8,128)S(1)} %dynamic-slice_bitcast_fusion.1), channel_id=1, source_target_pairs={{0,2},{1,3},{2,0},{3,1},{4,6},{5,7},{6,4},{7,5},{8,10},{9,11},{10,... | collective-permute-start | bytes 786440 | tf_op jit(solution)/shard_map/ppermute | solution.py:615
  73.8 1.2 copy-start
  73.9 27.6 %collective-permute-start.16 = (f32[576,128]{1,0:T(8,128)S(1)}, f32[576,128]{1,0:T(8,128)S(1)}, u32[]{:S(2)}, u32[]{:S(2)}) collective-permute-start(f32[576,128]{1,0:T(8,128)S(1)} %dynamic-slice_bitcast_fusion), channel_id=1, source_target_pairs={{0,2},{1,3},{2,0},{3,1},{4,6},{5,7},{6,4},{7,5},{8,10},{9,11},{10,... | collective-permute-start | bytes 884744 | tf_op jit(solution)/shard_map/ppermute | solution.py:615
  75.0 9.8 %copy-start.5 = (f32[896,128]{1,0:T(8,128)S(1)}, f32[896,128]{1,0:T(8,128)}, u32[]{:S(2)}) copy-start(f32[896,128]{1,0:T(8,128)} %copy-done.4) | copy-start | bytes 1376260
  81.4 23.5 %all-to-all-start.3 = ((f32[4,4,3328]{2,1,0:T(4,128)}), f32[4,4,3328]{2,1,0:T(4,128)S(1)}, u32[]{:S(2)}, u32[]{:S(2)}) async-start(f32[4,4,3328]{2,1,0:T(4,128)} %shard_map.228), calls=%async_computation.3 | async-start | bytes 425984 | tf_op jit(solution)/shard_map/all_to_all | solution.py:665
  84.7 2.1 %copy-start.3 = (f32[1024,128]{1,0:T(8,128)S(1)}, f32[1024,128]{1,0:T(8,128)}, u32[]{:S(2)}) copy-start(f32[1024,128]{1,0:T(8,128)} %copy-done.2) | copy-start | bytes 1572868
  84.8 8.6 %collective-permute-start.10 = (f32[224,128]{1,0:T(8,128)S(1)}, f32[224,128]{1,0:T(8,128)S(1)}, u32[]{:S(2)}, u32[]{:S(2)}) collective-permute-start(f32[224,128]{1,0:T(8,128)S(1)} %dynamic-slice_bitcast_fusion.5), channel_id=1, source_target_pairs={{0,4},{4,0},{8,12},{12,8},{1,5},{5,1},{9,13},{13,9},{2,6},{6,2},{1... | collective-permute-start | bytes 344072 | tf_op jit(solution)/shard_map/ppermute | solution.py:615
  86.9 14.6 %copy-start.1 = (f32[1152,128]{1,0:T(8,128)S(1)}, f32[1152,128]{1,0:T(8,128)}, u32[]{:S(2)}) copy-start(f32[1152,128]{1,0:T(8,128)} %copy-done) | copy-start | bytes 1769476
  93.5 5.7 %collective-permute-start.11 = (f32[112,128]{1,0:T(8,128)S(1)}, f32[112,128]{1,0:T(8,128)S(1)}, u32[]{:S(2)}, u32[]{:S(2)}) collective-permute-start(f32[112,128]{1,0:T(8,128)S(1)} %dynamic-slice_bitcast_fusion.8), channel_id=1, source_target_pairs={{0,8},{4,12},{8,0},{12,4},{1,9},{5,13},{9,1},{13,5},{2,10},{6,14},... | collective-permute-start | bytes 172040 | tf_op jit(solution)/shard_map/ppermute | solution.py:615
  96.0 9.9 %collective-permute-start.24 = (f32[256,128]{1,0:T(8,128)S(1)}, f32[256,128]{1,0:T(8,128)S(1)}, u32[]{:S(2)}, u32[]{:S(2)}) collective-permute-start(f32[256,128]{1,0:T(8,128)S(1)} %dynamic-slice_bitcast_fusion.4), channel_id=1, source_target_pairs={{0,4},{4,0},{8,12},{12,8},{1,5},{5,1},{9,13},{13,9},{2,6},{6,2},{1... | collective-permute-start | bytes 393224 | tf_op jit(solution)/shard_map/ppermute | solution.py:615
  99.3 5.1 %collective-permute-start.12 = (bf16[112,128]{1,0:T(8,128)(2,1)S(1)}, bf16[112,128]{1,0:T(8,128)(2,1)S(1)}, u32[]{:S(2)}, u32[]{:S(2)}) collective-permute-start(bf16[112,128]{1,0:T(8,128)(2,1)S(1)} %fusion.2), channel_id=1, source_target_pairs={{0,8},{4,12},{8,0},{12,4},{1,9},{5,13},{9,1},{13,5},{2,10},{6,14},... | collective-permute-start | bytes 86024 | tf_op jit(solution)/shard_map/ppermute | solution.py:615
  101.6 16.5 %collective-permute-start.17 = (f32[288,128]{1,0:T(8,128)S(1)}, f32[288,128]{1,0:T(8,128)S(1)}, u32[]{:S(2)}, u32[]{:S(2)}) collective-permute-start(f32[288,128]{1,0:T(8,128)S(1)} %dynamic-slice_bitcast_fusion.3), channel_id=1, source_target_pairs={{0,4},{4,0},{8,12},{12,8},{1,5},{5,1},{9,13},{13,9},{2,6},{6,2},{1... | collective-permute-start | bytes 442376 | tf_op jit(solution)/shard_map/ppermute | solution.py:615
  104.4 4.2 %collective-permute-start.13 = (bf16[224,128]{1,0:T(8,128)(2,1)S(1)}, bf16[224,128]{1,0:T(8,128)(2,1)S(1)}, u32[]{:S(2)}, u32[]{:S(2)}) collective-permute-start(bf16[224,128]{1,0:T(8,128)(2,1)S(1)} %pad_maximum_fusion.8), channel_id=1, source_target_pairs={{0,4},{4,0},{8,12},{12,8},{1,5},{5,1},{9,13},{13,9},{2,6},{6,2},{1... | collective-permute-start | bytes 172040 | tf_op jit(solution)/shard_map/ppermute | solution.py:615
  104.9 1.0 copy-start.16
  104.9 22.7 %collective-permute-start.7 = (f32[4,4,3328]{2,1,0:T(4,128)S(1)}, f32[4,4,3328]{2,1,0:T(4,128)S(1)}, u32[]{:S(2)}, u32[]{:S(2)}) collective-permute-start(f32[4,4,3328]{2,1,0:T(4,128)S(1)} %all-to-all-done.3.rest_0_), channel_id=1, source_target_pairs={{0,2},{1,3},{2,0},{3,1},{4,6},{5,7},{6,4},{7,5},{8,10},{9,11},{10,... | collective-permute-start | bytes 638984 | tf_op jit(solution)/shard_map/ppermute | solution.py:615
  105.9 32.5 %collective-permute-start.6 = (f32[4,4,3328]{2,1,0:T(4,128)S(1)}, f32[4,4,3328]{2,1,0:T(4,128)S(1)}, u32[]{:S(2)}, u32[]{:S(2)}) collective-permute-start(f32[4,4,3328]{2,1,0:T(4,128)S(1)} %all-to-all-done.3.rest_0_), channel_id=1, source_target_pairs={{0,1},{1,0},{2,3},{3,2},{4,5},{5,4},{6,7},{7,6},{8,9},{9,8},{10,11... | collective-permute-start | bytes 638984 | tf_op jit(solution)/shard_map/ppermute | solution.py:615
  105.9 6.9 %collective-permute-start.25 = (f32[128,128]{1,0:T(8,128)S(1)}, f32[128,128]{1,0:T(8,128)S(1)}, u32[]{:S(2)}, u32[]{:S(2)}) collective-permute-start(f32[128,128]{1,0:T(8,128)S(1)} %dynamic-slice_bitcast_fusion.7), channel_id=1, source_target_pairs={{0,8},{4,12},{8,0},{12,4},{1,9},{5,13},{9,1},{13,5},{2,10},{6,14},... | collective-permute-start | bytes 196616 | tf_op jit(solution)/shard_map/ppermute | solution.py:615
  112.8 5.0 %collective-permute-start.26 = (bf16[128,128]{1,0:T(8,128)(2,1)S(1)}, bf16[128,128]{1,0:T(8,128)(2,1)S(1)}, u32[]{:S(2)}, u32[]{:S(2)}) collective-permute-start(bf16[128,128]{1,0:T(8,128)(2,1)S(1)} %fusion.1), channel_id=1, source_target_pairs={{0,8},{4,12},{8,0},{12,4},{1,9},{5,13},{9,1},{13,5},{2,10},{6,14},... | collective-permute-start | bytes 98312 | tf_op jit(solution)/shard_map/ppermute | solution.py:615
  113.4 7.8 %collective-permute-start.14 = (bf16[448,128]{1,0:T(8,128)(2,1)S(1)}, bf16[448,128]{1,0:T(8,128)(2,1)S(1)}, u32[]{:S(2)}, u32[]{:S(2)}) collective-permute-start(bf16[448,128]{1,0:T(8,128)(2,1)S(1)} %pad_maximum_fusion.5), channel_id=1, source_target_pairs={{0,2},{1,3},{2,0},{3,1},{4,6},{5,7},{6,4},{7,5},{8,10},{9,11},{10,... | collective-permute-start | bytes 344072 | tf_op jit(solution)/shard_map/ppermute | solution.py:615
  117.8 4.7 %collective-permute-start.27 = (bf16[256,128]{1,0:T(8,128)(2,1)S(1)}, bf16[256,128]{1,0:T(8,128)(2,1)S(1)}, u32[]{:S(2)}, u32[]{:S(2)}) collective-permute-start(bf16[256,128]{1,0:T(8,128)(2,1)S(1)} %pad_maximum_fusion.7), channel_id=1, source_target_pairs={{0,4},{4,0},{8,12},{12,8},{1,5},{5,1},{9,13},{13,9},{2,6},{6,2},{1... | collective-permute-start | bytes 196616 | tf_op jit(solution)/shard_map/ppermute | solution.py:615
  118.2 5.3 %collective-permute-start.18 = (f32[144,128]{1,0:T(8,128)S(1)}, f32[144,128]{1,0:T(8,128)S(1)}, u32[]{:S(2)}, u32[]{:S(2)}) collective-permute-start(f32[144,128]{1,0:T(8,128)S(1)} %dynamic-slice_bitcast_fusion.6), channel_id=1, source_target_pairs={{0,8},{4,12},{8,0},{12,4},{1,9},{5,13},{9,1},{13,5},{2,10},{6,14},... | collective-permute-start | bytes 221192 | tf_op jit(solution)/shard_map/ppermute | solution.py:615
  121.2 5.3 %copy-start.15 = (bf16[896,128]{1,0:T(8,128)(2,1)}, bf16[896,128]{1,0:T(8,128)(2,1)S(1)}, u32[]{:S(2)}) copy-start(bf16[896,128]{1,0:T(8,128)(2,1)S(1)} %pad_maximum_fusion.2.mine) | copy-start | bytes 688132
  121.2 12.9 %collective-permute-start.15 = (bf16[896,128]{1,0:T(8,128)(2,1)S(1)}, bf16[896,128]{1,0:T(8,128)(2,1)S(1)}, u32[]{:S(2)}, u32[]{:S(2)}) collective-permute-start(bf16[896,128]{1,0:T(8,128)(2,1)S(1)} %pad_maximum_fusion.2.mine), channel_id=1, source_target_pairs={{0,1},{1,0},{2,3},{3,2},{4,5},{5,4},{6,7},{7,6},{8,9},{9,8},{10,11... | collective-permute-start | bytes 688136 | tf_op jit(solution)/shard_map/ppermute | solution.py:615
  123.5 4.9 %collective-permute-start.19 = (bf16[144,128]{1,0:T(8,128)(2,1)S(1)}, bf16[144,128]{1,0:T(8,128)(2,1)S(1)}, u32[]{:S(2)}, u32[]{:S(2)}) collective-permute-start(bf16[144,128]{1,0:T(8,128)(2,1)S(1)} %fusion), channel_id=1, source_target_pairs={{0,8},{4,12},{8,0},{12,4},{1,9},{5,13},{9,1},{13,5},{2,10},{6,14},... | collective-permute-start | bytes 110600 | tf_op jit(solution)/shard_map/ppermute | solution.py:615
  126.5 5.0 %collective-permute-start.28 = (bf16[512,128]{1,0:T(8,128)(2,1)S(1)}, bf16[512,128]{1,0:T(8,128)(2,1)S(1)}, u32[]{:S(2)}, u32[]{:S(2)}) collective-permute-start(bf16[512,128]{1,0:T(8,128)(2,1)S(1)} %pad_maximum_fusion.4), channel_id=1, source_target_pairs={{0,2},{1,3},{2,0},{3,1},{4,6},{5,7},{6,4},{7,5},{8,10},{9,11},{10,... | collective-permute-start | bytes 393224 | tf_op jit(solution)/shard_map/ppermute | solution.py:615
  127.6 4.0 %copy-start.27 = (f32[4,4,3328]{2,1,0:T(4,128)}, f32[4,4,3328]{2,1,0:T(4,128)S(1)}, u32[]{:S(2)}) copy-start(f32[4,4,3328]{2,1,0:T(4,128)S(1)} %collective-permute-done.7.rest_2_) | copy-start | bytes 638980
  127.6 10.7 %collective-permute-start.8 = (f32[4,4,3328]{2,1,0:T(4,128)S(1)}, f32[4,4,3328]{2,1,0:T(4,128)S(1)}, u32[]{:S(2)}, u32[]{:S(2)}) collective-permute-start(f32[4,4,3328]{2,1,0:T(4,128)S(1)} %collective-permute-done.7.rest_2_), channel_id=1, source_target_pairs={{0,1},{1,0},{2,3},{3,2},{4,5},{5,4},{6,7},{7,6},{8,9},{9,8},{10,11... | collective-permute-start | bytes 638984 | tf_op jit(solution)/shard_map/ppermute | solution.py:615
  128.4 4.4 %collective-permute-start.20 = (bf16[288,128]{1,0:T(8,128)(2,1)S(1)}, bf16[288,128]{1,0:T(8,128)(2,1)S(1)}, u32[]{:S(2)}, u32[]{:S(2)}) collective-permute-start(bf16[288,128]{1,0:T(8,128)(2,1)S(1)} %pad_maximum_fusion.6), channel_id=1, source_target_pairs={{0,4},{4,0},{8,12},{12,8},{1,5},{5,1},{9,13},{13,9},{2,6},{6,2},{1... | collective-permute-start | bytes 221192 | tf_op jit(solution)/shard_map/ppermute | solution.py:615
  132.9 5.2 %collective-permute-start.21 = (bf16[576,128]{1,0:T(8,128)(2,1)S(1)}, bf16[576,128]{1,0:T(8,128)(2,1)S(1)}, u32[]{:S(2)}, u32[]{:S(2)}) collective-permute-start(bf16[576,128]{1,0:T(8,128)(2,1)S(1)} %pad_maximum_fusion.3), channel_id=1, source_target_pairs={{0,2},{1,3},{2,0},{3,1},{4,6},{5,7},{6,4},{7,5},{8,10},{9,11},{10,... | collective-permute-start | bytes 442376 | tf_op jit(solution)/shard_map/ppermute | solution.py:615
  134.1 2.8 %copy-start.14 = (bf16[1024,128]{1,0:T(8,128)(2,1)}, bf16[1024,128]{1,0:T(8,128)(2,1)S(1)}, u32[]{:S(2)}) copy-start(bf16[1024,128]{1,0:T(8,128)(2,1)S(1)} %pad_maximum_fusion.1.mine) | copy-start | bytes 786436
  134.1 10.1 %collective-permute-start.29 = (bf16[1024,128]{1,0:T(8,128)(2,1)S(1)}, bf16[1024,128]{1,0:T(8,128)(2,1)S(1)}, u32[]{:S(2)}, u32[]{:S(2)}) collective-permute-start(bf16[1024,128]{1,0:T(8,128)(2,1)S(1)} %pad_maximum_fusion.1.mine), channel_id=1, source_target_pairs={{0,1},{1,0},{2,3},{3,2},{4,5},{5,4},{6,7},{7,6},{8,9},{9,8},{10,11... | collective-permute-start | bytes 786440 | tf_op jit(solution)/shard_map/ppermute | solution.py:615
  134.2 0.7 copy-start.26
  138.2 4.0 %copy-start.13 = (bf16[1152,128]{1,0:T(8,128)(2,1)}, bf16[1152,128]{1,0:T(8,128)(2,1)S(1)}, u32[]{:S(2)}) copy-start(bf16[1152,128]{1,0:T(8,128)(2,1)S(1)} %pad_maximum_fusion.mine) | copy-start | bytes 884740
  138.2 8.6 %collective-permute-start.22 = (bf16[1152,128]{1,0:T(8,128)(2,1)S(1)}, bf16[1152,128]{1,0:T(8,128)(2,1)S(1)}, u32[]{:S(2)}, u32[]{:S(2)}) collective-permute-start(bf16[1152,128]{1,0:T(8,128)(2,1)S(1)} %pad_maximum_fusion.mine), channel_id=1, source_target_pairs={{0,1},{1,0},{2,3},{3,2},{4,5},{5,4},{6,7},{7,6},{8,9},{9,8},{10,11... | collective-permute-start | bytes 884744 | tf_op jit(solution)/shard_map/ppermute | solution.py:615
  138.3 0.7 copy-start.28
  144.2 0.7 copy-start.25
  146.9 0.7 copy-start.24
  (3 other events, 2.0 us)

commit v2 on v1

--- a/solution.py
+++ b/solution.py
@@ -18,6 +18,8 @@
 BLOCKS = (FLAT + LANES - 1) // LANES
 COLS = BLOCKS * LANES
 WIDE = COLS + LANES
+TABLE = 2 * COLS + LANES
+PEAK_AT, DOT_AT, NAME_AT = HEADS, 2 * HEADS, 3 * HEADS
 DIM0 = (LMAX + 1) * CH
 DIM1 = LMAX * CH
 DIM2 = (LMAX - 1) * CH
@@ -140,11 +142,22 @@
         out_ref[g, :, cols] = value[g * cap : (g + 1) * cap].astype(out_ref.dtype)
 
 
-def slot_sums(terms, one_hot, out_ref):
+def slot_sums(terms, one_hot, out_ref, factor=None):
     both = jnp.concatenate([one_hot, one_hot], axis=1)
+    products = 0.0
     for start in range(0, COLS, PANEL):
         size = min(PANEL, COLS - start)
-        put_rows(out_ref, pl.ds(start, size), dot_nt(both, terms[pl.ds(start, size), :]))
+        sums = dot_nt(both, terms[pl.ds(start, size), :])
+        put_rows(out_ref, pl.ds(start, size), sums)
+        if factor is None:
+            continue
+        for at in range(0, size, LANES):
+            width = min(LANES, FLAT - start - at)
+            product = sums[:, at : at + width] * factor[:, pl.ds(start + at, width)]
+            if width < LANES:
+                product = jnp.concatenate([product, jnp.zeros_like(product)], axis=1)
+            products = products + product
+    return products
 
 
 def store_terms(terms, edges):
@@ -166,78 +179,107 @@
     return result
 
 
-def outgoing_kernel(send, recv, embed, out):
-    atoms = embed.shape[0]
+def put_coeffs(out, first, coeff_rows):
+    for block in range(BLOCKS):
+        left = coeff_rows(2 * block)
+        right = coeff_rows(2 * block + 1) if 2 * block + 1 < COEFFS else jnp.zeros_like(left)
+        put_rows(out, pl.ds(first + block * LANES, LANES), jnp.concatenate([left, right], axis=1))
+
+
+def outgoing_kernel(place, send, recv, embed, cot, out):
+    atoms = embed.shape[1]
     slots = out.shape[0] * out.shape[1]
     sent = listed_rows(send, (slots, LANES))
     received = listed_rows(recv, (slots, LANES))
-    picked = mask_to(iota((slots, atoms), 1) == sent[:, :atoms], bf16)
-    put_rows(out, pl.ds(0, FLAT), dot_nn(picked, embed[...]))
+    for first, listed, values in ((0, sent, embed), (COLS, received, cot)):
+        picked = mask_to(iota((slots, atoms), 1) == listed[:, :atoms], bf16)
+        put_coeffs(out, first, lambda k: dot_nn(picked, values[k]))
     lane = iota((slots, LANES), 1)
-    put_rows(out, pl.ds(FLAT, COLS - FLAT), jnp.zeros((slots, COLS - FLAT), f32))
     side = jnp.where(lane == 0, received, jnp.where(lane == 1, sent, 0))
-    put_rows(out, pl.ds(COLS, LANES), side.astype(f32))
+    put_rows(out, pl.ds(2 * COLS, LANES), side.astype(f32))
 
 
 def swapped_halves(value, edges):
     return jnp.concatenate([-value[:, edges:], value[:, :edges]], axis=1)
 
 
-def forward_kernel(
-    table, source_slot, target_slot, rot, feats, bias, wzero, wone, wtwo, ain, aedge, adot,
-    sums_out, x0, x1, x2, v0, v1, v2, pre_out, logit_out, lists_out,
-    rows, gathered, weights, terms,
-):
-    edges = source_slot.shape[1]
-    slots = table.shape[0] * table.shape[1]
-    stack_table(table, rows)
-    picked = mask_to(one_hot_rows(source_slot, slots), bf16)
-    gathered[...] = dot_tn(rows[:, pl.ds(0, FLAT)].astype(bf16), picked)
-    lists = rows[:, pl.ds(COLS, LANES)]
-    lists_out[...] = lists
-
-    def emit(degree, order, half, value):
-        ref, row, second = frame_place(degree, order, (x0, x1, x2))
-        ref[pl.ds(row, CH), lane_at(half, edges, second)] = value.astype(bf16)
-
-    to_frame(gathered, rot, edges, emit)
-
-    pre = dot_nn(ain[...], x0[pl.ds(0, CH), :]) + dot_nt(aedge[...], feats[...])
-    pre_out[...] = pre
-    hidden = jnp.where(pre > 0, pre, leak_slope * pre) * adot[...]
-    aims = one_hot_rows(target_slot, slots)
-    lane = iota((slots, LANES), 1)
-    side = jnp.where(lane == 2 * HEADS, lists[:, :1], 0.0)
-    for h in range(HEADS):
-        logit = jnp.sum(hidden[h * ALPHA : (h + 1) * ALPHA], axis=0, keepdims=True)
-        logit = logit + bias[pl.ds(h, 1), :]
-        logit_out[pl.ds(h, 1), :] = logit
-        peak = jnp.max(jnp.where(aims, logit, floor_value), axis=1, keepdims=True)
-        of_edge = jnp.sum(jnp.where(aims, peak, 0.0), axis=0, keepdims=True)
-        weight = jnp.exp(logit - of_edge)
-        weights[pl.ds(h, 1), :] = weight
-        den = jnp.sum(jnp.where(aims, weight, 0.0), axis=1, keepdims=True)
-        side = jnp.where(lane == h, den, jnp.where(lane == HEADS + h, peak, side))
-    put_rows(sums_out, pl.ds(COLS, LANES), side)
-
-    v0[...] = dot_nn(wzero[...], x0[...])
-    for out, weight, value in ((v1, wone, x1[...]), (v2, wtwo, x2[...])):
-        out[...] = dot_nn(weight[0], value) + swapped_halves(dot_nn(weight[1], value), edges)
-
-    def load(degree, order, half):
-        ref, row, second = frame_place(degree, order, (v0, v1, v2))
-        return ref[pl.ds(row, CH), lane_at(half, edges, second)]
-
-    store = store_terms(terms, edges)
-
-    def weigh(coeff, half, value):
-        lanes = lane_at(half, edges, False)
-        spread = spread_heads([weights[pl.ds(h, 1), lanes] for h in range(HEADS)])
-        store(coeff, half, value * spread)
-
-    terms[pl.ds(FLAT, COLS - FLAT), :] = jnp.zeros((COLS - FLAT, 2 * edges), bf16)
-    from_frame(load, rot, edges, weigh)
-    slot_sums(terms, mask_to(aims, bf16), sums_out)
+def make_forward(atoms):
+    def forward_kernel(
+        table, source_slot, target_slot, rot, feats, bias, wzero, wone, wtwo, ain, aedge, adot,
+        out_proj,
+        sums_out, stats_out, x0, x1, x2, v0, v1, v2, pre_out, logit_out, lists_out, agg_grad,
+        rows, gathered, weights, terms,
+    ):
+        edges = source_slot.shape[1]
+        slots = table.shape[0] * table.shape[1]
+        stack_table(table, rows)
+        picked = mask_to(one_hot_rows(source_slot, slots), bf16)
+        gathered[...] = dot_tn(rows[:, pl.ds(0, FLAT)].astype(bf16), picked)
+        lists = rows[:, pl.ds(2 * COLS, LANES)]
+        lists_out[...] = lists
+        for degree in range(LMAX + 1):
+            ids = range(degree * degree, (degree + 1) * (degree + 1))
+            cot = jnp.concatenate([rows[:, pl.ds(COLS + k * CH, CH)] for k in ids], axis=0)
+            grad = dot_nt(cot.astype(bf16), out_proj[degree])
+            for n, k in enumerate(ids):
+                agg_grad[:, pl.ds(k * CH, CH)] = grad[n * slots : (n + 1) * slots]
+
+        def emit(degree, order, half, value):
+            ref, row, second = frame_place(degree, order, (x0, x1, x2))
+            ref[pl.ds(row, CH), lane_at(half, edges, second)] = value.astype(bf16)
+
+        to_frame(gathered, rot, edges, emit)
+
+        pre = dot_nn(ain[...], x0[pl.ds(0, CH), :]) + dot_nt(aedge[...], feats[...])
+        pre_out[...] = pre
+        hidden = jnp.where(pre > 0, pre, leak_slope * pre) * adot[...]
+        aims = one_hot_rows(target_slot, slots)
+        lane = iota((slots, LANES), 1)
+        peer = iota((slots, 1), 0) // table.shape[1]
+        name = lists[:, :1] + (peer * atoms).astype(f32)
+        side = jnp.where(lane == NAME_AT, name, 0.0)
+        for h in range(HEADS):
+            logit = jnp.sum(hidden[h * ALPHA : (h + 1) * ALPHA], axis=0, keepdims=True)
+            logit = logit + bias[pl.ds(h, 1), :]
+            logit_out[pl.ds(h, 1), :] = logit
+            peak = jnp.max(jnp.where(aims, logit, floor_value), axis=1, keepdims=True)
+            of_edge = jnp.sum(jnp.where(aims, peak, 0.0), axis=0, keepdims=True)
+            weight = jnp.exp(logit - of_edge)
+            weights[pl.ds(h, 1), :] = weight
+            den = jnp.sum(jnp.where(aims, weight, 0.0), axis=1, keepdims=True)
+            side = jnp.where(lane == h, den, jnp.where(lane == PEAK_AT + h, peak, side))
+
+        v0[...] = dot_nn(wzero[...], x0[...])
+        for out, weight, value in ((v1, wone, x1[...]), (v2, wtwo, x2[...])):
+            out[...] = dot_nn(weight[0], value) + swapped_halves(dot_nn(weight[1], value), edges)
+
+        def load(degree, order, half):
+            ref, row, second = frame_place(degree, order, (v0, v1, v2))
+            return ref[pl.ds(row, CH), lane_at(half, edges, second)]
+
+        store = store_terms(terms, edges)
+
+        def weigh(coeff, half, value):
+            lanes = lane_at(half, edges, False)
+            spread = spread_heads([weights[pl.ds(h, 1), lanes] for h in range(HEADS)])
+            store(coeff, half, value * spread)
+
+        terms[pl.ds(FLAT, COLS - FLAT), :] = jnp.zeros((COLS - FLAT, 2 * edges), bf16)
+        from_frame(load, rot, edges, weigh)
+        dots = slot_sums(terms, mask_to(aims, bf16), sums_out, agg_grad)
+        head = (lane % CH) // VAL
+        for h in range(HEADS):
+            dot = jnp.sum(jnp.where(head == h, dots, 0.0), axis=1, keepdims=True)
+            side = jnp.where(lane == DOT_AT + h, dot, side)
+        put_rows(sums_out, pl.ds(COLS, LANES), side)
+
+        def copy_to(n, carry):
+            stats_out[n] = side
+            return carry
+
+        lax.fori_loop(0, stats_out.shape[0], copy_to, 0)
+
+    return forward_kernel
 
 
 def lane_heads(values, shape):
@@ -258,21 +300,6 @@
             rows_ref[at, :] = jnp.concatenate(parts, axis=0)
 
 
-def pair_weight(out_proj, block):
-    first = out_proj[degree_of(2 * block)]
-    if 2 * block + 1 >= COEFFS:
-        return first
-    second = out_proj[degree_of(2 * block + 1)]
-    blank = jnp.zeros((CH, CH), f32)
-    top = jnp.concatenate([first.astype(f32), blank], axis=1)
-    low = jnp.concatenate([blank, second.astype(f32)], axis=1)
-    return jnp.concatenate([top, low], axis=0).astype(bf16)
-
-
-def pair_key(block):
-    return degree_of(2 * block), min(degree_of(min(2 * block + 1, COEFFS)), LMAX)
-
-
 def block_cols(block):
     return pl.ds(block * LANES, min(LANES, FLAT - block * LANES))
 
@@ -280,20 +307,17 @@
 def make_finish(lanes_total):
     def finish_kernel(place, cot, out_proj, *rest):
         arrivals = rest[:lanes_total]
-        agg_out, back, rows, terms, num_grad = rest[lanes_total:]
-        atoms = cot.shape[0]
-        slots = back.shape[0] * back.shape[1]
-        total = lanes_total * slots
+        out, proj, rows, terms, agg_low = rest[lanes_total:]
+        atoms = cot.shape[1]
+        total = rows.shape[0]
         collect_rows(place, arrivals, rows)
         side = rows[:, pl.ds(COLS, LANES)]
-        at_atom = iota((total, atoms), 1).astype(f32)
-        names = at_atom == side[:, 2 * HEADS : 2 * HEADS + 1]
-        own_side = jnp.concatenate([arrivals[0][g][:, COLS:] for g in range(back.shape[0])], axis=0)
-        own = at_atom[:slots] == own_side[:, 2 * HEADS : 2 * HEADS + 1]
+        owner = (place[1] * atoms).astype(f32)
+        names = iota((total, atoms), 1).astype(f32) + owner == side[:, NAME_AT : NAME_AT + 1]
         eye = iota((atoms, atoms), 0) == iota((atoms, atoms), 1)
-        scales, dens, own_peaks = [], [], []
+        scales, dens = [], []
         for h in range(HEADS):
-            peak_rows = side[:, HEADS + h : HEADS + h + 1]
+            peak_rows = side[:, PEAK_AT + h : PEAK_AT + h + 1]
             peak = jnp.max(jnp.where(names, peak_rows, floor_value), axis=0, keepdims=True)
             of_row = jnp.sum(jnp.where(names, peak, 0.0), axis=1, keepdims=True)
             scale = jnp.exp(peak_rows - of_row)
@@ -301,7 +325,6 @@
             den = jnp.sum(jnp.where(names, scaled_den, 0.0), axis=0, keepdims=True)
             scales.append(scale)
             dens.append(jnp.sum(jnp.where(eye, den, 0.0), axis=1, keepdims=True))
-            own_peaks.append(jnp.sum(jnp.where(own, peak, 0.0), axis=1, keepdims=True))
         scale_full = lane_heads(scales, (total, LANES))
         den_full = lane_heads(dens, (atoms, LANES))
         picked = mask_to(names, bf16)
@@ -311,96 +334,80 @@
             high, low = split_two(rows[:, cols] * scale_full)
             terms[pl.ds(0, total), cols] = high
             terms[pl.ds(total, total), cols] = low
-
-        den_sum = jnp.zeros((atoms, LANES), f32)
-        weights = {}
         for block in range(BLOCKS):
-            cols = block_cols(block)
-            width = cols.size
-            agg = dot_tn(twice, terms[:, cols]) / den_full[:, :width]
-            agg_out[:, cols] = agg.astype(bf16)
-            key = pair_key(block)
-            if key not in weights:
-                weights = {key: pair_weight(out_proj, block)}
-            weight = weights[key] if width == LANES else out_proj[LMAX]
-            agg_grad = dot_nt(cot[:, cols], weight)
-            num_grad[:, cols] = (agg_grad / den_full[:, :width]).astype(bf16)
-            product = agg_grad * agg
-            if width < LANES:
-                product = jnp.concatenate([product, jnp.zeros_like(product)], axis=1)
-            den_sum = den_sum + product
-
-        own_low = mask_to(own, bf16)
-        put_rows(back, pl.ds(0, FLAT), dot_nn(own_low, num_grad[...]))
-        put_rows(back, pl.ds(FLAT, COLS - FLAT), jnp.zeros((slots, COLS - FLAT), f32))
-        head = (iota((atoms, LANES), 1) % CH) // VAL
-        lane = iota((slots, LANES), 1)
-        extra = jnp.zeros((slots, LANES), f32)
+            cols = pl.ds(block * LANES, LANES)
+            agg = (dot_tn(twice, terms[:, cols]) / den_full).astype(bf16)
+            agg_low[2 * block] = agg[:, :CH]
+            if 2 * block + 1 < COEFFS:
+                agg_low[2 * block + 1] = agg[:, CH:]
+        for degree in range(LMAX + 1):
+            ids = pl.ds(degree * degree, 2 * degree + 1)
+            stacked = ((2 * degree + 1) * atoms, CH)
+            left = agg_low[ids].reshape(stacked)
+            right = cot[ids].reshape(stacked)
+            value = dot_nn(left, out_proj[degree]).astype(bf16)
+            out[ids] = value.reshape((2 * degree + 1, atoms, CH))
+            proj[pl.ds(degree * CH, CH), :] = dot_tn(left, right)
+
+    return finish_kernel
+
+
+def combine_stats(stats, own):
+    blocks, slots = stats.shape[0], stats.shape[1]
+    chunk = max(1, PANEL // slots)
+    name = own[:, NAME_AT : NAME_AT + 1]
+
+    def part(at):
+        turned = jnp.transpose(stats[pl.ds(at * chunk, chunk)].reshape(chunk * slots, LANES))
+        same = name == turned[NAME_AT : NAME_AT + 1]
+        result = []
         for h in range(HEADS):
-            summed = jnp.sum(jnp.where(head == h, den_sum, 0.0), axis=1, keepdims=True)
-            den_grad = (-summed / dens[h]).astype(bf16).astype(f32)
-            as_row = jnp.sum(jnp.where(eye, den_grad, 0.0), axis=0, keepdims=True)
-            of_row = jnp.sum(jnp.where(own, as_row, 0.0), axis=1, keepdims=True)
-            high = own_peaks[h].astype(bf16).astype(f32)
-            rest_one = own_peaks[h] - high
-            mid = rest_one.astype(bf16).astype(f32)
-            for n, value in enumerate((of_row, high, mid, rest_one - mid)):
-                extra = jnp.where(lane == n * HEADS + h, value, extra)
-        put_rows(back, pl.ds(COLS, LANES), extra)
-
-    return finish_kernel
-
-
-def make_project(lanes_total):
-    def project_kernel(agg_low, cot, out_proj, out, proj):
-        tops = [None] * (LMAX + 1)
-        lows = [None] * (LMAX + 1)
-        weights = {}
-        for block in range(BLOCKS):
-            cols = block_cols(block)
-            width = cols.size
-            left, right = agg_low[:, cols], cot[:, cols]
-            key = pair_key(block)
-            if key not in weights:
-                weights = {key: pair_weight(out_proj, block)}
-            weight = weights[key] if width == LANES else out_proj[LMAX]
-            out[:, cols] = dot_nn(left, weight).astype(bf16)
-            outer = dot_tn(left, right)
-            first = degree_of(2 * block)
-            top = outer[:CH, :CH]
-            tops[first] = top if tops[first] is None else tops[first] + top
-            if width == LANES:
-                second = degree_of(2 * block + 1)
-                low = outer[CH:]
-                lows[second] = low if lows[second] is None else lows[second] + low
-        for degree in range(LMAX + 1):
-            piece = jnp.zeros((CH, CH), f32)
-            if tops[degree] is not None:
-                piece = piece + tops[degree]
-            if lows[degree] is not None:
-                piece = piece + lows[degree][:, CH:]
-            proj[pl.ds(degree * CH, CH), :] = piece * (1.0 / lanes_total)
-
-    return project_kernel
+            peaks = turned[PEAK_AT + h : PEAK_AT + h + 1]
+            peak = jnp.max(jnp.where(same, peaks, floor_value), axis=1, keepdims=True)
+            scale = jnp.where(same, jnp.exp(jnp.where(same, peaks - peak, 0.0)), 0.0)
+            den = jnp.sum(turned[h : h + 1] * scale, axis=1, keepdims=True)
+            dot = jnp.sum(turned[DOT_AT + h : DOT_AT + h + 1] * scale, axis=1, keepdims=True)
+            result += [peak, den, dot]
+        return tuple(result)
+
+    def step(at, held):
+        fresh = part(at)
+        result = []
+        for h in range(HEADS):
+            peak, den, dot = held[3 * h : 3 * h + 3]
+            new_peak, new_den, new_dot = fresh[3 * h : 3 * h + 3]
+            most = jnp.maximum(peak, new_peak)
+            old, new = jnp.exp(peak - most), jnp.exp(new_peak - most)
+            result += [most, den * old + new_den * new, dot * old + new_dot * new]
+        return tuple(result)
+
+    held = part(0)
+    if blocks > chunk:
+        held = lax.fori_loop(1, blocks // chunk, step, held)
+    return [held[3 * h : 3 * h + 3] for h in range(HEADS)]
 
 
 def gradient_kernel(
-    place, table, target_slot, rot, feats, x0, x1, x2, v0, v1, v2, pre, logits, adot, proj,
-    g0, top1, top2, pre_grad_out, kept0, sent0, kept1, sent1, kept2, sent2,
-    rows, spread_grad, weights, g1, g2, packed, semaphores,
+    place, stats, own, agg_grad, target_slot, rot, feats,
+    x0, x1, x2, v0, v1, v2, pre, logits, adot,
+    g0, top1, top2, pre_grad_out, kept0, sent0, kept1, sent1,
+    num_grad, spread_grad, weights, g1, g2, packed, semaphores,
 ):
     edges = target_slot.shape[1]
-    slots = table.shape[0] * table.shape[1]
-    stack_table(table, rows)
-    picked = mask_to(one_hot_rows(target_slot, slots), bf16)
-    low_rows = rows[...].astype(bf16)
-    spread_grad[...] = dot_tn(low_rows[:, :COLS], picked)
-    side = dot_tn(low_rows[:, COLS:], picked)
-    for h in range(HEADS):
-        peak = (side[HEADS + h : HEADS + h + 1] + side[2 * HEADS + h : 2 * HEADS + h + 1]) + side[
-            3 * HEADS + h : 3 * HEADS + h + 1
-        ]
-        weights[pl.ds(h, 1), :] = jnp.exp(logits[pl.ds(h, 1), :] - peak)
+    slots = agg_grad.shape[0]
+    aims = one_hot_rows(target_slot, slots)
+    combined = combine_stats(stats, own[...])
+    den_grads = []
+    for h, (peak, den, dot) in enumerate(combined):
+        of_edge = jnp.sum(jnp.where(aims, peak, 0.0), axis=0, keepdims=True)
+        weights[pl.ds(h, 1), :] = jnp.exp(logits[pl.ds(h, 1), :] - of_edge)
+        den_grad = (-(dot / den) / den).astype(bf16).astype(f32)
+        den_grads.append(jnp.sum(jnp.where(aims, den_grad, 0.0), axis=0, keepdims=True))
+    den_full = lane_heads([den for peak, den, dot in combined], (slots, LANES))
+    for block in range(BLOCKS):
+        cols = block_cols(block)
+        num_grad[:, cols] = (agg_grad[:, cols] / den_full[:, : cols.size]).astype(bf16)
+    spread_grad[...] = dot_tn(num_grad[...], mask_to(aims, bf16))
 
     state = {}
 
@@ -429,7 +436,7 @@
 
     hidden = jnp.where(pre[...] > 0, pre[...], leak_slope * pre[...])
     logit_grads = [
-        weights[pl.ds(h, 1), :] * (weights[pl.ds(HEADS + h, 1), :] + side[h : h + 1])
+        weights[pl.ds(h, 1), :] * (weights[pl.ds(HEADS + h, 1), :] + den_grads[h])
         for h in range(HEADS)
     ]
     tall = jnp.concatenate(
@@ -463,26 +470,12 @@
             copy.start()
             copies.append(copy)
 
-    row = CHUNKS[1][0]
-    for start in range(0, 2 * DIM1, PANEL):
-        put(row, dot_nt(x1[...], g1[pl.ds(start, PANEL), :]))
-        row += DIM1
-    send(1, kept1, sent1)
-
     row = 0
-    for start in range(0, DIM0, PANEL):
-        size = min(PANEL, DIM0 - start)
-        put(row, dot_nt(x0[...], g0[pl.ds(start, size), :]))
-        if size < PANEL:
-            put(row, proj[...], size)
-        row += DIM0
-    send(0, kept0, sent0)
-
-    row = CHUNKS[2][0]
-    for start in range(0, 2 * DIM2, PANEL):
-        size = min(PANEL, 2 * DIM2 - start)
-        put(row, dot_nt(x2[...], g2[pl.ds(start, size), :]))
-        row += DIM2
+    for left, right, dim in ((x1, g1, DIM1), (x2, g2, DIM2)):
+        for start in range(0, 2 * dim, PANEL):
+            size = min(PANEL, 2 * dim - start)
+            put(row, dot_nt(left[...], right[pl.ds(start, size), :]))
+            row += dim
     row -= DIM2
     edge_ch = feats.shape[1]
     edge_grad = lax.dot_general(
@@ -498,12 +491,21 @@
     put(row + 2 * edge_ch, jnp.where(tail == 0, first, jnp.where(tail == 1, second, 0.0)), LANES)
     row += DIM2
     put(row, dot_nt(x0[pl.ds(0, CH), :], pre_grad))
-    send(2, kept2, sent2)
+    send(0, kept0, sent0)
+
+    row = CHUNKS[1][0]
+    for start in range(0, DIM0, PANEL):
+        size = min(PANEL, DIM0 - start)
+        put(row, dot_nt(x0[...], g0[pl.ds(start, size), :]))
+        if size < PANEL:
+            put(row, jnp.zeros((DIM0, PANEL - size), f32), size)
+        row += DIM0
+    send(1, kept1, sent1)
     for copy in copies:
         copy.wait()
 
 
-CHUNKS = ((0, 2 * DIM0), (2 * DIM0, 3 * DIM1), (2 * DIM0 + 3 * DIM1, 3 * DIM2 + CH))
+CHUNKS = ((0, 3 * DIM1 + 3 * DIM2 + CH), (3 * DIM1 + 3 * DIM2 + CH, 2 * DIM0))
 PACKED_ROWS = sum(size for start, size in CHUNKS)
 
 
@@ -513,27 +515,21 @@
     return jnp.where(first, left, right), jnp.where(first, right, left)
 
 
-def unpack_zero_kernel(place, mine, other, zero, proj):
+def unpack_zero_kernel(place, mine, other, zero):
     left, right = halves_of(place, mine, other)
     zero[:, pl.ds(0, LANES)] = left[:DIM0].astype(bf16)
     zero[:, pl.ds(LANES, LANES)] = right[:DIM0].astype(bf16)
     zero[:, pl.ds(2 * LANES, LANES)] = left[DIM0:].astype(bf16)
     zero[:, pl.ds(3 * LANES, DIM0 - 3 * LANES)] = right[DIM0:, : DIM0 - 3 * LANES].astype(bf16)
-    for degree in range(LMAX + 1):
-        start = DIM0 + degree * CH
-        proj[degree] = right[start : start + CH, DIM0 - 3 * LANES :].astype(bf16)
-
-
-def unpack_one_kernel(place, mine, other, one):
+
+
+def unpack_rest_kernel(place, mine, other, one, two, alpha_in, alpha_edge, alpha_dot):
     left, right = halves_of(place, mine, other)
     for n in range(2 * DIM1 // LANES):
         panel = (left, right)[n % 2][(n // 2) * DIM1 : (n // 2 + 1) * DIM1]
         per = DIM1 // LANES
         one[n // per, :, pl.ds((n % per) * LANES, LANES)] = panel.astype(bf16)
-
-
-def unpack_two_kernel(place, mine, other, two, alpha_in, alpha_edge, alpha_dot):
-    left, right = halves_of(place, mine, other)
+    left, right = left[3 * DIM1 :], right[3 * DIM1 :]
     panels = [(left, right)[n % 2][(n // 2) * DIM2 : (n // 2 + 1) * DIM2] for n in range(5)]
     whole = jnp.concatenate(panels, axis=1)
     two[0] = whole[:, :DIM2].astype(bf16)
@@ -573,16 +569,18 @@
     def collect_kernel(place, *rest):
         arrivals = rest[:lanes_total]
         out, rows = rest[lanes_total:]
-        atoms = out.shape[0]
+        atoms = out.shape[1]
         total = rows.shape[0]
         collect_rows(place, arrivals, rows)
         index = rows[:, pl.ds(COLS, LANES)][:, 1:2]
         picked = mask_to(iota((total, atoms), 1).astype(f32) == index, bf16)
         twice = jnp.concatenate([picked, picked], axis=0)
         for block in range(BLOCKS):
-            cols = block_cols(block)
-            high, low = split_two(rows[:, cols])
-            out[:, cols] = dot_tn(twice, jnp.concatenate([high, low], axis=0)).astype(bf16)
+            high, low = split_two(rows[:, pl.ds(block * LANES, LANES)])
+            sums = dot_tn(twice, jnp.concatenate([high, low], axis=0)).astype(bf16)
+            out[2 * block] = sums[:, :CH]
+            if 2 * block + 1 < COEFFS:
+                out[2 * block + 1] = sums[:, CH:]
 
     return collect_kernel
 
@@ -630,9 +628,10 @@
     return (lax.axis_index(axis) >> bit) & 1
 
 
-def sum_all(current):
+def sum_all(current, first):
     steps = [("edge", n) for n in range(1, bits_of("edge"))]
     steps += [("graph", n) for n in range(bits_of("graph"))]
+    steps.sort(key=lambda step: step[0] != first)
     for axis, bit in steps:
         mine = own_bit(axis, bit)
         parts = current.reshape(2, current.shape[0] // 2, -1)
@@ -659,15 +658,18 @@
     edges = rotation.shape[0]
     cap = send_rows.shape[3]
     slots = peers * cap
-    place = lax.axis_index("edge").astype(jnp.int32).reshape(1)
+    own_place = [lax.axis_index("edge"), lax.axis_index("graph")]
+    place = jnp.stack(own_place).astype(jnp.int32)
+    blocks = peers * lanes_total
 
     def exchange(value):
         return lax.all_to_all(value, "graph", split_axis=0, concat_axis=0, tiled=True)
 
+    cot = jnp.transpose(out_cotangent, (1, 0, 2))
     (outgoing,) = call(
-        outgoing_kernel, [((peers, cap, WIDE), bf16)], [],
-        send_rows, recv_rows, atom_embed.reshape(atoms, FLAT),
-        scalars=2, work=1,
+        outgoing_kernel, [((peers, cap, TABLE), bf16)], [],
+        place, send_rows, recv_rows, jnp.transpose(atom_embed, (1, 0, 2)), cot,
+        scalars=3, work=2,
     )
     table = exchange(outgoing)
 
@@ -676,12 +678,12 @@
     rot = rotation.T.astype(f32)
     bias = edge_bias.T
     adot = alpha_dot.astype(f32).reshape(-1, 1)
-    cot = out_cotangent.reshape(atoms, FLAT)
-
-    sums, x0, x1, x2, v0, v1, v2, pre, logits, lists = call(
-        forward_kernel,
+
+    sums, stats, x0, x1, x2, v0, v1, v2, pre, logits, lists, agg_grad = call(
+        make_forward(atoms),
         [
             ((peers, cap, WIDE), f32),
+            ((blocks, slots, LANES), f32),
             ((DIM0, edges), bf16),
             ((DIM1, 2 * edges), bf16),
             ((DIM2, 2 * edges), bf16),
@@ -691,34 +693,21 @@
             ((HEADS * ALPHA, edges), f32),
             ((8, edges), f32),
             ((slots, LANES), f32),
+            ((slots, FLAT), f32),
         ],
         [
-            ((slots, WIDE), f32),
+            ((slots, TABLE), f32),
             ((FLAT, edges), f32),
             ((8, edges), f32),
             ((COLS, 2 * edges), bf16),
         ],
         table, source_row, target_row, rot, edge_feats, bias,
         conv_zero.T, jnp.swapaxes(conv_one, 1, 2), jnp.swapaxes(conv_two, 1, 2),
-        alpha_in.T, alpha_edge.T, adot,
+        alpha_in.T, alpha_edge.T, adot, out_proj,
         work=8,
     )
-
-    arrivals = gather_lanes(exchange(sums))
-    total = lanes_total * slots
-    agg_low, back = call(
-        make_finish(lanes_total),
-        [((atoms, FLAT), bf16), ((peers, cap, WIDE), bf16)],
-        [((total, WIDE), f32), ((2 * total, COLS), bf16), ((atoms, FLAT), bf16)],
-        place, cot, out_proj, *arrivals,
-        scalars=1,
-    )
-    out, proj = call(
-        make_project(lanes_total),
-        [((atoms, FLAT), bf16), (((LMAX + 1) * CH, CH), f32)],
-        [],
-        agg_low, cot, out_proj,
-    )
+    own_stats = stats[0]
+    all_stats = lax.all_to_all(stats, ("graph", "edge"), split_axis=0, concat_axis=0, tiled=True)
 
     halves = [((size, LANES), f32) for start, size in CHUNKS for _ in range(2)]
     g0, g1, g2, pre_grad, *halves = call(
@@ -731,21 +720,23 @@
         ]
         + halves,
         [
-            ((slots, WIDE), f32),
-            ((COLS, edges), f32),
+            ((slots, FLAT), bf16),
+            ((FLAT, edges), f32),
             ((8, edges), f32),
             ((2 * DIM1, 2 * edges), bf16),
             ((2 * DIM2, 2 * edges), bf16),
             ((2, PACKED_ROWS, LANES), f32),
             pltpu.SemaphoreType.DMA((len(halves),)),
         ],
-        place, exchange(back), target_row, rot, edge_feats,
-        x0, x1, x2, v0, v1, v2, pre, logits, adot, proj,
+        place, all_stats, own_stats, agg_grad, target_row, rot, edge_feats,
+        x0, x1, x2, v0, v1, v2, pre, logits, adot,
         scalars=1, apart=len(halves), work=8,
     )
     currents = [
         halves[2 * n] + swap(halves[2 * n + 1], "edge", 0) for n in range(len(CHUNKS))
     ]
+
+    total = lanes_total * slots
     (source_sums,) = call(
         source_kernel,
         [((peers, cap, WIDE), f32)],
@@ -758,40 +749,46 @@
         source_row, lists, rot, g0, g1, g2, pre_grad, conv_zero, conv_one, conv_two, alpha_in,
         after=currents, work=6,
     )
+    out, proj = call(
+        make_finish(lanes_total),
+        [((COEFFS, atoms, CH), bf16), (((LMAX + 1) * CH, CH), f32)],
+        [((total, WIDE), f32), ((2 * total, COLS), bf16), ((COEFFS, atoms, CH), bf16)],
+        place, cot, out_proj, *gather_lanes(exchange(sums)),
+        scalars=1,
+    )
+    for bit in range(bits_of("graph")):
+        proj = proj + swap(proj, "graph", bit)
     (embed,) = call(
         make_collect(lanes_total),
-        [((atoms, FLAT), bf16)],
+        [((COEFFS, atoms, CH), bf16)],
         [((total, WIDE), f32)],
         place, *gather_lanes(exchange(source_sums)),
         scalars=1,
     )
 
-    pairs = [sum_all(current) for current in currents]
-    zero, proj_grad = call(
-        unpack_zero_kernel,
-        [((DIM0, DIM0), bf16), ((LMAX + 1, CH, CH), bf16)],
-        [], place, *pairs[0], scalars=1, work=1,
-    )
-    (one,) = call(
-        unpack_one_kernel, [((2, DIM1, DIM1), bf16)], [], place, *pairs[1], scalars=1, work=1
-    )
-    two, grad_in, grad_edge, grad_dot = call(
-        unpack_two_kernel,
+    rest_pair = sum_all(currents[0], "edge")
+    zero_pair = sum_all(currents[1], "graph")
+    (zero,) = call(
+        unpack_zero_kernel, [((DIM0, DIM0), bf16)], [], place, *zero_pair, scalars=1, work=1
+    )
+    one, two, grad_in, grad_edge, grad_dot = call(
+        unpack_rest_kernel,
         [
+            ((2, DIM1, DIM1), bf16),
             ((2, DIM2, DIM2), bf16),
             (alpha_in.shape, bf16),
             (alpha_edge.shape, bf16),
             ((2, LANES), bf16),
         ],
-        [], place, *pairs[2], scalars=1, work=1,
-    )
-
-    def shaped(rows):
-        return rows.reshape(atoms, COEFFS, CH)
+        [], place, *rest_pair, scalars=1, work=1,
+    )
+
+    def shaped(value):
+        return jnp.transpose(value, (1, 0, 2))
 
     return (
         shaped(out), shaped(embed), zero, one, two, grad_in, grad_edge, grad_dot.reshape(-1),
-        proj_grad,
+        proj.astype(bf16).reshape(LMAX + 1, CH, CH),
     )
 
 

time: 151 us -> 149 us (0.987)
  waiting for transfers between devices: 34.8 us -> 55.7 us
  blocking collectives: 12.6 us -> 0 us
  local copies, waits for them, and re-layouts: 17.9 us -> 12.2 us
  starting transfers between devices: 42.4 us -> 37.5 us
  other arithmetic: 1.45 us -> 3.99 us
    all_to_all x1 -> x0, blocking collectives: 12.6 us -> none  [exchange(): lax.all_to_all(value, 'graph', split_axis=0, concat_axis=0, tiled=True)]
    ppermute x30 -> x24, starting transfers between devices: 29.1 us -> 18.9 us  [swap(): return lax.ppermute(value, axis, [(i, i ^ 1 << bit) for i in range(size)])]
    all_to_all x3, waiting for transfers between devices: 3.36 us -> 11 us  [exchange(): lax.all_to_all(value, 'graph', split_axis=0, concat_axis=0, tiled=True)]
    all_to_all x0 -> x1, waiting for transfers between devices: none -> 6.64 us  [shards(): lax.all_to_all(stats, ('graph', 'edge'), split_axis=0, concat_axis=0, til...]
    ppermute x30 -> x24, waiting for transfers between devices: 31.4 us -> 38 us  [swap(): return lax.ppermute(value, axis, [(i, i ^ 1 << bit) for i in range(size)])]
    all_to_all x0 -> x1, starting transfers between devices: none -> 4.44 us  [shards(): lax.all_to_all(stats, ('graph', 'edge'), split_axis=0, concat_axis=0, til...]
    unnamed x77 -> x53, local copies, waits for them, and re-layouts: 13.5 us -> 9.93 us
    reshape x4 -> x0, local copies, waits for them, and re-layouts: 3.37 us -> none  [the longest x2 1.44 us: shaped(): return rows.reshape(atoms, COEFFS, CH)]
  transfers between devices with their start and end apart: 33 -> 28, of which waited for: 15 -> 14; matrix products, arithmetic and copies ran while one was open for 7% -> 7% of each run, Pallas kernels for 10% -> 10%
where the time goes in v2:
time: 149 us; the launch traced here: 148 us
  waiting for transfers between devices  55.7 us (37%)
  Pallas kernels  37.8 us (25%)
  starting transfers between devices  37.5 us (25%)
  local copies, waits for them, and re-layouts  12.2 us (8%)
  other arithmetic  3.99 us (3%)
    ppermute x24, waiting for transfers between devices, swap(): return lax.ppermute(value, axis, [(i, i ^ 1 << bit) for i in range(size)])  38 us
    pallas_call x8, Pallas kernels, call(): pl.pallas_call(kernel, out_shape=[jax.ShapeDtypeStruct(shape, kind) for s...  37.8 us
    ppermute x24, starting transfers between devices, swap(): return lax.ppermute(value, axis, [(i, i ^ 1 << bit) for i in range(size)])  18.9 us
    all_to_all x3, starting transfers between devices, exchange(): lax.all_to_all(value, 'graph', split_axis=0, concat_axis=0, tiled=True)  14.2 us
    all_to_all x3, waiting for transfers between devices, exchange(): lax.all_to_all(value, 'graph', split_axis=0, concat_axis=0, tiled=True)  11 us
    unnamed x53, local copies, waits for them, and re-layouts  9.93 us
    all_to_all x1, waiting for transfers between devices, shards(): lax.all_to_all(stats, ('graph', 'edge'), split_axis=0, concat_axis=0, til...  6.64 us
    all_to_all x1, starting transfers between devices, shards(): lax.all_to_all(stats, ('graph', 'edge'), split_axis=0, concat_axis=0, til...  4.44 us
  transfers between devices with their start and end apart: 28, of which 14 were waited for; matrix products, arithmetic and copies ran while one was open for 7% of the time, Pallas kernels for 10%

profile of v2, /device:TPU:0, one launch (start us, length us, event | category | flops | bytes accessed | tf_op | source)
XLA Modules:
  0.0 148.1 jit_solution(4366830359521685031)
XLA Ops:
  0.6 0.7 pad_add_fusion.place
  1.3 2.3 %shard_map.223 = bf16[4,4,6528]{2,1,0:T(4,128)(2,1)} custom-call(s32[2]{0:T(128)} %pad_add_fusion.place, s32[1,4,1,4]{3,2,1,0:T(1,128)} %send.1, s32[1,4,1,4]{3,2,1,0:T(1,128)} %recv.1, bf16[49,32,64]{2,1,0:T(8,128)(2,1)} %bitcast.74, bf16[49,32,64]{2,1,0:T(8,128)(2,1)} %bitcast.75), custom_call_target="tpu_custom_call" | custom-call | flops 2000000000 | bytes 401544 | tf_op jit(solution)/shard_map/pallas_call | solution.py:598
  3.6 6.4 %all-to-all-start = ((bf16[4,4,6528]{2,1,0:T(4,128)(2,1)}), bf16[4,4,6528]{2,1,0:T(4,128)(2,1)S(1)}, u32[]{:S(2)}, u32[]{:S(2)}) async-start(bf16[4,4,6528]{2,1,0:T(4,128)(2,1)} %shard_map.223), calls=%async_computation | async-start | bytes 417792 | tf_op jit(solution)/shard_map/all_to_all | solution.py:666
  10.1 0.8 copy.35.adot
  10.9 1.1 copy.31
  12.0 1.0 copy.32
  13.0 1.0 copy.30
  13.9 0.7 copy.33
  14.7 0.7 copy.34
  15.4 0.7 convert_bitcast_fusion.rot
  16.2 1.7 %all-to-all-done.table = bf16[4,4,6528]{2,1,0:T(4,128)(2,1)S(1)} async-done(((bf16[4,4,6528]{2,1,0:T(4,128)(2,1)}), bf16[4,4,6528]{2,1,0:T(4,128)(2,1)S(1)}, u32[]{:S(2)}, u32[]{:S(2)}) %all-to-all-start) | async-done | bytes 208928 | tf_op jit(solution)/shard_map/all_to_all | solution.py:666
  17.9 0.7 copy-done.11
  18.6 10.0 %shard_map.224 = (f32[4,4,3328]{2,1,0:T(4,128)}, f32[16,16,128]{2,1,0:T(8,128)}, bf16[448,256]{1,0:T(8,128)(2,1)}, bf16[384,512]{1,0:T(8,128)(2,1)}, bf16[320,51...) custom-call(bf16[4,4,6528]{2,1,0:T(4,128)(2,1)} %copy-done.11, ...), custom_call_target="tpu_custom_call" | custom-call | flops 8000000000 | bytes 2078720 | tf_op jit(solution)/shard_map/pallas_call | solution.py:598
  28.5 4.4 %all-to-all-start.2 = ((f32[16,16,128]{2,1,0:T(8,128)}), f32[16,16,128]{2,1,0:T(8,128)S(1)}, u32[]{:S(2)}, u32[]{:S(2)}) async-start(f32[16,16,128]{2,1,0:T(8,128)} %get-tuple-element.39), calls=%async_computation.2 | async-start | bytes 262144 | tf_op jit(solution)/shard_map/all_to_all | solution.py:710
  33.0 1.3 slice_bitcast_fusion.own
  34.3 6.6 %all-to-all-done.2.stats = f32[16,16,128]{2,1,0:T(8,128)S(1)} async-done(((f32[16,16,128]{2,1,0:T(8,128)}), f32[16,16,128]{2,1,0:T(8,128)S(1)}, u32[]{:S(2)}, u32[]{:S(2)}) %all-to-all-start.2) | async-done | bytes 131104 | tf_op jit(solution)/shard_map/all_to_all | solution.py:710
  40.9 0.7 copy-done.12
  41.6 8.9 %shard_map.226 = (bf16[448,256]{1,0:T(8,128)(2,1)}, bf16[384,512]{1,0:T(8,128)(2,1)}, bf16[320,512]{1,0:T(8,128)(2,1)}, bf16[256,256]{1,0:T(8,128)(2,1)}, f32[21...) custom-call(s32[2]{0:T(128)} %pad_add_fusion.place, f32[16,16,128]{2,1,0:T(8,128)} %copy-done.12, ...), custom_call_target="tpu_custom_call" | custom-call | flops 8000000000 | bytes 3769352 | tf_op jit(solution)/shard_map/pallas_call | solution.py:598
  50.6 0.5 collective-permute-start.3
  51.1 3.6 %all-to-all-start.1 = ((f32[4,4,3328]{2,1,0:T(4,128)}), f32[4,4,3328]{2,1,0:T(4,128)S(1)}, u32[]{:S(2)}, u32[]{:S(2)}) async-start(f32[4,4,3328]{2,1,0:T(4,128)} %get-tuple-element.36), calls=%async_computation.1 | async-start | bytes 425984 | tf_op jit(solution)/shard_map/all_to_all | solution.py:666
  54.6 1.2 add.64.rest_1_
  55.8 1.9 %collective-permute-start.8 = (f32[448,128]{1,0:T(8,128)S(1)}, f32[448,128]{1,0:T(8,128)S(1)}, u32[]{:S(2)}, u32[]{:S(2)}) collective-permute-start(f32[448,128]{1,0:T(8,128)S(1)} %dynamic-slice_bitcast_fusion.2), channel_id=1, source_target_pairs={{0,4},{4,0},{8,12},{12,8},{1,5},{5,1},{9,13},{13,9},{2,6},{6,2},{1... | collective-permute-start | bytes 688136 | tf_op jit(solution)/shard_map/ppermute | solution.py:613
  57.7 4.5 %all-to-all-done.1.rest_0_ = f32[4,4,3328]{2,1,0:T(4,128)S(1)} async-done(((f32[4,4,3328]{2,1,0:T(4,128)}), f32[4,4,3328]{2,1,0:T(4,128)S(1)}, u32[]{:S(2)}, u32[]{:S(2)}) %all-to-all-start.1) | async-done | bytes 213024 | tf_op jit(solution)/shard_map/all_to_all | solution.py:666
  62.2 0.3 collective-permute-start.1
  62.5 5.7 %collective-permute-done.1.rest_2_ = f32[4,4,3328]{2,1,0:T(4,128)} collective-permute-done((f32[4,4,3328]{2,1,0:T(4,128)S(1)}, f32[4,4,3328]{2,1,0:T(4,128)}, u32[]{:S(2)}, u32[]{:S(2)}) %collective-permute-start.1) | collective-permute-done | bytes 213024 | tf_op jit(solution)/shard_map/ppermute | solution.py:613
  68.2 0.8 collective-permute-start.9
  69.0 0.1 add.63.rest_0_
  69.2 0.4 collective-permute-start.15
  69.6 0.3 collective-permute-done.2.rest_3_
  69.9 0.4 copy-done.20
  70.3 0.7 copy-done.22
  71.0 3.3 %shard_map.225 = (bf16[49,32,64]{2,1,0:T(8,128)(2,1)}, f32[448,64]{1,0:T(8,128)}) custom-call(s32[2]{0:T(128)} %pad_add_fusion.place, bf16[49,32,64]{2,1,0:T(8,128)(2,1)} %bitcast.76, bf16[7,64,64]{2,1,0:T(8,128)(2,1)} %out_proj.3, f32[4,4,3328]{2,1,0:T(4,128)} %copy-done.10, f32[4,4,3328]{2,1,0:T(4,128)} %copy-done.20, ...), custom_call_target="tpu_custom_call" | custom-call | flops 4000000000 | bytes 1110024 | tf_op jit(solution)/shard_map/pallas_call | solution.py:598
  74.3 2.5 %collective-permute-start.22 = (f32[448,64]{1,0:T(8,128)}, f32[448,64]{1,0:T(8,128)S(1)}, u32[]{:S(2)}, u32[]{:S(2)}) collective-permute-start(f32[448,64]{1,0:T(8,128)} %get-tuple-element.62), channel_id=1, source_target_pairs={{0,4},{4,0},{8,12},{12,8},{1,5},{5,1},{9,13},{13,9},{2,6},{6,2},{1... | collective-permute-start | bytes 344072 | tf_op jit(solution)/shard_map/ppermute | solution.py:613
  76.8 0.4 collective-permute-done.9
  77.3 1.1 collective-permute-start.10
  78.4 6.2 %collective-permute-done.15 = f32[1088,128]{1,0:T(8,128)S(1)} collective-permute-done((f32[1088,128]{1,0:T(8,128)S(1)}, f32[1088,128]{1,0:T(8,128)S(1)}, u32[]{:S(2)}, u32[]{:S(2)}) %collective-permute-start.15) | collective-permute-done | bytes 557088 | tf_op jit(solution)/shard_map/ppermute | solution.py:613
  84.8 2.3 %collective-permute-start.16 = (f32[544,128]{1,0:T(8,128)S(1)}, f32[544,128]{1,0:T(8,128)S(1)}, u32[]{:S(2)}, u32[]{:S(2)}) collective-permute-start(f32[544,128]{1,0:T(8,128)S(1)} %dynamic-slice_bitcast_fusion.1), channel_id=1, source_target_pairs={{0,4},{4,0},{8,12},{12,8},{1,5},{5,1},{9,13},{13,9},{2,6},{6,2},{1... | collective-permute-start | bytes 835592 | tf_op jit(solution)/shard_map/ppermute | solution.py:613
  87.1 1.7 %collective-permute-start.23 = (f32[448,64]{1,0:T(8,128)S(1)}, f32[448,64]{1,0:T(8,128)S(1)}, u32[]{:S(2)}, u32[]{:S(2)}) collective-permute-start(f32[448,64]{1,0:T(8,128)S(1)} %add.77), channel_id=1, source_target_pairs={{0,8},{4,12},{8,0},{12,4},{1,9},{5,13},{9,1},{13,5},{2,10},{6,14},... | collective-permute-start | bytes 344072 | tf_op jit(solution)/shard_map/ppermute | solution.py:613
  88.9 0.2 collective-permute-start.11
  89.1 8.3 %collective-permute-done.16 = f32[544,128]{1,0:T(8,128)S(1)} collective-permute-done((f32[544,128]{1,0:T(8,128)S(1)}, f32[544,128]{1,0:T(8,128)S(1)}, u32[]{:S(2)}, u32[]{:S(2)}) %collective-permute-start.16) | collective-permute-done | bytes 278560 | tf_op jit(solution)/shard_map/ppermute | solution.py:613
  97.5 1.2 collective-permute-start.17
  98.7 1.8 %collective-permute-start.12 = (bf16[224,128]{1,0:T(8,128)(2,1)S(1)}, bf16[224,128]{1,0:T(8,128)(2,1)S(1)}, u32[]{:S(2)}, u32[]{:S(2)}) collective-permute-start(bf16[224,128]{1,0:T(8,128)(2,1)S(1)} %pad_maximum_fusion.5), channel_id=1, source_target_pairs={{0,8},{4,12},{8,0},{12,4},{1,9},{5,13},{9,1},{13,5},{2,10},{6,14},... | collective-permute-start | bytes 172040 | tf_op jit(solution)/shard_map/ppermute | solution.py:613
  100.6 7.1 %collective-permute-done.17 = f32[272,128]{1,0:T(8,128)S(1)} collective-permute-done((f32[272,128]{1,0:T(8,128)S(1)}, f32[272,128]{1,0:T(8,128)S(1)}, u32[]{:S(2)}, u32[]{:S(2)}) %collective-permute-start.17) | collective-permute-done | bytes 139296 | tf_op jit(solution)/shard_map/ppermute | solution.py:613
  107.7 6.4 %shard_map.227 = f32[4,4,3328]{2,1,0:T(4,128)} custom-call(s32[1,256]{1,0:T(1,128)} %bitcast.81, f32[16,128]{1,0:T(8,128)} %get-tuple-element.38.lists, f32[235,256]{1,0:T(8,128)} %convert_bitcast_fusion.rot, bf16[448,256]{1,0:T(8,128)(2,1)} %get-tuple-element.49.g0, bf16[384,512]{1,0:T(8,128)(2,1)} %get-tuple-element.50.g1, ...), custom_call_target="tpu_custom_call" | custom-call | flops 6000000000 | bytes 2764800 | tf_op jit(solution)/shard_map/pallas_call | solution.py:598
  114.1 4.2 %all-to-all-start.3 = ((f32[4,4,3328]{2,1,0:T(4,128)}), f32[4,4,3328]{2,1,0:T(4,128)S(1)}, u32[]{:S(2)}, u32[]{:S(2)}) async-start(f32[4,4,3328]{2,1,0:T(4,128)} %shard_map.227), calls=%async_computation.3 | async-start | bytes 425984 | tf_op jit(solution)/shard_map/all_to_all | solution.py:666
  118.3 2.2 %collective-permute-start.19 = (bf16[544,128]{1,0:T(8,128)(2,1)S(1)}, bf16[544,128]{1,0:T(8,128)(2,1)S(1)}, u32[]{:S(2)}, u32[]{:S(2)}) collective-permute-start(bf16[544,128]{1,0:T(8,128)(2,1)S(1)} %pad_maximum_fusion.3), channel_id=1, source_target_pairs={{0,4},{4,0},{8,12},{12,8},{1,5},{5,1},{9,13},{13,9},{2,6},{6,2},{1... | collective-permute-start | bytes 417800 | tf_op jit(solution)/shard_map/ppermute | solution.py:613
  120.6 0.1 collective-permute-start.13
  120.6 4.8 %all-to-all-done.3.rest_0_ = f32[4,4,3328]{2,1,0:T(4,128)S(1)} async-done(((f32[4,4,3328]{2,1,0:T(4,128)}), f32[4,4,3328]{2,1,0:T(4,128)S(1)}, u32[]{:S(2)}, u32[]{:S(2)}) %all-to-all-start.3) | async-done | bytes 213024 | tf_op jit(solution)/shard_map/all_to_all | solution.py:666
  125.4 0.5 collective-permute-start.6
  126.0 2.4 %collective-permute-done.19 = bf16[544,128]{1,0:T(8,128)(2,1)S(1)} collective-permute-done((bf16[544,128]{1,0:T(8,128)(2,1)S(1)}, bf16[544,128]{1,0:T(8,128)(2,1)S(1)}, u32[]{:S(2)}, u32[]{:S(2)}) %collective-permute-start.19) | collective-permute-done | bytes 139296 | tf_op jit(solution)/shard_map/ppermute | solution.py:613
  128.5 0.6 collective-permute-start.20
  129.1 0.8 collective-permute-done.13
  130.1 0.5 collective-permute-start.5
  130.6 2.7 %collective-permute-done.6.rest_2_ = f32[4,4,3328]{2,1,0:T(4,128)S(1)} collective-permute-done((f32[4,4,3328]{2,1,0:T(4,128)S(1)}, f32[4,4,3328]{2,1,0:T(4,128)S(1)}, u32[]{:S(2)}, u32[]{:S(2)}) %collective-permute-start.6) | collective-permute-done | bytes 213024 | tf_op jit(solution)/shard_map/ppermute | solution.py:613
  133.3 4.0 %collective-permute-done.20 = bf16[1088,128]{1,0:T(8,128)(2,1)S(1)} collective-permute-done((bf16[1088,128]{1,0:T(8,128)(2,1)S(1)}, bf16[1088,128]{1,0:T(8,128)(2,1)S(1)}, u32[]{:S(2)}, u32[]{:S(2)}) %collective-permute-start.20) | collective-permute-done | bytes 278560 | tf_op jit(solution)/shard_map/ppermute | solution.py:613
  137.2 0.1 broadcast_select_fusion.1
  137.6 0.7 add_convert_fusion
  138.3 0.7 copy-done.17
  139.0 1.9 %shard_map.229 = bf16[448,448]{1,0:T(8,128)(2,1)} custom-call(s32[2]{0:T(128)} %pad_add_fusion.place, bf16[896,128]{1,0:T(8,128)(2,1)} %copy-done.7, bf16[896,128]{1,0:T(8,128)(2,1)} %copy-done.17), custom_call_target="tpu_custom_call" | custom-call | flops 1000000000 | bytes 458760 | tf_op jit(solution)/shard_map/pallas_call | solution.py:598
  140.9 0.7 copy-done.19
  141.6 0.7 copy-done.21
  142.3 2.6 %shard_map.228 = bf16[49,32,64]{2,1,0:T(8,128)(2,1)} custom-call(s32[2]{0:T(128)} %pad_add_fusion.place, f32[4,4,3328]{2,1,0:T(4,128)} %copy-done.9, f32[4,4,3328]{2,1,0:T(4,128)} %copy-done.19, f32[4,4,3328]{2,1,0:T(4,128)} %copy-done.18, f32[4,4,3328]{2,1,0:T(4,128)} %copy-done.21), custom_call_target="tpu_custom_call" | custom-call | flops 4000000000 | bytes 851976 | tf_op jit(solution)/shard_map/pallas_call | solution.py:598
  144.9 0.8 copy-done.16
  145.7 2.4 %shard_map.230 = (bf16[2,384,384]{2,1,0:T(8,128)(2,1)}, bf16[2,320,320]{2,1,0:T(8,128)(2,1)}, bf16[64,256]{1,0:T(8,128)(2,1)}, bf16[128,256]{1,0:T(8,128)(2,1)}, bf16[2,128]{1,0:T(2,128)(2,1)}) custom-call(s32[2]{0:T(128)} %pad_add_fusion.place, bf16[2176,128]{1,0:T(8,128)(2,1)} %copy-done.4, bf16[2176,128]{1,0:T(8,128)(2,1)} %copy-done.16), custom_call_target="tpu_custom_call" | custom-call | flops 1000000000 | bytes 1114120 | tf_op jit(solution)/shard_map/pallas_call | solution.py:598
  (86 shorter events, 1.0 us)
Async XLA Ops:
  1.3 8.8 %copy-start.23 = (bf16[256]{0:T(256)(128)(2,1)S(1)}, bf16[256]{0:T(256)(128)(2,1)}, u32[]{:S(2)}) copy-start(bf16[256]{0:T(256)(128)(2,1)} %param.30) | copy-start | bytes 1540
  1.3 9.6 %copy-start.3 = (bf16[2,384,384]{2,1,0:T(8,128)(2,1)S(1)}, bf16[2,384,384]{2,1,0:T(8,128)(2,1)}, u32[]{:S(2)}) copy-start(bf16[2,384,384]{2,1,0:T(8,128)(2,1)} %wone.1) | copy-start | bytes 1769476
  3.6 8.3 %copy-start.5 = (bf16[2,320,320]{2,1,0:T(8,128)(2,1)S(1)}, bf16[2,320,320]{2,1,0:T(8,128)(2,1)}, u32[]{:S(2)}) copy-start(bf16[2,320,320]{2,1,0:T(8,128)(2,1)} %wtwo.1) | copy-start | bytes 1228804
  3.6 14.2 %all-to-all-start = ((bf16[4,4,6528]{2,1,0:T(4,128)(2,1)}), bf16[4,4,6528]{2,1,0:T(4,128)(2,1)S(1)}, u32[]{:S(2)}, u32[]{:S(2)}) async-start(bf16[4,4,6528]{2,1,0:T(4,128)(2,1)} %shard_map.223), calls=%async_computation | async-start | bytes 417792 | tf_op jit(solution)/shard_map/all_to_all | solution.py:666
  10.9 2.1 %copy-start.6 = (bf16[448,448]{1,0:T(8,128)(2,1)S(1)}, bf16[448,448]{1,0:T(8,128)(2,1)}, u32[]{:S(2)}) copy-start(bf16[448,448]{1,0:T(8,128)(2,1)} %wzero.1) | copy-start | bytes 1204228
  12.0 2.0 %copy-start.15 = (bf16[64,256]{1,0:T(8,128)(2,1)S(1)}, bf16[64,256]{1,0:T(8,128)(2,1)}, u32[]{:S(2)}) copy-start(bf16[64,256]{1,0:T(8,128)(2,1)} %ain.1) | copy-start | bytes 98308
  12.0 2.7 %copy-start.14 = (bf16[128,256]{1,0:T(8,128)(2,1)S(1)}, bf16[128,256]{1,0:T(8,128)(2,1)}, u32[]{:S(2)}) copy-start(bf16[128,256]{1,0:T(8,128)(2,1)} %param.29) | copy-start | bytes 196612
  12.0 3.5 %copy-start.13 = (bf16[256,235]{0,1:T(8,128)(2,1)S(1)}, bf16[256,235]{0,1:T(8,128)(2,1)}, u32[]{:S(2)}) copy-start(bf16[256,235]{0,1:T(8,128)(2,1)} %param.22) | copy-start | bytes 360964
  17.9 0.7 copy-start.11
  28.5 12.4 %all-to-all-start.2 = ((f32[16,16,128]{2,1,0:T(8,128)}), f32[16,16,128]{2,1,0:T(8,128)S(1)}, u32[]{:S(2)}, u32[]{:S(2)}) async-start(f32[16,16,128]{2,1,0:T(8,128)} %get-tuple-element.39), calls=%async_computation.2 | async-start | bytes 262144 | tf_op jit(solution)/shard_map/all_to_all | solution.py:710
  40.9 0.7 copy-start.12
  50.5 4.1 %collective-permute-start.4 = (f32[896,128]{1,0:T(8,128)}, f32[896,128]{1,0:T(8,128)S(1)}, u32[]{:S(2)}, u32[]{:S(2)}) collective-permute-start(f32[896,128]{1,0:T(8,128)} %get-tuple-element.56), channel_id=1, source_target_pairs={{0,1},{1,0},{2,3},{3,2},{4,5},{5,4},{6,7},{7,6},{8,9},{9,8},{10,11... | collective-permute-start | bytes 1376264 | tf_op jit(solution)/shard_map/ppermute | solution.py:613
  50.6 18.5 %collective-permute-start.3 = (f32[2176,128]{1,0:T(8,128)}, f32[2176,128]{1,0:T(8,128)S(1)}, u32[]{:S(2)}, u32[]{:S(2)}) collective-permute-start(f32[2176,128]{1,0:T(8,128)} %get-tuple-element.54), channel_id=1, source_target_pairs={{0,1},{1,0},{2,3},{3,2},{4,5},{5,4},{6,7},{7,6},{8,9},{9,8},{10,11... | collective-permute-start | bytes 3342344 | tf_op jit(solution)/shard_map/ppermute | solution.py:613
  51.1 11.2 %all-to-all-start.1 = ((f32[4,4,3328]{2,1,0:T(4,128)}), f32[4,4,3328]{2,1,0:T(4,128)S(1)}, u32[]{:S(2)}, u32[]{:S(2)}) async-start(f32[4,4,3328]{2,1,0:T(4,128)} %get-tuple-element.36), calls=%async_computation.1 | async-start | bytes 425984 | tf_op jit(solution)/shard_map/all_to_all | solution.py:666
  54.6 14.4 %copy-start.2 = (f32[2176,128]{1,0:T(8,128)S(1)}, f32[2176,128]{1,0:T(8,128)}, u32[]{:S(2)}) copy-start(f32[2176,128]{1,0:T(8,128)} %get-tuple-element.53) | copy-start | bytes 3342340
  55.8 13.3 %copy-start.1 = (f32[896,128]{1,0:T(8,128)}, f32[896,128]{1,0:T(8,128)S(1)}, u32[]{:S(2)}) copy-start(f32[896,128]{1,0:T(8,128)S(1)} %add.64.rest_1_) | copy-start | bytes 1376260
  55.8 12.3 %collective-permute-start.8 = (f32[448,128]{1,0:T(8,128)S(1)}, f32[448,128]{1,0:T(8,128)S(1)}, u32[]{:S(2)}, u32[]{:S(2)}) collective-permute-start(f32[448,128]{1,0:T(8,128)S(1)} %dynamic-slice_bitcast_fusion.2), channel_id=1, source_target_pairs={{0,4},{4,0},{8,12},{12,8},{1,5},{5,1},{9,13},{13,9},{2,6},{6,2},{1... | collective-permute-start | bytes 688136 | tf_op jit(solution)/shard_map/ppermute | solution.py:613
  62.2 6.9 %copy-start.10 = (f32[4,4,3328]{2,1,0:T(4,128)}, f32[4,4,3328]{2,1,0:T(4,128)S(1)}, u32[]{:S(2)}) copy-start(f32[4,4,3328]{2,1,0:T(4,128)S(1)} %all-to-all-done.1.rest_0_) | copy-start | bytes 638980
  62.2 6.0 %collective-permute-start.1 = (f32[4,4,3328]{2,1,0:T(4,128)S(1)}, f32[4,4,3328]{2,1,0:T(4,128)}, u32[]{:S(2)}, u32[]{:S(2)}) collective-permute-start(f32[4,4,3328]{2,1,0:T(4,128)S(1)} %all-to-all-done.1.rest_0_), channel_id=1, source_target_pairs={{0,2},{1,3},{2,0},{3,1},{4,6},{5,7},{6,4},{7,5},{8,10},{9,11},{10,... | collective-permute-start | bytes 638984 | tf_op jit(solution)/shard_map/ppermute | solution.py:613
  62.5 7.1 %collective-permute-start = (f32[4,4,3328]{2,1,0:T(4,128)S(1)}, f32[4,4,3328]{2,1,0:T(4,128)S(1)}, u32[]{:S(2)}, u32[]{:S(2)}) collective-permute-start(f32[4,4,3328]{2,1,0:T(4,128)S(1)} %all-to-all-done.1.rest_0_), channel_id=1, source_target_pairs={{0,1},{1,0},{2,3},{3,2},{4,5},{5,4},{6,7},{7,6},{8,9},{9,8},{10,11... | collective-permute-start | bytes 638984 | tf_op jit(solution)/shard_map/ppermute | solution.py:613
  68.2 1.7 %collective-permute-start.2 = (f32[4,4,3328]{2,1,0:T(4,128)}, f32[4,4,3328]{2,1,0:T(4,128)S(1)}, u32[]{:S(2)}, u32[]{:S(2)}) collective-permute-start(f32[4,4,3328]{2,1,0:T(4,128)} %collective-permute-done.1.rest_2_), channel_id=1, source_target_pairs={{0,1},{1,0},{2,3},{3,2},{4,5},{5,4},{6,7},{7,6},{8,9},{9,8},{10,11... | collective-permute-start | bytes 638984 | tf_op jit(solution)/shard_map/ppermute | solution.py:613
  68.2 9.0 %collective-permute-start.9 = (f32[224,128]{1,0:T(8,128)S(1)}, f32[224,128]{1,0:T(8,128)S(1)}, u32[]{:S(2)}, u32[]{:S(2)}) collective-permute-start(f32[224,128]{1,0:T(8,128)S(1)} %dynamic-slice_bitcast_fusion.4), channel_id=1, source_target_pairs={{0,8},{4,12},{8,0},{12,4},{1,9},{5,13},{9,1},{13,5},{2,10},{6,14},... | collective-permute-start | bytes 344072 | tf_op jit(solution)/shard_map/ppermute | solution.py:613
  69.2 15.5 %copy-start = (f32[2176,128]{1,0:T(8,128)}, f32[2176,128]{1,0:T(8,128)S(1)}, u32[]{:S(2)}) copy-start(f32[2176,128]{1,0:T(8,128)S(1)} %add.63.rest_0_) | copy-start | bytes 3342340
  69.2 15.4 %collective-permute-start.15 = (f32[1088,128]{1,0:T(8,128)S(1)}, f32[1088,128]{1,0:T(8,128)S(1)}, u32[]{:S(2)}, u32[]{:S(2)}) collective-permute-start(f32[1088,128]{1,0:T(8,128)S(1)} %dynamic-slice_bitcast_fusion), channel_id=1, source_target_pairs={{0,2},{1,3},{2,0},{3,1},{4,6},{5,7},{6,4},{7,5},{8,10},{9,11},{10,... | collective-permute-start | bytes 1671176 | tf_op jit(solution)/shard_map/ppermute | solution.py:613
  69.6 0.7 copy-start.20
  70.3 0.7 copy-start.22
  74.3 12.8 %collective-permute-start.22 = (f32[448,64]{1,0:T(8,128)}, f32[448,64]{1,0:T(8,128)S(1)}, u32[]{:S(2)}, u32[]{:S(2)}) collective-permute-start(f32[448,64]{1,0:T(8,128)} %get-tuple-element.62), channel_id=1, source_target_pairs={{0,4},{4,0},{8,12},{12,8},{1,5},{5,1},{9,13},{13,9},{2,6},{6,2},{1... | collective-permute-start | bytes 344072 | tf_op jit(solution)/shard_map/ppermute | solution.py:613
  77.3 9.8 %copy-start.8 = (f32[448,64]{1,0:T(8,128)S(1)}, f32[448,64]{1,0:T(8,128)}, u32[]{:S(2)}) copy-start(f32[448,64]{1,0:T(8,128)} %get-tuple-element.62) | copy-start | bytes 344068
  77.3 11.6 %collective-permute-start.10 = (f32[112,128]{1,0:T(8,128)S(1)}, f32[112,128]{1,0:T(8,128)S(1)}, u32[]{:S(2)}, u32[]{:S(2)}) collective-permute-start(f32[112,128]{1,0:T(8,128)S(1)} %dynamic-slice_bitcast_fusion.5), channel_id=1, source_target_pairs={{0,2},{1,3},{2,0},{3,1},{4,6},{5,7},{6,4},{7,5},{8,10},{9,11},{10,... | collective-permute-start | bytes 172040 | tf_op jit(solution)/shard_map/ppermute | solution.py:613
  84.8 12.6 %collective-permute-start.16 = (f32[544,128]{1,0:T(8,128)S(1)}, f32[544,128]{1,0:T(8,128)S(1)}, u32[]{:S(2)}, u32[]{:S(2)}) collective-permute-start(f32[544,128]{1,0:T(8,128)S(1)} %dynamic-slice_bitcast_fusion.1), channel_id=1, source_target_pairs={{0,4},{4,0},{8,12},{12,8},{1,5},{5,1},{9,13},{13,9},{2,6},{6,2},{1... | collective-permute-start | bytes 835592 | tf_op jit(solution)/shard_map/ppermute | solution.py:613
  87.1 50.4 %collective-permute-start.23 = (f32[448,64]{1,0:T(8,128)S(1)}, f32[448,64]{1,0:T(8,128)S(1)}, u32[]{:S(2)}, u32[]{:S(2)}) collective-permute-start(f32[448,64]{1,0:T(8,128)S(1)} %add.77), channel_id=1, source_target_pairs={{0,8},{4,12},{8,0},{12,4},{1,9},{5,13},{9,1},{13,5},{2,10},{6,14},... | collective-permute-start | bytes 344072 | tf_op jit(solution)/shard_map/ppermute | solution.py:613
  88.9 9.8 %collective-permute-start.11 = (bf16[112,128]{1,0:T(8,128)(2,1)S(1)}, bf16[112,128]{1,0:T(8,128)(2,1)S(1)}, u32[]{:S(2)}, u32[]{:S(2)}) collective-permute-start(bf16[112,128]{1,0:T(8,128)(2,1)S(1)} %fusion.1), channel_id=1, source_target_pairs={{0,2},{1,3},{2,0},{3,1},{4,6},{5,7},{6,4},{7,5},{8,10},{9,11},{10,... | collective-permute-start | bytes 86024 | tf_op jit(solution)/shard_map/ppermute | solution.py:613
  97.5 10.2 %collective-permute-start.17 = (f32[272,128]{1,0:T(8,128)S(1)}, f32[272,128]{1,0:T(8,128)S(1)}, u32[]{:S(2)}, u32[]{:S(2)}) collective-permute-start(f32[272,128]{1,0:T(8,128)S(1)} %dynamic-slice_bitcast_fusion.3), channel_id=1, source_target_pairs={{0,8},{4,12},{8,0},{12,4},{1,9},{5,13},{9,1},{13,5},{2,10},{6,14},... | collective-permute-start | bytes 417800 | tf_op jit(solution)/shard_map/ppermute | solution.py:613
  98.7 21.8 %collective-permute-start.12 = (bf16[224,128]{1,0:T(8,128)(2,1)S(1)}, bf16[224,128]{1,0:T(8,128)(2,1)S(1)}, u32[]{:S(2)}, u32[]{:S(2)}) collective-permute-start(bf16[224,128]{1,0:T(8,128)(2,1)S(1)} %pad_maximum_fusion.5), channel_id=1, source_target_pairs={{0,8},{4,12},{8,0},{12,4},{1,9},{5,13},{9,1},{13,5},{2,10},{6,14},... | collective-permute-start | bytes 172040 | tf_op jit(solution)/shard_map/ppermute | solution.py:613
  107.7 10.6 %collective-permute-start.18 = (bf16[272,128]{1,0:T(8,128)(2,1)S(1)}, bf16[272,128]{1,0:T(8,128)(2,1)S(1)}, u32[]{:S(2)}, u32[]{:S(2)}) collective-permute-start(bf16[272,128]{1,0:T(8,128)(2,1)S(1)} %fusion), channel_id=1, source_target_pairs={{0,8},{4,12},{8,0},{12,4},{1,9},{5,13},{9,1},{13,5},{2,10},{6,14},... | collective-permute-start | bytes 208904 | tf_op jit(solution)/shard_map/ppermute | solution.py:613
  114.1 11.3 %all-to-all-start.3 = ((f32[4,4,3328]{2,1,0:T(4,128)}), f32[4,4,3328]{2,1,0:T(4,128)S(1)}, u32[]{:S(2)}, u32[]{:S(2)}) async-start(f32[4,4,3328]{2,1,0:T(4,128)} %shard_map.227), calls=%async_computation.3 | async-start | bytes 425984 | tf_op jit(solution)/shard_map/all_to_all | solution.py:666
  118.3 10.1 %collective-permute-start.19 = (bf16[544,128]{1,0:T(8,128)(2,1)S(1)}, bf16[544,128]{1,0:T(8,128)(2,1)S(1)}, u32[]{:S(2)}, u32[]{:S(2)}) collective-permute-start(bf16[544,128]{1,0:T(8,128)(2,1)S(1)} %pad_maximum_fusion.3), channel_id=1, source_target_pairs={{0,4},{4,0},{8,12},{12,8},{1,5},{5,1},{9,13},{13,9},{2,6},{6,2},{1... | collective-permute-start | bytes 417800 | tf_op jit(solution)/shard_map/ppermute | solution.py:613
  120.6 9.4 %collective-permute-start.13 = (bf16[448,128]{1,0:T(8,128)(2,1)S(1)}, bf16[448,128]{1,0:T(8,128)(2,1)S(1)}, u32[]{:S(2)}, u32[]{:S(2)}) collective-permute-start(bf16[448,128]{1,0:T(8,128)(2,1)S(1)} %pad_maximum_fusion.4), channel_id=1, source_target_pairs={{0,4},{4,0},{8,12},{12,8},{1,5},{5,1},{9,13},{13,9},{2,6},{6,2},{1... | collective-permute-start | bytes 344072 | tf_op jit(solution)/shard_map/ppermute | solution.py:613
  125.4 12.0 %copy-start.9 = (f32[4,4,3328]{2,1,0:T(4,128)}, f32[4,4,3328]{2,1,0:T(4,128)S(1)}, u32[]{:S(2)}) copy-start(f32[4,4,3328]{2,1,0:T(4,128)S(1)} %all-to-all-done.3.rest_0_) | copy-start | bytes 638980
  125.4 7.8 %collective-permute-start.6 = (f32[4,4,3328]{2,1,0:T(4,128)S(1)}, f32[4,4,3328]{2,1,0:T(4,128)S(1)}, u32[]{:S(2)}, u32[]{:S(2)}) collective-permute-start(f32[4,4,3328]{2,1,0:T(4,128)S(1)} %all-to-all-done.3.rest_0_), channel_id=1, source_target_pairs={{0,2},{1,3},{2,0},{3,1},{4,6},{5,7},{6,4},{7,5},{8,10},{9,11},{10,... | collective-permute-start | bytes 638984 | tf_op jit(solution)/shard_map/ppermute | solution.py:613
  128.5 8.7 %collective-permute-start.20 = (bf16[1088,128]{1,0:T(8,128)(2,1)S(1)}, bf16[1088,128]{1,0:T(8,128)(2,1)S(1)}, u32[]{:S(2)}, u32[]{:S(2)}) collective-permute-start(bf16[1088,128]{1,0:T(8,128)(2,1)S(1)} %pad_maximum_fusion.1), channel_id=1, source_target_pairs={{0,2},{1,3},{2,0},{3,1},{4,6},{5,7},{6,4},{7,5},{8,10},{9,11},{10,... | collective-permute-start | bytes 835592 | tf_op jit(solution)/shard_map/ppermute | solution.py:613
  130.0 7.4 %copy-start.7 = (bf16[896,128]{1,0:T(8,128)(2,1)}, bf16[896,128]{1,0:T(8,128)(2,1)S(1)}, u32[]{:S(2)}) copy-start(bf16[896,128]{1,0:T(8,128)(2,1)S(1)} %pad_maximum_fusion.2.mine) | copy-start | bytes 688132
  130.0 8.3 %collective-permute-start.14 = (bf16[896,128]{1,0:T(8,128)(2,1)S(1)}, bf16[896,128]{1,0:T(8,128)(2,1)S(1)}, u32[]{:S(2)}, u32[]{:S(2)}) collective-permute-start(bf16[896,128]{1,0:T(8,128)(2,1)S(1)} %pad_maximum_fusion.2.mine), channel_id=1, source_target_pairs={{0,1},{1,0},{2,3},{3,2},{4,5},{5,4},{6,7},{7,6},{8,9},{9,8},{10,11... | collective-permute-start | bytes 688136 | tf_op jit(solution)/shard_map/ppermute | solution.py:613
  130.1 10.8 %collective-permute-start.5 = (f32[4,4,3328]{2,1,0:T(4,128)S(1)}, f32[4,4,3328]{2,1,0:T(4,128)S(1)}, u32[]{:S(2)}, u32[]{:S(2)}) collective-permute-start(f32[4,4,3328]{2,1,0:T(4,128)S(1)} %all-to-all-done.3.rest_0_), channel_id=1, source_target_pairs={{0,1},{1,0},{2,3},{3,2},{4,5},{5,4},{6,7},{7,6},{8,9},{9,8},{10,11... | collective-permute-start | bytes 638984 | tf_op jit(solution)/shard_map/ppermute | solution.py:613
  133.3 4.2 %copy-start.18 = (f32[4,4,3328]{2,1,0:T(4,128)}, f32[4,4,3328]{2,1,0:T(4,128)S(1)}, u32[]{:S(2)}) copy-start(f32[4,4,3328]{2,1,0:T(4,128)S(1)} %collective-permute-done.6.rest_2_) | copy-start | bytes 638980
  133.3 7.7 %collective-permute-start.7 = (f32[4,4,3328]{2,1,0:T(4,128)S(1)}, f32[4,4,3328]{2,1,0:T(4,128)S(1)}, u32[]{:S(2)}, u32[]{:S(2)}) collective-permute-start(f32[4,4,3328]{2,1,0:T(4,128)S(1)} %collective-permute-done.6.rest_2_), channel_id=1, source_target_pairs={{0,1},{1,0},{2,3},{3,2},{4,5},{5,4},{6,7},{7,6},{8,9},{9,8},{10,11... | collective-permute-start | bytes 638984 | tf_op jit(solution)/shard_map/ppermute | solution.py:613
  137.5 3.5 %copy-start.4 = (bf16[2176,128]{1,0:T(8,128)(2,1)}, bf16[2176,128]{1,0:T(8,128)(2,1)S(1)}, u32[]{:S(2)}) copy-start(bf16[2176,128]{1,0:T(8,128)(2,1)S(1)} %pad_maximum_fusion.mine) | copy-start | bytes 1671172
  137.5 7.4 %collective-permute-start.21 = (bf16[2176,128]{1,0:T(8,128)(2,1)S(1)}, bf16[2176,128]{1,0:T(8,128)(2,1)S(1)}, u32[]{:S(2)}, u32[]{:S(2)}) collective-permute-start(bf16[2176,128]{1,0:T(8,128)(2,1)S(1)} %pad_maximum_fusion.mine), channel_id=1, source_target_pairs={{0,1},{1,0},{2,3},{3,2},{4,5},{5,4},{6,7},{7,6},{8,9},{9,8},{10,11... | collective-permute-start | bytes 1671176 | tf_op jit(solution)/shard_map/ppermute | solution.py:613
  138.3 0.7 copy-start.17
  140.9 0.7 copy-start.19
  141.6 0.7 copy-start.21
  144.9 0.8 copy-start.16

commit v3 on v2

--- a/solution.py
+++ b/solution.py
@@ -20,6 +20,7 @@
 WIDE = COLS + LANES
 TABLE = 2 * COLS + LANES
 PEAK_AT, DOT_AT, NAME_AT = HEADS, 2 * HEADS, 3 * HEADS
+STATS = 16
 DIM0 = (LMAX + 1) * CH
 DIM1 = LMAX * CH
 DIM2 = (LMAX - 1) * CH
@@ -186,7 +187,7 @@
         put_rows(out, pl.ds(first + block * LANES, LANES), jnp.concatenate([left, right], axis=1))
 
 
-def outgoing_kernel(place, send, recv, embed, cot, out):
+def outgoing_kernel(send, recv, embed, cot, out):
     atoms = embed.shape[1]
     slots = out.shape[0] * out.shape[1]
     sent = listed_rows(send, (slots, LANES))
@@ -205,11 +206,24 @@
 
 def make_forward(atoms):
     def forward_kernel(
-        table, source_slot, target_slot, rot, feats, bias, wzero, wone, wtwo, ain, aedge, adot,
-        out_proj,
-        sums_out, stats_out, x0, x1, x2, v0, v1, v2, pre_out, logit_out, lists_out, agg_grad,
-        rows, gathered, weights, terms,
+        table, source_slot, target_slot, rotation, feats, bias, wzero_at, wone_at, wtwo_at,
+        ain, aedge, adot, out_proj,
+        sums_out, stats_out, x0_at, x1_at, x2_at, v0_at, v1_at, v2_at, pre_at, logit_out,
+        lists_out, agg_grad, rot, own_out,
+        rows, gathered, weights, terms, wzero, wone, wtwo, x0, x1, x2, v0, v1, v2, pre_out,
+        semaphores,
     ):
+        copies = []
+
+        def move(source, target):
+            copy = pltpu.make_async_copy(source, target, semaphores.at[len(copies)])
+            copy.start()
+            copies.append(copy)
+
+        move(wzero_at, wzero)
+        move(wone_at, wone)
+        move(wtwo_at, wtwo)
+        rot[...] = jnp.transpose(rotation[...].astype(f32))
         edges = source_slot.shape[1]
         slots = table.shape[0] * table.shape[1]
         stack_table(table, rows)
@@ -229,10 +243,15 @@
             ref[pl.ds(row, CH), lane_at(half, edges, second)] = value.astype(bf16)
 
         to_frame(gathered, rot, edges, emit)
-
-        pre = dot_nn(ain[...], x0[pl.ds(0, CH), :]) + dot_nt(aedge[...], feats[...])
+        for source, target in ((x0, x0_at), (x1, x1_at), (x2, x2_at)):
+            move(source, target)
+
+        pre = dot_tn(ain[...], x0[pl.ds(0, CH), :]) + lax.dot_general(
+            aedge[...], feats[...], (((0,), (1,)), ((), ())), preferred_element_type=f32
+        )
         pre_out[...] = pre
-        hidden = jnp.where(pre > 0, pre, leak_slope * pre) * adot[...]
+        move(pre_out, pre_at)
+        hidden = jnp.where(pre > 0, pre, leak_slope * pre) * turned_column(adot[...].astype(f32))
         aims = one_hot_rows(target_slot, slots)
         lane = iota((slots, LANES), 1)
         peer = iota((slots, 1), 0) // table.shape[1]
@@ -249,9 +268,13 @@
             den = jnp.sum(jnp.where(aims, weight, 0.0), axis=1, keepdims=True)
             side = jnp.where(lane == h, den, jnp.where(lane == PEAK_AT + h, peak, side))
 
-        v0[...] = dot_nn(wzero[...], x0[...])
+        for copy in copies[:3]:
+            copy.wait()
+        v0[...] = dot_tn(wzero[...], x0[...])
         for out, weight, value in ((v1, wone, x1[...]), (v2, wtwo, x2[...])):
-            out[...] = dot_nn(weight[0], value) + swapped_halves(dot_nn(weight[1], value), edges)
+            out[...] = dot_tn(weight[0], value) + swapped_halves(dot_tn(weight[1], value), edges)
+        for source, target in ((v0, v0_at), (v1, v1_at), (v2, v2_at)):
+            move(source, target)
 
         def load(degree, order, half):
             ref, row, second = frame_place(degree, order, (v0, v1, v2))
@@ -272,12 +295,18 @@
             dot = jnp.sum(jnp.where(head == h, dots, 0.0), axis=1, keepdims=True)
             side = jnp.where(lane == DOT_AT + h, dot, side)
         put_rows(sums_out, pl.ds(COLS, LANES), side)
+        own_out[...] = side
+        spread = jnp.concatenate([side[:, :STATS]] * (LANES // STATS), axis=1)
+        spread = jnp.where(lane // STATS == iota((slots, LANES), 0) % 8, spread, 0.0)
+        packed = jnp.sum(spread.reshape(slots // 8, 8, LANES), axis=1)
 
         def copy_to(n, carry):
-            stats_out[n] = side
+            stats_out[n] = packed
             return carry
 
         lax.fori_loop(0, stats_out.shape[0], copy_to, 0)
+        for copy in copies[3:]:
+            copy.wait()
 
     return forward_kernel
 
@@ -290,10 +319,11 @@
     return result
 
 
-def collect_rows(place, arrivals, rows_ref):
+def collect_rows(arrivals, rows_ref):
+    own = lax.axis_index("edge")
     for k, arrival in enumerate(arrivals):
         peers, cap, width = arrival.shape
-        base = (place[0] ^ k) * (peers * cap)
+        base = (own ^ k) * (peers * cap)
         for start in range(0, peers * cap, 8):
             parts = [arrival[g] for g in range(start // cap, (start + 8) // cap)]
             at = pl.ds(pl.multiple_of(base + start, 8), 8)
@@ -305,14 +335,14 @@
 
 
 def make_finish(lanes_total):
-    def finish_kernel(place, cot, out_proj, *rest):
+    def finish_kernel(cot, out_proj, *rest):
         arrivals = rest[:lanes_total]
         out, proj, rows, terms, agg_low = rest[lanes_total:]
         atoms = cot.shape[1]
         total = rows.shape[0]
-        collect_rows(place, arrivals, rows)
+        collect_rows(arrivals, rows)
         side = rows[:, pl.ds(COLS, LANES)]
-        owner = (place[1] * atoms).astype(f32)
+        owner = (lax.axis_index("graph") * atoms).astype(f32)
         names = iota((total, atoms), 1).astype(f32) + owner == side[:, NAME_AT : NAME_AT + 1]
         eye = iota((atoms, atoms), 0) == iota((atoms, atoms), 1)
         scales, dens = [], []
@@ -347,18 +377,22 @@
             right = cot[ids].reshape(stacked)
             value = dot_nn(left, out_proj[degree]).astype(bf16)
             out[ids] = value.reshape((2 * degree + 1, atoms, CH))
-            proj[pl.ds(degree * CH, CH), :] = dot_tn(left, right)
+            at = (pl.ds(degree // 2 * CH, CH), pl.ds(degree % 2 * CH, CH))
+            proj[at] = dot_tn(left, right)
+        proj[pl.ds(LMAX // 2 * CH, CH), pl.ds(CH, CH)] = jnp.zeros((CH, CH), f32)
 
     return finish_kernel
 
 
 def combine_stats(stats, own):
-    blocks, slots = stats.shape[0], stats.shape[1]
+    blocks, slots = stats.shape[0], stats.shape[1] * 8
     chunk = max(1, PANEL // slots)
     name = own[:, NAME_AT : NAME_AT + 1]
 
     def part(at):
-        turned = jnp.transpose(stats[pl.ds(at * chunk, chunk)].reshape(chunk * slots, LANES))
+        part_rows = jnp.concatenate([stats[at * chunk + n] for n in range(chunk)], axis=0)
+        entries = [part_rows[:, n : n + STATS] for n in range(0, LANES, STATS)]
+        turned = jnp.transpose(jnp.concatenate(entries, axis=0))
         same = name == turned[NAME_AT : NAME_AT + 1]
         result = []
         for h in range(HEADS):
@@ -388,11 +422,18 @@
 
 
 def gradient_kernel(
-    place, stats, own, agg_grad, target_slot, rot, feats,
-    x0, x1, x2, v0, v1, v2, pre, logits, adot,
+    stats, own, agg_grad, target_slot, rot, feats,
+    x0_at, x1_at, x2_at, v0_at, v1_at, v2_at, pre, logits, adot,
     g0, top1, top2, pre_grad_out, kept0, sent0, kept1, sent1,
-    num_grad, spread_grad, weights, g1, g2, packed, semaphores,
+    num_grad, spread_grad, weights, g1, g2, packed, x0, x1, x2, v0, v1, v2, semaphores,
 ):
+    loads = []
+    for source, target in (
+        (v0_at, v0), (v1_at, v1), (v2_at, v2), (x0_at, x0), (x1_at, x1), (x2_at, x2)
+    ):
+        load = pltpu.make_async_copy(source, target, semaphores.at[4 + len(loads)])
+        load.start()
+        loads.append(load)
     edges = target_slot.shape[1]
     slots = agg_grad.shape[0]
     aims = one_hot_rows(target_slot, slots)
@@ -432,6 +473,8 @@
                 part = state["sum"][h * VAL : (h + 1) * VAL]
                 weights[pl.ds(HEADS + h, 1), lanes] = jnp.sum(part, axis=0, keepdims=True)
 
+    for load in loads:
+        load.wait()
     to_frame(spread_grad, rot, edges, emit)
 
     hidden = jnp.where(pre[...] > 0, pre[...], leak_slope * pre[...])
@@ -443,13 +486,13 @@
         [jnp.broadcast_to(row, (ALPHA, edges)) for row in logit_grads], axis=0
     )
     slope = jnp.where(pre[...] > 0, 1.0, leak_slope)
-    pre_grad = (tall * adot[...] * slope).astype(bf16)
+    pre_grad = (tall * turned_column(adot[...].astype(f32)) * slope).astype(bf16)
     pre_grad_out[...] = pre_grad
     dot_grad = jnp.sum(tall * hidden, axis=1, keepdims=True)
 
     top1[...] = g1[pl.ds(0, DIM1), :]
     top2[...] = g2[pl.ds(0, DIM2), :]
-    mine = place[0] & 1
+    mine = lax.axis_index("edge") & 1
     copies = []
 
     def put(row, value, at=0):
@@ -509,22 +552,22 @@
 PACKED_ROWS = sum(size for start, size in CHUNKS)
 
 
-def halves_of(place, mine, other):
-    first = (place[0] & 1) == 0
+def halves_of(mine, other):
+    first = (lax.axis_index("edge") & 1) == 0
     left, right = mine[...].astype(f32), other[...].astype(f32)
     return jnp.where(first, left, right), jnp.where(first, right, left)
 
 
-def unpack_zero_kernel(place, mine, other, zero):
-    left, right = halves_of(place, mine, other)
+def unpack_zero_kernel(mine, other, zero):
+    left, right = halves_of(mine, other)
     zero[:, pl.ds(0, LANES)] = left[:DIM0].astype(bf16)
     zero[:, pl.ds(LANES, LANES)] = right[:DIM0].astype(bf16)
     zero[:, pl.ds(2 * LANES, LANES)] = left[DIM0:].astype(bf16)
     zero[:, pl.ds(3 * LANES, DIM0 - 3 * LANES)] = right[DIM0:, : DIM0 - 3 * LANES].astype(bf16)
 
 
-def unpack_rest_kernel(place, mine, other, one, two, alpha_in, alpha_edge, alpha_dot):
-    left, right = halves_of(place, mine, other)
+def unpack_rest_kernel(mine, other, one, two, alpha_in, alpha_edge, alpha_dot):
+    left, right = halves_of(mine, other)
     for n in range(2 * DIM1 // LANES):
         panel = (left, right)[n % 2][(n // 2) * DIM1 : (n // 2 + 1) * DIM1]
         per = DIM1 // LANES
@@ -566,12 +609,12 @@
 
 
 def make_collect(lanes_total):
-    def collect_kernel(place, *rest):
+    def collect_kernel(*rest):
         arrivals = rest[:lanes_total]
         out, rows = rest[lanes_total:]
         atoms = out.shape[1]
         total = rows.shape[0]
-        collect_rows(place, arrivals, rows)
+        collect_rows(arrivals, rows)
         index = rows[:, pl.ds(COLS, LANES)][:, 1:2]
         picked = mask_to(iota((total, atoms), 1).astype(f32) == index, bf16)
         twice = jnp.concatenate([picked, picked], axis=0)
@@ -590,9 +633,10 @@
 anywhere = pl.BlockSpec(memory_space=pl.ANY)
 
 
-def call(kernel, outs, scratch, *args, scalars=0, apart=0, after=(), work=4):
-    specs = [smem if n < scalars else vmem for n in range(len(args))] + [anywhere] * len(after)
-    out_specs = [vmem if n < len(outs) - apart else anywhere for n in range(len(outs))]
+def call(kernel, outs, scratch, *args, scalars=0, far=(), apart=(), after=(), work=4):
+    specs = [smem if n < scalars else anywhere if n in far else vmem for n in range(len(args))]
+    specs += [anywhere] * len(after)
+    out_specs = [anywhere if n in apart else vmem for n in range(len(outs))]
     shapes = [pltpu.VMEM(*entry) if isinstance(entry, tuple) else entry for entry in scratch]
     moved = sum(int(np.prod(a.shape)) * a.dtype.itemsize for a in args)
     return pl.pallas_call(
@@ -608,6 +652,14 @@
     )(*args, *after)
 
 
+def tie(value, *earlier):
+    return lax.optimization_barrier((value, *earlier))[0]
+
+
+def turned_column(row):
+    return jnp.transpose(jnp.broadcast_to(row, (8, row.shape[1])))[:, :1]
+
+
 def swap(value, axis, bit):
     size = lax.axis_size(axis)
     return lax.ppermute(value, axis, [(i, i ^ (1 << bit)) for i in range(size)])
@@ -628,7 +680,7 @@
     return (lax.axis_index(axis) >> bit) & 1
 
 
-def sum_all(current, first):
+def sum_all(current, first, earlier=()):
     steps = [("edge", n) for n in range(1, bits_of("edge"))]
     steps += [("graph", n) for n in range(bits_of("graph"))]
     steps.sort(key=lambda step: step[0] != first)
@@ -636,6 +688,8 @@
         mine = own_bit(axis, bit)
         parts = current.reshape(2, current.shape[0] // 2, -1)
         other = swap(lax.dynamic_index_in_dim(parts, 1 - mine, 0, False), axis, bit)
+        if earlier:
+            other, earlier = tie(other, *earlier), ()
         current = lax.dynamic_index_in_dim(parts, mine, 0, False) + other
     current = current.astype(bf16)
     for axis, bit in reversed(steps):
@@ -658,8 +712,6 @@
     edges = rotation.shape[0]
     cap = send_rows.shape[3]
     slots = peers * cap
-    own_place = [lax.axis_index("edge"), lax.axis_index("graph")]
-    place = jnp.stack(own_place).astype(jnp.int32)
     blocks = peers * lanes_total
 
     def exchange(value):
@@ -668,45 +720,52 @@
     cot = jnp.transpose(out_cotangent, (1, 0, 2))
     (outgoing,) = call(
         outgoing_kernel, [((peers, cap, TABLE), bf16)], [],
-        place, send_rows, recv_rows, jnp.transpose(atom_embed, (1, 0, 2)), cot,
-        scalars=3, work=2,
+        send_rows, recv_rows, jnp.transpose(atom_embed, (1, 0, 2)), cot,
+        scalars=2, work=2,
     )
     table = exchange(outgoing)
 
     source_row = source_slot.reshape(1, edges)
     target_row = target_slot.reshape(1, edges)
-    rot = rotation.T.astype(f32)
     bias = edge_bias.T
-    adot = alpha_dot.astype(f32).reshape(-1, 1)
-
-    sums, stats, x0, x1, x2, v0, v1, v2, pre, logits, lists, agg_grad = call(
+    adot = alpha_dot.reshape(1, -1)
+
+    frames = [
+        ((DIM0, edges), bf16),
+        ((DIM1, 2 * edges), bf16),
+        ((DIM2, 2 * edges), bf16),
+        ((DIM0, edges), f32),
+        ((DIM1, 2 * edges), f32),
+        ((DIM2, 2 * edges), f32),
+    ]
+    pre_shape = ((HEADS * ALPHA, edges), f32)
+    sums, stats, x0, x1, x2, v0, v1, v2, pre, logits, lists, agg_grad, rot, own_stats = call(
         make_forward(atoms),
-        [
-            ((peers, cap, WIDE), f32),
-            ((blocks, slots, LANES), f32),
-            ((DIM0, edges), bf16),
-            ((DIM1, 2 * edges), bf16),
-            ((DIM2, 2 * edges), bf16),
-            ((DIM0, edges), f32),
-            ((DIM1, 2 * edges), f32),
-            ((DIM2, 2 * edges), f32),
-            ((HEADS * ALPHA, edges), f32),
+        [((peers, cap, WIDE), f32), ((blocks, slots // 8, LANES), f32)]
+        + frames
+        + [
+            pre_shape,
             ((8, edges), f32),
             ((slots, LANES), f32),
             ((slots, FLAT), f32),
+            ((rotation.shape[1], edges), f32),
+            ((slots, LANES), f32),
         ],
         [
             ((slots, TABLE), f32),
             ((FLAT, edges), f32),
             ((8, edges), f32),
             ((COLS, 2 * edges), bf16),
-        ],
-        table, source_row, target_row, rot, edge_feats, bias,
-        conv_zero.T, jnp.swapaxes(conv_one, 1, 2), jnp.swapaxes(conv_two, 1, 2),
-        alpha_in.T, alpha_edge.T, adot, out_proj,
-        work=8,
-    )
-    own_stats = stats[0]
+            (conv_zero.shape, bf16),
+            (conv_one.shape, bf16),
+            (conv_two.shape, bf16),
+        ]
+        + frames
+        + [pre_shape, pltpu.SemaphoreType.DMA((10,))],
+        table, source_row, target_row, rotation, edge_feats, bias,
+        conv_zero, conv_one, conv_two, alpha_in, alpha_edge, adot, out_proj,
+        far=(6, 7, 8), apart=range(2, 9), work=8,
+    )
     all_stats = lax.all_to_all(stats, ("graph", "edge"), split_axis=0, concat_axis=0, tiled=True)
 
     halves = [((size, LANES), f32) for start, size in CHUNKS for _ in range(2)]
@@ -726,11 +785,12 @@
             ((2 * DIM1, 2 * edges), bf16),
             ((2 * DIM2, 2 * edges), bf16),
             ((2, PACKED_ROWS, LANES), f32),
-            pltpu.SemaphoreType.DMA((len(halves),)),
-        ],
-        place, all_stats, own_stats, agg_grad, target_row, rot, edge_feats,
+        ]
+        + frames
+        + [pltpu.SemaphoreType.DMA((10,))],
+        all_stats, own_stats, agg_grad, target_row, rot, edge_feats,
         x0, x1, x2, v0, v1, v2, pre, logits, adot,
-        scalars=1, apart=len(halves), work=8,
+        far=range(6, 12), apart=range(4, 8), work=8,
     )
     currents = [
         halves[2 * n] + swap(halves[2 * n + 1], "edge", 0) for n in range(len(CHUNKS))
@@ -749,12 +809,12 @@
         source_row, lists, rot, g0, g1, g2, pre_grad, conv_zero, conv_one, conv_two, alpha_in,
         after=currents, work=6,
     )
+    returned = exchange(source_sums)
     out, proj = call(
         make_finish(lanes_total),
-        [((COEFFS, atoms, CH), bf16), (((LMAX + 1) * CH, CH), f32)],
+        [((COEFFS, atoms, CH), bf16), (((LMAX // 2 + 1) * CH, LANES), f32)],
         [((total, WIDE), f32), ((2 * total, COLS), bf16), ((COEFFS, atoms, CH), bf16)],
-        place, cot, out_proj, *gather_lanes(exchange(sums)),
-        scalars=1,
+        cot, out_proj, *gather_lanes(tie(exchange(tie(sums, halves[1])), source_sums)),
     )
     for bit in range(bits_of("graph")):
         proj = proj + swap(proj, "graph", bit)
@@ -762,14 +822,13 @@
         make_collect(lanes_total),
         [((COEFFS, atoms, CH), bf16)],
         [((total, WIDE), f32)],
-        place, *gather_lanes(exchange(source_sums)),
-        scalars=1,
-    )
-
-    rest_pair = sum_all(currents[0], "edge")
+        *gather_lanes(returned),
+    )
+
+    rest_pair = sum_all(currents[0], "edge", [source_sums])
     zero_pair = sum_all(currents[1], "graph")
     (zero,) = call(
-        unpack_zero_kernel, [((DIM0, DIM0), bf16)], [], place, *zero_pair, scalars=1, work=1
+        unpack_zero_kernel, [((DIM0, DIM0), bf16)], [], *zero_pair, work=1
     )
     one, two, grad_in, grad_edge, grad_dot = call(
         unpack_rest_kernel,
@@ -780,7 +839,7 @@
             (alpha_edge.shape, bf16),
             ((2, LANES), bf16),
         ],
-        [], place, *rest_pair, scalars=1, work=1,
+        [], *rest_pair, work=1,
     )
 
     def shaped(value):
@@ -788,7 +847,7 @@
 
     return (
         shaped(out), shaped(embed), zero, one, two, grad_in, grad_edge, grad_dot.reshape(-1),
-        proj.astype(bf16).reshape(LMAX + 1, CH, CH),
+        jnp.swapaxes(proj.astype(bf16).reshape(-1, CH, 2, CH), 1, 2).reshape(-1, CH, CH)[: LMAX + 1],
     )
 
 

time: 149 us -> 146 us (0.980)
  blocking collectives: 0 us -> 10.7 us
  waiting for transfers between devices: 55.7 us -> 50.2 us
  local copies, waits for them, and re-layouts: 12.2 us -> 7.37 us
    all_to_all x0 -> x1, blocking collectives: none -> 10.7 us  [shards(): lax.all_to_all(stats, ('graph', 'edge'), split_axis=0, concat_axis=0, til...]
    all_to_all x1 -> x0, waiting for transfers between devices: 6.64 us -> none  [shards(): lax.all_to_all(stats, ('graph', 'edge'), split_axis=0, concat_axis=0, til...]
    ppermute x24, waiting for transfers between devices: 38 us -> 43.4 us  [swap(): return lax.ppermute(value, axis, [(i, i ^ 1 << bit) for i in range(size)])]
    all_to_all x1 -> x0, starting transfers between devices: 4.44 us -> none  [shards(): lax.all_to_all(stats, ('graph', 'edge'), split_axis=0, concat_axis=0, til...]
    ppermute x24, starting transfers between devices: 18.9 us -> 23.2 us  [swap(): return lax.ppermute(value, axis, [(i, i ^ 1 << bit) for i in range(size)])]
    all_to_all x3, waiting for transfers between devices: 11 us -> 6.79 us  [exchange(): lax.all_to_all(value, 'graph', split_axis=0, concat_axis=0, tiled=True)]
    unnamed x53 -> x39, local copies, waits for them, and re-layouts: 9.93 us -> 5.87 us
  transfers between devices with their start and end apart: 28 -> 27, of which waited for: 14 -> 13; matrix products, arithmetic and copies ran while one was open for 7% -> 3% of each run, Pallas kernels for 10% -> 10%
where the time goes in v3:
time: 146 us; the launch traced here: 145 us
  waiting for transfers between devices  50.2 us (34%)
  starting transfers between devices  36.5 us (25%)
  Pallas kernels  36.4 us (25%)
  blocking collectives  10.7 us (7%)
  local copies, waits for them, and re-layouts  7.37 us (5%)
  other arithmetic  2.82 us (2%)
    ppermute x24, waiting for transfers between devices, swap(): return lax.ppermute(value, axis, [(i, i ^ 1 << bit) for i in range(size)])  43.4 us
    pallas_call x8, Pallas kernels, call(): pl.pallas_call(kernel, out_shape=[jax.ShapeDtypeStruct(shape, kind) for s...  36.4 us
    ppermute x24, starting transfers between devices, swap(): return lax.ppermute(value, axis, [(i, i ^ 1 << bit) for i in range(size)])  23.2 us
    all_to_all x3, starting transfers between devices, exchange(): lax.all_to_all(value, 'graph', split_axis=0, concat_axis=0, tiled=True)  13.3 us
    all_to_all x1, blocking collectives, shards(): lax.all_to_all(stats, ('graph', 'edge'), split_axis=0, concat_axis=0, til...  10.7 us
    all_to_all x3, waiting for transfers between devices, exchange(): lax.all_to_all(value, 'graph', split_axis=0, concat_axis=0, tiled=True)  6.79 us
    unnamed x39, local copies, waits for them, and re-layouts  5.87 us
  transfers between devices with their start and end apart: 27, of which 13 were waited for; matrix products, arithmetic and copies ran while one was open for 3% of the time, Pallas kernels for 10%

profile of v3, /device:TPU:0, one launch (start us, length us, event | category | flops | bytes accessed | tf_op | source)
XLA Modules:
  0.0 145.0 jit_solution(13297992652804999621)
XLA Ops:
  0.7 2.3 %shard_map.223 = bf16[4,4,6528]{2,1,0:T(4,128)(2,1)} custom-call(s32[1,4,1,4]{3,2,1,0:T(1,128)} %send.1, s32[1,4,1,4]{3,2,1,0:T(1,128)} %recv.1, bf16[49,32,64]{2,1,0:T(8,128)(2,1)} %bitcast.58, bf16[49,32,64]{2,1,0:T(8,128)(2,1)} %bitcast.59), custom_call_target="tpu_custom_call" | custom-call | flops 2000000000 | bytes 401536 | tf_op jit(solution)/shard_map/pallas_call | solution.py:642
  2.9 6.3 %all-to-all-start = ((bf16[4,4,6528]{2,1,0:T(4,128)(2,1)}), bf16[4,4,6528]{2,1,0:T(4,128)(2,1)S(1)}, u32[]{:S(2)}, u32[]{:S(2)}) async-start(bf16[4,4,6528]{2,1,0:T(4,128)(2,1)} %shard_map.223), calls=%async_computation | async-start | bytes 417792 | tf_op jit(solution)/shard_map/all_to_all | solution.py:718
  9.3 0.6 reshape.56.adot
  9.8 0.8 copy.25.rotation
  10.6 6.4 %all-to-all-done.table = bf16[4,4,6528]{2,1,0:T(4,128)(2,1)S(1)} async-done(((bf16[4,4,6528]{2,1,0:T(4,128)(2,1)}), bf16[4,4,6528]{2,1,0:T(4,128)(2,1)S(1)}, u32[]{:S(2)}, u32[]{:S(2)}) %all-to-all-start) | async-done | bytes 208928 | tf_op jit(solution)/shard_map/all_to_all | solution.py:718
  17.0 0.7 copy-done.7
  17.7 9.0 %shard_map.224 = (f32[4,4,3328]{2,1,0:T(4,128)}, f32[16,2,128]{2,1,0:T(2,128)}, bf16[448,256]{1,0:T(8,128)(2,1)}, bf16[384,512]{1,0:T(8,128)(2,1)}, bf16[320,512...) custom-call(bf16[4,4,6528]{2,1,0:T(4,128)(2,1)} %copy-done.7, ...), custom_call_target="tpu_custom_call" | custom-call | flops 8000000000 | bytes 1957888 | tf_op jit(solution)/shard_map/pallas_call | solution.py:642
  26.7 10.7 %all_to_all.20.stats = f32[16,2,128]{2,1,0:T(2,128)} all-to-all(f32[16,2,128]{2,1,0:T(2,128)} %get-tuple-element.42), channel_id=1, replica_groups=mesh['groups'=2,'graph'=4,'edge'=4] {'graph','edge'}, dimensions={0} | all-to-all | bytes 32768 | tf_op jit(solution)/shard_map/all_to_all | solution.py:769
  37.4 8.6 %shard_map.225 = (bf16[448,256]{1,0:T(8,128)(2,1)}, bf16[384,512]{1,0:T(8,128)(2,1)}, bf16[320,512]{1,0:T(8,128)(2,1)}, bf16[256,256]{1,0:T(8,128)(2,1)}, f32[21...) custom-call(f32[16,2,128]{2,1,0:T(2,128)} %all_to_all.20.stats, ...), custom_call_target="tpu_custom_call" | custom-call | flops 8000000000 | bytes 3654144 | tf_op jit(solution)/shard_map/pallas_call | solution.py:642
  45.9 0.1 collective-permute-start.1
  46.0 2.0 %collective-permute-done.1 = f32[896,128]{1,0:T(8,128)S(1)} collective-permute-done((f32[896,128]{1,0:T(8,128)}, f32[896,128]{1,0:T(8,128)S(1)}, u32[]{:S(2)}, u32[]{:S(2)}) %collective-permute-start.1) | collective-permute-done | bytes 458784 | tf_op jit(solution)/shard_map/ppermute | solution.py:665
  48.0 1.1 add.64.rest_1_
  49.2 0.5 collective-permute-start.8
  49.7 7.2 %collective-permute-done.8 = f32[448,128]{1,0:T(8,128)S(1)} collective-permute-done((f32[448,128]{1,0:T(8,128)S(1)}, f32[448,128]{1,0:T(8,128)S(1)}, u32[]{:S(2)}, u32[]{:S(2)}) %collective-permute-start.8) | collective-permute-done | bytes 229408 | tf_op jit(solution)/shard_map/ppermute | solution.py:665
  56.9 0.5 collective-permute-start.9
  57.5 7.1 %collective-permute-done.9 = f32[224,128]{1,0:T(8,128)S(1)} collective-permute-done((f32[224,128]{1,0:T(8,128)S(1)}, f32[224,128]{1,0:T(8,128)S(1)}, u32[]{:S(2)}, u32[]{:S(2)}) %collective-permute-start.9) | collective-permute-done | bytes 114720 | tf_op jit(solution)/shard_map/ppermute | solution.py:665
  64.6 0.6 collective-permute-start.10
  65.3 3.4 %all-to-all-start.2 = ((f32[4,4,3328]{2,1,0:T(4,128)}), f32[4,4,3328]{2,1,0:T(4,128)S(1)}, u32[]{:S(2)}, u32[]{:S(2)}) async-start(f32[4,4,3328]{2,1,0:T(4,128)} %get-tuple-element.55), calls=%async_computation.2 | async-start | bytes 425984 | tf_op jit(solution)/shard_map/all_to_all | solution.py:718
  68.6 0.2 collective-permute-done.10
  68.9 1.3 collective-permute-start.11
  70.2 0.1 add.63.rest_0_
  70.4 0.8 collective-permute-start.15
  71.2 0.2 copy-done
  71.4 6.3 %shard_map.226 = f32[4,4,3328]{2,1,0:T(4,128)} custom-call(s32[1,256]{1,0:T(1,128)} %bitcast.65, f32[16,128]{1,0:T(8,128)} %get-tuple-element.56.lists, f32[235,256]{1,0:T(8,128)} %get-tuple-element.45.rot, bf16[448,256]{1,0:T(8,128)(2,1)} %get-tuple-element.57.g0, bf16[384,512]{1,0:T(8,128)(2,1)} %get-tuple-element.58.g1, ...), custom_call_target="tpu_custom_call" | custom-call | flops 6000000000 | bytes 2764800 | tf_op jit(solution)/shard_map/pallas_call | solution.py:642
  77.8 6.6 %collective-permute-done.15 = f32[1088,128]{1,0:T(8,128)S(1)} collective-permute-done((f32[1088,128]{1,0:T(8,128)S(1)}, f32[1088,128]{1,0:T(8,128)S(1)}, u32[]{:S(2)}, u32[]{:S(2)}) %collective-permute-start.15) | collective-permute-done | bytes 557088 | tf_op jit(solution)/shard_map/ppermute | solution.py:665
  84.4 1.1 bitcast_add_fusion
  85.5 1.8 %collective-permute-start.16 = (f32[544,128]{1,0:T(8,128)S(1)}, f32[544,128]{1,0:T(8,128)S(1)}, u32[]{:S(2)}, u32[]{:S(2)}) collective-permute-start(f32[544,128]{1,0:T(8,128)S(1)} %dynamic-slice_bitcast_fusion.1), channel_id=1, source_target_pairs={{0,4},{4,0},{8,12},{12,8},{1,5},{5,1},{9,13},{13,9},{2,6},{6,2},{1... | collective-permute-start | bytes 835592 | tf_op jit(solution)/shard_map/ppermute | solution.py:665
  87.3 2.4 %collective-permute-start.12 = (bf16[224,128]{1,0:T(8,128)(2,1)S(1)}, bf16[224,128]{1,0:T(8,128)(2,1)S(1)}, u32[]{:S(2)}, u32[]{:S(2)}) collective-permute-start(bf16[224,128]{1,0:T(8,128)(2,1)S(1)} %pad_maximum_fusion.5), channel_id=1, source_target_pairs={{0,8},{4,12},{8,0},{12,4},{1,9},{5,13},{9,1},{13,5},{2,10},{6,14},... | collective-permute-start | bytes 172040 | tf_op jit(solution)/shard_map/ppermute | solution.py:665
  89.7 4.1 %collective-permute-done.16 = f32[544,128]{1,0:T(8,128)S(1)} collective-permute-done((f32[544,128]{1,0:T(8,128)S(1)}, f32[544,128]{1,0:T(8,128)S(1)}, u32[]{:S(2)}, u32[]{:S(2)}) %collective-permute-start.16) | collective-permute-done | bytes 278560 | tf_op jit(solution)/shard_map/ppermute | solution.py:665
  93.9 1.8 %collective-permute-start.17 = (f32[272,128]{1,0:T(8,128)S(1)}, f32[272,128]{1,0:T(8,128)S(1)}, u32[]{:S(2)}, u32[]{:S(2)}) collective-permute-start(f32[272,128]{1,0:T(8,128)S(1)} %dynamic-slice_bitcast_fusion.3), channel_id=1, source_target_pairs={{0,8},{4,12},{8,0},{12,4},{1,9},{5,13},{9,1},{13,5},{2,10},{6,14},... | collective-permute-start | bytes 417800 | tf_op jit(solution)/shard_map/ppermute | solution.py:665
  95.7 7.0 %collective-permute-done.17 = f32[272,128]{1,0:T(8,128)S(1)} collective-permute-done((f32[272,128]{1,0:T(8,128)S(1)}, f32[272,128]{1,0:T(8,128)S(1)}, u32[]{:S(2)}, u32[]{:S(2)}) %collective-permute-start.17) | collective-permute-done | bytes 139296 | tf_op jit(solution)/shard_map/ppermute | solution.py:665
  102.7 0.1 collective-permute-start.18
  102.8 3.5 %collective-permute-start.13 = (bf16[448,128]{1,0:T(8,128)(2,1)S(1)}, bf16[448,128]{1,0:T(8,128)(2,1)S(1)}, u32[]{:S(2)}, u32[]{:S(2)}) collective-permute-start(bf16[448,128]{1,0:T(8,128)(2,1)S(1)} %pad_maximum_fusion.4), channel_id=1, source_target_pairs={{0,4},{4,0},{8,12},{12,8},{1,5},{5,1},{9,13},{13,9},{2,6},{6,2},{1... | collective-permute-start | bytes 344072 | tf_op jit(solution)/shard_map/ppermute | solution.py:665
  106.3 3.6 %all-to-all-start.3 = ((f32[4,4,3328]{2,1,0:T(4,128)}), f32[4,4,3328]{2,1,0:T(4,128)S(1)}, u32[]{:S(2)}, u32[]{:S(2)}) async-start(f32[4,4,3328]{2,1,0:T(4,128)} %shard_map.226), calls=%async_computation.3 | async-start | bytes 425984 | tf_op jit(solution)/shard_map/all_to_all | solution.py:718
  109.9 0.6 collective-permute-start.3
  110.6 1.8 %collective-permute-start.19 = (bf16[544,128]{1,0:T(8,128)(2,1)S(1)}, bf16[544,128]{1,0:T(8,128)(2,1)S(1)}, u32[]{:S(2)}, u32[]{:S(2)}) collective-permute-start(bf16[544,128]{1,0:T(8,128)(2,1)S(1)} %pad_maximum_fusion.3), channel_id=1, source_target_pairs={{0,4},{4,0},{8,12},{12,8},{1,5},{5,1},{9,13},{13,9},{2,6},{6,2},{1... | collective-permute-start | bytes 417800 | tf_op jit(solution)/shard_map/ppermute | solution.py:665
  112.4 0.0 copy-start.4
  112.5 0.1 collective-permute-start.14
  112.5 0.5 collective-permute-start.2
  113.0 2.8 %collective-permute-done.3.rest_2_ = f32[4,4,3328]{2,1,0:T(4,128)S(1)} collective-permute-done((f32[4,4,3328]{2,1,0:T(4,128)S(1)}, f32[4,4,3328]{2,1,0:T(4,128)S(1)}, u32[]{:S(2)}, u32[]{:S(2)}) %collective-permute-start.3) | collective-permute-done | bytes 213024 | tf_op jit(solution)/shard_map/ppermute | solution.py:665
  115.8 0.4 all-to-all-done.3.rest_0_
  116.2 0.5 collective-permute-start.6
  116.7 0.1 collective-permute-done.19
  116.8 0.1 broadcast_select_fusion.3
  116.9 1.4 %collective-permute-start.20 = (bf16[1088,128]{1,0:T(8,128)(2,1)S(1)}, bf16[1088,128]{1,0:T(8,128)(2,1)S(1)}, u32[]{:S(2)}, u32[]{:S(2)}) collective-permute-start(bf16[1088,128]{1,0:T(8,128)(2,1)S(1)} %pad_maximum_fusion.1), channel_id=1, source_target_pairs={{0,2},{1,3},{2,0},{3,1},{4,6},{5,7},{6,4},{7,5},{8,10},{9,11},{10,... | collective-permute-start | bytes 835592 | tf_op jit(solution)/shard_map/ppermute | solution.py:665
  118.4 0.7 copy-done.16
  119.1 0.7 copy-done.17
  119.7 3.3 %shard_map.227 = (bf16[49,32,64]{2,1,0:T(8,128)(2,1)}, f32[256,128]{1,0:T(8,128)}) custom-call(bf16[49,32,64]{2,1,0:T(8,128)(2,1)} %bitcast.60, bf16[7,64,64]{2,1,0:T(8,128)(2,1)} %out_proj.3, f32[4,4,3328]{2,1,0:T(4,128)} %copy-done.5, f32[4,4,3328]{2,1,0:T(4,128)} %copy-done.16, f32[4,4,3328]{2,1,0:T(4,128)} %copy-done.13, f32[4,4,3328]{2,1,0:T(4,128)} %copy-done.17), custom_call_target="tpu_custom_call" | custom-call | flops 4000000000 | bytes 1110016 | tf_op jit(solution)/shard_map/pallas_call | solution.py:642
  123.0 1.5 %collective-permute-start.22 = (f32[256,128]{1,0:T(8,128)}, f32[256,128]{1,0:T(8,128)S(1)}, u32[]{:S(2)}, u32[]{:S(2)}) collective-permute-start(f32[256,128]{1,0:T(8,128)} %get-tuple-element.72), channel_id=1, source_target_pairs={{0,4},{4,0},{8,12},{12,8},{1,5},{5,1},{9,13},{13,9},{2,6},{6,2},{1... | collective-permute-start | bytes 393224 | tf_op jit(solution)/shard_map/ppermute | solution.py:665
  124.6 0.7 copy-done.11
  125.2 1.9 %shard_map.229 = bf16[448,448]{1,0:T(8,128)(2,1)} custom-call(bf16[896,128]{1,0:T(8,128)(2,1)} %copy-done.4, bf16[896,128]{1,0:T(8,128)(2,1)} %copy-done.11), custom_call_target="tpu_custom_call" | custom-call | flops 1000000000 | bytes 458752 | tf_op jit(solution)/shard_map/pallas_call | solution.py:642
  127.2 0.5 collective-permute-start.7
  127.7 0.6 collective-permute-done.22
  128.3 2.7 %collective-permute-start.23 = (f32[256,128]{1,0:T(8,128)S(1)}, f32[256,128]{1,0:T(8,128)S(1)}, u32[]{:S(2)}, u32[]{:S(2)}) collective-permute-start(f32[256,128]{1,0:T(8,128)S(1)} %add.77), channel_id=1, source_target_pairs={{0,8},{4,12},{8,0},{12,4},{1,9},{5,13},{9,1},{13,5},{2,10},{6,14},... | collective-permute-start | bytes 393224 | tf_op jit(solution)/shard_map/ppermute | solution.py:665
  131.0 0.1 broadcast_select_fusion.1
  131.2 0.1 collective-permute-start.21
  131.3 5.7 %collective-permute-done.23 = f32[256,128]{1,0:T(8,128)S(1)} collective-permute-done((f32[256,128]{1,0:T(8,128)S(1)}, f32[256,128]{1,0:T(8,128)S(1)}, u32[]{:S(2)}, u32[]{:S(2)}) %collective-permute-start.23) | collective-permute-done | bytes 131104 | tf_op jit(solution)/shard_map/ppermute | solution.py:665
  137.0 0.1 reshape.64
  137.1 0.7 slice.4
  137.8 0.7 copy-done.14
  138.5 0.7 copy-done.15
  139.1 2.6 %shard_map.228 = bf16[49,32,64]{2,1,0:T(8,128)(2,1)} custom-call(f32[4,4,3328]{2,1,0:T(4,128)} %copy-done.6, f32[4,4,3328]{2,1,0:T(4,128)} %copy-done.14, f32[4,4,3328]{2,1,0:T(4,128)} %copy-done.12, f32[4,4,3328]{2,1,0:T(4,128)} %copy-done.15), custom_call_target="tpu_custom_call" | custom-call | flops 4000000000 | bytes 851968 | tf_op jit(solution)/shard_map/pallas_call | solution.py:642
  141.7 0.8 copy-done.10
  142.6 2.4 %shard_map.230 = (bf16[2,384,384]{2,1,0:T(8,128)(2,1)}, bf16[2,320,320]{2,1,0:T(8,128)(2,1)}, bf16[64,256]{1,0:T(8,128)(2,1)}, bf16[128,256]{1,0:T(8,128)(2,1)}, bf16[2,128]{1,0:T(2,128)(2,1)}) custom-call(bf16[2176,128]{1,0:T(8,128)(2,1)} %copy-done.3, bf16[2176,128]{1,0:T(8,128)(2,1)} %copy-done.10), custom_call_target="tpu_custom_call" | custom-call | flops 1000000000 | bytes 1114112 | tf_op jit(solution)/shard_map/pallas_call | solution.py:642
  (70 shorter events, 0.6 us)
Async XLA Ops:
  0.6 8.6 %copy-start.18 = (bf16[256]{0:T(256)(128)(2,1)S(1)}, bf16[256]{0:T(256)(128)(2,1)}, u32[]{:S(2)}) copy-start(bf16[256]{0:T(256)(128)(2,1)} %param.30) | copy-start | bytes 1540
  0.7 9.2 %copy-start.9 = (bf16[256,235]{0,1:T(8,128)(2,1)S(1)}, bf16[256,235]{0,1:T(8,128)(2,1)}, u32[]{:S(2)}) copy-start(bf16[256,235]{0,1:T(8,128)(2,1)} %param.22) | copy-start | bytes 360964
  2.9 14.1 %all-to-all-start = ((bf16[4,4,6528]{2,1,0:T(4,128)(2,1)}), bf16[4,4,6528]{2,1,0:T(4,128)(2,1)S(1)}, u32[]{:S(2)}, u32[]{:S(2)}) async-start(bf16[4,4,6528]{2,1,0:T(4,128)(2,1)} %shard_map.223), calls=%async_computation | async-start | bytes 417792 | tf_op jit(solution)/shard_map/all_to_all | solution.py:718
  17.0 0.7 copy-start.7
  45.9 2.1 %collective-permute-start.1 = (f32[896,128]{1,0:T(8,128)}, f32[896,128]{1,0:T(8,128)S(1)}, u32[]{:S(2)}, u32[]{:S(2)}) collective-permute-start(f32[896,128]{1,0:T(8,128)} %get-tuple-element.63), channel_id=1, source_target_pairs={{0,1},{1,0},{2,3},{3,2},{4,5},{5,4},{6,7},{7,6},{8,9},{9,8},{10,11... | collective-permute-start | bytes 1376264 | tf_op jit(solution)/shard_map/ppermute | solution.py:665
  49.1 16.2 %copy-start.1 = (f32[896,128]{1,0:T(8,128)}, f32[896,128]{1,0:T(8,128)S(1)}, u32[]{:S(2)}) copy-start(f32[896,128]{1,0:T(8,128)S(1)} %add.64.rest_1_) | copy-start | bytes 1376260
  49.2 21.1 %copy-start.2 = (f32[2176,128]{1,0:T(8,128)S(1)}, f32[2176,128]{1,0:T(8,128)}, u32[]{:S(2)}) copy-start(f32[2176,128]{1,0:T(8,128)} %get-tuple-element.61) | copy-start | bytes 3342340
  49.2 7.7 %collective-permute-start.8 = (f32[448,128]{1,0:T(8,128)S(1)}, f32[448,128]{1,0:T(8,128)S(1)}, u32[]{:S(2)}, u32[]{:S(2)}) collective-permute-start(f32[448,128]{1,0:T(8,128)S(1)} %dynamic-slice_bitcast_fusion.2), channel_id=1, source_target_pairs={{0,4},{4,0},{8,12},{12,8},{1,5},{5,1},{9,13},{13,9},{2,6},{6,2},{1... | collective-permute-start | bytes 688136 | tf_op jit(solution)/shard_map/ppermute | solution.py:665
  49.7 20.5 %collective-permute-start = (f32[2176,128]{1,0:T(8,128)}, f32[2176,128]{1,0:T(8,128)S(1)}, u32[]{:S(2)}, u32[]{:S(2)}) collective-permute-start(f32[2176,128]{1,0:T(8,128)} %get-tuple-element.54), channel_id=1, source_target_pairs={{0,1},{1,0},{2,3},{3,2},{4,5},{5,4},{6,7},{7,6},{8,9},{9,8},{10,11... | collective-permute-start | bytes 3342344 | tf_op jit(solution)/shard_map/ppermute | solution.py:665
  56.9 7.7 %collective-permute-start.9 = (f32[224,128]{1,0:T(8,128)S(1)}, f32[224,128]{1,0:T(8,128)S(1)}, u32[]{:S(2)}, u32[]{:S(2)}) collective-permute-start(f32[224,128]{1,0:T(8,128)S(1)} %dynamic-slice_bitcast_fusion.4), channel_id=1, source_target_pairs={{0,8},{4,12},{8,0},{12,4},{1,9},{5,13},{9,1},{13,5},{2,10},{6,14},... | collective-permute-start | bytes 344072 | tf_op jit(solution)/shard_map/ppermute | solution.py:665
  64.6 4.2 %collective-permute-start.10 = (f32[112,128]{1,0:T(8,128)S(1)}, f32[112,128]{1,0:T(8,128)S(1)}, u32[]{:S(2)}, u32[]{:S(2)}) collective-permute-start(f32[112,128]{1,0:T(8,128)S(1)} %dynamic-slice_bitcast_fusion.5), channel_id=1, source_target_pairs={{0,2},{1,3},{2,0},{3,1},{4,6},{5,7},{6,4},{7,5},{8,10},{9,11},{10,... | collective-permute-start | bytes 172040 | tf_op jit(solution)/shard_map/ppermute | solution.py:665
  65.3 41.1 %all-to-all-start.2 = ((f32[4,4,3328]{2,1,0:T(4,128)}), f32[4,4,3328]{2,1,0:T(4,128)S(1)}, u32[]{:S(2)}, u32[]{:S(2)}) async-start(f32[4,4,3328]{2,1,0:T(4,128)} %get-tuple-element.55), calls=%async_computation.2 | async-start | bytes 425984 | tf_op jit(solution)/shard_map/all_to_all | solution.py:718
  68.9 18.4 %collective-permute-start.11 = (bf16[112,128]{1,0:T(8,128)(2,1)S(1)}, bf16[112,128]{1,0:T(8,128)(2,1)S(1)}, u32[]{:S(2)}, u32[]{:S(2)}) collective-permute-start(bf16[112,128]{1,0:T(8,128)(2,1)S(1)} %fusion.1), channel_id=1, source_target_pairs={{0,2},{1,3},{2,0},{3,1},{4,6},{5,7},{6,4},{7,5},{8,10},{9,11},{10,... | collective-permute-start | bytes 86024 | tf_op jit(solution)/shard_map/ppermute | solution.py:665
  70.3 1.1 copy-start
  70.4 14.0 %collective-permute-start.15 = (f32[1088,128]{1,0:T(8,128)S(1)}, f32[1088,128]{1,0:T(8,128)S(1)}, u32[]{:S(2)}, u32[]{:S(2)}) collective-permute-start(f32[1088,128]{1,0:T(8,128)S(1)} %dynamic-slice_bitcast_fusion), channel_id=1, source_target_pairs={{0,2},{1,3},{2,0},{3,1},{4,6},{5,7},{6,4},{7,5},{8,10},{9,11},{10,... | collective-permute-start | bytes 1671176 | tf_op jit(solution)/shard_map/ppermute | solution.py:665
  85.5 8.3 %collective-permute-start.16 = (f32[544,128]{1,0:T(8,128)S(1)}, f32[544,128]{1,0:T(8,128)S(1)}, u32[]{:S(2)}, u32[]{:S(2)}) collective-permute-start(f32[544,128]{1,0:T(8,128)S(1)} %dynamic-slice_bitcast_fusion.1), channel_id=1, source_target_pairs={{0,4},{4,0},{8,12},{12,8},{1,5},{5,1},{9,13},{13,9},{2,6},{6,2},{1... | collective-permute-start | bytes 835592 | tf_op jit(solution)/shard_map/ppermute | solution.py:665
  87.3 8.3 %collective-permute-start.12 = (bf16[224,128]{1,0:T(8,128)(2,1)S(1)}, bf16[224,128]{1,0:T(8,128)(2,1)S(1)}, u32[]{:S(2)}, u32[]{:S(2)}) collective-permute-start(bf16[224,128]{1,0:T(8,128)(2,1)S(1)} %pad_maximum_fusion.5), channel_id=1, source_target_pairs={{0,8},{4,12},{8,0},{12,4},{1,9},{5,13},{9,1},{13,5},{2,10},{6,14},... | collective-permute-start | bytes 172040 | tf_op jit(solution)/shard_map/ppermute | solution.py:665
  93.9 8.8 %collective-permute-start.17 = (f32[272,128]{1,0:T(8,128)S(1)}, f32[272,128]{1,0:T(8,128)S(1)}, u32[]{:S(2)}, u32[]{:S(2)}) collective-permute-start(f32[272,128]{1,0:T(8,128)S(1)} %dynamic-slice_bitcast_fusion.3), channel_id=1, source_target_pairs={{0,8},{4,12},{8,0},{12,4},{1,9},{5,13},{9,1},{13,5},{2,10},{6,14},... | collective-permute-start | bytes 417800 | tf_op jit(solution)/shard_map/ppermute | solution.py:665
  102.7 7.8 %collective-permute-start.18 = (bf16[272,128]{1,0:T(8,128)(2,1)S(1)}, bf16[272,128]{1,0:T(8,128)(2,1)S(1)}, u32[]{:S(2)}, u32[]{:S(2)}) collective-permute-start(bf16[272,128]{1,0:T(8,128)(2,1)S(1)} %fusion), channel_id=1, source_target_pairs={{0,8},{4,12},{8,0},{12,4},{1,9},{5,13},{9,1},{13,5},{2,10},{6,14},... | collective-permute-start | bytes 208904 | tf_op jit(solution)/shard_map/ppermute | solution.py:665
  102.8 9.6 %collective-permute-start.13 = (bf16[448,128]{1,0:T(8,128)(2,1)S(1)}, bf16[448,128]{1,0:T(8,128)(2,1)S(1)}, u32[]{:S(2)}, u32[]{:S(2)}) collective-permute-start(bf16[448,128]{1,0:T(8,128)(2,1)S(1)} %pad_maximum_fusion.4), channel_id=1, source_target_pairs={{0,4},{4,0},{8,12},{12,8},{1,5},{5,1},{9,13},{13,9},{2,6},{6,2},{1... | collective-permute-start | bytes 344072 | tf_op jit(solution)/shard_map/ppermute | solution.py:665
  106.3 10.6 %copy-start.5 = (f32[4,4,3328]{2,1,0:T(4,128)}, f32[4,4,3328]{2,1,0:T(4,128)S(1)}, u32[]{:S(2)}) copy-start(f32[4,4,3328]{2,1,0:T(4,128)S(1)} %all-to-all-done.2.rest_0_) | copy-start | bytes 638980
  106.3 9.8 %all-to-all-start.3 = ((f32[4,4,3328]{2,1,0:T(4,128)}), f32[4,4,3328]{2,1,0:T(4,128)S(1)}, u32[]{:S(2)}, u32[]{:S(2)}) async-start(f32[4,4,3328]{2,1,0:T(4,128)} %shard_map.226), calls=%async_computation.3 | async-start | bytes 425984 | tf_op jit(solution)/shard_map/all_to_all | solution.py:718
  109.9 5.9 %collective-permute-start.3 = (f32[4,4,3328]{2,1,0:T(4,128)S(1)}, f32[4,4,3328]{2,1,0:T(4,128)S(1)}, u32[]{:S(2)}, u32[]{:S(2)}) collective-permute-start(f32[4,4,3328]{2,1,0:T(4,128)S(1)} %all-to-all-done.2.rest_0_), channel_id=1, source_target_pairs={{0,2},{1,3},{2,0},{3,1},{4,6},{5,7},{6,4},{7,5},{8,10},{9,11},{10,... | collective-permute-start | bytes 638984 | tf_op jit(solution)/shard_map/ppermute | solution.py:665
  110.6 6.3 %collective-permute-start.19 = (bf16[544,128]{1,0:T(8,128)(2,1)S(1)}, bf16[544,128]{1,0:T(8,128)(2,1)S(1)}, u32[]{:S(2)}, u32[]{:S(2)}) collective-permute-start(bf16[544,128]{1,0:T(8,128)(2,1)S(1)} %pad_maximum_fusion.3), channel_id=1, source_target_pairs={{0,4},{4,0},{8,12},{12,8},{1,5},{5,1},{9,13},{13,9},{2,6},{6,2},{1... | collective-permute-start | bytes 417800 | tf_op jit(solution)/shard_map/ppermute | solution.py:665
  112.4 10.6 %copy-start.4 = (bf16[896,128]{1,0:T(8,128)(2,1)}, bf16[896,128]{1,0:T(8,128)(2,1)S(1)}, u32[]{:S(2)}) copy-start(bf16[896,128]{1,0:T(8,128)(2,1)S(1)} %pad_maximum_fusion.2.mine) | copy-start | bytes 688132
  112.5 12.1 %collective-permute-start.14 = (bf16[896,128]{1,0:T(8,128)(2,1)S(1)}, bf16[896,128]{1,0:T(8,128)(2,1)S(1)}, u32[]{:S(2)}, u32[]{:S(2)}) collective-permute-start(bf16[896,128]{1,0:T(8,128)(2,1)S(1)} %pad_maximum_fusion.2.mine), channel_id=1, source_target_pairs={{0,1},{1,0},{2,3},{3,2},{4,5},{5,4},{6,7},{7,6},{8,9},{9,8},{10,11... | collective-permute-start | bytes 688136 | tf_op jit(solution)/shard_map/ppermute | solution.py:665
  112.5 5.8 %collective-permute-start.2 = (f32[4,4,3328]{2,1,0:T(4,128)S(1)}, f32[4,4,3328]{2,1,0:T(4,128)S(1)}, u32[]{:S(2)}, u32[]{:S(2)}) collective-permute-start(f32[4,4,3328]{2,1,0:T(4,128)S(1)} %all-to-all-done.2.rest_0_), channel_id=1, source_target_pairs={{0,1},{1,0},{2,3},{3,2},{4,5},{5,4},{6,7},{7,6},{8,9},{9,8},{10,11... | collective-permute-start | bytes 638984 | tf_op jit(solution)/shard_map/ppermute | solution.py:665
  115.8 2.6 %copy-start.13 = (f32[4,4,3328]{2,1,0:T(4,128)}, f32[4,4,3328]{2,1,0:T(4,128)S(1)}, u32[]{:S(2)}) copy-start(f32[4,4,3328]{2,1,0:T(4,128)S(1)} %collective-permute-done.3.rest_2_) | copy-start | bytes 638980
  115.8 2.6 %collective-permute-start.4 = (f32[4,4,3328]{2,1,0:T(4,128)S(1)}, f32[4,4,3328]{2,1,0:T(4,128)S(1)}, u32[]{:S(2)}, u32[]{:S(2)}) collective-permute-start(f32[4,4,3328]{2,1,0:T(4,128)S(1)} %collective-permute-done.3.rest_2_), channel_id=1, source_target_pairs={{0,1},{1,0},{2,3},{3,2},{4,5},{5,4},{6,7},{7,6},{8,9},{9,8},{10,11... | collective-permute-start | bytes 638984 | tf_op jit(solution)/shard_map/ppermute | solution.py:665
  116.2 11.0 %copy-start.6 = (f32[4,4,3328]{2,1,0:T(4,128)}, f32[4,4,3328]{2,1,0:T(4,128)S(1)}, u32[]{:S(2)}) copy-start(f32[4,4,3328]{2,1,0:T(4,128)S(1)} %all-to-all-done.3.rest_0_) | copy-start | bytes 638980
  116.2 11.0 %collective-permute-start.6 = (f32[4,4,3328]{2,1,0:T(4,128)S(1)}, f32[4,4,3328]{2,1,0:T(4,128)S(1)}, u32[]{:S(2)}, u32[]{:S(2)}) collective-permute-start(f32[4,4,3328]{2,1,0:T(4,128)S(1)} %all-to-all-done.3.rest_0_), channel_id=1, source_target_pairs={{0,2},{1,3},{2,0},{3,1},{4,6},{5,7},{6,4},{7,5},{8,10},{9,11},{10,... | collective-permute-start | bytes 638984 | tf_op jit(solution)/shard_map/ppermute | solution.py:665
  116.9 14.1 %collective-permute-start.20 = (bf16[1088,128]{1,0:T(8,128)(2,1)S(1)}, bf16[1088,128]{1,0:T(8,128)(2,1)S(1)}, u32[]{:S(2)}, u32[]{:S(2)}) collective-permute-start(bf16[1088,128]{1,0:T(8,128)(2,1)S(1)} %pad_maximum_fusion.1), channel_id=1, source_target_pairs={{0,2},{1,3},{2,0},{3,1},{4,6},{5,7},{6,4},{7,5},{8,10},{9,11},{10,... | collective-permute-start | bytes 835592 | tf_op jit(solution)/shard_map/ppermute | solution.py:665
  118.4 0.7 copy-start.16
  119.1 0.7 copy-start.17
  123.0 5.3 %copy-start.8 = (f32[256,128]{1,0:T(8,128)S(1)}, f32[256,128]{1,0:T(8,128)}, u32[]{:S(2)}) copy-start(f32[256,128]{1,0:T(8,128)} %get-tuple-element.72) | copy-start | bytes 393220
  123.0 5.3 %collective-permute-start.22 = (f32[256,128]{1,0:T(8,128)}, f32[256,128]{1,0:T(8,128)S(1)}, u32[]{:S(2)}, u32[]{:S(2)}) collective-permute-start(f32[256,128]{1,0:T(8,128)} %get-tuple-element.72), channel_id=1, source_target_pairs={{0,4},{4,0},{8,12},{12,8},{1,5},{5,1},{9,13},{13,9},{2,6},{6,2},{1... | collective-permute-start | bytes 393224 | tf_op jit(solution)/shard_map/ppermute | solution.py:665
  124.5 0.7 copy-start.11
  127.2 10.6 %collective-permute-start.5 = (f32[4,4,3328]{2,1,0:T(4,128)S(1)}, f32[4,4,3328]{2,1,0:T(4,128)S(1)}, u32[]{:S(2)}, u32[]{:S(2)}) collective-permute-start(f32[4,4,3328]{2,1,0:T(4,128)S(1)} %all-to-all-done.3.rest_0_), channel_id=1, source_target_pairs={{0,1},{1,0},{2,3},{3,2},{4,5},{5,4},{6,7},{7,6},{8,9},{9,8},{10,11... | collective-permute-start | bytes 638984 | tf_op jit(solution)/shard_map/ppermute | solution.py:665
  127.2 4.0 %copy-start.12 = (f32[4,4,3328]{2,1,0:T(4,128)}, f32[4,4,3328]{2,1,0:T(4,128)S(1)}, u32[]{:S(2)}) copy-start(f32[4,4,3328]{2,1,0:T(4,128)S(1)} %collective-permute-done.6.rest_2_) | copy-start | bytes 638980
  127.2 10.6 %collective-permute-start.7 = (f32[4,4,3328]{2,1,0:T(4,128)S(1)}, f32[4,4,3328]{2,1,0:T(4,128)S(1)}, u32[]{:S(2)}, u32[]{:S(2)}) collective-permute-start(f32[4,4,3328]{2,1,0:T(4,128)S(1)} %collective-permute-done.6.rest_2_), channel_id=1, source_target_pairs={{0,1},{1,0},{2,3},{3,2},{4,5},{5,4},{6,7},{7,6},{8,9},{9,8},{10,11... | collective-permute-start | bytes 638984 | tf_op jit(solution)/shard_map/ppermute | solution.py:665
  128.3 8.6 %collective-permute-start.23 = (f32[256,128]{1,0:T(8,128)S(1)}, f32[256,128]{1,0:T(8,128)S(1)}, u32[]{:S(2)}, u32[]{:S(2)}) collective-permute-start(f32[256,128]{1,0:T(8,128)S(1)} %add.77), channel_id=1, source_target_pairs={{0,8},{4,12},{8,0},{12,4},{1,9},{5,13},{9,1},{13,5},{2,10},{6,14},... | collective-permute-start | bytes 393224 | tf_op jit(solution)/shard_map/ppermute | solution.py:665
  131.2 10.5 %copy-start.3 = (bf16[2176,128]{1,0:T(8,128)(2,1)}, bf16[2176,128]{1,0:T(8,128)(2,1)S(1)}, u32[]{:S(2)}) copy-start(bf16[2176,128]{1,0:T(8,128)(2,1)S(1)} %pad_maximum_fusion.mine) | copy-start | bytes 1671172
  131.2 10.5 %collective-permute-start.21 = (bf16[2176,128]{1,0:T(8,128)(2,1)S(1)}, bf16[2176,128]{1,0:T(8,128)(2,1)S(1)}, u32[]{:S(2)}, u32[]{:S(2)}) collective-permute-start(bf16[2176,128]{1,0:T(8,128)(2,1)S(1)} %pad_maximum_fusion.mine), channel_id=1, source_target_pairs={{0,1},{1,0},{2,3},{3,2},{4,5},{5,4},{6,7},{7,6},{8,9},{9,8},{10,11... | collective-permute-start | bytes 1671176 | tf_op jit(solution)/shard_map/ppermute | solution.py:665
  137.8 0.7 copy-start.14
  138.5 0.7 copy-start.15
  141.7 0.8 copy-start.10

commit v4 on v3

--- a/solution.py
+++ b/solution.py
@@ -72,8 +72,8 @@
 
 
 def to_frame(source, rot, edges, emit):
-    def body(half, carry):
-        lanes = pl.ds(pl.multiple_of(half * LANES, LANES), LANES)
+    for half in range(edges // LANES):
+        lanes = pl.ds(half * LANES, LANES)
         for degree, centre, row_total, col_total, offset in degree_blocks():
             sums = [None] * row_total
             for j in range(col_total):
@@ -83,14 +83,11 @@
                     sums[i] = term if j == 0 else sums[i] + term
             for i in range(row_total):
                 emit(degree, i - centre, half, sums[i])
-        return carry
-
-    lax.fori_loop(0, edges // LANES, body, 0)
 
 
 def from_frame(load, rot, edges, emit):
-    def body(half, carry):
-        lanes = pl.ds(pl.multiple_of(half * LANES, LANES), LANES)
+    for half in range(edges // LANES):
+        lanes = pl.ds(half * LANES, LANES)
         for degree, centre, row_total, col_total, offset in degree_blocks():
             rows = [load(degree, i - centre, half) for i in range(row_total)]
             for j in range(col_total):
@@ -99,13 +96,10 @@
                     term = rot[pl.ds(offset + i * col_total + j, 1), lanes] * rows[i]
                     total = term if i == 0 else total + term
                 emit(degree * degree + j, half, total)
-        return carry
-
-    lax.fori_loop(0, edges // LANES, body, 0)
 
 
 def lane_at(half, edges, second):
-    return pl.ds(pl.multiple_of(half * LANES + (edges if second else 0), LANES), LANES)
+    return pl.ds(half * LANES + (edges if second else 0), LANES)
 
 
 def frame_place(degree, order, refs):
@@ -121,26 +115,38 @@
     )
 
 
-def one_hot_rows(slot_ref, slots):
+def is_direct(peers):
+    return peers <= 4
+
+
+def flip_of(peers):
+    return lax.axis_index("graph") if is_direct(peers) else 0
+
+
+def one_hot_rows(slot_ref, peers, slots):
     edges = slot_ref.shape[1]
-    return iota((slots, edges), 0) == slot_ref[...]
+    first = flip_of(peers) * (slots // peers)
+    return jnp.bitwise_xor(iota((slots, edges), 0), first) == slot_ref[...]
 
 
 def mask_to(mask, dtype):
     return jnp.where(mask, 1.0, 0.0).astype(dtype)
 
 
-def stack_table(table_ref, rows_ref):
-    peers, cap, width = table_ref.shape
-    for start in range(0, peers * cap, 8):
-        parts = [table_ref[g].astype(f32) for g in range(start // cap, (start + 8) // cap)]
-        rows_ref[pl.ds(start, 8), :] = jnp.concatenate(parts, axis=0)
+def stack_table(tables, rows_ref):
+    cap = tables[0].shape[0]
+    per = 8 // cap
+    for n in range(0, len(tables), per):
+        parts = [table[...].astype(f32) for table in tables[n : n + per]]
+        rows_ref[pl.ds(n * cap, 8), :] = jnp.concatenate(parts, axis=0)
 
 
 def put_rows(out_ref, cols, value):
     peers, cap = out_ref.shape[0], out_ref.shape[1]
-    for g in range(peers):
-        out_ref[g, :, cols] = value[g * cap : (g + 1) * cap].astype(out_ref.dtype)
+    flip = flip_of(peers)
+    for n in range(peers):
+        place = jnp.bitwise_xor(flip, n) if is_direct(peers) else n
+        out_ref[place, :, cols] = value[n * cap : (n + 1) * cap].astype(out_ref.dtype)
 
 
 def slot_sums(terms, one_hot, out_ref, factor=None):
@@ -173,46 +179,57 @@
 
 def listed_rows(list_ref, shape):
     peers, cap = list_ref.shape[1], list_ref.shape[3]
+    flip = flip_of(peers)
     row = iota(shape, 0)
     result = jnp.zeros(shape, jnp.int32)
     for slot in range(peers * cap):
-        result = jnp.where(row == slot, list_ref[0, slot // cap, 0, slot % cap], result)
+        owner = jnp.bitwise_xor(flip, slot // cap) if is_direct(peers) else slot // cap
+        result = jnp.where(row == slot, list_ref[0, owner, 0, slot % cap], result)
     return result
 
 
-def put_coeffs(out, first, coeff_rows):
+def put_coeffs(outs, first, coeff_rows):
     for block in range(BLOCKS):
         left = coeff_rows(2 * block)
         right = coeff_rows(2 * block + 1) if 2 * block + 1 < COEFFS else jnp.zeros_like(left)
-        put_rows(out, pl.ds(first + block * LANES, LANES), jnp.concatenate([left, right], axis=1))
-
-
-def outgoing_kernel(send, recv, embed, cot, out):
+        put_pieces(outs, first + block * LANES, jnp.concatenate([left, right], axis=1))
+
+
+def put_pieces(outs, first, value):
+    cap = outs[0].shape[0]
+    for n, out in enumerate(outs):
+        out[:, pl.ds(first, LANES)] = value[n * cap : (n + 1) * cap].astype(out.dtype)
+
+
+def outgoing_kernel(send, recv, embed, cot, *outs):
     atoms = embed.shape[1]
-    slots = out.shape[0] * out.shape[1]
+    slots = send.shape[1] * send.shape[3]
     sent = listed_rows(send, (slots, LANES))
     received = listed_rows(recv, (slots, LANES))
     for first, listed, values in ((0, sent, embed), (COLS, received, cot)):
         picked = mask_to(iota((slots, atoms), 1) == listed[:, :atoms], bf16)
-        put_coeffs(out, first, lambda k: dot_nn(picked, values[k]))
+        put_coeffs(outs, first, lambda k: dot_nn(picked, values[k]))
     lane = iota((slots, LANES), 1)
     side = jnp.where(lane == 0, received, jnp.where(lane == 1, sent, 0))
-    put_rows(out, pl.ds(2 * COLS, LANES), side.astype(f32))
+    put_pieces(outs, 2 * COLS, side.astype(f32))
 
 
 def swapped_halves(value, edges):
     return jnp.concatenate([-value[:, edges:], value[:, :edges]], axis=1)
 
 
-def make_forward(atoms):
+def make_forward(atoms, peers):
     def forward_kernel(
-        table, source_slot, target_slot, rotation, feats, bias, wzero_at, wone_at, wtwo_at,
-        ain, aedge, adot, out_proj,
+        source_slot, target_slot, rotation, feats, bias, wzero_at, wone_at, wtwo_at,
+        ain, aedge, adot, out_proj, *rest,
+    ):
+        tables, rest = rest[:peers], rest[peers:]
+        (
         sums_out, stats_out, x0_at, x1_at, x2_at, v0_at, v1_at, v2_at, pre_at, logit_out,
         lists_out, agg_grad, rot, own_out,
         rows, gathered, weights, terms, wzero, wone, wtwo, x0, x1, x2, v0, v1, v2, pre_out,
         semaphores,
-    ):
+        ) = rest
         copies = []
 
         def move(source, target):
@@ -225,10 +242,13 @@
         move(wtwo_at, wtwo)
         rot[...] = jnp.transpose(rotation[...].astype(f32))
         edges = source_slot.shape[1]
-        slots = table.shape[0] * table.shape[1]
-        stack_table(table, rows)
-        picked = mask_to(one_hot_rows(source_slot, slots), bf16)
-        gathered[...] = dot_tn(rows[:, pl.ds(0, FLAT)].astype(bf16), picked)
+        cap = tables[0].shape[0]
+        slots = peers * cap
+        stack_table(tables, rows)
+        picked = mask_to(one_hot_rows(source_slot, peers, slots), bf16)
+        for degree in range(LMAX + 1):
+            ids = pl.ds(degree * degree * CH, (2 * degree + 1) * CH)
+            gathered[ids, :] = dot_tn(rows[:, ids].astype(bf16), picked)
         lists = rows[:, pl.ds(2 * COLS, LANES)]
         lists_out[...] = lists
         for degree in range(LMAX + 1):
@@ -252,9 +272,9 @@
         pre_out[...] = pre
         move(pre_out, pre_at)
         hidden = jnp.where(pre > 0, pre, leak_slope * pre) * turned_column(adot[...].astype(f32))
-        aims = one_hot_rows(target_slot, slots)
+        aims = one_hot_rows(target_slot, peers, slots)
         lane = iota((slots, LANES), 1)
-        peer = iota((slots, 1), 0) // table.shape[1]
+        peer = jnp.bitwise_xor(iota((slots, 1), 0) // cap, flip_of(peers))
         name = lists[:, :1] + (peer * atoms).astype(f32)
         side = jnp.where(lane == NAME_AT, name, 0.0)
         for h in range(HEADS):
@@ -300,11 +320,7 @@
         spread = jnp.where(lane // STATS == iota((slots, LANES), 0) % 8, spread, 0.0)
         packed = jnp.sum(spread.reshape(slots // 8, 8, LANES), axis=1)
 
-        def copy_to(n, carry):
-            stats_out[n] = packed
-            return carry
-
-        lax.fori_loop(0, stats_out.shape[0], copy_to, 0)
+        stats_out[...] = packed
         for copy in copies[3:]:
             copy.wait()
 
@@ -385,12 +401,10 @@
 
 
 def combine_stats(stats, own):
-    blocks, slots = stats.shape[0], stats.shape[1] * 8
-    chunk = max(1, PANEL // slots)
+    chunk = 32
     name = own[:, NAME_AT : NAME_AT + 1]
 
-    def part(at):
-        part_rows = jnp.concatenate([stats[at * chunk + n] for n in range(chunk)], axis=0)
+    def part(part_rows):
         entries = [part_rows[:, n : n + STATS] for n in range(0, LANES, STATS)]
         turned = jnp.transpose(jnp.concatenate(entries, axis=0))
         same = name == turned[NAME_AT : NAME_AT + 1]
@@ -405,7 +419,7 @@
         return tuple(result)
 
     def step(at, held):
-        fresh = part(at)
+        fresh = part(stats[0][pl.ds(pl.multiple_of(at * chunk, chunk), chunk), :])
         result = []
         for h in range(HEADS):
             peak, den, dot = held[3 * h : 3 * h + 3]
@@ -415,14 +429,23 @@
             result += [most, den * old + new_den * new, dot * old + new_dot * new]
         return tuple(result)
 
-    held = part(0)
-    if blocks > chunk:
-        held = lax.fori_loop(1, blocks // chunk, step, held)
+    if len(stats) > 1:
+        held = part(jnp.concatenate([rows[...] for rows in stats], axis=0))
+    else:
+        held = part(stats[0][pl.ds(0, chunk), :])
+        held = lax.fori_loop(1, stats[0].shape[0] // chunk, step, held)
     return [held[3 * h : 3 * h + 3] for h in range(HEADS)]
 
 
+def make_gradient(peers, parts):
+    def kernel(*refs):
+        gradient_kernel(peers, refs[:parts], *refs[parts:])
+
+    return kernel
+
+
 def gradient_kernel(
-    stats, own, agg_grad, target_slot, rot, feats,
+    peers, stats, own, agg_grad, target_slot, rot, feats,
     x0_at, x1_at, x2_at, v0_at, v1_at, v2_at, pre, logits, adot,
     g0, top1, top2, pre_grad_out, kept0, sent0, kept1, sent1,
     num_grad, spread_grad, weights, g1, g2, packed, x0, x1, x2, v0, v1, v2, semaphores,
@@ -436,7 +459,7 @@
         loads.append(load)
     edges = target_slot.shape[1]
     slots = agg_grad.shape[0]
-    aims = one_hot_rows(target_slot, slots)
+    aims = one_hot_rows(target_slot, peers, slots)
     combined = combine_stats(stats, own[...])
     den_grads = []
     for h, (peak, den, dot) in enumerate(combined):
@@ -448,7 +471,10 @@
     for block in range(BLOCKS):
         cols = block_cols(block)
         num_grad[:, cols] = (agg_grad[:, cols] / den_full[:, : cols.size]).astype(bf16)
-    spread_grad[...] = dot_tn(num_grad[...], mask_to(aims, bf16))
+    picked = mask_to(aims, bf16)
+    for degree in range(LMAX + 1):
+        ids = pl.ds(degree * degree * CH, (2 * degree + 1) * CH)
+        spread_grad[ids, :] = dot_tn(num_grad[:, ids], picked)
 
     state = {}
 
@@ -604,7 +630,7 @@
 
     terms[pl.ds(FLAT, COLS - FLAT), :] = jnp.zeros((COLS - FLAT, 2 * edges), bf16)
     from_frame(load, rot, edges, store_terms(terms, edges))
-    slot_sums(terms, mask_to(one_hot_rows(source_slot, slots), bf16), sums_out)
+    slot_sums(terms, mask_to(one_hot_rows(source_slot, sums_out.shape[0], slots), bf16), sums_out)
     put_rows(sums_out, pl.ds(COLS, LANES), lists[...])
 
 
@@ -652,8 +678,18 @@
     )(*args, *after)
 
 
-def tie(value, *earlier):
-    return lax.optimization_barrier((value, *earlier))[0]
+class Order:
+    def __init__(self):
+        self.last = None
+
+    def hold(self, value):
+        if self.last is None:
+            return value
+        return lax.optimization_barrier((value, self.last))[0]
+
+    def mark(self, value):
+        self.last = value
+        return value
 
 
 def turned_column(row):
@@ -680,25 +716,43 @@
     return (lax.axis_index(axis) >> bit) & 1
 
 
-def sum_all(current, first, earlier=()):
+def sum_all(kept, sent, first, order):
     steps = [("edge", n) for n in range(1, bits_of("edge"))]
     steps += [("graph", n) for n in range(bits_of("graph"))]
     steps.sort(key=lambda step: step[0] != first)
+    other = swap(sent, "edge", 0)
+    yield
+    current = kept + order.hold(other)
     for axis, bit in steps:
         mine = own_bit(axis, bit)
         parts = current.reshape(2, current.shape[0] // 2, -1)
-        other = swap(lax.dynamic_index_in_dim(parts, 1 - mine, 0, False), axis, bit)
-        if earlier:
-            other, earlier = tie(other, *earlier), ()
-        current = lax.dynamic_index_in_dim(parts, mine, 0, False) + other
-    current = current.astype(bf16)
+        sent = order.mark(lax.dynamic_index_in_dim(parts, 1 - mine, 0, False))
+        other = swap(sent, axis, bit)
+        yield
+        current = lax.dynamic_index_in_dim(parts, mine, 0, False) + order.hold(other)
+    current = order.mark(current.astype(bf16))
     for axis, bit in reversed(steps):
         mine = own_bit(axis, bit)
         other = swap(current, axis, bit)
-        current = jnp.concatenate(
-            [jnp.where(mine == 0, current, other), jnp.where(mine == 0, other, current)], axis=0
+        yield
+        other = order.hold(other)
+        current = order.mark(
+            jnp.concatenate(
+                [jnp.where(mine == 0, current, other), jnp.where(mine == 0, other, current)],
+                axis=0,
+            )
         )
-    return current, swap(current, "edge", 0)
+    other = swap(current, "edge", 0)
+    yield
+    return current, other
+
+
+def finish_steps(chain):
+    while True:
+        try:
+            next(chain)
+        except StopIteration as end:
+            return end.value
 
 
 def shards(
@@ -713,17 +767,25 @@
     cap = send_rows.shape[3]
     slots = peers * cap
     blocks = peers * lanes_total
+    direct = is_direct(peers)
+    order = Order()
 
     def exchange(value):
         return lax.all_to_all(value, "graph", split_axis=0, concat_axis=0, tiled=True)
 
     cot = jnp.transpose(out_cotangent, (1, 0, 2))
-    (outgoing,) = call(
-        outgoing_kernel, [((peers, cap, TABLE), bf16)], [],
+    outgoing = call(
+        outgoing_kernel, [((cap, TABLE), bf16)] * peers, [],
         send_rows, recv_rows, jnp.transpose(atom_embed, (1, 0, 2)), cot,
         scalars=2, work=2,
     )
-    table = exchange(outgoing)
+    if direct:
+        tables = [outgoing[0]] + [
+            lax.ppermute(outgoing[k], "graph", [(i, i ^ k) for i in range(peers)])
+            for k in range(1, peers)
+        ]
+    else:
+        tables = list(exchange(jnp.stack(outgoing)))
 
     source_row = source_slot.reshape(1, edges)
     target_row = target_slot.reshape(1, edges)
@@ -740,8 +802,8 @@
     ]
     pre_shape = ((HEADS * ALPHA, edges), f32)
     sums, stats, x0, x1, x2, v0, v1, v2, pre, logits, lists, agg_grad, rot, own_stats = call(
-        make_forward(atoms),
-        [((peers, cap, WIDE), f32), ((blocks, slots // 8, LANES), f32)]
+        make_forward(atoms, peers),
+        [((peers, cap, WIDE), f32), ((slots // 8, LANES), f32)]
         + frames
         + [
             pre_shape,
@@ -762,15 +824,27 @@
         ]
         + frames
         + [pre_shape, pltpu.SemaphoreType.DMA((10,))],
-        table, source_row, target_row, rotation, edge_feats, bias,
-        conv_zero, conv_one, conv_two, alpha_in, alpha_edge, adot, out_proj,
-        far=(6, 7, 8), apart=range(2, 9), work=8,
-    )
-    all_stats = lax.all_to_all(stats, ("graph", "edge"), split_axis=0, concat_axis=0, tiled=True)
+        source_row, target_row, rotation, edge_feats, bias,
+        conv_zero, conv_one, conv_two, alpha_in, alpha_edge, adot, out_proj, *tables,
+        far=(5, 6, 7), apart=range(2, 9), work=8,
+    )
+    if direct:
+        lanes_stats = [stats] + [
+            lax.ppermute(stats, "edge", [(i, i ^ k) for i in range(lanes_total)])
+            for k in range(1, lanes_total)
+        ]
+        graph_stats = jnp.concatenate(lanes_stats, axis=0)
+        all_stats = [graph_stats] + [
+            lax.ppermute(graph_stats, "graph", [(i, i ^ k) for i in range(peers)])
+            for k in range(1, peers)
+        ]
+    else:
+        all_stats = [lax.all_gather(stats, ("graph", "edge"), tiled=True)]
+    messages = exchange(sums)
 
     halves = [((size, LANES), f32) for start, size in CHUNKS for _ in range(2)]
     g0, g1, g2, pre_grad, *halves = call(
-        gradient_kernel,
+        make_gradient(peers, len(all_stats)),
         [
             ((DIM0, edges), bf16),
             ((DIM1, 2 * edges), bf16),
@@ -788,15 +862,20 @@
         ]
         + frames
         + [pltpu.SemaphoreType.DMA((10,))],
-        all_stats, own_stats, agg_grad, target_row, rot, edge_feats,
+        *all_stats, own_stats, agg_grad, target_row, rot, edge_feats,
         x0, x1, x2, v0, v1, v2, pre, logits, adot,
-        far=range(6, 12), apart=range(4, 8), work=8,
-    )
-    currents = [
-        halves[2 * n] + swap(halves[2 * n + 1], "edge", 0) for n in range(len(CHUNKS))
-    ]
+        far=range(len(all_stats) + 5, len(all_stats) + 11), apart=range(4, 8), work=8,
+    )
 
     total = lanes_total * slots
+    order.mark(halves[0])
+    message_rows = gather_lanes(order.hold(messages))
+    zero_steps = sum_all(halves[2], halves[3], "graph", order)
+    rest_steps = sum_all(halves[0], halves[1], "edge", order)
+    next(zero_steps)
+    next(rest_steps)
+    next(zero_steps)
+    next(rest_steps)
     (source_sums,) = call(
         source_kernel,
         [((peers, cap, WIDE), f32)],
@@ -806,30 +885,46 @@
             ((DIM2, 2 * edges), f32),
             ((COLS, 2 * edges), bf16),
         ],
-        source_row, lists, rot, g0, g1, g2, pre_grad, conv_zero, conv_one, conv_two, alpha_in,
-        after=currents, work=6,
-    )
+        source_row, lists, rot, g0, g1, g2, order.hold(pre_grad),
+        conv_zero, conv_one, conv_two, alpha_in,
+        work=6,
+    )
+    order.mark(source_sums)
     returned = exchange(source_sums)
+    next(zero_steps)
     out, proj = call(
         make_finish(lanes_total),
         [((COEFFS, atoms, CH), bf16), (((LMAX // 2 + 1) * CH, LANES), f32)],
         [((total, WIDE), f32), ((2 * total, COLS), bf16), ((COEFFS, atoms, CH), bf16)],
-        cot, out_proj, *gather_lanes(tie(exchange(tie(sums, halves[1])), source_sums)),
-    )
-    for bit in range(bits_of("graph")):
-        proj = proj + swap(proj, "graph", bit)
+        order.hold(cot), out_proj, *message_rows,
+    )
+    order.mark(proj)
+    next(rest_steps)
+    next(zero_steps)
+    source_rows = gather_lanes(order.hold(returned))
+    next(zero_steps)
+    next(rest_steps)
+    next(zero_steps)
     (embed,) = call(
         make_collect(lanes_total),
         [((COEFFS, atoms, CH), bf16)],
         [((total, WIDE), f32)],
-        *gather_lanes(returned),
-    )
-
-    rest_pair = sum_all(currents[0], "edge", [source_sums])
-    zero_pair = sum_all(currents[1], "graph")
+        order.hold(source_rows[0]), *source_rows[1:],
+    )
+    order.mark(embed)
+    next(rest_steps)
+    next(zero_steps)
+    for bit in range(bits_of("graph")):
+        proj = proj + order.hold(swap(proj, "graph", bit))
+        order.mark(proj)
+        next(rest_steps)
+    zero_pair = finish_steps(zero_steps)
     (zero,) = call(
-        unpack_zero_kernel, [((DIM0, DIM0), bf16)], [], *zero_pair, work=1
-    )
+        unpack_zero_kernel, [((DIM0, DIM0), bf16)], [], order.hold(zero_pair[0]), zero_pair[1],
+        work=1,
+    )
+    order.mark(zero)
+    rest_pair = finish_steps(rest_steps)
     one, two, grad_in, grad_edge, grad_dot = call(
         unpack_rest_kernel,
         [
@@ -839,7 +934,7 @@
             (alpha_edge.shape, bf16),
             ((2, LANES), bf16),
         ],
-        [], *rest_pair, work=1,
+        [], order.hold(rest_pair[0]), rest_pair[1], work=1,
     )
 
     def shaped(value):

time: 146 us -> 134 us (0.918)
  starting transfers between devices: 36.5 us -> 30.8 us
  waiting for transfers between devices: 50.2 us -> 45.6 us
    ppermute x0 -> x9, starting transfers between devices: none -> 12 us  [the longest x3 5.61 us: shards(): lax.ppermute(outgoing[k], 'graph', [(i, i ^ k) for i in range(peers)])]
    ppermute x0 -> x9, waiting for transfers between devices: none -> 10.3 us  [the longest x3 4.83 us: shards(): lax.ppermute(outgoing[k], 'graph', [(i, i ^ k) for i in range(peers)])]
    all_to_all x3 -> x1, starting transfers between devices: 13.3 us -> 3.38 us  [exchange(): lax.all_to_all(value, 'graph', split_axis=0, concat_axis=0, tiled=True)]
    ppermute x24, waiting for transfers between devices: 43.4 us -> 34.4 us  [swap(): return lax.ppermute(value, axis, [(i, i ^ 1 << bit) for i in range(size)])]
    ppermute x24, starting transfers between devices: 23.2 us -> 15.5 us  [swap(): return lax.ppermute(value, axis, [(i, i ^ 1 << bit) for i in range(size)])]
    all_to_all x3 -> x1, waiting for transfers between devices: 6.79 us -> 0.98 us  [exchange(): lax.all_to_all(value, 'graph', split_axis=0, concat_axis=0, tiled=True)]
    all_to_all x1, blocking collectives: 10.7 us -> 12.1 us  [exchange(): lax.all_to_all(value, 'graph', split_axis=0, concat_axis=0, tiled=True)]
    pallas_call x8, Pallas kernels: 36.4 us -> 35 us  [call(): pl.pallas_call(kernel, out_shape=[jax.ShapeDtypeStruct(shape, kind) for s...]
  transfers between devices with their start and end apart: 27 -> 34, of which waited for: 13 -> 18; matrix products, arithmetic and copies ran while one was open for 3% -> 3% of each run, Pallas kernels for 10% -> 10%
where the time goes in v4:
time: 134 us; the launch traced here: 133 us
  waiting for transfers between devices  45.6 us (34%)
  Pallas kernels  35 us (26%)
  starting transfers between devices  30.8 us (23%)
  blocking collectives  12.1 us (9%)
  local copies, waits for them, and re-layouts  6.3 us (5%)
  other arithmetic  2.47 us (2%)
    pallas_call x8, Pallas kernels, call(): pl.pallas_call(kernel, out_shape=[jax.ShapeDtypeStruct(shape, kind) for s...  35 us
    ppermute x24, waiting for transfers between devices, swap(): return lax.ppermute(value, axis, [(i, i ^ 1 << bit) for i in range(size)])  34.4 us
    ppermute x24, starting transfers between devices, swap(): return lax.ppermute(value, axis, [(i, i ^ 1 << bit) for i in range(size)])  15.5 us
    all_to_all x1, blocking collectives, exchange(): lax.all_to_all(value, 'graph', split_axis=0, concat_axis=0, tiled=True)  12.1 us
    ppermute x3, starting transfers between devices, shards(): lax.ppermute(outgoing[k], 'graph', [(i, i ^ k) for i in range(peers)])  5.61 us
    unnamed x43, local copies, waits for them, and re-layouts  4.85 us
    ppermute x3, waiting for transfers between devices, shards(): lax.ppermute(outgoing[k], 'graph', [(i, i ^ k) for i in range(peers)])  4.83 us
    ppermute x3, starting transfers between devices, shards(): lax.ppermute(graph_stats, 'graph', [(i, i ^ k) for i in range(peers)])  4.44 us
  transfers between devices with their start and end apart: 34, of which 18 were waited for; matrix products, arithmetic and copies ran while one was open for 3% of the time, Pallas kernels for 10%

profile of v4, /device:TPU:0, one launch (start us, length us, event | category | flops | bytes accessed | tf_op | source)
XLA Modules:
  0.0 133.4 jit_solution(4327641424895211821)
XLA Ops:
  0.7 2.3 %shard_map.223 = (bf16[4,6528]{1,0:T(4,128)(2,1)}, bf16[4,6528]{1,0:T(4,128)(2,1)}, bf16[4,6528]{1,0:T(4,128)(2,1)}, bf16[4,6528]{1,0:T(4,128)(2,1)}) custom-call(s32[1,4,1,4]{3,2,1,0:T(1,128)} %send.1, s32[1,4,1,4]{3,2,1,0:T(1,128)} %recv.1, bf16[49,32,64]{2,1,0:T(8,128)(2,1)} %bitcast.58, bf16[49,32,64]{2,1,0:T(8,128)(2,1)} %bitcast.59), custom_call_target="tpu_custom_call" | custom-call | flops 2000000000 | bytes 401536 | tf_op jit(solution)/shard_map/pallas_call | solution.py:668
  3.0 3.0 %collective-permute-start = (bf16[4,6528]{1,0:T(4,128)(2,1)}, bf16[4,6528]{1,0:T(4,128)(2,1)S(1)}, u32[]{:S(2)}, u32[]{:S(2)}) collective-permute-start(bf16[4,6528]{1,0:T(4,128)(2,1)} %get-tuple-element.66), channel_id=1, source_target_pairs={{0,4},{4,0},{8,12},{12,8},{1,5},{5,1},{9,13},{13,9},{2,6},{6,2},{1... | collective-permute-start | bytes 156680 | tf_op jit(solution)/shard_map/ppermute | solution.py:784
  6.0 2.6 %collective-permute-start.1 = (bf16[4,6528]{1,0:T(4,128)(2,1)}, bf16[4,6528]{1,0:T(4,128)(2,1)S(1)}, u32[]{:S(2)}, u32[]{:S(2)}) collective-permute-start(bf16[4,6528]{1,0:T(4,128)(2,1)} %get-tuple-element.67), channel_id=1, source_target_pairs={{0,8},{4,12},{8,0},{12,4},{1,9},{5,13},{9,1},{13,5},{2,10},{6,14},... | collective-permute-start | bytes 156680 | tf_op jit(solution)/shard_map/ppermute | solution.py:784
  8.6 0.5 reshape.56.adot.refs_17_
  9.1 0.8 copy.25.rotation
  9.9 2.3 %collective-permute-done.1.rest_2_ = bf16[4,6528]{1,0:T(4,128)(2,1)S(1)} collective-permute-done((bf16[4,6528]{1,0:T(4,128)(2,1)}, bf16[4,6528]{1,0:T(4,128)(2,1)S(1)}, u32[]{:S(2)}, u32[]{:S(2)}) %collective-permute-start.1) | collective-permute-done | bytes 52256 | tf_op jit(solution)/shard_map/ppermute | solution.py:784
  12.2 2.5 %collective-permute-done.2.rest_3_ = bf16[4,6528]{1,0:T(4,128)(2,1)S(1)} collective-permute-done((bf16[4,6528]{1,0:T(4,128)(2,1)}, bf16[4,6528]{1,0:T(4,128)(2,1)S(1)}, u32[]{:S(2)}, u32[]{:S(2)}) %collective-permute-start.2) | collective-permute-done | bytes 52256 | tf_op jit(solution)/shard_map/ppermute | solution.py:784
  14.7 0.6 copy-done.16
  15.3 8.5 %shard_map.224 = (f32[4,4,3328]{2,1,0:T(4,128)}, f32[2,128]{1,0:T(2,128)}, bf16[448,256]{1,0:T(8,128)(2,1)}, bf16[384,512]{1,0:T(8,128)(2,1)}, bf16[320,512]{1,0...) custom-call(s32[1,256]{1,0:T(1,128)} %bitcast.64, ...), custom_call_target="tpu_custom_call" | custom-call | flops 8000000000 | bytes 1957888 | tf_op jit(solution)/shard_map/pallas_call | solution.py:668
  23.9 1.6 %collective-permute-start.4 = (f32[2,128]{1,0:T(2,128)}, f32[2,128]{1,0:T(2,128)S(1)}, u32[]{:S(2)}, u32[]{:S(2)}) collective-permute-start(f32[2,128]{1,0:T(2,128)} %get-tuple-element.69), channel_id=1, source_target_pairs={{0,2},{1,3},{2,0},{3,1},{4,6},{5,7},{6,4},{7,5},{8,10},{9,11},{10,... | collective-permute-start | bytes 3080 | tf_op jit(solution)/shard_map/ppermute | solution.py:833
  25.5 0.3 collective-permute-start.5
  25.8 2.0 %collective-permute-done.4 = f32[2,128]{1,0:T(2,128)S(1)} collective-permute-done((f32[2,128]{1,0:T(2,128)}, f32[2,128]{1,0:T(2,128)S(1)}, u32[]{:S(2)}, u32[]{:S(2)}) %collective-permute-start.4) | collective-permute-done | bytes 1056 | tf_op jit(solution)/shard_map/ppermute | solution.py:833
  27.8 0.9 collective-permute-done.5
  28.7 0.7 pad_maximum_fusion.6.refs_0_
  29.4 0.1 collective-permute-start.6
  29.5 1.5 %collective-permute-start.7 = (f32[8,128]{1,0:T(8,128)S(1)}, f32[8,128]{1,0:T(8,128)S(1)}, u32[]{:S(2)}, u32[]{:S(2)}) collective-permute-start(f32[8,128]{1,0:T(8,128)S(1)} %pad_maximum_fusion.6.refs_0_), channel_id=1, source_target_pairs={{0,8},{4,12},{8,0},{12,4},{1,9},{5,13},{9,1},{13,5},{2,10},{6,14},... | collective-permute-start | bytes 12296 | tf_op jit(solution)/shard_map/ppermute | solution.py:838
  31.0 2.9 %collective-permute-start.8 = (f32[8,128]{1,0:T(8,128)S(1)}, f32[8,128]{1,0:T(8,128)S(1)}, u32[]{:S(2)}, u32[]{:S(2)}) collective-permute-start(f32[8,128]{1,0:T(8,128)S(1)} %pad_maximum_fusion.6.refs_0_), channel_id=1, source_target_pairs={{0,12},{4,8},{8,4},{12,0},{1,13},{5,9},{9,5},{13,1},{2,14},{6,10},... | collective-permute-start | bytes 12296 | tf_op jit(solution)/shard_map/ppermute | solution.py:838
  33.8 0.2 collective-permute-done.7.refs_2_
  34.0 2.3 %collective-permute-done.8.refs_3_ = f32[8,128]{1,0:T(8,128)S(1)} collective-permute-done((f32[8,128]{1,0:T(8,128)S(1)}, f32[8,128]{1,0:T(8,128)S(1)}, u32[]{:S(2)}, u32[]{:S(2)}) %collective-permute-start.8) | collective-permute-done | bytes 4128 | tf_op jit(solution)/shard_map/ppermute | solution.py:838
  36.4 0.6 copy-done.19
  37.0 8.5 %shard_map.225 = (bf16[448,256]{1,0:T(8,128)(2,1)}, bf16[384,512]{1,0:T(8,128)(2,1)}, bf16[320,512]{1,0:T(8,128)(2,1)}, bf16[256,256]{1,0:T(8,128)(2,1)}, f32[21...) custom-call(f32[8,128]{1,0:T(8,128)} %copy-done.8, f32[8,128]{1,0:T(8,128)} %copy-done.17, ...), custom_call_target="tpu_custom_call" | custom-call | flops 8000000000 | bytes 3654144 | tf_op jit(solution)/shard_map/pallas_call | solution.py:668
  45.5 0.5 collective-permute-start.9
  46.0 12.1 %all_to_all.10.rest_0_ = f32[4,4,3328]{2,1,0:T(4,128)S(1)} all-to-all(f32[4,4,3328]{2,1,0:T(4,128)S(1)} %copy-done.5), channel_id=1, replica_groups=mesh['groups'=2,'graph'=4,'edge'=4] {'graph'}, dimensions={0} | all-to-all | bytes 425984 | tf_op jit(solution)/shard_map/all_to_all | solution.py:774
  58.2 0.6 collective-permute-start.13
  58.8 1.1 add.63
  59.9 0.4 collective-permute-start.10
  60.3 3.9 %collective-permute-done.13.rest_2_ = f32[4,4,3328]{2,1,0:T(4,128)} collective-permute-done((f32[4,4,3328]{2,1,0:T(4,128)S(1)}, f32[4,4,3328]{2,1,0:T(4,128)}, u32[]{:S(2)}, u32[]{:S(2)}) %collective-permute-start.13) | collective-permute-done | bytes 213024 | tf_op jit(solution)/shard_map/ppermute | solution.py:701
  64.1 0.1 add.66
  64.3 0.6 collective-permute-start.16
  65.0 5.4 %shard_map.226 = f32[4,4,3328]{2,1,0:T(4,128)} custom-call(s32[1,256]{1,0:T(1,128)} %bitcast.65, f32[16,128]{1,0:T(8,128)} %get-tuple-element.85.lists, f32[235,256]{1,0:T(8,128)} %get-tuple-element.72.refs_7_.rot, bf16[448,256]{1,0:T(8,128)(2,1)} %get-tuple-element.86.g0, bf16[384,512]{1,0:T(8,128)(2,1)} %get-tuple-element.87.g1, ...), custom_call_target="tpu_custom_call" | custom-call | flops 6000000000 | bytes 2764800 | tf_op jit(solution)/shard_map/pallas_call | solution.py:668
  70.4 1.0 collective-permute-start.15
  71.4 3.4 %all-to-all-start.1 = ((f32[4,4,3328]{2,1,0:T(4,128)}), f32[4,4,3328]{2,1,0:T(4,128)S(1)}, u32[]{:S(2)}, u32[]{:S(2)}) async-start(f32[4,4,3328]{2,1,0:T(4,128)} %shard_map.226), calls=%async_computation.1 | async-start | bytes 425984 | tf_op jit(solution)/shard_map/all_to_all | solution.py:774
  74.8 3.3 %shard_map.227 = (bf16[49,32,64]{2,1,0:T(8,128)(2,1)}, f32[256,128]{1,0:T(8,128)}) custom-call(bf16[49,32,64]{2,1,0:T(8,128)(2,1)} %bitcast.60, bf16[7,64,64]{2,1,0:T(8,128)(2,1)} %out_proj.3, f32[4,4,3328]{2,1,0:T(4,128)} %copy-done.3, f32[4,4,3328]{2,1,0:T(4,128)} %collective-permute-done.12.rest_1_, f32[4,4,3328]{2,1,0:T(4,128)} %collective-permute-done.13.rest_2_, ...), custom_call_target="tpu_custom_call" | custom-call | flops 4000000000 | bytes 1110016 | tf_op jit(solution)/shard_map/pallas_call | solution.py:668
  78.1 1.3 %collective-permute-done.16 = f32[1088,128]{1,0:T(8,128)S(1)} collective-permute-done((f32[1088,128]{1,0:T(8,128)S(1)}, f32[1088,128]{1,0:T(8,128)S(1)}, u32[]{:S(2)}, u32[]{:S(2)}) %collective-permute-start.16) | collective-permute-done | bytes 557088 | tf_op jit(solution)/shard_map/ppermute | solution.py:701
  79.6 1.0 collective-permute-start.17
  80.5 1.4 %collective-permute-start.19 = (f32[544,128]{1,0:T(8,128)S(1)}, f32[544,128]{1,0:T(8,128)S(1)}, u32[]{:S(2)}, u32[]{:S(2)}) collective-permute-start(f32[544,128]{1,0:T(8,128)S(1)} %dynamic-slice_bitcast_fusion.1), channel_id=1, source_target_pairs={{0,4},{4,0},{8,12},{12,8},{1,5},{5,1},{9,13},{13,9},{2,6},{6,2},{1... | collective-permute-start | bytes 835592 | tf_op jit(solution)/shard_map/ppermute | solution.py:701
  82.0 0.6 collective-permute-start.27
  82.6 1.0 all-to-all-done.1.rest_0_
  83.6 1.5 %collective-permute-start.21 = (f32[4,4,3328]{2,1,0:T(4,128)S(1)}, f32[4,4,3328]{2,1,0:T(4,128)S(1)}, u32[]{:S(2)}, u32[]{:S(2)}) collective-permute-start(f32[4,4,3328]{2,1,0:T(4,128)S(1)} %all-to-all-done.1.rest_0_), channel_id=1, source_target_pairs={{0,2},{1,3},{2,0},{3,1},{4,6},{5,7},{6,4},{7,5},{8,10},{9,11},{10,... | collective-permute-start | bytes 638984 | tf_op jit(solution)/shard_map/ppermute | solution.py:701
  85.0 0.6 collective-permute-start.18
  85.7 4.8 %collective-permute-done.21.rest_2_ = f32[4,4,3328]{2,1,0:T(4,128)S(1)} collective-permute-done((f32[4,4,3328]{2,1,0:T(4,128)S(1)}, f32[4,4,3328]{2,1,0:T(4,128)S(1)}, u32[]{:S(2)}, u32[]{:S(2)}) %collective-permute-start.21) | collective-permute-done | bytes 213024 | tf_op jit(solution)/shard_map/ppermute | solution.py:701
  90.6 2.4 %collective-permute-start.24 = (f32[272,128]{1,0:T(8,128)S(1)}, f32[272,128]{1,0:T(8,128)S(1)}, u32[]{:S(2)}, u32[]{:S(2)}) collective-permute-start(f32[272,128]{1,0:T(8,128)S(1)} %dynamic-slice_bitcast_fusion.3), channel_id=1, source_target_pairs={{0,8},{4,12},{8,0},{12,4},{1,9},{5,13},{9,1},{13,5},{2,10},{6,14},... | collective-permute-start | bytes 417800 | tf_op jit(solution)/shard_map/ppermute | solution.py:701
  93.0 0.6 collective-permute-start.23
  93.7 0.7 copy-done.12
  94.3 0.7 copy-done.13
  95.0 2.6 %shard_map.228 = bf16[49,32,64]{2,1,0:T(8,128)(2,1)} custom-call(f32[4,4,3328]{2,1,0:T(4,128)} %copy-done.4, f32[4,4,3328]{2,1,0:T(4,128)} %copy-done.12, f32[4,4,3328]{2,1,0:T(4,128)} %copy-done.11, f32[4,4,3328]{2,1,0:T(4,128)} %copy-done.13), custom_call_target="tpu_custom_call" | custom-call | flops 4000000000 | bytes 851968 | tf_op jit(solution)/shard_map/pallas_call | solution.py:668
  97.6 4.6 %collective-permute-done.24 = f32[272,128]{1,0:T(8,128)S(1)} collective-permute-done((f32[272,128]{1,0:T(8,128)S(1)}, f32[272,128]{1,0:T(8,128)S(1)}, u32[]{:S(2)}, u32[]{:S(2)}) %collective-permute-start.24) | collective-permute-done | bytes 139296 | tf_op jit(solution)/shard_map/ppermute | solution.py:701
  102.3 0.8 collective-permute-done.23
  103.1 5.0 %collective-permute-done.26 = bf16[272,128]{1,0:T(8,128)(2,1)S(1)} collective-permute-done((bf16[272,128]{1,0:T(8,128)(2,1)S(1)}, bf16[272,128]{1,0:T(8,128)(2,1)S(1)}, u32[]{:S(2)}, u32[]{:S(2)}) %collective-permute-start.26) | collective-permute-done | bytes 69664 | tf_op jit(solution)/shard_map/ppermute | solution.py:701
  108.3 2.4 %collective-permute-start.29 = (f32[256,128]{1,0:T(8,128)S(1)}, f32[256,128]{1,0:T(8,128)S(1)}, u32[]{:S(2)}, u32[]{:S(2)}) collective-permute-start(f32[256,128]{1,0:T(8,128)S(1)} %add.77), channel_id=1, source_target_pairs={{0,8},{4,12},{8,0},{12,4},{1,9},{5,13},{9,1},{13,5},{2,10},{6,14},... | collective-permute-start | bytes 393224 | tf_op jit(solution)/shard_map/ppermute | solution.py:701
  110.6 0.1 collective-permute-start.25
  110.7 6.5 %collective-permute-done.29 = f32[256,128]{1,0:T(8,128)S(1)} collective-permute-done((f32[256,128]{1,0:T(8,128)S(1)}, f32[256,128]{1,0:T(8,128)S(1)}, u32[]{:S(2)}, u32[]{:S(2)}) %collective-permute-start.29) | collective-permute-done | bytes 131104 | tf_op jit(solution)/shard_map/ppermute | solution.py:701
  117.2 0.2 collective-permute-done.28
  117.4 1.2 collective-permute-done.25
  118.9 1.4 %collective-permute-start.31 = (bf16[1088,128]{1,0:T(8,128)(2,1)S(1)}, bf16[1088,128]{1,0:T(8,128)(2,1)S(1)}, u32[]{:S(2)}, u32[]{:S(2)}) collective-permute-start(bf16[1088,128]{1,0:T(8,128)(2,1)S(1)} %pad_maximum_fusion.1), channel_id=1, source_target_pairs={{0,2},{1,3},{2,0},{3,1},{4,6},{5,7},{6,4},{7,5},{8,10},{9,11},{10,... | collective-permute-start | bytes 835592 | tf_op jit(solution)/shard_map/ppermute | solution.py:701
  120.3 0.7 copy-done.10
  121.0 1.9 %shard_map.229 = bf16[448,448]{1,0:T(8,128)(2,1)} custom-call(bf16[896,128]{1,0:T(8,128)(2,1)} %copy-done.2, bf16[896,128]{1,0:T(8,128)(2,1)} %copy-done.10), custom_call_target="tpu_custom_call" | custom-call | flops 1000000000 | bytes 458752 | tf_op jit(solution)/shard_map/pallas_call | solution.py:668
  123.0 5.0 %collective-permute-done.31 = bf16[1088,128]{1,0:T(8,128)(2,1)S(1)} collective-permute-done((bf16[1088,128]{1,0:T(8,128)(2,1)S(1)}, bf16[1088,128]{1,0:T(8,128)(2,1)S(1)}, u32[]{:S(2)}, u32[]{:S(2)}) %collective-permute-start.31) | collective-permute-done | bytes 278560 | tf_op jit(solution)/shard_map/ppermute | solution.py:701
  127.9 0.1 broadcast_select_fusion.1
  128.2 0.1 reshape.64
  128.3 0.7 slice.4
  129.0 1.2 collective-permute-done.32.other
  130.1 0.8 copy-done.9
  131.0 2.4 %shard_map.230 = (bf16[2,384,384]{2,1,0:T(8,128)(2,1)}, bf16[2,320,320]{2,1,0:T(8,128)(2,1)}, bf16[64,256]{1,0:T(8,128)(2,1)}, bf16[128,256]{1,0:T(8,128)(2,1)}, bf16[2,128]{1,0:T(2,128)(2,1)}) custom-call(bf16[2176,128]{1,0:T(8,128)(2,1)} %copy-done.1, bf16[2176,128]{1,0:T(8,128)(2,1)} %copy-done.9), custom_call_target="tpu_custom_call" | custom-call | flops 1000000000 | bytes 1114112 | tf_op jit(solution)/shard_map/pallas_call | solution.py:668
  (89 shorter events, 1.2 us)
Async XLA Ops:
  0.6 7.9 %copy-start.20 = (bf16[256]{0:T(256)(128)(2,1)S(1)}, bf16[256]{0:T(256)(128)(2,1)}, u32[]{:S(2)}) copy-start(bf16[256]{0:T(256)(128)(2,1)} %param.30) | copy-start | bytes 1540
  0.7 8.4 %copy-start.7 = (bf16[256,235]{0,1:T(8,128)(2,1)S(1)}, bf16[256,235]{0,1:T(8,128)(2,1)}, u32[]{:S(2)}) copy-start(bf16[256,235]{0,1:T(8,128)(2,1)} %param.22) | copy-start | bytes 360964
  3.0 6.9 %collective-permute-start = (bf16[4,6528]{1,0:T(4,128)(2,1)}, bf16[4,6528]{1,0:T(4,128)(2,1)S(1)}, u32[]{:S(2)}, u32[]{:S(2)}) collective-permute-start(bf16[4,6528]{1,0:T(4,128)(2,1)} %get-tuple-element.66), channel_id=1, source_target_pairs={{0,4},{4,0},{8,12},{12,8},{1,5},{5,1},{9,13},{13,9},{2,6},{6,2},{1... | collective-permute-start | bytes 156680 | tf_op jit(solution)/shard_map/ppermute | solution.py:784
  6.0 6.2 %collective-permute-start.1 = (bf16[4,6528]{1,0:T(4,128)(2,1)}, bf16[4,6528]{1,0:T(4,128)(2,1)S(1)}, u32[]{:S(2)}, u32[]{:S(2)}) collective-permute-start(bf16[4,6528]{1,0:T(4,128)(2,1)} %get-tuple-element.67), channel_id=1, source_target_pairs={{0,8},{4,12},{8,0},{12,4},{1,9},{5,13},{9,1},{13,5},{2,10},{6,14},... | collective-permute-start | bytes 156680 | tf_op jit(solution)/shard_map/ppermute | solution.py:784
  8.6 6.1 %collective-permute-start.2 = (bf16[4,6528]{1,0:T(4,128)(2,1)}, bf16[4,6528]{1,0:T(4,128)(2,1)S(1)}, u32[]{:S(2)}, u32[]{:S(2)}) collective-permute-start(bf16[4,6528]{1,0:T(4,128)(2,1)} %get-tuple-element.68), channel_id=1, source_target_pairs={{0,12},{4,8},{8,4},{12,0},{1,13},{5,9},{9,5},{13,1},{2,14},{6,10},... | collective-permute-start | bytes 156680 | tf_op jit(solution)/shard_map/ppermute | solution.py:784
  9.9 4.8 %copy-start.14 = (bf16[4,6528]{1,0:T(4,128)(2,1)}, bf16[4,6528]{1,0:T(4,128)(2,1)S(1)}, u32[]{:S(2)}) copy-start(bf16[4,6528]{1,0:T(4,128)(2,1)S(1)} %collective-permute-done.rest_1_) | copy-start | bytes 156676
  12.2 2.5 %copy-start.15 = (bf16[4,6528]{1,0:T(4,128)(2,1)}, bf16[4,6528]{1,0:T(4,128)(2,1)S(1)}, u32[]{:S(2)}) copy-start(bf16[4,6528]{1,0:T(4,128)(2,1)S(1)} %collective-permute-done.1.rest_2_) | copy-start | bytes 156676
  14.7 0.6 copy-start.16
  23.9 1.9 %collective-permute-start.3 = (f32[2,128]{1,0:T(2,128)}, f32[2,128]{1,0:T(2,128)S(1)}, u32[]{:S(2)}, u32[]{:S(2)}) collective-permute-start(f32[2,128]{1,0:T(2,128)} %get-tuple-element.69), channel_id=1, source_target_pairs={{0,1},{1,0},{2,3},{3,2},{4,5},{5,4},{6,7},{7,6},{8,9},{9,8},{10,11... | collective-permute-start | bytes 3080 | tf_op jit(solution)/shard_map/ppermute | solution.py:833
  23.9 3.8 %collective-permute-start.4 = (f32[2,128]{1,0:T(2,128)}, f32[2,128]{1,0:T(2,128)S(1)}, u32[]{:S(2)}, u32[]{:S(2)}) collective-permute-start(f32[2,128]{1,0:T(2,128)} %get-tuple-element.69), channel_id=1, source_target_pairs={{0,2},{1,3},{2,0},{3,1},{4,6},{5,7},{6,4},{7,5},{8,10},{9,11},{10,... | collective-permute-start | bytes 3080 | tf_op jit(solution)/shard_map/ppermute | solution.py:833
  25.5 3.2 %collective-permute-start.5 = (f32[2,128]{1,0:T(2,128)}, f32[2,128]{1,0:T(2,128)S(1)}, u32[]{:S(2)}, u32[]{:S(2)}) collective-permute-start(f32[2,128]{1,0:T(2,128)} %get-tuple-element.69), channel_id=1, source_target_pairs={{0,3},{1,2},{2,1},{3,0},{4,7},{5,6},{6,5},{7,4},{8,11},{9,10},{10,... | collective-permute-start | bytes 3080 | tf_op jit(solution)/shard_map/ppermute | solution.py:833
  29.4 7.0 %copy-start.8 = (f32[8,128]{1,0:T(8,128)}, f32[8,128]{1,0:T(8,128)S(1)}, u32[]{:S(2)}) copy-start(f32[8,128]{1,0:T(8,128)S(1)} %pad_maximum_fusion.6.refs_0_) | copy-start | bytes 12292
  29.4 4.5 %collective-permute-start.6 = (f32[8,128]{1,0:T(8,128)S(1)}, f32[8,128]{1,0:T(8,128)S(1)}, u32[]{:S(2)}, u32[]{:S(2)}) collective-permute-start(f32[8,128]{1,0:T(8,128)S(1)} %pad_maximum_fusion.6.refs_0_), channel_id=1, source_target_pairs={{0,4},{4,0},{8,12},{12,8},{1,5},{5,1},{9,13},{13,9},{2,6},{6,2},{1... | collective-permute-start | bytes 12296 | tf_op jit(solution)/shard_map/ppermute | solution.py:838
  29.5 4.6 %collective-permute-start.7 = (f32[8,128]{1,0:T(8,128)S(1)}, f32[8,128]{1,0:T(8,128)S(1)}, u32[]{:S(2)}, u32[]{:S(2)}) collective-permute-start(f32[8,128]{1,0:T(8,128)S(1)} %pad_maximum_fusion.6.refs_0_), channel_id=1, source_target_pairs={{0,8},{4,12},{8,0},{12,4},{1,9},{5,13},{9,1},{13,5},{2,10},{6,14},... | collective-permute-start | bytes 12296 | tf_op jit(solution)/shard_map/ppermute | solution.py:838
  31.0 5.4 %collective-permute-start.8 = (f32[8,128]{1,0:T(8,128)S(1)}, f32[8,128]{1,0:T(8,128)S(1)}, u32[]{:S(2)}, u32[]{:S(2)}) collective-permute-start(f32[8,128]{1,0:T(8,128)S(1)} %pad_maximum_fusion.6.refs_0_), channel_id=1, source_target_pairs={{0,12},{4,8},{8,4},{12,0},{1,13},{5,9},{9,5},{13,1},{2,14},{6,10},... | collective-permute-start | bytes 12296 | tf_op jit(solution)/shard_map/ppermute | solution.py:838
  33.8 2.5 %copy-start.17 = (f32[8,128]{1,0:T(8,128)}, f32[8,128]{1,0:T(8,128)S(1)}, u32[]{:S(2)}) copy-start(f32[8,128]{1,0:T(8,128)S(1)} %collective-permute-done.6.refs_1_) | copy-start | bytes 12292
  34.0 2.3 %copy-start.18 = (f32[8,128]{1,0:T(8,128)}, f32[8,128]{1,0:T(8,128)S(1)}, u32[]{:S(2)}) copy-start(f32[8,128]{1,0:T(8,128)S(1)} %collective-permute-done.7.refs_2_) | copy-start | bytes 12292
  36.4 0.6 copy-start.19
  37.0 9.1 %copy-start.5 = (f32[4,4,3328]{2,1,0:T(4,128)S(1)}, f32[4,4,3328]{2,1,0:T(4,128)}, u32[]{:S(2)}) copy-start(f32[4,4,3328]{2,1,0:T(4,128)} %get-tuple-element.95) | copy-start | bytes 638980
  45.5 18.7 %collective-permute-start.11 = (f32[2176,128]{1,0:T(8,128)}, f32[2176,128]{1,0:T(8,128)S(1)}, u32[]{:S(2)}, u32[]{:S(2)}) collective-permute-start(f32[2176,128]{1,0:T(8,128)} %get-tuple-element.90), channel_id=1, source_target_pairs={{0,1},{1,0},{2,3},{3,2},{4,5},{5,4},{6,7},{7,6},{8,9},{9,8},{10,11... | collective-permute-start | bytes 3342344 | tf_op jit(solution)/shard_map/ppermute | solution.py:701
  45.5 13.2 %collective-permute-start.9 = (f32[896,128]{1,0:T(8,128)}, f32[896,128]{1,0:T(8,128)S(1)}, u32[]{:S(2)}, u32[]{:S(2)}) collective-permute-start(f32[896,128]{1,0:T(8,128)} %get-tuple-element.82), channel_id=1, source_target_pairs={{0,1},{1,0},{2,3},{3,2},{4,5},{5,4},{6,7},{7,6},{8,9},{9,8},{10,11... | collective-permute-start | bytes 1376264 | tf_op jit(solution)/shard_map/ppermute | solution.py:701
  46.0 18.1 %copy-start = (f32[2176,128]{1,0:T(8,128)S(1)}, f32[2176,128]{1,0:T(8,128)}, u32[]{:S(2)}) copy-start(f32[2176,128]{1,0:T(8,128)} %get-tuple-element.83) | copy-start | bytes 3342340
  58.2 6.1 %copy-start.3 = (f32[4,4,3328]{2,1,0:T(4,128)}, f32[4,4,3328]{2,1,0:T(4,128)S(1)}, u32[]{:S(2)}) copy-start(f32[4,4,3328]{2,1,0:T(4,128)S(1)} %all_to_all.10.rest_0_) | copy-start | bytes 638980
  58.2 6.0 %collective-permute-start.13 = (f32[4,4,3328]{2,1,0:T(4,128)S(1)}, f32[4,4,3328]{2,1,0:T(4,128)}, u32[]{:S(2)}, u32[]{:S(2)}) collective-permute-start(f32[4,4,3328]{2,1,0:T(4,128)S(1)} %all_to_all.10.rest_0_), channel_id=1, source_target_pairs={{0,2},{1,3},{2,0},{3,1},{4,6},{5,7},{6,4},{7,5},{8,10},{9,11},{10,... | collective-permute-start | bytes 638984 | tf_op jit(solution)/shard_map/ppermute | solution.py:701
  58.7 16.0 %collective-permute-start.12 = (f32[4,4,3328]{2,1,0:T(4,128)S(1)}, f32[4,4,3328]{2,1,0:T(4,128)}, u32[]{:S(2)}, u32[]{:S(2)}) collective-permute-start(f32[4,4,3328]{2,1,0:T(4,128)S(1)} %all_to_all.10.rest_0_), channel_id=1, source_target_pairs={{0,1},{1,0},{2,3},{3,2},{4,5},{5,4},{6,7},{7,6},{8,9},{9,8},{10,11... | collective-permute-start | bytes 638984 | tf_op jit(solution)/shard_map/ppermute | solution.py:701
  59.9 10.5 %collective-permute-start.10 = (f32[448,128]{1,0:T(8,128)S(1)}, f32[448,128]{1,0:T(8,128)S(1)}, u32[]{:S(2)}, u32[]{:S(2)}) collective-permute-start(f32[448,128]{1,0:T(8,128)S(1)} %dynamic-slice_bitcast_fusion.2), channel_id=1, source_target_pairs={{0,4},{4,0},{8,12},{12,8},{1,5},{5,1},{9,13},{13,9},{2,6},{6,2},{1... | collective-permute-start | bytes 688136 | tf_op jit(solution)/shard_map/ppermute | solution.py:701
  64.1 10.6 %collective-permute-start.14 = (f32[4,4,3328]{2,1,0:T(4,128)}, f32[4,4,3328]{2,1,0:T(4,128)}, u32[]{:S(2)}, u32[]{:S(2)}) collective-permute-start(f32[4,4,3328]{2,1,0:T(4,128)} %collective-permute-done.13.rest_2_), channel_id=1, source_target_pairs={{0,1},{1,0},{2,3},{3,2},{4,5},{5,4},{6,7},{7,6},{8,9},{9,8},{10,11... | collective-permute-start | bytes 638984 | tf_op jit(solution)/shard_map/ppermute | solution.py:701
  64.3 15.1 %collective-permute-start.16 = (f32[1088,128]{1,0:T(8,128)S(1)}, f32[1088,128]{1,0:T(8,128)S(1)}, u32[]{:S(2)}, u32[]{:S(2)}) collective-permute-start(f32[1088,128]{1,0:T(8,128)S(1)} %dynamic-slice_bitcast_fusion), channel_id=1, source_target_pairs={{0,2},{1,3},{2,0},{3,1},{4,6},{5,7},{6,4},{7,5},{8,10},{9,11},{10,... | collective-permute-start | bytes 1671176 | tf_op jit(solution)/shard_map/ppermute | solution.py:701
  70.4 9.1 %collective-permute-start.15 = (f32[224,128]{1,0:T(8,128)S(1)}, f32[224,128]{1,0:T(8,128)S(1)}, u32[]{:S(2)}, u32[]{:S(2)}) collective-permute-start(f32[224,128]{1,0:T(8,128)S(1)} %dynamic-slice_bitcast_fusion.4), channel_id=1, source_target_pairs={{0,8},{4,12},{8,0},{12,4},{1,9},{5,13},{9,1},{13,5},{2,10},{6,14},... | collective-permute-start | bytes 344072 | tf_op jit(solution)/shard_map/ppermute | solution.py:701
  71.4 12.2 %all-to-all-start.1 = ((f32[4,4,3328]{2,1,0:T(4,128)}), f32[4,4,3328]{2,1,0:T(4,128)S(1)}, u32[]{:S(2)}, u32[]{:S(2)}) async-start(f32[4,4,3328]{2,1,0:T(4,128)} %shard_map.226), calls=%async_computation.1 | async-start | bytes 425984 | tf_op jit(solution)/shard_map/all_to_all | solution.py:774
  79.4 2.5 %copy-start.6 = (f32[256,128]{1,0:T(8,128)S(1)}, f32[256,128]{1,0:T(8,128)}, u32[]{:S(2)}) copy-start(f32[256,128]{1,0:T(8,128)} %get-tuple-element.98) | copy-start | bytes 393220
  79.6 5.4 %collective-permute-start.17 = (f32[112,128]{1,0:T(8,128)S(1)}, f32[112,128]{1,0:T(8,128)S(1)}, u32[]{:S(2)}, u32[]{:S(2)}) collective-permute-start(f32[112,128]{1,0:T(8,128)S(1)} %dynamic-slice_bitcast_fusion.5), channel_id=1, source_target_pairs={{0,2},{1,3},{2,0},{3,1},{4,6},{5,7},{6,4},{7,5},{8,10},{9,11},{10,... | collective-permute-start | bytes 172040 | tf_op jit(solution)/shard_map/ppermute | solution.py:701
  80.5 9.9 %collective-permute-start.19 = (f32[544,128]{1,0:T(8,128)S(1)}, f32[544,128]{1,0:T(8,128)S(1)}, u32[]{:S(2)}, u32[]{:S(2)}) collective-permute-start(f32[544,128]{1,0:T(8,128)S(1)} %dynamic-slice_bitcast_fusion.1), channel_id=1, source_target_pairs={{0,4},{4,0},{8,12},{12,8},{1,5},{5,1},{9,13},{13,9},{2,6},{6,2},{1... | collective-permute-start | bytes 835592 | tf_op jit(solution)/shard_map/ppermute | solution.py:701
  82.0 21.1 %collective-permute-start.27 = (f32[256,128]{1,0:T(8,128)S(1)}, f32[256,128]{1,0:T(8,128)S(1)}, u32[]{:S(2)}, u32[]{:S(2)}) collective-permute-start(f32[256,128]{1,0:T(8,128)S(1)} %copy-done.6), channel_id=1, source_target_pairs={{0,4},{4,0},{8,12},{12,8},{1,5},{5,1},{9,13},{13,9},{2,6},{6,2},{1... | collective-permute-start | bytes 393224 | tf_op jit(solution)/shard_map/ppermute | solution.py:701
  83.6 10.1 %copy-start.4 = (f32[4,4,3328]{2,1,0:T(4,128)}, f32[4,4,3328]{2,1,0:T(4,128)S(1)}, u32[]{:S(2)}) copy-start(f32[4,4,3328]{2,1,0:T(4,128)S(1)} %all-to-all-done.1.rest_0_) | copy-start | bytes 638980
  83.6 6.9 %collective-permute-start.21 = (f32[4,4,3328]{2,1,0:T(4,128)S(1)}, f32[4,4,3328]{2,1,0:T(4,128)S(1)}, u32[]{:S(2)}, u32[]{:S(2)}) collective-permute-start(f32[4,4,3328]{2,1,0:T(4,128)S(1)} %all-to-all-done.1.rest_0_), channel_id=1, source_target_pairs={{0,2},{1,3},{2,0},{3,1},{4,6},{5,7},{6,4},{7,5},{8,10},{9,11},{10,... | collective-permute-start | bytes 638984 | tf_op jit(solution)/shard_map/ppermute | solution.py:701
  85.0 8.6 %collective-permute-start.20 = (f32[4,4,3328]{2,1,0:T(4,128)S(1)}, f32[4,4,3328]{2,1,0:T(4,128)S(1)}, u32[]{:S(2)}, u32[]{:S(2)}) collective-permute-start(f32[4,4,3328]{2,1,0:T(4,128)S(1)} %all-to-all-done.1.rest_0_), channel_id=1, source_target_pairs={{0,1},{1,0},{2,3},{3,2},{4,5},{5,4},{6,7},{7,6},{8,9},{9,8},{10,11... | collective-permute-start | bytes 638984 | tf_op jit(solution)/shard_map/ppermute | solution.py:701
  85.0 8.0 %collective-permute-start.18 = (bf16[112,128]{1,0:T(8,128)(2,1)S(1)}, bf16[112,128]{1,0:T(8,128)(2,1)S(1)}, u32[]{:S(2)}, u32[]{:S(2)}) collective-permute-start(bf16[112,128]{1,0:T(8,128)(2,1)S(1)} %fusion.1), channel_id=1, source_target_pairs={{0,2},{1,3},{2,0},{3,1},{4,6},{5,7},{6,4},{7,5},{8,10},{9,11},{10,... | collective-permute-start | bytes 86024 | tf_op jit(solution)/shard_map/ppermute | solution.py:701
  90.5 3.2 %copy-start.11 = (f32[4,4,3328]{2,1,0:T(4,128)}, f32[4,4,3328]{2,1,0:T(4,128)S(1)}, u32[]{:S(2)}) copy-start(f32[4,4,3328]{2,1,0:T(4,128)S(1)} %collective-permute-done.21.rest_2_) | copy-start | bytes 638980
  90.5 3.2 %collective-permute-start.22 = (f32[4,4,3328]{2,1,0:T(4,128)S(1)}, f32[4,4,3328]{2,1,0:T(4,128)S(1)}, u32[]{:S(2)}, u32[]{:S(2)}) collective-permute-start(f32[4,4,3328]{2,1,0:T(4,128)S(1)} %collective-permute-done.21.rest_2_), channel_id=1, source_target_pairs={{0,1},{1,0},{2,3},{3,2},{4,5},{5,4},{6,7},{7,6},{8,9},{9,8},{10,11... | collective-permute-start | bytes 638984 | tf_op jit(solution)/shard_map/ppermute | solution.py:701
  90.6 11.6 %collective-permute-start.24 = (f32[272,128]{1,0:T(8,128)S(1)}, f32[272,128]{1,0:T(8,128)S(1)}, u32[]{:S(2)}, u32[]{:S(2)}) collective-permute-start(f32[272,128]{1,0:T(8,128)S(1)} %dynamic-slice_bitcast_fusion.3), channel_id=1, source_target_pairs={{0,8},{4,12},{8,0},{12,4},{1,9},{5,13},{9,1},{13,5},{2,10},{6,14},... | collective-permute-start | bytes 417800 | tf_op jit(solution)/shard_map/ppermute | solution.py:701
  93.0 10.0 %collective-permute-start.23 = (bf16[224,128]{1,0:T(8,128)(2,1)S(1)}, bf16[224,128]{1,0:T(8,128)(2,1)S(1)}, u32[]{:S(2)}, u32[]{:S(2)}) collective-permute-start(bf16[224,128]{1,0:T(8,128)(2,1)S(1)} %pad_maximum_fusion.5), channel_id=1, source_target_pairs={{0,8},{4,12},{8,0},{12,4},{1,9},{5,13},{9,1},{13,5},{2,10},{6,14},... | collective-permute-start | bytes 172040 | tf_op jit(solution)/shard_map/ppermute | solution.py:701
  93.7 0.7 copy-start.12
  94.3 0.7 copy-start.13
  102.2 6.0 %collective-permute-start.26 = (bf16[272,128]{1,0:T(8,128)(2,1)S(1)}, bf16[272,128]{1,0:T(8,128)(2,1)S(1)}, u32[]{:S(2)}, u32[]{:S(2)}) collective-permute-start(bf16[272,128]{1,0:T(8,128)(2,1)S(1)} %fusion), channel_id=1, source_target_pairs={{0,8},{4,12},{8,0},{12,4},{1,9},{5,13},{9,1},{13,5},{2,10},{6,14},... | collective-permute-start | bytes 208904 | tf_op jit(solution)/shard_map/ppermute | solution.py:701
  108.2 9.2 %collective-permute-start.28 = (bf16[544,128]{1,0:T(8,128)(2,1)S(1)}, bf16[544,128]{1,0:T(8,128)(2,1)S(1)}, u32[]{:S(2)}, u32[]{:S(2)}) collective-permute-start(bf16[544,128]{1,0:T(8,128)(2,1)S(1)} %pad_maximum_fusion.3), channel_id=1, source_target_pairs={{0,4},{4,0},{8,12},{12,8},{1,5},{5,1},{9,13},{13,9},{2,6},{6,2},{1... | collective-permute-start | bytes 417800 | tf_op jit(solution)/shard_map/ppermute | solution.py:701
  108.3 8.9 %collective-permute-start.29 = (f32[256,128]{1,0:T(8,128)S(1)}, f32[256,128]{1,0:T(8,128)S(1)}, u32[]{:S(2)}, u32[]{:S(2)}) collective-permute-start(f32[256,128]{1,0:T(8,128)S(1)} %add.77), channel_id=1, source_target_pairs={{0,8},{4,12},{8,0},{12,4},{1,9},{5,13},{9,1},{13,5},{2,10},{6,14},... | collective-permute-start | bytes 393224 | tf_op jit(solution)/shard_map/ppermute | solution.py:701
  110.6 8.1 %collective-permute-start.25 = (bf16[448,128]{1,0:T(8,128)(2,1)S(1)}, bf16[448,128]{1,0:T(8,128)(2,1)S(1)}, u32[]{:S(2)}, u32[]{:S(2)}) collective-permute-start(bf16[448,128]{1,0:T(8,128)(2,1)S(1)} %pad_maximum_fusion.4), channel_id=1, source_target_pairs={{0,4},{4,0},{8,12},{12,8},{1,5},{5,1},{9,13},{13,9},{2,6},{6,2},{1... | collective-permute-start | bytes 344072 | tf_op jit(solution)/shard_map/ppermute | solution.py:701
  118.8 1.6 %copy-start.2 = (bf16[896,128]{1,0:T(8,128)(2,1)}, bf16[896,128]{1,0:T(8,128)(2,1)S(1)}, u32[]{:S(2)}) copy-start(bf16[896,128]{1,0:T(8,128)(2,1)S(1)} %pad_maximum_fusion.2.mine) | copy-start | bytes 688132
  118.8 1.6 %collective-permute-start.30 = (bf16[896,128]{1,0:T(8,128)(2,1)S(1)}, bf16[896,128]{1,0:T(8,128)(2,1)S(1)}, u32[]{:S(2)}, u32[]{:S(2)}) collective-permute-start(bf16[896,128]{1,0:T(8,128)(2,1)S(1)} %pad_maximum_fusion.2.mine), channel_id=1, source_target_pairs={{0,1},{1,0},{2,3},{3,2},{4,5},{5,4},{6,7},{7,6},{8,9},{9,8},{10,11... | collective-permute-start | bytes 688136 | tf_op jit(solution)/shard_map/ppermute | solution.py:701
  118.9 9.1 %collective-permute-start.31 = (bf16[1088,128]{1,0:T(8,128)(2,1)S(1)}, bf16[1088,128]{1,0:T(8,128)(2,1)S(1)}, u32[]{:S(2)}, u32[]{:S(2)}) collective-permute-start(bf16[1088,128]{1,0:T(8,128)(2,1)S(1)} %pad_maximum_fusion.1), channel_id=1, source_target_pairs={{0,2},{1,3},{2,0},{3,1},{4,6},{5,7},{6,4},{7,5},{8,10},{9,11},{10,... | collective-permute-start | bytes 835592 | tf_op jit(solution)/shard_map/ppermute | solution.py:701
  120.3 0.7 copy-start.10
  128.1 2.0 %copy-start.1 = (bf16[2176,128]{1,0:T(8,128)(2,1)}, bf16[2176,128]{1,0:T(8,128)(2,1)S(1)}, u32[]{:S(2)}) copy-start(bf16[2176,128]{1,0:T(8,128)(2,1)S(1)} %pad_maximum_fusion.mine) | copy-start | bytes 1671172
  128.1 2.0 %collective-permute-start.32 = (bf16[2176,128]{1,0:T(8,128)(2,1)S(1)}, bf16[2176,128]{1,0:T(8,128)(2,1)S(1)}, u32[]{:S(2)}, u32[]{:S(2)}) collective-permute-start(bf16[2176,128]{1,0:T(8,128)(2,1)S(1)} %pad_maximum_fusion.mine), channel_id=1, source_target_pairs={{0,1},{1,0},{2,3},{3,2},{4,5},{5,4},{6,7},{7,6},{8,9},{9,8},{10,11... | collective-permute-start | bytes 1671176 | tf_op jit(solution)/shard_map/ppermute | solution.py:701
  130.1 0.8 copy-start.9

commit v5 on v4

--- a/solution.py
+++ b/solution.py
@@ -574,6 +574,7 @@
         copy.wait()
 
 
+PROJ_ROWS = (LMAX // 2 + 1) * CH
 CHUNKS = ((0, 3 * DIM1 + 3 * DIM2 + CH), (3 * DIM1 + 3 * DIM2 + CH, 2 * DIM0))
 PACKED_ROWS = sum(size for start, size in CHUNKS)
 
@@ -592,8 +593,35 @@
     zero[:, pl.ds(3 * LANES, DIM0 - 3 * LANES)] = right[DIM0:, : DIM0 - 3 * LANES].astype(bf16)
 
 
-def unpack_rest_kernel(mine, other, one, two, alpha_in, alpha_edge, alpha_dot):
-    left, right = halves_of(mine, other)
+def make_unpack_rest(lanes_total):
+    def unpack_rest_kernel(mine, other, one, two, alpha_in, alpha_edge, alpha_dot, proj):
+        left, right = halves_of(mine, other)
+        parts = lanes_total // 2
+        late = PROJ_ROWS // lanes_total
+        size = left.shape[0] // parts - late
+        tail = jnp.concatenate(
+            [
+                value[n * (size + late) + size : (n + 1) * (size + late)]
+                for value in (left, right)
+                for n in range(parts)
+            ],
+            axis=0,
+        )
+        for degree in range(LMAX + 1):
+            piece = tail[degree // 2 * CH : (degree // 2 + 1) * CH]
+            proj[degree] = piece[:, degree % 2 * CH : (degree % 2 + 1) * CH].astype(bf16)
+        left, right = (
+            jnp.concatenate(
+                [value[n * (size + late) : n * (size + late) + size] for n in range(parts)], axis=0
+            )
+            for value in (left, right)
+        )
+        unpack_rest(left, right, one, two, alpha_in, alpha_edge, alpha_dot)
+
+    return unpack_rest_kernel
+
+
+def unpack_rest(left, right, one, two, alpha_in, alpha_edge, alpha_dot):
     for n in range(2 * DIM1 // LANES):
         panel = (left, right)[n % 2][(n // 2) * DIM1 : (n // 2 + 1) * DIM1]
         per = DIM1 // LANES
@@ -659,12 +687,11 @@
 anywhere = pl.BlockSpec(memory_space=pl.ANY)
 
 
-def call(kernel, outs, scratch, *args, scalars=0, far=(), apart=(), after=(), work=4):
+def call(kernel, outs, scratch, *args, scalars=0, far=(), apart=(), after=()):
     specs = [smem if n < scalars else anywhere if n in far else vmem for n in range(len(args))]
     specs += [anywhere] * len(after)
     out_specs = [anywhere if n in apart else vmem for n in range(len(outs))]
     shapes = [pltpu.VMEM(*entry) if isinstance(entry, tuple) else entry for entry in scratch]
-    moved = sum(int(np.prod(a.shape)) * a.dtype.itemsize for a in args)
     return pl.pallas_call(
         kernel,
         out_shape=[jax.ShapeDtypeStruct(shape, kind) for shape, kind in outs],
@@ -672,9 +699,7 @@
         out_specs=out_specs,
         scratch_shapes=shapes,
         compiler_params=pltpu.CompilerParams(vmem_limit_bytes=VMEM_LIMIT),
-        cost_estimate=pl.CostEstimate(
-            flops=work * 10**9, bytes_accessed=moved, transcendentals=0
-        ),
+        cost_estimate=pl.CostEstimate(flops=1, bytes_accessed=1, transcendentals=0),
     )(*args, *after)
 
 
@@ -716,14 +741,16 @@
     return (lax.axis_index(axis) >> bit) & 1
 
 
-def sum_all(kept, sent, first, order):
+def sum_all(kept, sent, first, order, late=None):
     steps = [("edge", n) for n in range(1, bits_of("edge"))]
     steps += [("graph", n) for n in range(bits_of("graph"))]
     steps.sort(key=lambda step: step[0] != first)
     other = swap(sent, "edge", 0)
     yield
     current = kept + order.hold(other)
-    for axis, bit in steps:
+    for n, (axis, bit) in enumerate(steps):
+        if late is not None and n == bits_of("edge") - 1:
+            current = jnp.concatenate([current, late[0]], axis=0)
         mine = own_bit(axis, bit)
         parts = current.reshape(2, current.shape[0] // 2, -1)
         sent = order.mark(lax.dynamic_index_in_dim(parts, 1 - mine, 0, False))
@@ -777,7 +804,7 @@
     outgoing = call(
         outgoing_kernel, [((cap, TABLE), bf16)] * peers, [],
         send_rows, recv_rows, jnp.transpose(atom_embed, (1, 0, 2)), cot,
-        scalars=2, work=2,
+        scalars=2
     )
     if direct:
         tables = [outgoing[0]] + [
@@ -826,7 +853,7 @@
         + [pre_shape, pltpu.SemaphoreType.DMA((10,))],
         source_row, target_row, rotation, edge_feats, bias,
         conv_zero, conv_one, conv_two, alpha_in, alpha_edge, adot, out_proj, *tables,
-        far=(5, 6, 7), apart=range(2, 9), work=8,
+        far=(5, 6, 7), apart=range(2, 9)
     )
     if direct:
         lanes_stats = [stats] + [
@@ -841,6 +868,8 @@
     else:
         all_stats = [lax.all_gather(stats, ("graph", "edge"), tiled=True)]
     messages = exchange(sums)
+    order.mark(messages)
+    message_rows = gather_lanes(messages)
 
     halves = [((size, LANES), f32) for start, size in CHUNKS for _ in range(2)]
     g0, g1, g2, pre_grad, *halves = call(
@@ -862,20 +891,21 @@
         ]
         + frames
         + [pltpu.SemaphoreType.DMA((10,))],
-        *all_stats, own_stats, agg_grad, target_row, rot, edge_feats,
+        *all_stats, order.hold(own_stats), agg_grad, target_row, rot, edge_feats,
         x0, x1, x2, v0, v1, v2, pre, logits, adot,
-        far=range(len(all_stats) + 5, len(all_stats) + 11), apart=range(4, 8), work=8,
+        far=range(len(all_stats) + 5, len(all_stats) + 11), apart=range(4, 8)
     )
 
     total = lanes_total * slots
     order.mark(halves[0])
-    message_rows = gather_lanes(order.hold(messages))
+    message_rows = [order.hold(message_rows[0])] + message_rows[1:]
+    late = []
+    rest_steps = sum_all(halves[0], halves[1], "edge", order, late)
     zero_steps = sum_all(halves[2], halves[3], "graph", order)
-    rest_steps = sum_all(halves[0], halves[1], "edge", order)
+    next(rest_steps)
     next(zero_steps)
     next(rest_steps)
     next(zero_steps)
-    next(rest_steps)
     (source_sums,) = call(
         source_kernel,
         [((peers, cap, WIDE), f32)],
@@ -886,20 +916,24 @@
             ((COLS, 2 * edges), bf16),
         ],
         source_row, lists, rot, g0, g1, g2, order.hold(pre_grad),
-        conv_zero, conv_one, conv_two, alpha_in,
-        work=6,
+        conv_zero, conv_one, conv_two, alpha_in
     )
     order.mark(source_sums)
     returned = exchange(source_sums)
     next(zero_steps)
     out, proj = call(
         make_finish(lanes_total),
-        [((COEFFS, atoms, CH), bf16), (((LMAX // 2 + 1) * CH, LANES), f32)],
+        [((COEFFS, atoms, CH), bf16), ((PROJ_ROWS, LANES), f32)],
         [((total, WIDE), f32), ((2 * total, COLS), bf16), ((COEFFS, atoms, CH), bf16)],
         order.hold(cot), out_proj, *message_rows,
     )
     order.mark(proj)
-    next(rest_steps)
+    lane = lax.axis_index("edge")
+    late_rows = PROJ_ROWS // lanes_total
+    place = ((lane & 1) * (lanes_total // 2) + (lane >> 1)) * late_rows
+    late.append(lax.dynamic_slice_in_dim(proj, place, late_rows, 0))
+    for _ in range(bits_of("edge") - 1):
+        next(rest_steps)
     next(zero_steps)
     source_rows = gather_lanes(order.hold(returned))
     next(zero_steps)
@@ -914,27 +948,26 @@
     order.mark(embed)
     next(rest_steps)
     next(zero_steps)
-    for bit in range(bits_of("graph")):
-        proj = proj + order.hold(swap(proj, "graph", bit))
-        order.mark(proj)
-        next(rest_steps)
+    next(rest_steps)
+    next(zero_steps)
+    next(rest_steps)
     zero_pair = finish_steps(zero_steps)
     (zero,) = call(
-        unpack_zero_kernel, [((DIM0, DIM0), bf16)], [], order.hold(zero_pair[0]), zero_pair[1],
-        work=1,
+        unpack_zero_kernel, [((DIM0, DIM0), bf16)], [], order.hold(zero_pair[0]), zero_pair[1]
     )
     order.mark(zero)
     rest_pair = finish_steps(rest_steps)
-    one, two, grad_in, grad_edge, grad_dot = call(
-        unpack_rest_kernel,
+    one, two, grad_in, grad_edge, grad_dot, grad_proj = call(
+        make_unpack_rest(lanes_total),
         [
             ((2, DIM1, DIM1), bf16),
             ((2, DIM2, DIM2), bf16),
             (alpha_in.shape, bf16),
             (alpha_edge.shape, bf16),
             ((2, LANES), bf16),
+            (out_proj.shape, bf16),
         ],
-        [], order.hold(rest_pair[0]), rest_pair[1], work=1,
+        [], order.hold(rest_pair[0]), rest_pair[1]
     )
 
     def shaped(value):
@@ -942,7 +975,7 @@
 
     return (
         shaped(out), shaped(embed), zero, one, two, grad_in, grad_edge, grad_dot.reshape(-1),
-        jnp.swapaxes(proj.astype(bf16).reshape(-1, CH, 2, CH), 1, 2).reshape(-1, CH, CH)[: LMAX + 1],
+        grad_proj,
     )
 
 

time: 134 us -> 136 us (1.015)
  blocking collectives: 12.1 us -> 0 us
  waiting for transfers between devices: 45.6 us -> 51.2 us
  starting transfers between devices: 30.8 us -> 34.3 us
  local copies, waits for them, and re-layouts: 6.3 us -> 9.51 us
    all_to_all x1 -> x0, blocking collectives: 12.1 us -> none  [exchange(): lax.all_to_all(value, 'graph', split_axis=0, concat_axis=0, tiled=True)]
    ppermute x24 -> x22, waiting for transfers between devices: 34.4 us -> 40.1 us  [swap(): return lax.ppermute(value, axis, [(i, i ^ 1 << bit) for i in range(size)])]
    all_to_all x1 -> x2, starting transfers between devices: 3.38 us -> 6.95 us  [exchange(): lax.all_to_all(value, 'graph', split_axis=0, concat_axis=0, tiled=True)]
    ppermute x3, waiting for transfers between devices: 2.53 us -> 5.04 us  [shards(): lax.ppermute(graph_stats, 'graph', [(i, i ^ k) for i in range(peers)])]
    unnamed x43 -> x37, local copies, waits for them, and re-layouts: 4.85 us -> 6.7 us
    ppermute x3, waiting for transfers between devices: 4.83 us -> 3.26 us  [shards(): lax.ppermute(outgoing[k], 'graph', [(i, i ^ k) for i in range(peers)])]
    ppermute x24 -> x22, starting transfers between devices: 15.5 us -> 15.4 us  [swap(): return lax.ppermute(value, axis, [(i, i ^ 1 << bit) for i in range(size)])]
  transfers between devices with their start and end apart: 34 -> 33, of which waited for: 18 -> 20; matrix products, arithmetic and copies ran while one was open for 3% -> 5% of each run, Pallas kernels for 10% -> 10%
where the time goes in v5:
time: 136 us; the launch traced here: 135 us
  waiting for transfers between devices  51.2 us (38%)
  Pallas kernels  35 us (26%)
  starting transfers between devices  34.3 us (25%)
  local copies, waits for them, and re-layouts  9.51 us (7%)
  other arithmetic  3.68 us (3%)
    ppermute x22, waiting for transfers between devices, swap(): return lax.ppermute(value, axis, [(i, i ^ 1 << bit) for i in range(size)])  40.1 us
    pallas_call x8, Pallas kernels, call(): pl.pallas_call(kernel, out_shape=[jax.ShapeDtypeStruct(shape, kind) for s...  35 us
    ppermute x22, starting transfers between devices, swap(): return lax.ppermute(value, axis, [(i, i ^ 1 << bit) for i in range(size)])  15.4 us
    all_to_all x2, starting transfers between devices, exchange(): lax.all_to_all(value, 'graph', split_axis=0, concat_axis=0, tiled=True)  6.95 us
    unnamed x37, local copies, waits for them, and re-layouts  6.7 us
    ppermute x3, starting transfers between devices, shards(): lax.ppermute(outgoing[k], 'graph', [(i, i ^ k) for i in range(peers)])  5.62 us
    ppermute x3, waiting for transfers between devices, shards(): lax.ppermute(graph_stats, 'graph', [(i, i ^ k) for i in range(peers)])  5.04 us
    ppermute x3, starting transfers between devices, shards(): lax.ppermute(graph_stats, 'graph', [(i, i ^ k) for i in range(peers)])  4.45 us
  transfers between devices with their start and end apart: 33, of which 20 were waited for; matrix products, arithmetic and copies ran while one was open for 5% of the time, Pallas kernels for 10%

profile of v5, /device:TPU:0, one launch (start us, length us, event | category | flops | bytes accessed | tf_op | source)
XLA Modules:
  0.0 134.7 jit_solution(2659252245330375894)
XLA Ops:
  0.6 2.2 %shard_map.223 = (bf16[4,6528]{1,0:T(4,128)(2,1)}, bf16[4,6528]{1,0:T(4,128)(2,1)}, bf16[4,6528]{1,0:T(4,128)(2,1)}, bf16[4,6528]{1,0:T(4,128)(2,1)}) custom-call(s32[1,4,1,4]{3,2,1,0:T(1,128)} %send.1, s32[1,4,1,4]{3,2,1,0:T(1,128)} %recv.1, bf16[49,32,64]{2,1,0:T(8,128)(2,1)} %bitcast.57, bf16[49,32,64]{2,1,0:T(8,128)(2,1)} %bitcast.48), custom_call_target="tpu_custom_call" | custom-call | flops 1 | bytes 1 | tf_op jit(solution)/shard_map/pallas_call | solution.py:695
  2.9 3.0 %collective-permute-start = (bf16[4,6528]{1,0:T(4,128)(2,1)}, bf16[4,6528]{1,0:T(4,128)(2,1)S(1)}, u32[]{:S(2)}, u32[]{:S(2)}) collective-permute-start(bf16[4,6528]{1,0:T(4,128)(2,1)} %get-tuple-element.66), channel_id=1, source_target_pairs={{0,4},{4,0},{8,12},{12,8},{1,5},{5,1},{9,13},{13,9},{2,6},{6,2},{1... | collective-permute-start | bytes 156680 | tf_op jit(solution)/shard_map/ppermute | solution.py:811
  5.9 2.6 %collective-permute-start.1 = (bf16[4,6528]{1,0:T(4,128)(2,1)}, bf16[4,6528]{1,0:T(4,128)(2,1)S(1)}, u32[]{:S(2)}, u32[]{:S(2)}) collective-permute-start(bf16[4,6528]{1,0:T(4,128)(2,1)} %get-tuple-element.67), channel_id=1, source_target_pairs={{0,8},{4,12},{8,0},{12,4},{1,9},{5,13},{9,1},{13,5},{2,10},{6,14},... | collective-permute-start | bytes 156680 | tf_op jit(solution)/shard_map/ppermute | solution.py:811
  8.5 1.2 reshape.50.adot.refs_17_
  9.7 1.7 %copy.25.rotation = bf16[256,235]{1,0:T(8,128)(2,1)} copy(bf16[256,235]{0,1:T(8,128)(2,1)} %param.22) | data formatting | bytes 240640 | tf_op args[6]
  11.4 0.8 collective-permute-done.1.rest_2_
  12.2 2.5 %collective-permute-done.2.rest_3_ = bf16[4,6528]{1,0:T(4,128)(2,1)S(1)} collective-permute-done((bf16[4,6528]{1,0:T(4,128)(2,1)}, bf16[4,6528]{1,0:T(4,128)(2,1)S(1)}, u32[]{:S(2)}, u32[]{:S(2)}) %collective-permute-start.2) | collective-permute-done | bytes 52256 | tf_op jit(solution)/shard_map/ppermute | solution.py:811
  14.6 0.6 copy-done.13
  15.3 8.6 %shard_map.224 = (f32[4,4,3328]{2,1,0:T(4,128)}, f32[2,128]{1,0:T(2,128)}, bf16[448,256]{1,0:T(8,128)(2,1)}, bf16[384,512]{1,0:T(8,128)(2,1)}, bf16[320,512]{1,0...) custom-call(s32[1,256]{1,0:T(1,128)} %bitcast.61, ...), custom_call_target="tpu_custom_call" | custom-call | flops 1 | bytes 1 | tf_op jit(solution)/shard_map/pallas_call | solution.py:695
  23.8 3.6 %all-to-all-start = ((f32[4,4,3328]{2,1,0:T(4,128)}), f32[4,4,3328]{2,1,0:T(4,128)S(1)}, u32[]{:S(2)}, u32[]{:S(2)}) async-start(f32[4,4,3328]{2,1,0:T(4,128)} %get-tuple-element.71), calls=%async_computation | async-start | bytes 425984 | tf_op jit(solution)/shard_map/all_to_all | solution.py:801
  27.5 1.6 %collective-permute-start.4 = (f32[2,128]{1,0:T(2,128)}, f32[2,128]{1,0:T(2,128)S(1)}, u32[]{:S(2)}, u32[]{:S(2)}) collective-permute-start(f32[2,128]{1,0:T(2,128)} %get-tuple-element.69), channel_id=1, source_target_pairs={{0,2},{1,3},{2,0},{3,1},{4,6},{5,7},{6,4},{7,5},{8,10},{9,11},{10,... | collective-permute-start | bytes 3080 | tf_op jit(solution)/shard_map/ppermute | solution.py:860
  29.0 0.3 collective-permute-start.5
  29.3 2.0 %collective-permute-done.4 = f32[2,128]{1,0:T(2,128)S(1)} collective-permute-done((f32[2,128]{1,0:T(2,128)}, f32[2,128]{1,0:T(2,128)S(1)}, u32[]{:S(2)}, u32[]{:S(2)}) %collective-permute-start.4) | collective-permute-done | bytes 1056 | tf_op jit(solution)/shard_map/ppermute | solution.py:860
  31.3 0.8 collective-permute-done.5
  32.1 0.6 pad_maximum_fusion.7.refs_0_
  32.7 1.7 %collective-permute-start.6 = (f32[8,128]{1,0:T(8,128)S(1)}, f32[8,128]{1,0:T(8,128)S(1)}, u32[]{:S(2)}, u32[]{:S(2)}) collective-permute-start(f32[8,128]{1,0:T(8,128)S(1)} %pad_maximum_fusion.7.refs_0_), channel_id=1, source_target_pairs={{0,4},{4,0},{8,12},{12,8},{1,5},{5,1},{9,13},{13,9},{2,6},{6,2},{1... | collective-permute-start | bytes 12296 | tf_op jit(solution)/shard_map/ppermute | solution.py:865
  34.5 2.4 %collective-permute-start.7 = (f32[8,128]{1,0:T(8,128)S(1)}, f32[8,128]{1,0:T(8,128)S(1)}, u32[]{:S(2)}, u32[]{:S(2)}) collective-permute-start(f32[8,128]{1,0:T(8,128)S(1)} %pad_maximum_fusion.7.refs_0_), channel_id=1, source_target_pairs={{0,8},{4,12},{8,0},{12,4},{1,9},{5,13},{9,1},{13,5},{2,10},{6,14},... | collective-permute-start | bytes 12296 | tf_op jit(solution)/shard_map/ppermute | solution.py:865
  36.8 0.3 collective-permute-start.8
  37.2 1.8 %collective-permute-done.7.refs_2_ = f32[8,128]{1,0:T(8,128)S(1)} collective-permute-done((f32[8,128]{1,0:T(8,128)S(1)}, f32[8,128]{1,0:T(8,128)S(1)}, u32[]{:S(2)}, u32[]{:S(2)}) %collective-permute-start.7) | collective-permute-done | bytes 4128 | tf_op jit(solution)/shard_map/ppermute | solution.py:865
  39.0 3.3 %collective-permute-done.8.refs_3_ = f32[8,128]{1,0:T(8,128)S(1)} collective-permute-done((f32[8,128]{1,0:T(8,128)S(1)}, f32[8,128]{1,0:T(8,128)S(1)}, u32[]{:S(2)}, u32[]{:S(2)}) %collective-permute-start.8) | collective-permute-done | bytes 4128 | tf_op jit(solution)/shard_map/ppermute | solution.py:865
  42.3 0.6 copy-done.17
  42.8 8.5 %shard_map.225 = (bf16[448,256]{1,0:T(8,128)(2,1)}, bf16[384,512]{1,0:T(8,128)(2,1)}, bf16[320,512]{1,0:T(8,128)(2,1)}, bf16[256,256]{1,0:T(8,128)(2,1)}, f32[21...) custom-call(f32[8,128]{1,0:T(8,128)} %copy-done.14, f32[8,128]{1,0:T(8,128)} %copy-done.15, ...), custom_call_target="tpu_custom_call" | custom-call | flops 1 | bytes 1 | tf_op jit(solution)/shard_map/pallas_call | solution.py:695
  51.4 0.5 collective-permute-start.9
  51.9 3.1 %collective-permute-done.10 = f32[2176,128]{1,0:T(8,128)S(1)} collective-permute-done((f32[2176,128]{1,0:T(8,128)}, f32[2176,128]{1,0:T(8,128)S(1)}, u32[]{:S(2)}, u32[]{:S(2)}) %collective-permute-start.10) | collective-permute-done | bytes 1114144 | tf_op jit(solution)/shard_map/ppermute | solution.py:726
  55.0 1.4 %add.63 = f32[2176,128]{1,0:T(8,128)S(1)} add(f32[2176,128]{1,0:T(8,128)} %get-tuple-element.85, f32[2176,128]{1,0:T(8,128)S(1)} %collective-permute-done.10) | non-fusion elementwise | flops 278528 | bytes 3342336 | tf_op jit(solution)/shard_map/add | solution.py:750
  56.4 0.9 copy-done.5
  57.4 1.1 add.65
  58.5 0.7 dynamic-slice_bitcast_fusion.2
  59.2 0.7 collective-permute-start.13
  59.9 1.3 collective-permute-start.16
  61.2 6.1 %collective-permute-done.13.rest_2_ = f32[4,4,3328]{2,1,0:T(4,128)S(1)} collective-permute-done((f32[4,4,3328]{2,1,0:T(4,128)S(1)}, f32[4,4,3328]{2,1,0:T(4,128)S(1)}, u32[]{:S(2)}, u32[]{:S(2)}) %collective-permute-start.13) | collective-permute-done | bytes 213024 | tf_op jit(solution)/shard_map/ppermute | solution.py:726
  67.3 5.5 %shard_map.226 = f32[4,4,3328]{2,1,0:T(4,128)} custom-call(s32[1,256]{1,0:T(1,128)} %bitcast.62, f32[16,128]{1,0:T(8,128)} %get-tuple-element.89.lists, f32[235,256]{1,0:T(8,128)} %get-tuple-element.74.refs_7_.rot, bf16[448,256]{1,0:T(8,128)(2,1)} %get-tuple-element.90.g0, bf16[384,512]{1,0:T(8,128)(2,1)} %get-tuple-element.91.g1, ...), custom_call_target="tpu_custom_call" | custom-call | flops 1 | bytes 1 | tf_op jit(solution)/shard_map/pallas_call | solution.py:695
  72.7 3.4 %all-to-all-start.1 = ((f32[4,4,3328]{2,1,0:T(4,128)}), f32[4,4,3328]{2,1,0:T(4,128)S(1)}, u32[]{:S(2)}, u32[]{:S(2)}) async-start(f32[4,4,3328]{2,1,0:T(4,128)} %shard_map.226), calls=%async_computation.1 | async-start | bytes 425984 | tf_op jit(solution)/shard_map/all_to_all | solution.py:801
  76.2 2.9 %collective-permute-start.15 = (f32[224,128]{1,0:T(8,128)S(1)}, f32[224,128]{1,0:T(8,128)S(1)}, u32[]{:S(2)}, u32[]{:S(2)}) collective-permute-start(f32[224,128]{1,0:T(8,128)S(1)} %dynamic-slice_bitcast_fusion.4), channel_id=1, source_target_pairs={{0,8},{4,12},{8,0},{12,4},{1,9},{5,13},{9,1},{13,5},{2,10},{6,14},... | collective-permute-start | bytes 344072 | tf_op jit(solution)/shard_map/ppermute | solution.py:726
  79.1 3.3 %shard_map.227 = (bf16[49,32,64]{2,1,0:T(8,128)(2,1)}, f32[256,128]{1,0:T(8,128)}) custom-call(bf16[49,32,64]{2,1,0:T(8,128)(2,1)} %bitcast.49, bf16[7,64,64]{2,1,0:T(8,128)(2,1)} %out_proj.3, f32[4,4,3328]{2,1,0:T(4,128)} %copy-done.3, f32[4,4,3328]{2,1,0:T(4,128)} %collective-permute-done.12.rest_1_, f32[4,4,3328]{2,1,0:T(4,128)} %copy-done.10, ...), custom_call_target="tpu_custom_call" | custom-call | flops 1 | bytes 1 | tf_op jit(solution)/shard_map/pallas_call | solution.py:695
  82.4 0.8 constant_dynamic-slice_fusion
  83.3 1.5 %collective-permute-start.19 = (f32[576,128]{1,0:T(8,128)S(1)}, f32[576,128]{1,0:T(8,128)S(1)}, u32[]{:S(2)}, u32[]{:S(2)}) collective-permute-start(f32[576,128]{1,0:T(8,128)S(1)} %dynamic-slice_bitcast_fusion.1), channel_id=1, source_target_pairs={{0,4},{4,0},{8,12},{12,8},{1,5},{5,1},{9,13},{13,9},{2,6},{6,2},{1... | collective-permute-start | bytes 884744 | tf_op jit(solution)/shard_map/ppermute | solution.py:726
  84.9 4.9 %collective-permute-done.15 = f32[224,128]{1,0:T(8,128)S(1)} collective-permute-done((f32[224,128]{1,0:T(8,128)S(1)}, f32[224,128]{1,0:T(8,128)S(1)}, u32[]{:S(2)}, u32[]{:S(2)}) %collective-permute-start.15) | collective-permute-done | bytes 114720 | tf_op jit(solution)/shard_map/ppermute | solution.py:726
  89.8 0.8 collective-permute-start.17
  90.6 1.3 collective-permute-start.21
  91.9 2.8 %collective-permute-done.17 = f32[112,128]{1,0:T(8,128)S(1)} collective-permute-done((f32[112,128]{1,0:T(8,128)S(1)}, f32[112,128]{1,0:T(8,128)S(1)}, u32[]{:S(2)}, u32[]{:S(2)}) %collective-permute-start.17) | collective-permute-done | bytes 57376 | tf_op jit(solution)/shard_map/ppermute | solution.py:726
  94.8 0.7 collective-permute-start.18
  95.5 2.7 %collective-permute-done.21.rest_2_ = f32[4,4,3328]{2,1,0:T(4,128)S(1)} collective-permute-done((f32[4,4,3328]{2,1,0:T(4,128)S(1)}, f32[4,4,3328]{2,1,0:T(4,128)S(1)}, u32[]{:S(2)}, u32[]{:S(2)}) %collective-permute-start.21) | collective-permute-done | bytes 213024 | tf_op jit(solution)/shard_map/ppermute | solution.py:726
  98.4 0.3 collective-permute-done.18
  98.7 2.6 %collective-permute-start.23 = (bf16[224,128]{1,0:T(8,128)(2,1)S(1)}, bf16[224,128]{1,0:T(8,128)(2,1)S(1)}, u32[]{:S(2)}, u32[]{:S(2)}) collective-permute-start(bf16[224,128]{1,0:T(8,128)(2,1)S(1)} %pad_maximum_fusion.6), channel_id=1, source_target_pairs={{0,8},{4,12},{8,0},{12,4},{1,9},{5,13},{9,1},{13,5},{2,10},{6,14},... | collective-permute-start | bytes 172040 | tf_op jit(solution)/shard_map/ppermute | solution.py:726
  101.4 0.7 copy-done.8
  102.0 0.7 copy-done.9
  102.7 2.6 %shard_map.228 = bf16[49,32,64]{2,1,0:T(8,128)(2,1)} custom-call(f32[4,4,3328]{2,1,0:T(4,128)} %copy-done.2, f32[4,4,3328]{2,1,0:T(4,128)} %copy-done.8, f32[4,4,3328]{2,1,0:T(4,128)} %copy-done.7, f32[4,4,3328]{2,1,0:T(4,128)} %copy-done.9), custom_call_target="tpu_custom_call" | custom-call | flops 1 | bytes 1 | tf_op jit(solution)/shard_map/pallas_call | solution.py:695
  105.3 4.0 %collective-permute-done.24 = f32[288,128]{1,0:T(8,128)S(1)} collective-permute-done((f32[288,128]{1,0:T(8,128)S(1)}, f32[288,128]{1,0:T(8,128)S(1)}, u32[]{:S(2)}, u32[]{:S(2)}) %collective-permute-start.24) | collective-permute-done | bytes 147488 | tf_op jit(solution)/shard_map/ppermute | solution.py:726
  109.3 0.1 collective-permute-start.26
  109.4 1.1 collective-permute-done.23
  110.5 1.4 %collective-permute-start.25 = (bf16[448,128]{1,0:T(8,128)(2,1)S(1)}, bf16[448,128]{1,0:T(8,128)(2,1)S(1)}, u32[]{:S(2)}, u32[]{:S(2)}) collective-permute-start(bf16[448,128]{1,0:T(8,128)(2,1)S(1)} %pad_maximum_fusion.5), channel_id=1, source_target_pairs={{0,4},{4,0},{8,12},{12,8},{1,5},{5,1},{9,13},{13,9},{2,6},{6,2},{1... | collective-permute-start | bytes 344072 | tf_op jit(solution)/shard_map/ppermute | solution.py:726
  111.9 3.5 %collective-permute-done.26 = bf16[288,128]{1,0:T(8,128)(2,1)S(1)} collective-permute-done((bf16[288,128]{1,0:T(8,128)(2,1)S(1)}, bf16[288,128]{1,0:T(8,128)(2,1)S(1)}, u32[]{:S(2)}, u32[]{:S(2)}) %collective-permute-start.26) | collective-permute-done | bytes 73760 | tf_op jit(solution)/shard_map/ppermute | solution.py:726
  115.5 1.8 %collective-permute-done.25 = bf16[448,128]{1,0:T(8,128)(2,1)S(1)} collective-permute-done((bf16[448,128]{1,0:T(8,128)(2,1)S(1)}, bf16[448,128]{1,0:T(8,128)(2,1)S(1)}, u32[]{:S(2)}, u32[]{:S(2)}) %collective-permute-start.25) | collective-permute-done | bytes 114720 | tf_op jit(solution)/shard_map/ppermute | solution.py:726
  117.4 3.7 %collective-permute-done.27 = bf16[576,128]{1,0:T(8,128)(2,1)S(1)} collective-permute-done((bf16[576,128]{1,0:T(8,128)(2,1)S(1)}, bf16[576,128]{1,0:T(8,128)(2,1)S(1)}, u32[]{:S(2)}, u32[]{:S(2)}) %collective-permute-start.27) | collective-permute-done | bytes 147488 | tf_op jit(solution)/shard_map/ppermute | solution.py:726
  121.2 1.2 collective-permute-start.29
  122.4 1.5 %collective-permute-done.28.other = bf16[896,128]{1,0:T(8,128)(2,1)S(1)} collective-permute-done((bf16[896,128]{1,0:T(8,128)(2,1)S(1)}, bf16[896,128]{1,0:T(8,128)(2,1)S(1)}, u32[]{:S(2)}, u32[]{:S(2)}) %collective-permute-start.28) | collective-permute-done | bytes 229408 | tf_op jit(solution)/shard_map/ppermute | solution.py:726
  123.9 0.7 copy-done.6
  124.6 1.9 %shard_map.229 = bf16[448,448]{1,0:T(8,128)(2,1)} custom-call(bf16[896,128]{1,0:T(8,128)(2,1)} %copy-done.1, bf16[896,128]{1,0:T(8,128)(2,1)} %copy-done.6), custom_call_target="tpu_custom_call" | custom-call | flops 1 | bytes 1 | tf_op jit(solution)/shard_map/pallas_call | solution.py:695
  126.5 2.7 %collective-permute-done.29 = bf16[1152,128]{1,0:T(8,128)(2,1)S(1)} collective-permute-done((bf16[1152,128]{1,0:T(8,128)(2,1)S(1)}, bf16[1152,128]{1,0:T(8,128)(2,1)S(1)}, u32[]{:S(2)}, u32[]{:S(2)}) %collective-permute-start.29) | collective-permute-done | bytes 294944 | tf_op jit(solution)/shard_map/ppermute | solution.py:726
  129.2 0.1 broadcast_select_fusion.1
  129.4 2.0 %collective-permute-done.30.other = bf16[2304,128]{1,0:T(8,128)(2,1)S(1)} collective-permute-done((bf16[2304,128]{1,0:T(8,128)(2,1)S(1)}, bf16[2304,128]{1,0:T(8,128)(2,1)S(1)}, u32[]{:S(2)}, u32[]{:S(2)}) %collective-permute-start.30) | collective-permute-done | bytes 589856 | tf_op jit(solution)/shard_map/ppermute | solution.py:726
  131.4 0.8 copy-done.4
  132.2 2.5 %shard_map.230 = (bf16[2,384,384]{2,1,0:T(8,128)(2,1)}, bf16[2,320,320]{2,1,0:T(8,128)(2,1)}, bf16[64,256]{1,0:T(8,128)(2,1)}, bf16[128,256]{1,0:T(8,128)(2,1)},...) custom-call(bf16[2304,128]{1,0:T(8,128)(2,1)} %copy-done, bf16[2304,128]{1,0:T(8,128)(2,1)} %copy-done.4), custom_call_target="tpu_custom_call" | custom-call | flops 1 | bytes 1 | tf_op jit(solution)/shard_map/pallas_call | solution.py:695
  (77 shorter events, 1.1 us)
Async XLA Ops:
  2.9 8.5 %collective-permute-start = (bf16[4,6528]{1,0:T(4,128)(2,1)}, bf16[4,6528]{1,0:T(4,128)(2,1)S(1)}, u32[]{:S(2)}, u32[]{:S(2)}) collective-permute-start(bf16[4,6528]{1,0:T(4,128)(2,1)} %get-tuple-element.66), channel_id=1, source_target_pairs={{0,4},{4,0},{8,12},{12,8},{1,5},{5,1},{9,13},{13,9},{2,6},{6,2},{1... | collective-permute-start | bytes 156680 | tf_op jit(solution)/shard_map/ppermute | solution.py:811
  5.9 6.2 %collective-permute-start.1 = (bf16[4,6528]{1,0:T(4,128)(2,1)}, bf16[4,6528]{1,0:T(4,128)(2,1)S(1)}, u32[]{:S(2)}, u32[]{:S(2)}) collective-permute-start(bf16[4,6528]{1,0:T(4,128)(2,1)} %get-tuple-element.67), channel_id=1, source_target_pairs={{0,8},{4,12},{8,0},{12,4},{1,9},{5,13},{9,1},{13,5},{2,10},{6,14},... | collective-permute-start | bytes 156680 | tf_op jit(solution)/shard_map/ppermute | solution.py:811
  8.5 6.1 %collective-permute-start.2 = (bf16[4,6528]{1,0:T(4,128)(2,1)}, bf16[4,6528]{1,0:T(4,128)(2,1)S(1)}, u32[]{:S(2)}, u32[]{:S(2)}) collective-permute-start(bf16[4,6528]{1,0:T(4,128)(2,1)} %get-tuple-element.68), channel_id=1, source_target_pairs={{0,12},{4,8},{8,4},{12,0},{1,13},{5,9},{9,5},{13,1},{2,14},{6,10},... | collective-permute-start | bytes 156680 | tf_op jit(solution)/shard_map/ppermute | solution.py:811
  11.4 3.3 %copy-start.11 = (bf16[4,6528]{1,0:T(4,128)(2,1)}, bf16[4,6528]{1,0:T(4,128)(2,1)S(1)}, u32[]{:S(2)}) copy-start(bf16[4,6528]{1,0:T(4,128)(2,1)S(1)} %collective-permute-done.rest_1_) | copy-start | bytes 156676
  12.2 2.5 %copy-start.12 = (bf16[4,6528]{1,0:T(4,128)(2,1)}, bf16[4,6528]{1,0:T(4,128)(2,1)S(1)}, u32[]{:S(2)}) copy-start(bf16[4,6528]{1,0:T(4,128)(2,1)S(1)} %collective-permute-done.1.rest_2_) | copy-start | bytes 156676
  14.6 0.6 copy-start.13
  23.8 13.4 %all-to-all-start = ((f32[4,4,3328]{2,1,0:T(4,128)}), f32[4,4,3328]{2,1,0:T(4,128)S(1)}, u32[]{:S(2)}, u32[]{:S(2)}) async-start(f32[4,4,3328]{2,1,0:T(4,128)} %get-tuple-element.71), calls=%async_computation | async-start | bytes 425984 | tf_op jit(solution)/shard_map/all_to_all | solution.py:801
  27.4 1.9 %collective-permute-start.3 = (f32[2,128]{1,0:T(2,128)}, f32[2,128]{1,0:T(2,128)S(1)}, u32[]{:S(2)}, u32[]{:S(2)}) collective-permute-start(f32[2,128]{1,0:T(2,128)} %get-tuple-element.69), channel_id=1, source_target_pairs={{0,1},{1,0},{2,3},{3,2},{4,5},{5,4},{6,7},{7,6},{8,9},{9,8},{10,11... | collective-permute-start | bytes 3080 | tf_op jit(solution)/shard_map/ppermute | solution.py:860
  27.5 3.8 %collective-permute-start.4 = (f32[2,128]{1,0:T(2,128)}, f32[2,128]{1,0:T(2,128)S(1)}, u32[]{:S(2)}, u32[]{:S(2)}) collective-permute-start(f32[2,128]{1,0:T(2,128)} %get-tuple-element.69), channel_id=1, source_target_pairs={{0,2},{1,3},{2,0},{3,1},{4,6},{5,7},{6,4},{7,5},{8,10},{9,11},{10,... | collective-permute-start | bytes 3080 | tf_op jit(solution)/shard_map/ppermute | solution.py:860
  29.0 3.1 %collective-permute-start.5 = (f32[2,128]{1,0:T(2,128)}, f32[2,128]{1,0:T(2,128)S(1)}, u32[]{:S(2)}, u32[]{:S(2)}) collective-permute-start(f32[2,128]{1,0:T(2,128)} %get-tuple-element.69), channel_id=1, source_target_pairs={{0,3},{1,2},{2,1},{3,0},{4,7},{5,6},{6,5},{7,4},{8,11},{9,10},{10,... | collective-permute-start | bytes 3080 | tf_op jit(solution)/shard_map/ppermute | solution.py:860
  32.7 9.5 %copy-start.14 = (f32[8,128]{1,0:T(8,128)}, f32[8,128]{1,0:T(8,128)S(1)}, u32[]{:S(2)}) copy-start(f32[8,128]{1,0:T(8,128)S(1)} %pad_maximum_fusion.7.refs_0_) | copy-start | bytes 12292
  32.7 4.5 %collective-permute-start.6 = (f32[8,128]{1,0:T(8,128)S(1)}, f32[8,128]{1,0:T(8,128)S(1)}, u32[]{:S(2)}, u32[]{:S(2)}) collective-permute-start(f32[8,128]{1,0:T(8,128)S(1)} %pad_maximum_fusion.7.refs_0_), channel_id=1, source_target_pairs={{0,4},{4,0},{8,12},{12,8},{1,5},{5,1},{9,13},{13,9},{2,6},{6,2},{1... | collective-permute-start | bytes 12296 | tf_op jit(solution)/shard_map/ppermute | solution.py:865
  34.5 4.5 %collective-permute-start.7 = (f32[8,128]{1,0:T(8,128)S(1)}, f32[8,128]{1,0:T(8,128)S(1)}, u32[]{:S(2)}, u32[]{:S(2)}) collective-permute-start(f32[8,128]{1,0:T(8,128)S(1)} %pad_maximum_fusion.7.refs_0_), channel_id=1, source_target_pairs={{0,8},{4,12},{8,0},{12,4},{1,9},{5,13},{9,1},{13,5},{2,10},{6,14},... | collective-permute-start | bytes 12296 | tf_op jit(solution)/shard_map/ppermute | solution.py:865
  36.8 5.4 %collective-permute-start.8 = (f32[8,128]{1,0:T(8,128)S(1)}, f32[8,128]{1,0:T(8,128)S(1)}, u32[]{:S(2)}, u32[]{:S(2)}) collective-permute-start(f32[8,128]{1,0:T(8,128)S(1)} %pad_maximum_fusion.7.refs_0_), channel_id=1, source_target_pairs={{0,12},{4,8},{8,4},{12,0},{1,13},{5,9},{9,5},{13,1},{2,14},{6,10},... | collective-permute-start | bytes 12296 | tf_op jit(solution)/shard_map/ppermute | solution.py:865
  37.2 24.0 %copy-start.3 = (f32[4,4,3328]{2,1,0:T(4,128)}, f32[4,4,3328]{2,1,0:T(4,128)S(1)}, u32[]{:S(2)}) copy-start(f32[4,4,3328]{2,1,0:T(4,128)S(1)} %all-to-all-done.rest_0_) | copy-start | bytes 638980
  37.2 5.1 %copy-start.15 = (f32[8,128]{1,0:T(8,128)}, f32[8,128]{1,0:T(8,128)S(1)}, u32[]{:S(2)}) copy-start(f32[8,128]{1,0:T(8,128)S(1)} %collective-permute-done.6.refs_1_) | copy-start | bytes 12292
  39.0 3.3 %copy-start.16 = (f32[8,128]{1,0:T(8,128)}, f32[8,128]{1,0:T(8,128)S(1)}, u32[]{:S(2)}) copy-start(f32[8,128]{1,0:T(8,128)S(1)} %collective-permute-done.7.refs_2_) | copy-start | bytes 12292
  42.2 0.6 copy-start.17
  51.3 3.7 %collective-permute-start.10 = (f32[2176,128]{1,0:T(8,128)}, f32[2176,128]{1,0:T(8,128)S(1)}, u32[]{:S(2)}, u32[]{:S(2)}) collective-permute-start(f32[2176,128]{1,0:T(8,128)} %get-tuple-element.86), channel_id=1, source_target_pairs={{0,1},{1,0},{2,3},{3,2},{4,5},{5,4},{6,7},{7,6},{8,9},{9,8},{10,11... | collective-permute-start | bytes 3342344 | tf_op jit(solution)/shard_map/ppermute | solution.py:726
  51.4 5.0 %collective-permute-start.9 = (f32[896,128]{1,0:T(8,128)}, f32[896,128]{1,0:T(8,128)}, u32[]{:S(2)}, u32[]{:S(2)}) collective-permute-start(f32[896,128]{1,0:T(8,128)} %get-tuple-element.84), channel_id=1, source_target_pairs={{0,1},{1,0},{2,3},{3,2},{4,5},{5,4},{6,7},{7,6},{8,9},{9,8},{10,11... | collective-permute-start | bytes 1376264 | tf_op jit(solution)/shard_map/ppermute | solution.py:726
  56.4 1.0 copy-start.5
  59.2 16.9 %collective-permute-start.11 = (f32[448,128]{1,0:T(8,128)}, f32[448,128]{1,0:T(8,128)S(1)}, u32[]{:S(2)}, u32[]{:S(2)}) collective-permute-start(f32[448,128]{1,0:T(8,128)} %dynamic-slice_bitcast_fusion.2), channel_id=1, source_target_pairs={{0,4},{4,0},{8,12},{12,8},{1,5},{5,1},{9,13},{13,9},{2,6},{6,2},{1... | collective-permute-start | bytes 688136 | tf_op jit(solution)/shard_map/ppermute | solution.py:726
  59.2 8.1 %collective-permute-start.13 = (f32[4,4,3328]{2,1,0:T(4,128)S(1)}, f32[4,4,3328]{2,1,0:T(4,128)S(1)}, u32[]{:S(2)}, u32[]{:S(2)}) collective-permute-start(f32[4,4,3328]{2,1,0:T(4,128)S(1)} %all-to-all-done.rest_0_), channel_id=1, source_target_pairs={{0,2},{1,3},{2,0},{3,1},{4,6},{5,7},{6,4},{7,5},{8,10},{9,11},{10,... | collective-permute-start | bytes 638984 | tf_op jit(solution)/shard_map/ppermute | solution.py:726
  59.9 23.3 %collective-permute-start.16 = (f32[1088,128]{1,0:T(8,128)S(1)}, f32[1088,128]{1,0:T(8,128)S(1)}, u32[]{:S(2)}, u32[]{:S(2)}) collective-permute-start(f32[1088,128]{1,0:T(8,128)S(1)} %dynamic-slice_bitcast_fusion), channel_id=1, source_target_pairs={{0,2},{1,3},{2,0},{3,1},{4,6},{5,7},{6,4},{7,5},{8,10},{9,11},{10,... | collective-permute-start | bytes 1671176 | tf_op jit(solution)/shard_map/ppermute | solution.py:726
  61.2 17.9 %collective-permute-start.12 = (f32[4,4,3328]{2,1,0:T(4,128)S(1)}, f32[4,4,3328]{2,1,0:T(4,128)}, u32[]{:S(2)}, u32[]{:S(2)}) collective-permute-start(f32[4,4,3328]{2,1,0:T(4,128)S(1)} %all-to-all-done.rest_0_), channel_id=1, source_target_pairs={{0,1},{1,0},{2,3},{3,2},{4,5},{5,4},{6,7},{7,6},{8,9},{9,8},{10,11... | collective-permute-start | bytes 638984 | tf_op jit(solution)/shard_map/ppermute | solution.py:726
  67.3 5.5 %copy-start.10 = (f32[4,4,3328]{2,1,0:T(4,128)}, f32[4,4,3328]{2,1,0:T(4,128)S(1)}, u32[]{:S(2)}) copy-start(f32[4,4,3328]{2,1,0:T(4,128)S(1)} %collective-permute-done.13.rest_2_) | copy-start | bytes 638980
  67.3 11.9 %collective-permute-start.14 = (f32[4,4,3328]{2,1,0:T(4,128)S(1)}, f32[4,4,3328]{2,1,0:T(4,128)}, u32[]{:S(2)}, u32[]{:S(2)}) collective-permute-start(f32[4,4,3328]{2,1,0:T(4,128)S(1)} %collective-permute-done.13.rest_2_), channel_id=1, source_target_pairs={{0,1},{1,0},{2,3},{3,2},{4,5},{5,4},{6,7},{7,6},{8,9},{9,8},{10,11... | collective-permute-start | bytes 638984 | tf_op jit(solution)/shard_map/ppermute | solution.py:726
  72.7 17.9 %all-to-all-start.1 = ((f32[4,4,3328]{2,1,0:T(4,128)}), f32[4,4,3328]{2,1,0:T(4,128)S(1)}, u32[]{:S(2)}, u32[]{:S(2)}) async-start(f32[4,4,3328]{2,1,0:T(4,128)} %shard_map.226), calls=%async_computation.1 | async-start | bytes 425984 | tf_op jit(solution)/shard_map/all_to_all | solution.py:801
  76.2 13.6 %collective-permute-start.15 = (f32[224,128]{1,0:T(8,128)S(1)}, f32[224,128]{1,0:T(8,128)S(1)}, u32[]{:S(2)}, u32[]{:S(2)}) collective-permute-start(f32[224,128]{1,0:T(8,128)S(1)} %dynamic-slice_bitcast_fusion.4), channel_id=1, source_target_pairs={{0,8},{4,12},{8,0},{12,4},{1,9},{5,13},{9,1},{13,5},{2,10},{6,14},... | collective-permute-start | bytes 344072 | tf_op jit(solution)/shard_map/ppermute | solution.py:726
  83.3 14.9 %collective-permute-start.19 = (f32[576,128]{1,0:T(8,128)S(1)}, f32[576,128]{1,0:T(8,128)S(1)}, u32[]{:S(2)}, u32[]{:S(2)}) collective-permute-start(f32[576,128]{1,0:T(8,128)S(1)} %dynamic-slice_bitcast_fusion.1), channel_id=1, source_target_pairs={{0,4},{4,0},{8,12},{12,8},{1,5},{5,1},{9,13},{13,9},{2,6},{6,2},{1... | collective-permute-start | bytes 884744 | tf_op jit(solution)/shard_map/ppermute | solution.py:726
  89.8 4.9 %collective-permute-start.17 = (f32[112,128]{1,0:T(8,128)S(1)}, f32[112,128]{1,0:T(8,128)S(1)}, u32[]{:S(2)}, u32[]{:S(2)}) collective-permute-start(f32[112,128]{1,0:T(8,128)S(1)} %dynamic-slice_bitcast_fusion.5), channel_id=1, source_target_pairs={{0,2},{1,3},{2,0},{3,1},{4,6},{5,7},{6,4},{7,5},{8,10},{9,11},{10,... | collective-permute-start | bytes 172040 | tf_op jit(solution)/shard_map/ppermute | solution.py:726
  90.6 10.7 %copy-start.2 = (f32[4,4,3328]{2,1,0:T(4,128)}, f32[4,4,3328]{2,1,0:T(4,128)S(1)}, u32[]{:S(2)}) copy-start(f32[4,4,3328]{2,1,0:T(4,128)S(1)} %all-to-all-done.1.rest_0_) | copy-start | bytes 638980
  90.6 7.6 %collective-permute-start.21 = (f32[4,4,3328]{2,1,0:T(4,128)S(1)}, f32[4,4,3328]{2,1,0:T(4,128)S(1)}, u32[]{:S(2)}, u32[]{:S(2)}) collective-permute-start(f32[4,4,3328]{2,1,0:T(4,128)S(1)} %all-to-all-done.1.rest_0_), channel_id=1, source_target_pairs={{0,2},{1,3},{2,0},{3,1},{4,6},{5,7},{6,4},{7,5},{8,10},{9,11},{10,... | collective-permute-start | bytes 638984 | tf_op jit(solution)/shard_map/ppermute | solution.py:726
  91.9 9.4 %collective-permute-start.20 = (f32[4,4,3328]{2,1,0:T(4,128)S(1)}, f32[4,4,3328]{2,1,0:T(4,128)S(1)}, u32[]{:S(2)}, u32[]{:S(2)}) collective-permute-start(f32[4,4,3328]{2,1,0:T(4,128)S(1)} %all-to-all-done.1.rest_0_), channel_id=1, source_target_pairs={{0,1},{1,0},{2,3},{3,2},{4,5},{5,4},{6,7},{7,6},{8,9},{9,8},{10,11... | collective-permute-start | bytes 638984 | tf_op jit(solution)/shard_map/ppermute | solution.py:726
  94.8 3.9 %collective-permute-start.18 = (bf16[112,128]{1,0:T(8,128)(2,1)S(1)}, bf16[112,128]{1,0:T(8,128)(2,1)S(1)}, u32[]{:S(2)}, u32[]{:S(2)}) collective-permute-start(bf16[112,128]{1,0:T(8,128)(2,1)S(1)} %fusion.1), channel_id=1, source_target_pairs={{0,2},{1,3},{2,0},{3,1},{4,6},{5,7},{6,4},{7,5},{8,10},{9,11},{10,... | collective-permute-start | bytes 86024 | tf_op jit(solution)/shard_map/ppermute | solution.py:726
  98.2 3.2 %copy-start.7 = (f32[4,4,3328]{2,1,0:T(4,128)}, f32[4,4,3328]{2,1,0:T(4,128)S(1)}, u32[]{:S(2)}) copy-start(f32[4,4,3328]{2,1,0:T(4,128)S(1)} %collective-permute-done.21.rest_2_) | copy-start | bytes 638980
  98.2 3.2 %collective-permute-start.22 = (f32[4,4,3328]{2,1,0:T(4,128)S(1)}, f32[4,4,3328]{2,1,0:T(4,128)S(1)}, u32[]{:S(2)}, u32[]{:S(2)}) collective-permute-start(f32[4,4,3328]{2,1,0:T(4,128)S(1)} %collective-permute-done.21.rest_2_), channel_id=1, source_target_pairs={{0,1},{1,0},{2,3},{3,2},{4,5},{5,4},{6,7},{7,6},{8,9},{9,8},{10,11... | collective-permute-start | bytes 638984 | tf_op jit(solution)/shard_map/ppermute | solution.py:726
  98.3 11.0 %collective-permute-start.24 = (f32[288,128]{1,0:T(8,128)S(1)}, f32[288,128]{1,0:T(8,128)S(1)}, u32[]{:S(2)}, u32[]{:S(2)}) collective-permute-start(f32[288,128]{1,0:T(8,128)S(1)} %dynamic-slice_bitcast_fusion.3), channel_id=1, source_target_pairs={{0,8},{4,12},{8,0},{12,4},{1,9},{5,13},{9,1},{13,5},{2,10},{6,14},... | collective-permute-start | bytes 442376 | tf_op jit(solution)/shard_map/ppermute | solution.py:726
  98.7 11.7 %collective-permute-start.23 = (bf16[224,128]{1,0:T(8,128)(2,1)S(1)}, bf16[224,128]{1,0:T(8,128)(2,1)S(1)}, u32[]{:S(2)}, u32[]{:S(2)}) collective-permute-start(bf16[224,128]{1,0:T(8,128)(2,1)S(1)} %pad_maximum_fusion.6), channel_id=1, source_target_pairs={{0,8},{4,12},{8,0},{12,4},{1,9},{5,13},{9,1},{13,5},{2,10},{6,14},... | collective-permute-start | bytes 172040 | tf_op jit(solution)/shard_map/ppermute | solution.py:726
  101.4 0.7 copy-start.8
  102.0 0.7 copy-start.9
  109.3 6.0 %collective-permute-start.26 = (bf16[288,128]{1,0:T(8,128)(2,1)S(1)}, bf16[288,128]{1,0:T(8,128)(2,1)S(1)}, u32[]{:S(2)}, u32[]{:S(2)}) collective-permute-start(bf16[288,128]{1,0:T(8,128)(2,1)S(1)} %fusion), channel_id=1, source_target_pairs={{0,8},{4,12},{8,0},{12,4},{1,9},{5,13},{9,1},{13,5},{2,10},{6,14},... | collective-permute-start | bytes 221192 | tf_op jit(solution)/shard_map/ppermute | solution.py:726
  110.5 6.7 %collective-permute-start.25 = (bf16[448,128]{1,0:T(8,128)(2,1)S(1)}, bf16[448,128]{1,0:T(8,128)(2,1)S(1)}, u32[]{:S(2)}, u32[]{:S(2)}) collective-permute-start(bf16[448,128]{1,0:T(8,128)(2,1)S(1)} %pad_maximum_fusion.5), channel_id=1, source_target_pairs={{0,4},{4,0},{8,12},{12,8},{1,5},{5,1},{9,13},{13,9},{2,6},{6,2},{1... | collective-permute-start | bytes 344072 | tf_op jit(solution)/shard_map/ppermute | solution.py:726
  115.4 5.7 %collective-permute-start.27 = (bf16[576,128]{1,0:T(8,128)(2,1)S(1)}, bf16[576,128]{1,0:T(8,128)(2,1)S(1)}, u32[]{:S(2)}, u32[]{:S(2)}) collective-permute-start(bf16[576,128]{1,0:T(8,128)(2,1)S(1)} %pad_maximum_fusion.4), channel_id=1, source_target_pairs={{0,4},{4,0},{8,12},{12,8},{1,5},{5,1},{9,13},{13,9},{2,6},{6,2},{1... | collective-permute-start | bytes 442376 | tf_op jit(solution)/shard_map/ppermute | solution.py:726
  117.3 6.5 %copy-start.1 = (bf16[896,128]{1,0:T(8,128)(2,1)}, bf16[896,128]{1,0:T(8,128)(2,1)S(1)}, u32[]{:S(2)}) copy-start(bf16[896,128]{1,0:T(8,128)(2,1)S(1)} %pad_maximum_fusion.3.mine) | copy-start | bytes 688132
  121.2 8.0 %collective-permute-start.29 = (bf16[1152,128]{1,0:T(8,128)(2,1)S(1)}, bf16[1152,128]{1,0:T(8,128)(2,1)S(1)}, u32[]{:S(2)}, u32[]{:S(2)}) collective-permute-start(bf16[1152,128]{1,0:T(8,128)(2,1)S(1)} %pad_maximum_fusion.2), channel_id=1, source_target_pairs={{0,2},{1,3},{2,0},{3,1},{4,6},{5,7},{6,4},{7,5},{8,10},{9,11},{10,... | collective-permute-start | bytes 884744 | tf_op jit(solution)/shard_map/ppermute | solution.py:726
  122.4 1.5 %collective-permute-start.28 = (bf16[896,128]{1,0:T(8,128)(2,1)S(1)}, bf16[896,128]{1,0:T(8,128)(2,1)S(1)}, u32[]{:S(2)}, u32[]{:S(2)}) collective-permute-start(bf16[896,128]{1,0:T(8,128)(2,1)S(1)} %pad_maximum_fusion.3.mine), channel_id=1, source_target_pairs={{0,1},{1,0},{2,3},{3,2},{4,5},{5,4},{6,7},{7,6},{8,9},{9,8},{10,11... | collective-permute-start | bytes 688136 | tf_op jit(solution)/shard_map/ppermute | solution.py:726
  123.9 0.7 copy-start.6
  129.3 2.1 %copy-start = (bf16[2304,128]{1,0:T(8,128)(2,1)}, bf16[2304,128]{1,0:T(8,128)(2,1)S(1)}, u32[]{:S(2)}) copy-start(bf16[2304,128]{1,0:T(8,128)(2,1)S(1)} %pad_maximum_fusion.1.mine) | copy-start | bytes 1769476
  129.4 2.1 %collective-permute-start.30 = (bf16[2304,128]{1,0:T(8,128)(2,1)S(1)}, bf16[2304,128]{1,0:T(8,128)(2,1)S(1)}, u32[]{:S(2)}, u32[]{:S(2)}) collective-permute-start(bf16[2304,128]{1,0:T(8,128)(2,1)S(1)} %pad_maximum_fusion.1.mine), channel_id=1, source_target_pairs={{0,1},{1,0},{2,3},{3,2},{4,5},{5,4},{6,7},{7,6},{8,9},{9,8},{10,11... | collective-permute-start | bytes 1769480 | tf_op jit(solution)/shard_map/ppermute | solution.py:726
  131.4 0.8 copy-start.4

commit v6 on v5

--- a/solution.py
+++ b/solution.py
@@ -335,69 +335,60 @@
     return result
 
 
-def collect_rows(arrivals, rows_ref):
-    own = lax.axis_index("edge")
-    for k, arrival in enumerate(arrivals):
-        peers, cap, width = arrival.shape
-        base = (own ^ k) * (peers * cap)
-        for start in range(0, peers * cap, 8):
-            parts = [arrival[g] for g in range(start // cap, (start + 8) // cap)]
-            at = pl.ds(pl.multiple_of(base + start, 8), 8)
-            rows_ref[at, :] = jnp.concatenate(parts, axis=0)
+def collect_rows(arrived, rows_ref):
+    cap = arrived.shape[1]
+    for start in range(0, arrived.shape[0] * cap, 8):
+        parts = [arrived[n] for n in range(start // cap, (start + 8) // cap)]
+        rows_ref[pl.ds(start, 8), :] = jnp.concatenate(parts, axis=0)
 
 
 def block_cols(block):
     return pl.ds(block * LANES, min(LANES, FLAT - block * LANES))
 
 
-def make_finish(lanes_total):
-    def finish_kernel(cot, out_proj, *rest):
-        arrivals = rest[:lanes_total]
-        out, proj, rows, terms, agg_low = rest[lanes_total:]
-        atoms = cot.shape[1]
-        total = rows.shape[0]
-        collect_rows(arrivals, rows)
-        side = rows[:, pl.ds(COLS, LANES)]
-        owner = (lax.axis_index("graph") * atoms).astype(f32)
-        names = iota((total, atoms), 1).astype(f32) + owner == side[:, NAME_AT : NAME_AT + 1]
-        eye = iota((atoms, atoms), 0) == iota((atoms, atoms), 1)
-        scales, dens = [], []
-        for h in range(HEADS):
-            peak_rows = side[:, PEAK_AT + h : PEAK_AT + h + 1]
-            peak = jnp.max(jnp.where(names, peak_rows, floor_value), axis=0, keepdims=True)
-            of_row = jnp.sum(jnp.where(names, peak, 0.0), axis=1, keepdims=True)
-            scale = jnp.exp(peak_rows - of_row)
-            scaled_den = side[:, h : h + 1] * scale
-            den = jnp.sum(jnp.where(names, scaled_den, 0.0), axis=0, keepdims=True)
-            scales.append(scale)
-            dens.append(jnp.sum(jnp.where(eye, den, 0.0), axis=1, keepdims=True))
-        scale_full = lane_heads(scales, (total, LANES))
-        den_full = lane_heads(dens, (atoms, LANES))
-        picked = mask_to(names, bf16)
-        twice = jnp.concatenate([picked, picked], axis=0)
-        for block in range(BLOCKS):
-            cols = pl.ds(block * LANES, LANES)
-            high, low = split_two(rows[:, cols] * scale_full)
-            terms[pl.ds(0, total), cols] = high
-            terms[pl.ds(total, total), cols] = low
-        for block in range(BLOCKS):
-            cols = pl.ds(block * LANES, LANES)
-            agg = (dot_tn(twice, terms[:, cols]) / den_full).astype(bf16)
-            agg_low[2 * block] = agg[:, :CH]
-            if 2 * block + 1 < COEFFS:
-                agg_low[2 * block + 1] = agg[:, CH:]
-        for degree in range(LMAX + 1):
-            ids = pl.ds(degree * degree, 2 * degree + 1)
-            stacked = ((2 * degree + 1) * atoms, CH)
-            left = agg_low[ids].reshape(stacked)
-            right = cot[ids].reshape(stacked)
-            value = dot_nn(left, out_proj[degree]).astype(bf16)
-            out[ids] = value.reshape((2 * degree + 1, atoms, CH))
-            at = (pl.ds(degree // 2 * CH, CH), pl.ds(degree % 2 * CH, CH))
-            proj[at] = dot_tn(left, right)
-        proj[pl.ds(LMAX // 2 * CH, CH), pl.ds(CH, CH)] = jnp.zeros((CH, CH), f32)
-
-    return finish_kernel
+def finish_kernel(cot, out_proj, arrived, out, proj, rows, terms, agg_low):
+    atoms = cot.shape[1]
+    total = rows.shape[0]
+    collect_rows(arrived, rows)
+    side = rows[:, pl.ds(COLS, LANES)]
+    owner = (lax.axis_index("graph") * atoms).astype(f32)
+    names = iota((total, atoms), 1).astype(f32) + owner == side[:, NAME_AT : NAME_AT + 1]
+    eye = iota((atoms, atoms), 0) == iota((atoms, atoms), 1)
+    scales, dens = [], []
+    for h in range(HEADS):
+        peak_rows = side[:, PEAK_AT + h : PEAK_AT + h + 1]
+        peak = jnp.max(jnp.where(names, peak_rows, floor_value), axis=0, keepdims=True)
+        of_row = jnp.sum(jnp.where(names, peak, 0.0), axis=1, keepdims=True)
+        scale = jnp.exp(peak_rows - of_row)
+        scaled_den = side[:, h : h + 1] * scale
+        den = jnp.sum(jnp.where(names, scaled_den, 0.0), axis=0, keepdims=True)
+        scales.append(scale)
+        dens.append(jnp.sum(jnp.where(eye, den, 0.0), axis=1, keepdims=True))
+    scale_full = lane_heads(scales, (total, LANES))
+    den_full = lane_heads(dens, (atoms, LANES))
+    picked = mask_to(names, bf16)
+    twice = jnp.concatenate([picked, picked], axis=0)
+    for block in range(BLOCKS):
+        cols = pl.ds(block * LANES, LANES)
+        high, low = split_two(rows[:, cols] * scale_full)
+        terms[pl.ds(0, total), cols] = high
+        terms[pl.ds(total, total), cols] = low
+    for block in range(BLOCKS):
+        cols = pl.ds(block * LANES, LANES)
+        agg = (dot_tn(twice, terms[:, cols]) / den_full).astype(bf16)
+        agg_low[2 * block] = agg[:, :CH]
+        if 2 * block + 1 < COEFFS:
+            agg_low[2 * block + 1] = agg[:, CH:]
+    for degree in range(LMAX + 1):
+        ids = pl.ds(degree * degree, 2 * degree + 1)
+        stacked = ((2 * degree + 1) * atoms, CH)
+        left = agg_low[ids].reshape(stacked)
+        right = cot[ids].reshape(stacked)
+        value = dot_nn(left, out_proj[degree]).astype(bf16)
+        out[ids] = value.reshape((2 * degree + 1, atoms, CH))
+        at = (pl.ds(degree // 2 * CH, CH), pl.ds(degree % 2 * CH, CH))
+        proj[at] = dot_tn(left, right)
+    proj[pl.ds(LMAX // 2 * CH, CH), pl.ds(CH, CH)] = jnp.zeros((CH, CH), f32)
 
 
 def combine_stats(stats, own):
@@ -419,7 +410,7 @@
         return tuple(result)
 
     def step(at, held):
-        fresh = part(stats[0][pl.ds(pl.multiple_of(at * chunk, chunk), chunk), :])
+        fresh = part(stats[pl.ds(pl.multiple_of(at * chunk, chunk), chunk), :])
         result = []
         for h in range(HEADS):
             peak, den, dot = held[3 * h : 3 * h + 3]
@@ -429,17 +420,15 @@
             result += [most, den * old + new_den * new, dot * old + new_dot * new]
         return tuple(result)
 
-    if len(stats) > 1:
-        held = part(jnp.concatenate([rows[...] for rows in stats], axis=0))
-    else:
-        held = part(stats[0][pl.ds(0, chunk), :])
-        held = lax.fori_loop(1, stats[0].shape[0] // chunk, step, held)
+    held = part(stats[pl.ds(0, chunk), :])
+    if stats.shape[0] > chunk:
+        held = lax.fori_loop(1, stats.shape[0] // chunk, step, held)
     return [held[3 * h : 3 * h + 3] for h in range(HEADS)]
 
 
-def make_gradient(peers, parts):
+def make_gradient(peers):
     def kernel(*refs):
-        gradient_kernel(peers, refs[:parts], *refs[parts:])
+        gradient_kernel(peers, *refs)
 
     return kernel
 
@@ -579,46 +568,45 @@
 PACKED_ROWS = sum(size for start, size in CHUNKS)
 
 
-def halves_of(mine, other):
-    first = (lax.axis_index("edge") & 1) == 0
-    left, right = mine[...].astype(f32), other[...].astype(f32)
-    return jnp.where(first, left, right), jnp.where(first, right, left)
-
-
-def unpack_zero_kernel(mine, other, zero):
-    left, right = halves_of(mine, other)
-    zero[:, pl.ds(0, LANES)] = left[:DIM0].astype(bf16)
-    zero[:, pl.ds(LANES, LANES)] = right[:DIM0].astype(bf16)
-    zero[:, pl.ds(2 * LANES, LANES)] = left[DIM0:].astype(bf16)
-    zero[:, pl.ds(3 * LANES, DIM0 - 3 * LANES)] = right[DIM0:, : DIM0 - 3 * LANES].astype(bf16)
-
-
-def make_unpack_rest(lanes_total):
-    def unpack_rest_kernel(mine, other, one, two, alpha_in, alpha_edge, alpha_dot, proj):
-        left, right = halves_of(mine, other)
-        parts = lanes_total // 2
+def reversed_bits(value, count):
+    return sum(((value >> n) & 1) << (count - 1 - n) for n in range(count))
+
+
+def make_unpack(lanes_total, peers):
+    def unpack_kernel(shares, zero, one, two, alpha_in, alpha_edge, alpha_dot, proj):
+        cols = lanes_total // 2
+        col_bits, peer_bits = (cols - 1).bit_length(), (peers - 1).bit_length()
         late = PROJ_ROWS // lanes_total
-        size = left.shape[0] // parts - late
-        tail = jnp.concatenate(
-            [
-                value[n * (size + late) + size : (n + 1) * (size + late)]
-                for value in (left, right)
-                for n in range(parts)
-            ],
-            axis=0,
-        )
+        first_rows = (CHUNKS[0][1] // cols + late) // peers
+        share = shares.shape[1]
+        main, zeros, tail = [], [], []
+        for core in range(2):
+            parts, zero_parts = [], {}
+            for col in range(cols):
+                col_of = reversed_bits(col, col_bits)
+                rows = []
+                for at in range(peers):
+                    peer = reversed_bits(at, peer_bits)
+                    value = shares[(col_of * 2 + core) * peers + peer].astype(f32)
+                    rows.append(value[:first_rows])
+                    zero_parts[at * cols + col] = value[first_rows:share]
+                rows = jnp.concatenate(rows, axis=0)
+                parts.append(rows[: CHUNKS[0][1] // cols])
+                tail.append((core * cols + col_of, rows[CHUNKS[0][1] // cols :]))
+            main.append(jnp.concatenate(parts, axis=0))
+            zeros.append(jnp.concatenate([zero_parts[n] for n in sorted(zero_parts)], axis=0))
+        tail = jnp.concatenate([rows for place, rows in sorted(tail, key=lambda e: e[0])], axis=0)
         for degree in range(LMAX + 1):
             piece = tail[degree // 2 * CH : (degree // 2 + 1) * CH]
             proj[degree] = piece[:, degree % 2 * CH : (degree % 2 + 1) * CH].astype(bf16)
-        left, right = (
-            jnp.concatenate(
-                [value[n * (size + late) : n * (size + late) + size] for n in range(parts)], axis=0
-            )
-            for value in (left, right)
-        )
-        unpack_rest(left, right, one, two, alpha_in, alpha_edge, alpha_dot)
-
-    return unpack_rest_kernel
+        left, right = zeros
+        zero[:, pl.ds(0, LANES)] = left[:DIM0].astype(bf16)
+        zero[:, pl.ds(LANES, LANES)] = right[:DIM0].astype(bf16)
+        zero[:, pl.ds(2 * LANES, LANES)] = left[DIM0:].astype(bf16)
+        zero[:, pl.ds(3 * LANES, DIM0 - 3 * LANES)] = right[DIM0:, : DIM0 - 3 * LANES].astype(bf16)
+        unpack_rest(*main, one, two, alpha_in, alpha_edge, alpha_dot)
+
+    return unpack_kernel
 
 
 def unpack_rest(left, right, one, two, alpha_in, alpha_edge, alpha_dot):
@@ -662,24 +650,19 @@
     put_rows(sums_out, pl.ds(COLS, LANES), lists[...])
 
 
-def make_collect(lanes_total):
-    def collect_kernel(*rest):
-        arrivals = rest[:lanes_total]
-        out, rows = rest[lanes_total:]
-        atoms = out.shape[1]
-        total = rows.shape[0]
-        collect_rows(arrivals, rows)
-        index = rows[:, pl.ds(COLS, LANES)][:, 1:2]
-        picked = mask_to(iota((total, atoms), 1).astype(f32) == index, bf16)
-        twice = jnp.concatenate([picked, picked], axis=0)
-        for block in range(BLOCKS):
-            high, low = split_two(rows[:, pl.ds(block * LANES, LANES)])
-            sums = dot_tn(twice, jnp.concatenate([high, low], axis=0)).astype(bf16)
-            out[2 * block] = sums[:, :CH]
-            if 2 * block + 1 < COEFFS:
-                out[2 * block + 1] = sums[:, CH:]
-
-    return collect_kernel
+def collect_kernel(arrived, out, rows):
+    atoms = out.shape[1]
+    total = rows.shape[0]
+    collect_rows(arrived, rows)
+    index = rows[:, pl.ds(COLS, LANES)][:, 1:2]
+    picked = mask_to(iota((total, atoms), 1).astype(f32) == index, bf16)
+    twice = jnp.concatenate([picked, picked], axis=0)
+    for block in range(BLOCKS):
+        high, low = split_two(rows[:, pl.ds(block * LANES, LANES)])
+        sums = dot_tn(twice, jnp.concatenate([high, low], axis=0)).astype(bf16)
+        out[2 * block] = sums[:, :CH]
+        if 2 * block + 1 < COEFFS:
+            out[2 * block + 1] = sums[:, CH:]
 
 
 vmem = pl.BlockSpec(memory_space=pltpu.VMEM)
@@ -728,13 +711,6 @@
 
 def bits_of(axis):
     return (lax.axis_size(axis) - 1).bit_length()
-
-
-def gather_lanes(value):
-    held = {0: value}
-    for bit in reversed(range(bits_of("edge"))):
-        held.update({k | (1 << bit): swap(v, "edge", bit) for k, v in list(held.items())})
-    return [held[k] for k in range(len(held))]
 
 
 def own_bit(axis, bit):
@@ -757,21 +733,7 @@
         other = swap(sent, axis, bit)
         yield
         current = lax.dynamic_index_in_dim(parts, mine, 0, False) + order.hold(other)
-    current = order.mark(current.astype(bf16))
-    for axis, bit in reversed(steps):
-        mine = own_bit(axis, bit)
-        other = swap(current, axis, bit)
-        yield
-        other = order.hold(other)
-        current = order.mark(
-            jnp.concatenate(
-                [jnp.where(mine == 0, current, other), jnp.where(mine == 0, other, current)],
-                axis=0,
-            )
-        )
-    other = swap(current, "edge", 0)
-    yield
-    return current, other
+    return order.mark(current.astype(bf16))
 
 
 def finish_steps(chain):
@@ -855,25 +817,13 @@
         conv_zero, conv_one, conv_two, alpha_in, alpha_edge, adot, out_proj, *tables,
         far=(5, 6, 7), apart=range(2, 9)
     )
-    if direct:
-        lanes_stats = [stats] + [
-            lax.ppermute(stats, "edge", [(i, i ^ k) for i in range(lanes_total)])
-            for k in range(1, lanes_total)
-        ]
-        graph_stats = jnp.concatenate(lanes_stats, axis=0)
-        all_stats = [graph_stats] + [
-            lax.ppermute(graph_stats, "graph", [(i, i ^ k) for i in range(peers)])
-            for k in range(1, peers)
-        ]
-    else:
-        all_stats = [lax.all_gather(stats, ("graph", "edge"), tiled=True)]
+    all_stats = lax.all_gather(stats, ("graph", "edge"), tiled=True)
     messages = exchange(sums)
-    order.mark(messages)
-    message_rows = gather_lanes(messages)
+    message_rows = lax.all_gather(messages, "edge", tiled=True)
 
     halves = [((size, LANES), f32) for start, size in CHUNKS for _ in range(2)]
     g0, g1, g2, pre_grad, *halves = call(
-        make_gradient(peers, len(all_stats)),
+        make_gradient(peers),
         [
             ((DIM0, edges), bf16),
             ((DIM1, 2 * edges), bf16),
@@ -891,14 +841,13 @@
         ]
         + frames
         + [pltpu.SemaphoreType.DMA((10,))],
-        *all_stats, order.hold(own_stats), agg_grad, target_row, rot, edge_feats,
+        all_stats, own_stats, agg_grad, target_row, rot, edge_feats,
         x0, x1, x2, v0, v1, v2, pre, logits, adot,
-        far=range(len(all_stats) + 5, len(all_stats) + 11), apart=range(4, 8)
+        far=range(6, 12), apart=range(4, 8)
     )
 
     total = lanes_total * slots
     order.mark(halves[0])
-    message_rows = [order.hold(message_rows[0])] + message_rows[1:]
     late = []
     rest_steps = sum_all(halves[0], halves[1], "edge", order, late)
     zero_steps = sum_all(halves[2], halves[3], "graph", order)
@@ -922,10 +871,10 @@
     returned = exchange(source_sums)
     next(zero_steps)
     out, proj = call(
-        make_finish(lanes_total),
+        finish_kernel,
         [((COEFFS, atoms, CH), bf16), ((PROJ_ROWS, LANES), f32)],
         [((total, WIDE), f32), ((2 * total, COLS), bf16), ((COEFFS, atoms, CH), bf16)],
-        order.hold(cot), out_proj, *message_rows,
+        order.hold(cot), out_proj, message_rows,
     )
     order.mark(proj)
     lane = lax.axis_index("edge")
@@ -935,31 +884,21 @@
     for _ in range(bits_of("edge") - 1):
         next(rest_steps)
     next(zero_steps)
-    source_rows = gather_lanes(order.hold(returned))
-    next(zero_steps)
+    source_rows = lax.all_gather(returned, "edge", tiled=True)
     next(rest_steps)
-    next(zero_steps)
+    zero_share = finish_steps(zero_steps)
+    share = jnp.concatenate([finish_steps(rest_steps), zero_share], axis=0)
+    shares = lax.all_gather(share, ("edge", "graph"))
     (embed,) = call(
-        make_collect(lanes_total),
+        collect_kernel,
         [((COEFFS, atoms, CH), bf16)],
         [((total, WIDE), f32)],
-        order.hold(source_rows[0]), *source_rows[1:],
-    )
-    order.mark(embed)
-    next(rest_steps)
-    next(zero_steps)
-    next(rest_steps)
-    next(zero_steps)
-    next(rest_steps)
-    zero_pair = finish_steps(zero_steps)
-    (zero,) = call(
-        unpack_zero_kernel, [((DIM0, DIM0), bf16)], [], order.hold(zero_pair[0]), zero_pair[1]
-    )
-    order.mark(zero)
-    rest_pair = finish_steps(rest_steps)
-    one, two, grad_in, grad_edge, grad_dot, grad_proj = call(
-        make_unpack_rest(lanes_total),
+        order.hold(source_rows),
+    )
+    zero, one, two, grad_in, grad_edge, grad_dot, grad_proj = call(
+        make_unpack(lanes_total, peers),
         [
+            ((DIM0, DIM0), bf16),
             ((2, DIM1, DIM1), bf16),
             ((2, DIM2, DIM2), bf16),
             (alpha_in.shape, bf16),
@@ -967,7 +906,8 @@
             ((2, LANES), bf16),
             (out_proj.shape, bf16),
         ],
-        [], order.hold(rest_pair[0]), rest_pair[1]
+        [],
+        shares.reshape(blocks, -1, LANES),
     )
 
     def shaped(value):

time: 136 us -> 166 us (1.22)
  blocking collectives: 0 us -> 54.8 us
  starting transfers between devices: 34.3 us -> 17.7 us
  between operations: 1 us -> 14.2 us
  waiting for transfers between devices: 51.2 us -> 38.6 us
  local copies, waits for them, and re-layouts: 9.51 us -> 4.89 us
  Pallas kernels: 35 us -> 33.2 us
    all_gather x0 -> x3, blocking collectives: none -> 42.3 us  [the longest x1 20.3 us: shards(): all_stats = lax.all_gather(stats, ('graph', 'edge'), tiled=True)]
    ppermute x22 -> x8, waiting for transfers between devices: 40.1 us -> 15.1 us  [swap(): return lax.ppermute(value, axis, [(i, i ^ 1 << bit) for i in range(size)])]
    all_gather x0 -> x1, waiting for transfers between devices: none -> 16.6 us  [shards(): shares = lax.all_gather(share, ('edge', 'graph'))]
    all_to_all x0 -> x1, blocking collectives: none -> 12.5 us  [exchange(): lax.all_to_all(value, 'graph', split_axis=0, concat_axis=0, tiled=True)]
    ppermute x6 -> x0, waiting for transfers between devices: 7.79 us -> none  [the longest x3 5.04 us: shards(): lax.ppermute(graph_stats, 'graph', [(i, i ^ k) for i in range(peers)])]
    ppermute x22 -> x8, starting transfers between devices: 15.4 us -> 8.65 us  [swap(): return lax.ppermute(value, axis, [(i, i ^ 1 << bit) for i in range(size)])]
    ppermute x6 -> x0, starting transfers between devices: 6.38 us -> none  [the longest x3 4.45 us: shards(): lax.ppermute(graph_stats, 'graph', [(i, i ^ k) for i in range(peers)])]
    unnamed x37 -> x11, local copies, waits for them, and re-layouts: 6.7 us -> 2.75 us
  transfers between devices with their start and end apart: 33 -> 13, of which waited for: 20 -> 7; matrix products, arithmetic and copies ran while one was open for 5% -> 3% of each run, Pallas kernels for 10% -> 7%
where the time goes in v6:
time: 166 us
  blocking collectives  54.8 us (33%)
  waiting for transfers between devices  38.6 us (23%)
  Pallas kernels  33.2 us (20%)
  starting transfers between devices  17.7 us (11%)
  between operations  14.2 us (9%)
  local copies, waits for them, and re-layouts  4.89 us (3%)
  other arithmetic  2.28 us (1%)
    pallas_call x7, Pallas kernels, call(): pl.pallas_call(kernel, out_shape=[jax.ShapeDtypeStruct(shape, kind) for s...  33.2 us
    all_gather x1, blocking collectives, shards(): all_stats = lax.all_gather(stats, ('graph', 'edge'), tiled=True)  20.3 us
    all_gather x1, waiting for transfers between devices, shards(): shares = lax.all_gather(share, ('edge', 'graph'))  16.6 us
    ppermute x8, waiting for transfers between devices, swap(): return lax.ppermute(value, axis, [(i, i ^ 1 << bit) for i in range(size)])  15.1 us
    all_gather x1, blocking collectives, shards(): message_rows = lax.all_gather(messages, 'edge', tiled=True)  14.1 us
    all_to_all x1, blocking collectives, exchange(): lax.all_to_all(value, 'graph', split_axis=0, concat_axis=0, tiled=True)  12.5 us
    ppermute x8, starting transfers between devices, swap(): return lax.ppermute(value, axis, [(i, i ^ 1 << bit) for i in range(size)])  8.65 us
    all_gather x1, blocking collectives, shards(): source_rows = lax.all_gather(returned, 'edge', tiled=True)  7.85 us
  transfers between devices with their start and end apart: 13, of which 7 were waited for; matrix products, arithmetic and copies ran while one was open for 3% of the time, Pallas kernels for 7%

profile of v6, /device:TPU:0, one launch (start us, length us, event | category | flops | bytes accessed | tf_op | source)
XLA Modules:
  0.0 165.6 jit_solution(15998039787804549319)
XLA Ops:
  7.2 2.2 %shard_map.223 = (bf16[4,6528]{1,0:T(4,128)(2,1)}, bf16[4,6528]{1,0:T(4,128)(2,1)}, bf16[4,6528]{1,0:T(4,128)(2,1)}, bf16[4,6528]{1,0:T(4,128)(2,1)}) custom-call(s32[1,4,1,4]{3,2,1,0:T(1,128)} %send.1, s32[1,4,1,4]{3,2,1,0:T(1,128)} %recv.1, bf16[49,32,64]{2,1,0:T(8,128)(2,1)} %bitcast.61, bf16[49,32,64]{2,1,0:T(8,128)(2,1)} %bitcast.52), custom_call_target="tpu_custom_call" | custom-call | flops 1 | bytes 1 | tf_op jit(solution)/shard_map/pallas_call | solution.py:678
  9.4 3.0 %collective-permute-start = (bf16[4,6528]{1,0:T(4,128)(2,1)}, bf16[4,6528]{1,0:T(4,128)(2,1)S(1)}, u32[]{:S(2)}, u32[]{:S(2)}) collective-permute-start(bf16[4,6528]{1,0:T(4,128)(2,1)} %get-tuple-element.56), channel_id=1, source_target_pairs={{0,4},{4,0},{8,12},{12,8},{1,5},{5,1},{9,13},{13,9},{2,6},{6,2},{1... | collective-permute-start | bytes 156680 | tf_op jit(solution)/shard_map/ppermute | solution.py:773
  12.4 2.6 %collective-permute-start.1 = (bf16[4,6528]{1,0:T(4,128)(2,1)}, bf16[4,6528]{1,0:T(4,128)(2,1)S(1)}, u32[]{:S(2)}, u32[]{:S(2)}) collective-permute-start(bf16[4,6528]{1,0:T(4,128)(2,1)} %get-tuple-element.57), channel_id=1, source_target_pairs={{0,8},{4,12},{8,0},{12,4},{1,9},{5,13},{9,1},{13,5},{2,10},{6,14},... | collective-permute-start | bytes 156680 | tf_op jit(solution)/shard_map/ppermute | solution.py:773
  15.0 0.0 collective-permute-start.2
  15.0 1.2 reshape.50.adot.refs_14_
  16.3 1.7 %copy.26.rotation = bf16[256,235]{1,0:T(8,128)(2,1)} copy(bf16[256,235]{0,1:T(8,128)(2,1)} %param.22) | data formatting | bytes 240640 | tf_op args[6]
  17.9 0.0 collective-permute-done.rest_1_
  17.9 0.0 copy-start.2
  17.9 0.7 collective-permute-done.1.rest_2_
  18.7 0.0 copy-start.3
  18.7 2.5 %collective-permute-done.2.rest_3_ = bf16[4,6528]{1,0:T(4,128)(2,1)S(1)} collective-permute-done((bf16[4,6528]{1,0:T(4,128)(2,1)}, bf16[4,6528]{1,0:T(4,128)(2,1)S(1)}, u32[]{:S(2)}, u32[]{:S(2)}) %collective-permute-start.2) | collective-permute-done | bytes 52256 | tf_op jit(solution)/shard_map/ppermute | solution.py:773
  21.2 0.0 copy-start.4
  21.2 0.0 copy-done.2
  21.2 0.0 copy-done.3
  21.2 0.6 copy-done.4
  21.8 8.6 %shard_map.224 = (f32[4,4,3328]{2,1,0:T(4,128)}, f32[2,128]{1,0:T(2,128)}, bf16[448,256]{1,0:T(8,128)(2,1)}, bf16[384,512]{1,0:T(8,128)(2,1)}, bf16[320,512]{1,0...) custom-call(s32[1,256]{1,0:T(1,128)} %bitcast.66, ...), custom_call_target="tpu_custom_call" | custom-call | flops 1 | bytes 1 | tf_op jit(solution)/shard_map/pallas_call | solution.py:678
  30.4 20.3 %all-gather.1 = f32[16,2,128]{2,1,0:T(2,128)} all-gather(f32[1,2,128]{2,1,0:T(2,128)} %bitcast.68), channel_id=1, replica_groups=mesh['groups'=2,'graph'=4,'edge'=4] {'graph','edge'}, dimensions={0}, use_global_device_ids=true | all-gather | bytes 17408 | tf_op jit(solution)/shard_map/all_gather | solution.py:820
  50.7 8.5 %shard_map.225 = (bf16[448,256]{1,0:T(8,128)(2,1)}, bf16[384,512]{1,0:T(8,128)(2,1)}, bf16[320,512]{1,0:T(8,128)(2,1)}, bf16[256,256]{1,0:T(8,128)(2,1)}, f32[21...) custom-call(f32[32,128]{1,0:T(8,128)} %bitcast.62, ...), custom_call_target="tpu_custom_call" | custom-call | flops 1 | bytes 1 | tf_op jit(solution)/shard_map/pallas_call | solution.py:678
  59.2 0.4 collective-permute-start.4
  59.6 0.2 collective-permute-start.3
  59.8 3.4 %all-to-all-start = ((f32[4,4,3328]{2,1,0:T(4,128)}), f32[4,4,3328]{2,1,0:T(4,128)S(1)}, u32[]{:S(2)}, u32[]{:S(2)}) async-start(f32[4,4,3328]{2,1,0:T(4,128)} %get-tuple-element.85), calls=%async_computation | async-start | bytes 425984 | tf_op jit(solution)/shard_map/all_to_all | solution.py:763
  63.1 0.0 all-gather.4.cloned.1.call-start
  63.2 0.0 collective-permute-done.4
  63.2 1.4 add.63
  64.6 0.0 copy-start.1
  64.6 0.5 collective-permute-start.6
  65.1 0.0 collective-permute-done.3
  65.1 0.5 copy-done.1
  65.7 2.0 %collective-permute-start.5 = (f32[448,128]{1,0:T(8,128)S(1)}, f32[448,128]{1,0:T(8,128)S(1)}, u32[]{:S(2)}, u32[]{:S(2)}) collective-permute-start(f32[448,128]{1,0:T(8,128)S(1)} %dynamic-slice_bitcast_fusion.2), channel_id=1, source_target_pairs={{0,4},{4,0},{8,12},{12,8},{1,5},{5,1},{9,13},{13,9},{2,6},{6,2},{1... | collective-permute-start | bytes 688136 | tf_op jit(solution)/shard_map/ppermute | solution.py:709
  67.7 3.7 %all-to-all-done = f32[4,4,3328]{2,1,0:T(4,128)S(1)} async-done(((f32[4,4,3328]{2,1,0:T(4,128)}), f32[4,4,3328]{2,1,0:T(4,128)S(1)}, u32[]{:S(2)}, u32[]{:S(2)}) %all-to-all-start) | async-done | bytes 213024 | tf_op jit(solution)/shard_map/all_to_all | solution.py:763
  71.3 14.1 %all_gather.16.arrived = f32[16,4,3328]{2,1,0:T(4,128)} all-gather(f32[4,4,3328]{2,1,0:T(4,128)S(1)} %all-to-all-done), channel_id=1, replica_groups=mesh['groups'=2,'graph'=4,'edge'=4] {'edge'}, dimensions={0}, use_global_device_ids=true | all-gather | bytes 1064960 | tf_op jit(solution)/shard_map/all_gather | solution.py:822
  85.5 5.4 %shard_map.226 = f32[4,4,3328]{2,1,0:T(4,128)} custom-call(s32[1,256]{1,0:T(1,128)} %bitcast.67, f32[16,128]{1,0:T(8,128)} %get-tuple-element.77.lists, f32[235,256]{1,0:T(8,128)} %get-tuple-element.62.refs_4_.rot, bf16[448,256]{1,0:T(8,128)(2,1)} %get-tuple-element.78.g0, bf16[384,512]{1,0:T(8,128)(2,1)} %get-tuple-element.79.g1, ...), custom_call_target="tpu_custom_call" | custom-call | flops 1 | bytes 1 | tf_op jit(solution)/shard_map/pallas_call | solution.py:678
  90.8 0.0 collective-permute-done.5
  90.9 2.6 %collective-permute-start.8 = (f32[224,128]{1,0:T(8,128)S(1)}, f32[224,128]{1,0:T(8,128)S(1)}, u32[]{:S(2)}, u32[]{:S(2)}) collective-permute-start(f32[224,128]{1,0:T(8,128)S(1)} %dynamic-slice_bitcast_fusion.4), channel_id=1, source_target_pairs={{0,8},{4,12},{8,0},{12,4},{1,9},{5,13},{9,1},{13,5},{2,10},{6,14},... | collective-permute-start | bytes 344072 | tf_op jit(solution)/shard_map/ppermute | solution.py:709
  93.5 3.2 %shard_map.227 = (bf16[49,32,64]{2,1,0:T(8,128)(2,1)}, f32[256,128]{1,0:T(8,128)}) custom-call(bf16[49,32,64]{2,1,0:T(8,128)(2,1)} %bitcast.53, bf16[7,64,64]{2,1,0:T(8,128)(2,1)} %out_proj.3, f32[16,4,3328]{2,1,0:T(4,128)} %all_gather.16.arrived), custom_call_target="tpu_custom_call" | custom-call | flops 1 | bytes 1 | tf_op jit(solution)/shard_map/pallas_call | solution.py:678
  96.7 0.8 constant_dynamic-slice_fusion
  97.5 0.0 collective-permute-done.6
  97.5 0.1 bitcast_add_fusion
  97.7 1.5 collective-permute-start.7
  99.2 0.5 collective-permute-done.8
  99.7 0.0 copy-start
  99.8 0.5 collective-permute-start.10
  100.3 6.4 %collective-permute-done.7 = f32[576,128]{1,0:T(8,128)S(1)} collective-permute-done((f32[576,128]{1,0:T(8,128)S(1)}, f32[576,128]{1,0:T(8,128)S(1)}, u32[]{:S(2)}, u32[]{:S(2)}) %collective-permute-start.7) | collective-permute-done | bytes 294944 | tf_op jit(solution)/shard_map/ppermute | solution.py:709
  106.8 0.9 collective-permute-start.9
  107.7 0.0 collective-permute-done.10
  107.7 8.1 %collective-permute-done.9 = f32[288,128]{1,0:T(8,128)S(1)} collective-permute-done((f32[288,128]{1,0:T(8,128)S(1)}, f32[288,128]{1,0:T(8,128)S(1)}, u32[]{:S(2)}, u32[]{:S(2)}) %collective-permute-start.9) | collective-permute-done | bytes 147488 | tf_op jit(solution)/shard_map/ppermute | solution.py:709
  115.9 0.7 pad_maximum_fusion.1
  116.6 0.0 all-gather.4.cloned.1.call-update
  116.6 0.0 copy-done
  116.6 12.5 %all_to_all.10 = f32[4,4,3328]{2,1,0:T(4,128)S(1)} all-to-all(f32[4,4,3328]{2,1,0:T(4,128)S(1)} %copy-done), channel_id=1, replica_groups=mesh['groups'=2,'graph'=4,'edge'=4] {'graph'}, dimensions={0} | all-to-all | bytes 425984 | tf_op jit(solution)/shard_map/all_to_all | solution.py:763
  129.1 7.8 %all_gather.17.arrived = f32[16,4,3328]{2,1,0:T(4,128)} all-gather(f32[4,4,3328]{2,1,0:T(4,128)S(1)} %all_to_all.10), channel_id=1, replica_groups=mesh['groups'=2,'graph'=4,'edge'=4] {'edge'}, dimensions={0}, use_global_device_ids=true | all-gather | bytes 1064960 | tf_op jit(solution)/shard_map/all_gather | solution.py:887
  136.9 2.4 %shard_map.228 = bf16[49,32,64]{2,1,0:T(8,128)(2,1)} custom-call(f32[16,4,3328]{2,1,0:T(4,128)} %all_gather.17.arrived), custom_call_target="tpu_custom_call" | custom-call | flops 1 | bytes 1 | tf_op jit(solution)/shard_map/pallas_call | solution.py:678
  139.3 16.6 %all-gather.4.cloned.1.call-done = bf16[6400,128]{1,0:T(8,128)(2,1)} async-done(((bf16[400,128]{1,0:T(8,128)(2,1)}), bf16[6400,128]{1,0:T(8,128)(2,1)}) %all-gather.4.cloned.1.call-update) | async-done | bytes 1638416 | tf_op jit(solution)/shard_map/all_gather | solution.py:891
  155.9 2.8 %shard_map.229 = (bf16[448,448]{1,0:T(8,128)(2,1)}, bf16[2,384,384]{2,1,0:T(8,128)(2,1)}, bf16[2,320,320]{2,1,0:T(8,128)(2,1)}, bf16[64,256]{1,0:T(8,128)(2,1)},...) custom-call(bf16[16,400,128]{2,1,0:T(8,128)(2,1)} %bitcast.51), custom_call_target="tpu_custom_call" | custom-call | flops 1 | bytes 1 | tf_op jit(solution)/shard_map/pallas_call | solution.py:678
  (13 shorter events, 0.4 us)
Async XLA Ops:
  9.4 8.5 %collective-permute-start = (bf16[4,6528]{1,0:T(4,128)(2,1)}, bf16[4,6528]{1,0:T(4,128)(2,1)S(1)}, u32[]{:S(2)}, u32[]{:S(2)}) collective-permute-start(bf16[4,6528]{1,0:T(4,128)(2,1)} %get-tuple-element.56), channel_id=1, source_target_pairs={{0,4},{4,0},{8,12},{12,8},{1,5},{5,1},{9,13},{13,9},{2,6},{6,2},{1... | collective-permute-start | bytes 156680 | tf_op jit(solution)/shard_map/ppermute | solution.py:773
  12.4 6.2 %collective-permute-start.1 = (bf16[4,6528]{1,0:T(4,128)(2,1)}, bf16[4,6528]{1,0:T(4,128)(2,1)S(1)}, u32[]{:S(2)}, u32[]{:S(2)}) collective-permute-start(bf16[4,6528]{1,0:T(4,128)(2,1)} %get-tuple-element.57), channel_id=1, source_target_pairs={{0,8},{4,12},{8,0},{12,4},{1,9},{5,13},{9,1},{13,5},{2,10},{6,14},... | collective-permute-start | bytes 156680 | tf_op jit(solution)/shard_map/ppermute | solution.py:773
  15.0 6.1 %collective-permute-start.2 = (bf16[4,6528]{1,0:T(4,128)(2,1)}, bf16[4,6528]{1,0:T(4,128)(2,1)S(1)}, u32[]{:S(2)}, u32[]{:S(2)}) collective-permute-start(bf16[4,6528]{1,0:T(4,128)(2,1)} %get-tuple-element.58), channel_id=1, source_target_pairs={{0,12},{4,8},{8,4},{12,0},{1,13},{5,9},{9,5},{13,1},{2,14},{6,10},... | collective-permute-start | bytes 156680 | tf_op jit(solution)/shard_map/ppermute | solution.py:773
  17.9 3.2 %copy-start.2 = (bf16[4,6528]{1,0:T(4,128)(2,1)}, bf16[4,6528]{1,0:T(4,128)(2,1)S(1)}, u32[]{:S(2)}) copy-start(bf16[4,6528]{1,0:T(4,128)(2,1)S(1)} %collective-permute-done.rest_1_) | copy-start | bytes 156676
  18.7 2.5 %copy-start.3 = (bf16[4,6528]{1,0:T(4,128)(2,1)}, bf16[4,6528]{1,0:T(4,128)(2,1)S(1)}, u32[]{:S(2)}) copy-start(bf16[4,6528]{1,0:T(4,128)(2,1)S(1)} %collective-permute-done.1.rest_2_) | copy-start | bytes 156676
  21.2 0.6 copy-start.4
  59.2 4.0 %collective-permute-start.4 = (f32[2176,128]{1,0:T(8,128)}, f32[2176,128]{1,0:T(8,128)S(1)}, u32[]{:S(2)}, u32[]{:S(2)}) collective-permute-start(f32[2176,128]{1,0:T(8,128)} %get-tuple-element.74), channel_id=1, source_target_pairs={{0,1},{1,0},{2,3},{3,2},{4,5},{5,4},{6,7},{7,6},{8,9},{9,8},{10,11... | collective-permute-start | bytes 3342344 | tf_op jit(solution)/shard_map/ppermute | solution.py:709
  59.6 5.6 %collective-permute-start.3 = (f32[896,128]{1,0:T(8,128)}, f32[896,128]{1,0:T(8,128)S(1)}, u32[]{:S(2)}, u32[]{:S(2)}) collective-permute-start(f32[896,128]{1,0:T(8,128)} %get-tuple-element.72), channel_id=1, source_target_pairs={{0,1},{1,0},{2,3},{3,2},{4,5},{5,4},{6,7},{7,6},{8,9},{9,8},{10,11... | collective-permute-start | bytes 1376264 | tf_op jit(solution)/shard_map/ppermute | solution.py:709
  59.8 11.6 %all-to-all-start = ((f32[4,4,3328]{2,1,0:T(4,128)}), f32[4,4,3328]{2,1,0:T(4,128)S(1)}, u32[]{:S(2)}, u32[]{:S(2)}) async-start(f32[4,4,3328]{2,1,0:T(4,128)} %get-tuple-element.85), calls=%async_computation | async-start | bytes 425984 | tf_op jit(solution)/shard_map/all_to_all | solution.py:763
  63.1 92.8 %all-gather.4.cloned.1.call-start = ((), (), s32[]{:S(2)}) async-start(), calls=%async_computation.2 | async-start | bytes 1740800 | tf_op jit(solution)/shard_map/all_gather | solution.py:891
  64.6 1.0 copy-start.1
  64.6 32.9 %collective-permute-start.6 = (f32[1088,128]{1,0:T(8,128)S(1)}, f32[1088,128]{1,0:T(8,128)S(1)}, u32[]{:S(2)}, u32[]{:S(2)}) collective-permute-start(f32[1088,128]{1,0:T(8,128)S(1)} %dynamic-slice_bitcast_fusion), channel_id=1, source_target_pairs={{0,2},{1,3},{2,0},{3,1},{4,6},{5,7},{6,4},{7,5},{8,10},{9,11},{10,... | collective-permute-start | bytes 1671176 | tf_op jit(solution)/shard_map/ppermute | solution.py:709
  65.7 25.2 %collective-permute-start.5 = (f32[448,128]{1,0:T(8,128)S(1)}, f32[448,128]{1,0:T(8,128)S(1)}, u32[]{:S(2)}, u32[]{:S(2)}) collective-permute-start(f32[448,128]{1,0:T(8,128)S(1)} %dynamic-slice_bitcast_fusion.2), channel_id=1, source_target_pairs={{0,4},{4,0},{8,12},{12,8},{1,5},{5,1},{9,13},{13,9},{2,6},{6,2},{1... | collective-permute-start | bytes 688136 | tf_op jit(solution)/shard_map/ppermute | solution.py:709
  90.9 8.8 %collective-permute-start.8 = (f32[224,128]{1,0:T(8,128)S(1)}, f32[224,128]{1,0:T(8,128)S(1)}, u32[]{:S(2)}, u32[]{:S(2)}) collective-permute-start(f32[224,128]{1,0:T(8,128)S(1)} %dynamic-slice_bitcast_fusion.4), channel_id=1, source_target_pairs={{0,8},{4,12},{8,0},{12,4},{1,9},{5,13},{9,1},{13,5},{2,10},{6,14},... | collective-permute-start | bytes 344072 | tf_op jit(solution)/shard_map/ppermute | solution.py:709
  97.7 9.0 %collective-permute-start.7 = (f32[576,128]{1,0:T(8,128)S(1)}, f32[576,128]{1,0:T(8,128)S(1)}, u32[]{:S(2)}, u32[]{:S(2)}) collective-permute-start(f32[576,128]{1,0:T(8,128)S(1)} %dynamic-slice_bitcast_fusion.1), channel_id=1, source_target_pairs={{0,4},{4,0},{8,12},{12,8},{1,5},{5,1},{9,13},{13,9},{2,6},{6,2},{1... | collective-permute-start | bytes 884744 | tf_op jit(solution)/shard_map/ppermute | solution.py:709
  99.7 16.8 %copy-start = (f32[4,4,3328]{2,1,0:T(4,128)S(1)}, f32[4,4,3328]{2,1,0:T(4,128)}, u32[]{:S(2)}) copy-start(f32[4,4,3328]{2,1,0:T(4,128)} %shard_map.226) | copy-start | bytes 638980
  99.8 7.9 %collective-permute-start.10 = (f32[112,128]{1,0:T(8,128)S(1)}, f32[112,128]{1,0:T(8,128)S(1)}, u32[]{:S(2)}, u32[]{:S(2)}) collective-permute-start(f32[112,128]{1,0:T(8,128)S(1)} %dynamic-slice_bitcast_fusion.5), channel_id=1, source_target_pairs={{0,2},{1,3},{2,0},{3,1},{4,6},{5,7},{6,4},{7,5},{8,10},{9,11},{10,... | collective-permute-start | bytes 172040 | tf_op jit(solution)/shard_map/ppermute | solution.py:709
  106.8 9.1 %collective-permute-start.9 = (f32[288,128]{1,0:T(8,128)S(1)}, f32[288,128]{1,0:T(8,128)S(1)}, u32[]{:S(2)}, u32[]{:S(2)}) collective-permute-start(f32[288,128]{1,0:T(8,128)S(1)} %dynamic-slice_bitcast_fusion.3), channel_id=1, source_target_pairs={{0,8},{4,12},{8,0},{12,4},{1,9},{5,13},{9,1},{13,5},{2,10},{6,14},... | collective-permute-start | bytes 442376 | tf_op jit(solution)/shard_map/ppermute | solution.py:709
Sparse Core Ops, SparseCore 0:
  116.7 39.1 all-gather.3

commit v7 on v5

--- a/solution.py
+++ b/solution.py
@@ -585,40 +585,44 @@
     return jnp.where(first, left, right), jnp.where(first, right, left)
 
 
-def unpack_zero_kernel(mine, other, zero):
-    left, right = halves_of(mine, other)
-    zero[:, pl.ds(0, LANES)] = left[:DIM0].astype(bf16)
-    zero[:, pl.ds(LANES, LANES)] = right[:DIM0].astype(bf16)
-    zero[:, pl.ds(2 * LANES, LANES)] = left[DIM0:].astype(bf16)
-    zero[:, pl.ds(3 * LANES, DIM0 - 3 * LANES)] = right[DIM0:, : DIM0 - 3 * LANES].astype(bf16)
-
-
-def make_unpack_rest(lanes_total):
-    def unpack_rest_kernel(mine, other, one, two, alpha_in, alpha_edge, alpha_dot, proj):
-        left, right = halves_of(mine, other)
-        parts = lanes_total // 2
+def reversed_bits(value, count):
+    return sum(((value >> n) & 1) << (count - 1 - n) for n in range(count))
+
+
+def make_unpack(lanes_total, peers):
+    def unpack_kernel(mine, other, zero, one, two, alpha_in, alpha_edge, alpha_dot, proj):
+        cols = lanes_total // 2
+        col_bits = (cols - 1).bit_length()
         late = PROJ_ROWS // lanes_total
-        size = left.shape[0] // parts - late
-        tail = jnp.concatenate(
-            [
-                value[n * (size + late) + size : (n + 1) * (size + late)]
-                for value in (left, right)
-                for n in range(parts)
-            ],
-            axis=0,
-        )
+        own_rows = CHUNKS[0][1] // cols
+        first_rows = (own_rows + late) // peers
+        share = first_rows + CHUNKS[1][1] // (cols * peers)
+        main, zeros, tail = [], [], {}
+        for core, value in enumerate(halves_of(mine, other)):
+            parts, zero_parts = [], {}
+            for col in range(cols):
+                rows = []
+                for peer in range(peers):
+                    start = (col * peers + peer) * share
+                    rows.append(value[start : start + first_rows])
+                    zero_parts[peer * cols + col] = value[start + first_rows : start + share]
+                rows = jnp.concatenate(rows, axis=0)
+                parts.append(rows[:own_rows])
+                tail[core * cols + reversed_bits(col, col_bits)] = rows[own_rows:]
+            main.append(jnp.concatenate(parts, axis=0))
+            zeros.append(jnp.concatenate([zero_parts[n] for n in sorted(zero_parts)], axis=0))
+        tail = jnp.concatenate([tail[n] for n in sorted(tail)], axis=0)
         for degree in range(LMAX + 1):
             piece = tail[degree // 2 * CH : (degree // 2 + 1) * CH]
             proj[degree] = piece[:, degree % 2 * CH : (degree % 2 + 1) * CH].astype(bf16)
-        left, right = (
-            jnp.concatenate(
-                [value[n * (size + late) : n * (size + late) + size] for n in range(parts)], axis=0
-            )
-            for value in (left, right)
-        )
-        unpack_rest(left, right, one, two, alpha_in, alpha_edge, alpha_dot)
-
-    return unpack_rest_kernel
+        left, right = zeros
+        zero[:, pl.ds(0, LANES)] = left[:DIM0].astype(bf16)
+        zero[:, pl.ds(LANES, LANES)] = right[:DIM0].astype(bf16)
+        zero[:, pl.ds(2 * LANES, LANES)] = left[DIM0:].astype(bf16)
+        zero[:, pl.ds(3 * LANES, DIM0 - 3 * LANES)] = right[DIM0:, : DIM0 - 3 * LANES].astype(bf16)
+        unpack_rest(*main, one, two, alpha_in, alpha_edge, alpha_dot)
+
+    return unpack_kernel
 
 
 def unpack_rest(left, right, one, two, alpha_in, alpha_edge, alpha_dot):
@@ -730,10 +734,14 @@
     return (lax.axis_size(axis) - 1).bit_length()
 
 
-def gather_lanes(value):
+def gather_lanes(value, order):
     held = {0: value}
     for bit in reversed(range(bits_of("edge"))):
-        held.update({k | (1 << bit): swap(v, "edge", bit) for k, v in list(held.items())})
+        fresh = {}
+        for k, v in held.items():
+            fresh[k | (1 << bit)] = swap(order.hold(v) if k else v, "edge", bit)
+        held.update(fresh)
+        yield
     return [held[k] for k in range(len(held))]
 
 
@@ -741,14 +749,17 @@
     return (lax.axis_index(axis) >> bit) & 1
 
 
-def sum_all(kept, sent, first, order, late=None):
+def share_steps(first):
     steps = [("edge", n) for n in range(1, bits_of("edge"))]
     steps += [("graph", n) for n in range(bits_of("graph"))]
-    steps.sort(key=lambda step: step[0] != first)
+    return sorted(steps, key=lambda step: step[0] != first)
+
+
+def halve(kept, sent, first, order, late=None):
     other = swap(sent, "edge", 0)
     yield
     current = kept + order.hold(other)
-    for n, (axis, bit) in enumerate(steps):
+    for n, (axis, bit) in enumerate(share_steps(first)):
         if late is not None and n == bits_of("edge") - 1:
             current = jnp.concatenate([current, late[0]], axis=0)
         mine = own_bit(axis, bit)
@@ -757,8 +768,11 @@
         other = swap(sent, axis, bit)
         yield
         current = lax.dynamic_index_in_dim(parts, mine, 0, False) + order.hold(other)
-    current = order.mark(current.astype(bf16))
-    for axis, bit in reversed(steps):
+    return order.mark(current.astype(bf16))
+
+
+def double(current, order):
+    for axis, bit in reversed(share_steps("edge")):
         mine = own_bit(axis, bit)
         other = swap(current, axis, bit)
         yield
@@ -769,9 +783,7 @@
                 axis=0,
             )
         )
-    other = swap(current, "edge", 0)
-    yield
-    return current, other
+    return current, swap(current, "edge", 0)
 
 
 def finish_steps(chain):
@@ -867,9 +879,6 @@
         ]
     else:
         all_stats = [lax.all_gather(stats, ("graph", "edge"), tiled=True)]
-    messages = exchange(sums)
-    order.mark(messages)
-    message_rows = gather_lanes(messages)
 
     halves = [((size, LANES), f32) for start, size in CHUNKS for _ in range(2)]
     g0, g1, g2, pre_grad, *halves = call(
@@ -891,21 +900,23 @@
         ]
         + frames
         + [pltpu.SemaphoreType.DMA((10,))],
-        *all_stats, order.hold(own_stats), agg_grad, target_row, rot, edge_feats,
+        *all_stats, own_stats, agg_grad, target_row, rot, edge_feats,
         x0, x1, x2, v0, v1, v2, pre, logits, adot,
         far=range(len(all_stats) + 5, len(all_stats) + 11), apart=range(4, 8)
     )
 
     total = lanes_total * slots
     order.mark(halves[0])
-    message_rows = [order.hold(message_rows[0])] + message_rows[1:]
+    messages = exchange(order.hold(sums))
     late = []
-    rest_steps = sum_all(halves[0], halves[1], "edge", order, late)
-    zero_steps = sum_all(halves[2], halves[3], "graph", order)
+    rest_steps = halve(halves[0], halves[1], "edge", order, late)
+    zero_steps = halve(halves[2], halves[3], "graph", order)
     next(rest_steps)
     next(zero_steps)
     next(rest_steps)
     next(zero_steps)
+    message_hops = gather_lanes(order.hold(messages), order)
+    next(message_hops)
     (source_sums,) = call(
         source_kernel,
         [((peers, cap, WIDE), f32)],
@@ -921,6 +932,7 @@
     order.mark(source_sums)
     returned = exchange(source_sums)
     next(zero_steps)
+    message_rows = finish_steps(message_hops)
     out, proj = call(
         make_finish(lanes_total),
         [((COEFFS, atoms, CH), bf16), ((PROJ_ROWS, LANES), f32)],
@@ -934,11 +946,17 @@
     late.append(lax.dynamic_slice_in_dim(proj, place, late_rows, 0))
     for _ in range(bits_of("edge") - 1):
         next(rest_steps)
-    next(zero_steps)
-    source_rows = gather_lanes(order.hold(returned))
+    source_hops = gather_lanes(order.mark(order.hold(returned)), order)
+    next(source_hops)
     next(zero_steps)
     next(rest_steps)
-    next(zero_steps)
+    zero_share = finish_steps(zero_steps)
+    source_rows = finish_steps(source_hops)
+    share = jnp.concatenate([finish_steps(rest_steps), zero_share], axis=0)
+    doubling = double(order.mark(share), order)
+    next(doubling)
+    for _ in share_steps("edge")[1:]:
+        next(doubling)
     (embed,) = call(
         make_collect(lanes_total),
         [((COEFFS, atoms, CH), bf16)],
@@ -946,20 +964,11 @@
         order.hold(source_rows[0]), *source_rows[1:],
     )
     order.mark(embed)
-    next(rest_steps)
-    next(zero_steps)
-    next(rest_steps)
-    next(zero_steps)
-    next(rest_steps)
-    zero_pair = finish_steps(zero_steps)
-    (zero,) = call(
-        unpack_zero_kernel, [((DIM0, DIM0), bf16)], [], order.hold(zero_pair[0]), zero_pair[1]
-    )
-    order.mark(zero)
-    rest_pair = finish_steps(rest_steps)
-    one, two, grad_in, grad_edge, grad_dot, grad_proj = call(
-        make_unpack_rest(lanes_total),
+    mine, other = finish_steps(doubling)
+    zero, one, two, grad_in, grad_edge, grad_dot, grad_proj = call(
+        make_unpack(lanes_total, peers),
         [
+            ((DIM0, DIM0), bf16),
             ((2, DIM1, DIM1), bf16),
             ((2, DIM2, DIM2), bf16),
             (alpha_in.shape, bf16),
@@ -967,7 +976,8 @@
             ((2, LANES), bf16),
             (out_proj.shape, bf16),
         ],
-        [], order.hold(rest_pair[0]), rest_pair[1]
+        [],
+        mine, other,
     )
 
     def shaped(value):

time: 136 us -> 131 us (0.963)
  starting transfers between devices: 34.3 us -> 31.7 us
  other arithmetic: 3.68 us -> 5.57 us
  Pallas kernels: 35 us -> 33.5 us
  waiting for transfers between devices: 51.2 us -> 49.8 us
    all_to_all x2, waiting for transfers between devices: 0.01 us -> 5.04 us  [exchange(): lax.all_to_all(value, 'graph', split_axis=0, concat_axis=0, tiled=True)]
    ppermute x22 -> x18, waiting for transfers between devices: 40.1 us -> 36.1 us  [swap(): return lax.ppermute(value, axis, [(i, i ^ 1 << bit) for i in range(size)])]
    ppermute x22 -> x18, starting transfers between devices: 15.4 us -> 12.1 us  [swap(): return lax.ppermute(value, axis, [(i, i ^ 1 << bit) for i in range(size)])]
    ppermute x3, waiting for transfers between devices: 5.04 us -> 2.52 us  [shards(): lax.ppermute(graph_stats, 'graph', [(i, i ^ k) for i in range(peers)])]
    add x6, other arithmetic: 2.57 us -> 4.4 us  [the longest x2 2.43 us: halve(): current = kept + order.hold(other)]
    pallas_call x8 -> x7, Pallas kernels: 35 us -> 33.5 us  [call(): pl.pallas_call(kernel, out_shape=[jax.ShapeDtypeStruct(shape, kind) for s...]
    unnamed x37 -> x35, local copies, waits for them, and re-layouts: 6.7 us -> 6.46 us
  transfers between devices with their start and end apart: 33 -> 29, of which waited for: 20 -> 17; matrix products, arithmetic and copies ran while one was open for 5% -> 6% of each run, Pallas kernels for 10% -> 9%
where the time goes in v7:
time: 131 us; the launch traced here: 130 us
  waiting for transfers between devices  49.8 us (38%)
  Pallas kernels  33.5 us (26%)
  starting transfers between devices  31.7 us (24%)
  local copies, waits for them, and re-layouts  8.61 us (7%)
  other arithmetic  5.57 us (4%)
    ppermute x18, waiting for transfers between devices, swap(): return lax.ppermute(value, axis, [(i, i ^ 1 << bit) for i in range(size)])  36.1 us
    pallas_call x7, Pallas kernels, call(): pl.pallas_call(kernel, out_shape=[jax.ShapeDtypeStruct(shape, kind) for s...  33.5 us
    ppermute x18, starting transfers between devices, swap(): return lax.ppermute(value, axis, [(i, i ^ 1 << bit) for i in range(size)])  12.1 us
    all_to_all x2, starting transfers between devices, exchange(): lax.all_to_all(value, 'graph', split_axis=0, concat_axis=0, tiled=True)  7.52 us
    unnamed x35, local copies, waits for them, and re-layouts  6.46 us
    ppermute x3, starting transfers between devices, shards(): lax.ppermute(outgoing[k], 'graph', [(i, i ^ k) for i in range(peers)])  5.62 us
    all_to_all x2, waiting for transfers between devices, exchange(): lax.all_to_all(value, 'graph', split_axis=0, concat_axis=0, tiled=True)  5.04 us
    ppermute x3, starting transfers between devices, shards(): lax.ppermute(graph_stats, 'graph', [(i, i ^ k) for i in range(peers)])  4.44 us
  transfers between devices with their start and end apart: 29, of which 17 were waited for; matrix products, arithmetic and copies ran while one was open for 6% of the time, Pallas kernels for 9%

profile of v7, /device:TPU:0, one launch (start us, length us, event | category | flops | bytes accessed | tf_op | source)
XLA Modules:
  0.0 130.1 jit_solution(12721521069226483623)
XLA Ops:
  0.6 2.2 %shard_map.223 = (bf16[4,6528]{1,0:T(4,128)(2,1)}, bf16[4,6528]{1,0:T(4,128)(2,1)}, bf16[4,6528]{1,0:T(4,128)(2,1)}, bf16[4,6528]{1,0:T(4,128)(2,1)}) custom-call(s32[1,4,1,4]{3,2,1,0:T(1,128)} %send.1, s32[1,4,1,4]{3,2,1,0:T(1,128)} %recv.1, bf16[49,32,64]{2,1,0:T(8,128)(2,1)} %bitcast.57, bf16[49,32,64]{2,1,0:T(8,128)(2,1)} %bitcast.48), custom_call_target="tpu_custom_call" | custom-call | flops 1 | bytes 1 | tf_op jit(solution)/shard_map/pallas_call | solution.py:699
  2.9 3.0 %collective-permute-start = (bf16[4,6528]{1,0:T(4,128)(2,1)}, bf16[4,6528]{1,0:T(4,128)(2,1)S(1)}, u32[]{:S(2)}, u32[]{:S(2)}) collective-permute-start(bf16[4,6528]{1,0:T(4,128)(2,1)} %get-tuple-element.64), channel_id=1, source_target_pairs={{0,4},{4,0},{8,12},{12,8},{1,5},{5,1},{9,13},{13,9},{2,6},{6,2},{1... | collective-permute-start | bytes 156680 | tf_op jit(solution)/shard_map/ppermute | solution.py:823
  5.9 2.6 %collective-permute-start.1 = (bf16[4,6528]{1,0:T(4,128)(2,1)}, bf16[4,6528]{1,0:T(4,128)(2,1)S(1)}, u32[]{:S(2)}, u32[]{:S(2)}) collective-permute-start(bf16[4,6528]{1,0:T(4,128)(2,1)} %get-tuple-element.65), channel_id=1, source_target_pairs={{0,8},{4,12},{8,0},{12,4},{1,9},{5,13},{9,1},{13,5},{2,10},{6,14},... | collective-permute-start | bytes 156680 | tf_op jit(solution)/shard_map/ppermute | solution.py:823
  8.5 1.2 reshape.50.adot.refs_17_
  9.7 1.7 %copy.25.rotation = bf16[256,235]{1,0:T(8,128)(2,1)} copy(bf16[256,235]{0,1:T(8,128)(2,1)} %param.22) | data formatting | bytes 240640 | tf_op args[6]
  11.4 0.7 collective-permute-done.1.rest_2_
  12.2 2.5 %collective-permute-done.2.rest_3_ = bf16[4,6528]{1,0:T(4,128)(2,1)S(1)} collective-permute-done((bf16[4,6528]{1,0:T(4,128)(2,1)}, bf16[4,6528]{1,0:T(4,128)(2,1)S(1)}, u32[]{:S(2)}, u32[]{:S(2)}) %collective-permute-start.2) | collective-permute-done | bytes 52256 | tf_op jit(solution)/shard_map/ppermute | solution.py:823
  14.6 0.6 copy-done.12
  15.3 8.5 %shard_map.224 = (f32[4,4,3328]{2,1,0:T(4,128)}, f32[2,128]{1,0:T(2,128)}, bf16[448,256]{1,0:T(8,128)(2,1)}, bf16[384,512]{1,0:T(8,128)(2,1)}, bf16[320,512]{1,0...) custom-call(s32[1,256]{1,0:T(1,128)} %bitcast.61, ...), custom_call_target="tpu_custom_call" | custom-call | flops 1 | bytes 1 | tf_op jit(solution)/shard_map/pallas_call | solution.py:699
  23.9 1.6 %collective-permute-start.4 = (f32[2,128]{1,0:T(2,128)}, f32[2,128]{1,0:T(2,128)S(1)}, u32[]{:S(2)}, u32[]{:S(2)}) collective-permute-start(f32[2,128]{1,0:T(2,128)} %get-tuple-element.67), channel_id=1, source_target_pairs={{0,2},{1,3},{2,0},{3,1},{4,6},{5,7},{6,4},{7,5},{8,10},{9,11},{10,... | collective-permute-start | bytes 3080 | tf_op jit(solution)/shard_map/ppermute | solution.py:872
  25.4 0.3 collective-permute-start.5
  25.7 2.0 %collective-permute-done.4 = f32[2,128]{1,0:T(2,128)S(1)} collective-permute-done((f32[2,128]{1,0:T(2,128)}, f32[2,128]{1,0:T(2,128)S(1)}, u32[]{:S(2)}, u32[]{:S(2)}) %collective-permute-start.4) | collective-permute-done | bytes 1056 | tf_op jit(solution)/shard_map/ppermute | solution.py:872
  27.7 0.9 collective-permute-done.5
  28.6 0.7 pad_maximum_fusion.5.refs_0_
  29.4 1.5 %collective-permute-start.7 = (f32[8,128]{1,0:T(8,128)S(1)}, f32[8,128]{1,0:T(8,128)S(1)}, u32[]{:S(2)}, u32[]{:S(2)}) collective-permute-start(f32[8,128]{1,0:T(8,128)S(1)} %pad_maximum_fusion.5.refs_0_), channel_id=1, source_target_pairs={{0,8},{4,12},{8,0},{12,4},{1,9},{5,13},{9,1},{13,5},{2,10},{6,14},... | collective-permute-start | bytes 12296 | tf_op jit(solution)/shard_map/ppermute | solution.py:877
  30.9 2.9 %collective-permute-start.8 = (f32[8,128]{1,0:T(8,128)S(1)}, f32[8,128]{1,0:T(8,128)S(1)}, u32[]{:S(2)}, u32[]{:S(2)}) collective-permute-start(f32[8,128]{1,0:T(8,128)S(1)} %pad_maximum_fusion.5.refs_0_), channel_id=1, source_target_pairs={{0,12},{4,8},{8,4},{12,0},{1,13},{5,9},{9,5},{13,1},{2,14},{6,10},... | collective-permute-start | bytes 12296 | tf_op jit(solution)/shard_map/ppermute | solution.py:877
  33.8 0.2 collective-permute-done.7.refs_2_
  34.0 2.3 %collective-permute-done.8.refs_3_ = f32[8,128]{1,0:T(8,128)S(1)} collective-permute-done((f32[8,128]{1,0:T(8,128)S(1)}, f32[8,128]{1,0:T(8,128)S(1)}, u32[]{:S(2)}, u32[]{:S(2)}) %collective-permute-start.8) | collective-permute-done | bytes 4128 | tf_op jit(solution)/shard_map/ppermute | solution.py:877
  36.3 0.6 copy-done.16
  36.9 8.5 %shard_map.225 = (bf16[448,256]{1,0:T(8,128)(2,1)}, bf16[384,512]{1,0:T(8,128)(2,1)}, bf16[320,512]{1,0:T(8,128)(2,1)}, bf16[256,256]{1,0:T(8,128)(2,1)}, f32[21...) custom-call(f32[8,128]{1,0:T(8,128)} %copy-done.13, f32[8,128]{1,0:T(8,128)} %copy-done.14, ...), custom_call_target="tpu_custom_call" | custom-call | flops 1 | bytes 1 | tf_op jit(solution)/shard_map/pallas_call | solution.py:699
  45.5 0.5 collective-permute-start.9
  46.0 4.1 %all-to-all-start = ((f32[4,4,3328]{2,1,0:T(4,128)}), f32[4,4,3328]{2,1,0:T(4,128)S(1)}, u32[]{:S(2)}, u32[]{:S(2)}) async-start(f32[4,4,3328]{2,1,0:T(4,128)} %get-tuple-element.94), calls=%async_computation | async-start | bytes 425984 | tf_op jit(solution)/shard_map/all_to_all | solution.py:813
  50.1 1.4 %add.63 = f32[2176,128]{1,0:T(8,128)S(1)} add(f32[2176,128]{1,0:T(8,128)} %get-tuple-element.81, f32[2176,128]{1,0:T(8,128)S(1)} %collective-permute-done.10) | non-fusion elementwise | flops 278528 | bytes 3342336 | tf_op jit(solution)/shard_map/add | solution.py:761
  51.6 0.9 copy-done.4
  52.5 1.1 add.65
  53.6 2.1 %collective-permute-start.11 = (f32[448,128]{1,0:T(8,128)S(1)}, f32[448,128]{1,0:T(8,128)}, u32[]{:S(2)}, u32[]{:S(2)}) collective-permute-start(f32[448,128]{1,0:T(8,128)S(1)} %dynamic-slice_bitcast_fusion.2), channel_id=1, source_target_pairs={{0,4},{4,0},{8,12},{12,8},{1,5},{5,1},{9,13},{13,9},{2,6},{6,2},{1... | collective-permute-start | bytes 688136 | tf_op jit(solution)/shard_map/ppermute | solution.py:730
  55.7 2.6 %all-to-all-done.rest_0_ = f32[4,4,3328]{2,1,0:T(4,128)S(1)} async-done(((f32[4,4,3328]{2,1,0:T(4,128)}), f32[4,4,3328]{2,1,0:T(4,128)S(1)}, u32[]{:S(2)}, u32[]{:S(2)}) %all-to-all-start) | async-done | bytes 213024 | tf_op jit(solution)/shard_map/all_to_all | solution.py:813
  58.3 0.6 collective-permute-start.13
  58.9 1.4 %collective-permute-start.15 = (f32[1088,128]{1,0:T(8,128)S(1)}, f32[1088,128]{1,0:T(8,128)S(1)}, u32[]{:S(2)}, u32[]{:S(2)}) collective-permute-start(f32[1088,128]{1,0:T(8,128)S(1)} %dynamic-slice_bitcast_fusion), channel_id=1, source_target_pairs={{0,2},{1,3},{2,0},{3,1},{4,6},{5,7},{6,4},{7,5},{8,10},{9,11},{10,... | collective-permute-start | bytes 1671176 | tf_op jit(solution)/shard_map/ppermute | solution.py:730
  60.4 5.4 %shard_map.226 = f32[4,4,3328]{2,1,0:T(4,128)} custom-call(s32[1,256]{1,0:T(1,128)} %bitcast.62, f32[16,128]{1,0:T(8,128)} %get-tuple-element.85.lists, f32[235,256]{1,0:T(8,128)} %get-tuple-element.70.refs_7_.rot, bf16[448,256]{1,0:T(8,128)(2,1)} %get-tuple-element.86.g0, bf16[384,512]{1,0:T(8,128)(2,1)} %get-tuple-element.87.g1, ...), custom_call_target="tpu_custom_call" | custom-call | flops 1 | bytes 1 | tf_op jit(solution)/shard_map/pallas_call | solution.py:699
  65.8 1.0 bitcast_add_fusion.2
  66.8 0.3 collective-permute-start.14
  67.1 3.4 %all-to-all-start.1 = ((f32[4,4,3328]{2,1,0:T(4,128)}), f32[4,4,3328]{2,1,0:T(4,128)S(1)}, u32[]{:S(2)}, u32[]{:S(2)}) async-start(f32[4,4,3328]{2,1,0:T(4,128)} %shard_map.226), calls=%async_computation.1 | async-start | bytes 425984 | tf_op jit(solution)/shard_map/all_to_all | solution.py:813
  70.5 2.9 %collective-permute-start.17 = (f32[224,128]{1,0:T(8,128)S(1)}, f32[224,128]{1,0:T(8,128)}, u32[]{:S(2)}, u32[]{:S(2)}) collective-permute-start(f32[224,128]{1,0:T(8,128)S(1)} %dynamic-slice_bitcast_fusion.4), channel_id=1, source_target_pairs={{0,8},{4,12},{8,0},{12,4},{1,9},{5,13},{9,1},{13,5},{2,10},{6,14},... | collective-permute-start | bytes 344072 | tf_op jit(solution)/shard_map/ppermute | solution.py:730
  73.4 0.7 copy-done.9
  74.1 3.3 %shard_map.227 = (bf16[49,32,64]{2,1,0:T(8,128)(2,1)}, f32[256,128]{1,0:T(8,128)}) custom-call(bf16[49,32,64]{2,1,0:T(8,128)(2,1)} %bitcast.49, bf16[7,64,64]{2,1,0:T(8,128)(2,1)} %out_proj.3, f32[4,4,3328]{2,1,0:T(4,128)} %copy-done.2, f32[4,4,3328]{2,1,0:T(4,128)} %collective-permute-done.12.rest_1_, f32[4,4,3328]{2,1,0:T(4,128)} %copy-done.8, ...), custom_call_target="tpu_custom_call" | custom-call | flops 1 | bytes 1 | tf_op jit(solution)/shard_map/pallas_call | solution.py:699
  77.4 0.8 constant_dynamic-slice_fusion
  78.3 1.5 %collective-permute-start.16 = (f32[576,128]{1,0:T(8,128)S(1)}, f32[576,128]{1,0:T(8,128)S(1)}, u32[]{:S(2)}, u32[]{:S(2)}) collective-permute-start(f32[576,128]{1,0:T(8,128)S(1)} %dynamic-slice_bitcast_fusion.1), channel_id=1, source_target_pairs={{0,4},{4,0},{8,12},{12,8},{1,5},{5,1},{9,13},{13,9},{2,6},{6,2},{1... | collective-permute-start | bytes 884744 | tf_op jit(solution)/shard_map/ppermute | solution.py:730
  79.8 2.4 %all-to-all-done.1.rest_0_ = f32[4,4,3328]{2,1,0:T(4,128)S(1)} async-done(((f32[4,4,3328]{2,1,0:T(4,128)}), f32[4,4,3328]{2,1,0:T(4,128)S(1)}, u32[]{:S(2)}, u32[]{:S(2)}) %all-to-all-start.1) | async-done | bytes 213024 | tf_op jit(solution)/shard_map/all_to_all | solution.py:813
  82.2 1.9 %collective-permute-done.17 = f32[224,128]{1,0:T(8,128)} collective-permute-done((f32[224,128]{1,0:T(8,128)S(1)}, f32[224,128]{1,0:T(8,128)}, u32[]{:S(2)}, u32[]{:S(2)}) %collective-permute-start.17) | collective-permute-done | bytes 114720 | tf_op jit(solution)/shard_map/ppermute | solution.py:730
  84.1 0.9 bitcast_add_fusion.4
  85.0 0.6 collective-permute-start.19
  85.7 3.9 %collective-permute-done.16 = f32[576,128]{1,0:T(8,128)S(1)} collective-permute-done((f32[576,128]{1,0:T(8,128)S(1)}, f32[576,128]{1,0:T(8,128)S(1)}, u32[]{:S(2)}, u32[]{:S(2)}) %collective-permute-start.16) | collective-permute-done | bytes 294944 | tf_op jit(solution)/shard_map/ppermute | solution.py:730
  89.7 0.1 collective-permute-start.18
  89.8 9.0 %collective-permute-done.18 = f32[288,128]{1,0:T(8,128)S(1)} collective-permute-done((f32[288,128]{1,0:T(8,128)S(1)}, f32[288,128]{1,0:T(8,128)S(1)}, u32[]{:S(2)}, u32[]{:S(2)}) %collective-permute-start.18) | collective-permute-done | bytes 147488 | tf_op jit(solution)/shard_map/ppermute | solution.py:730
  98.8 0.1 collective-permute-start.20
  98.9 6.9 %collective-permute-done.20 = bf16[400,128]{1,0:T(8,128)(2,1)S(1)} collective-permute-done((bf16[400,128]{1,0:T(8,128)(2,1)S(1)}, bf16[400,128]{1,0:T(8,128)(2,1)S(1)}, u32[]{:S(2)}, u32[]{:S(2)}) %collective-permute-start.20) | collective-permute-done | bytes 102432 | tf_op jit(solution)/shard_map/ppermute | solution.py:730
  105.8 0.1 collective-permute-start.21
  105.9 0.6 collective-permute-start.23
  106.5 6.3 %collective-permute-done.21 = bf16[800,128]{1,0:T(8,128)(2,1)S(1)} collective-permute-done((bf16[800,128]{1,0:T(8,128)(2,1)S(1)}, bf16[800,128]{1,0:T(8,128)(2,1)S(1)}, u32[]{:S(2)}, u32[]{:S(2)}) %collective-permute-start.21) | collective-permute-done | bytes 204832 | tf_op jit(solution)/shard_map/ppermute | solution.py:730
  112.9 0.1 broadcast_select_fusion.3
  113.0 0.6 collective-permute-start.25
  113.7 0.5 collective-permute-start.24
  114.2 0.9 collective-permute-done.22.rest_1_
  115.1 0.3 collective-permute-done.24.rest_3_
  115.4 0.4 copy-done.6
  115.8 0.7 copy-done.7
  116.5 2.6 %shard_map.228 = bf16[49,32,64]{2,1,0:T(8,128)(2,1)} custom-call(f32[4,4,3328]{2,1,0:T(4,128)} %copy-done.1, f32[4,4,3328]{2,1,0:T(4,128)} %copy-done.6, f32[4,4,3328]{2,1,0:T(4,128)} %copy-done.5, f32[4,4,3328]{2,1,0:T(4,128)} %copy-done.7), custom_call_target="tpu_custom_call" | custom-call | flops 1 | bytes 1 | tf_op jit(solution)/shard_map/pallas_call | solution.py:699
  119.1 4.6 %collective-permute-done.25 = bf16[1600,128]{1,0:T(8,128)(2,1)S(1)} collective-permute-done((bf16[1600,128]{1,0:T(8,128)(2,1)S(1)}, bf16[1600,128]{1,0:T(8,128)(2,1)S(1)}, u32[]{:S(2)}, u32[]{:S(2)}) %collective-permute-start.25) | collective-permute-done | bytes 409632 | tf_op jit(solution)/shard_map/ppermute | solution.py:730
  123.6 0.2 broadcast_select_fusion.1
  123.9 0.1 collective-permute-start.26
  124.0 2.3 %collective-permute-done.26.other = bf16[3200,128]{1,0:T(8,128)(2,1)S(1)} collective-permute-done((bf16[3200,128]{1,0:T(8,128)(2,1)S(1)}, bf16[3200,128]{1,0:T(8,128)(2,1)S(1)}, u32[]{:S(2)}, u32[]{:S(2)}) %collective-permute-start.26) | collective-permute-done | bytes 819232 | tf_op jit(solution)/shard_map/ppermute | solution.py:730
  126.3 0.9 copy-done.3
  127.2 3.0 %shard_map.229 = (bf16[448,448]{1,0:T(8,128)(2,1)}, bf16[2,384,384]{2,1,0:T(8,128)(2,1)}, bf16[2,320,320]{2,1,0:T(8,128)(2,1)}, bf16[64,256]{1,0:T(8,128)(2,1)},...) custom-call(bf16[3200,128]{1,0:T(8,128)(2,1)} %copy-done, bf16[3200,128]{1,0:T(8,128)(2,1)} %copy-done.3), custom_call_target="tpu_custom_call" | custom-call | flops 1 | bytes 1 | tf_op jit(solution)/shard_map/pallas_call | solution.py:699
  (61 shorter events, 0.8 us)
Async XLA Ops:
  2.9 8.5 %collective-permute-start = (bf16[4,6528]{1,0:T(4,128)(2,1)}, bf16[4,6528]{1,0:T(4,128)(2,1)S(1)}, u32[]{:S(2)}, u32[]{:S(2)}) collective-permute-start(bf16[4,6528]{1,0:T(4,128)(2,1)} %get-tuple-element.64), channel_id=1, source_target_pairs={{0,4},{4,0},{8,12},{12,8},{1,5},{5,1},{9,13},{13,9},{2,6},{6,2},{1... | collective-permute-start | bytes 156680 | tf_op jit(solution)/shard_map/ppermute | solution.py:823
  5.9 6.2 %collective-permute-start.1 = (bf16[4,6528]{1,0:T(4,128)(2,1)}, bf16[4,6528]{1,0:T(4,128)(2,1)S(1)}, u32[]{:S(2)}, u32[]{:S(2)}) collective-permute-start(bf16[4,6528]{1,0:T(4,128)(2,1)} %get-tuple-element.65), channel_id=1, source_target_pairs={{0,8},{4,12},{8,0},{12,4},{1,9},{5,13},{9,1},{13,5},{2,10},{6,14},... | collective-permute-start | bytes 156680 | tf_op jit(solution)/shard_map/ppermute | solution.py:823
  8.5 6.1 %collective-permute-start.2 = (bf16[4,6528]{1,0:T(4,128)(2,1)}, bf16[4,6528]{1,0:T(4,128)(2,1)S(1)}, u32[]{:S(2)}, u32[]{:S(2)}) collective-permute-start(bf16[4,6528]{1,0:T(4,128)(2,1)} %get-tuple-element.66), channel_id=1, source_target_pairs={{0,12},{4,8},{8,4},{12,0},{1,13},{5,9},{9,5},{13,1},{2,14},{6,10},... | collective-permute-start | bytes 156680 | tf_op jit(solution)/shard_map/ppermute | solution.py:823
  11.4 3.2 %copy-start.10 = (bf16[4,6528]{1,0:T(4,128)(2,1)}, bf16[4,6528]{1,0:T(4,128)(2,1)S(1)}, u32[]{:S(2)}) copy-start(bf16[4,6528]{1,0:T(4,128)(2,1)S(1)} %collective-permute-done.rest_1_) | copy-start | bytes 156676
  12.2 2.5 %copy-start.11 = (bf16[4,6528]{1,0:T(4,128)(2,1)}, bf16[4,6528]{1,0:T(4,128)(2,1)S(1)}, u32[]{:S(2)}) copy-start(bf16[4,6528]{1,0:T(4,128)(2,1)S(1)} %collective-permute-done.1.rest_2_) | copy-start | bytes 156676
  14.6 0.6 copy-start.12
  23.8 1.9 %collective-permute-start.3 = (f32[2,128]{1,0:T(2,128)}, f32[2,128]{1,0:T(2,128)S(1)}, u32[]{:S(2)}, u32[]{:S(2)}) collective-permute-start(f32[2,128]{1,0:T(2,128)} %get-tuple-element.67), channel_id=1, source_target_pairs={{0,1},{1,0},{2,3},{3,2},{4,5},{5,4},{6,7},{7,6},{8,9},{9,8},{10,11... | collective-permute-start | bytes 3080 | tf_op jit(solution)/shard_map/ppermute | solution.py:872
  23.9 3.8 %collective-permute-start.4 = (f32[2,128]{1,0:T(2,128)}, f32[2,128]{1,0:T(2,128)S(1)}, u32[]{:S(2)}, u32[]{:S(2)}) collective-permute-start(f32[2,128]{1,0:T(2,128)} %get-tuple-element.67), channel_id=1, source_target_pairs={{0,2},{1,3},{2,0},{3,1},{4,6},{5,7},{6,4},{7,5},{8,10},{9,11},{10,... | collective-permute-start | bytes 3080 | tf_op jit(solution)/shard_map/ppermute | solution.py:872
  25.4 3.2 %collective-permute-start.5 = (f32[2,128]{1,0:T(2,128)}, f32[2,128]{1,0:T(2,128)S(1)}, u32[]{:S(2)}, u32[]{:S(2)}) collective-permute-start(f32[2,128]{1,0:T(2,128)} %get-tuple-element.67), channel_id=1, source_target_pairs={{0,3},{1,2},{2,1},{3,0},{4,7},{5,6},{6,5},{7,4},{8,11},{9,10},{10,... | collective-permute-start | bytes 3080 | tf_op jit(solution)/shard_map/ppermute | solution.py:872
  29.3 7.0 %copy-start.13 = (f32[8,128]{1,0:T(8,128)}, f32[8,128]{1,0:T(8,128)S(1)}, u32[]{:S(2)}) copy-start(f32[8,128]{1,0:T(8,128)S(1)} %pad_maximum_fusion.5.refs_0_) | copy-start | bytes 12292
  29.3 4.5 %collective-permute-start.6 = (f32[8,128]{1,0:T(8,128)S(1)}, f32[8,128]{1,0:T(8,128)S(1)}, u32[]{:S(2)}, u32[]{:S(2)}) collective-permute-start(f32[8,128]{1,0:T(8,128)S(1)} %pad_maximum_fusion.5.refs_0_), channel_id=1, source_target_pairs={{0,4},{4,0},{8,12},{12,8},{1,5},{5,1},{9,13},{13,9},{2,6},{6,2},{1... | collective-permute-start | bytes 12296 | tf_op jit(solution)/shard_map/ppermute | solution.py:877
  29.4 4.6 %collective-permute-start.7 = (f32[8,128]{1,0:T(8,128)S(1)}, f32[8,128]{1,0:T(8,128)S(1)}, u32[]{:S(2)}, u32[]{:S(2)}) collective-permute-start(f32[8,128]{1,0:T(8,128)S(1)} %pad_maximum_fusion.5.refs_0_), channel_id=1, source_target_pairs={{0,8},{4,12},{8,0},{12,4},{1,9},{5,13},{9,1},{13,5},{2,10},{6,14},... | collective-permute-start | bytes 12296 | tf_op jit(solution)/shard_map/ppermute | solution.py:877
  30.9 5.4 %collective-permute-start.8 = (f32[8,128]{1,0:T(8,128)S(1)}, f32[8,128]{1,0:T(8,128)S(1)}, u32[]{:S(2)}, u32[]{:S(2)}) collective-permute-start(f32[8,128]{1,0:T(8,128)S(1)} %pad_maximum_fusion.5.refs_0_), channel_id=1, source_target_pairs={{0,12},{4,8},{8,4},{12,0},{1,13},{5,9},{9,5},{13,1},{2,14},{6,10},... | collective-permute-start | bytes 12296 | tf_op jit(solution)/shard_map/ppermute | solution.py:877
  33.8 2.5 %copy-start.14 = (f32[8,128]{1,0:T(8,128)}, f32[8,128]{1,0:T(8,128)S(1)}, u32[]{:S(2)}) copy-start(f32[8,128]{1,0:T(8,128)S(1)} %collective-permute-done.6.refs_1_) | copy-start | bytes 12292
  34.0 2.3 %copy-start.15 = (f32[8,128]{1,0:T(8,128)}, f32[8,128]{1,0:T(8,128)S(1)}, u32[]{:S(2)}) copy-start(f32[8,128]{1,0:T(8,128)S(1)} %collective-permute-done.7.refs_2_) | copy-start | bytes 12292
  36.3 0.6 copy-start.16
  45.4 4.7 %collective-permute-start.10 = (f32[2176,128]{1,0:T(8,128)}, f32[2176,128]{1,0:T(8,128)S(1)}, u32[]{:S(2)}, u32[]{:S(2)}) collective-permute-start(f32[2176,128]{1,0:T(8,128)} %get-tuple-element.82), channel_id=1, source_target_pairs={{0,1},{1,0},{2,3},{3,2},{4,5},{5,4},{6,7},{7,6},{8,9},{9,8},{10,11... | collective-permute-start | bytes 3342344 | tf_op jit(solution)/shard_map/ppermute | solution.py:730
  45.5 6.1 %collective-permute-start.9 = (f32[896,128]{1,0:T(8,128)}, f32[896,128]{1,0:T(8,128)}, u32[]{:S(2)}, u32[]{:S(2)}) collective-permute-start(f32[896,128]{1,0:T(8,128)} %get-tuple-element.80), channel_id=1, source_target_pairs={{0,1},{1,0},{2,3},{3,2},{4,5},{5,4},{6,7},{7,6},{8,9},{9,8},{10,11... | collective-permute-start | bytes 1376264 | tf_op jit(solution)/shard_map/ppermute | solution.py:730
  46.0 12.4 %all-to-all-start = ((f32[4,4,3328]{2,1,0:T(4,128)}), f32[4,4,3328]{2,1,0:T(4,128)S(1)}, u32[]{:S(2)}, u32[]{:S(2)}) async-start(f32[4,4,3328]{2,1,0:T(4,128)} %get-tuple-element.94), calls=%async_computation | async-start | bytes 425984 | tf_op jit(solution)/shard_map/all_to_all | solution.py:813
  51.5 1.0 copy-start.4
  53.6 12.2 %collective-permute-start.11 = (f32[448,128]{1,0:T(8,128)S(1)}, f32[448,128]{1,0:T(8,128)}, u32[]{:S(2)}, u32[]{:S(2)}) collective-permute-start(f32[448,128]{1,0:T(8,128)S(1)} %dynamic-slice_bitcast_fusion.2), channel_id=1, source_target_pairs={{0,4},{4,0},{8,12},{12,8},{1,5},{5,1},{9,13},{13,9},{2,6},{6,2},{1... | collective-permute-start | bytes 688136 | tf_op jit(solution)/shard_map/ppermute | solution.py:730
  58.3 7.4 %copy-start.2 = (f32[4,4,3328]{2,1,0:T(4,128)}, f32[4,4,3328]{2,1,0:T(4,128)S(1)}, u32[]{:S(2)}) copy-start(f32[4,4,3328]{2,1,0:T(4,128)S(1)} %all-to-all-done.rest_0_) | copy-start | bytes 638980
  58.3 8.4 %collective-permute-start.13 = (f32[4,4,3328]{2,1,0:T(4,128)S(1)}, f32[4,4,3328]{2,1,0:T(4,128)S(1)}, u32[]{:S(2)}, u32[]{:S(2)}) collective-permute-start(f32[4,4,3328]{2,1,0:T(4,128)S(1)} %all-to-all-done.rest_0_), channel_id=1, source_target_pairs={{0,2},{1,3},{2,0},{3,1},{4,6},{5,7},{6,4},{7,5},{8,10},{9,11},{10,... | collective-permute-start | bytes 638984 | tf_op jit(solution)/shard_map/ppermute | solution.py:730
  58.9 14.5 %collective-permute-start.12 = (f32[4,4,3328]{2,1,0:T(4,128)S(1)}, f32[4,4,3328]{2,1,0:T(4,128)}, u32[]{:S(2)}, u32[]{:S(2)}) collective-permute-start(f32[4,4,3328]{2,1,0:T(4,128)S(1)} %all-to-all-done.rest_0_), channel_id=1, source_target_pairs={{0,1},{1,0},{2,3},{3,2},{4,5},{5,4},{6,7},{7,6},{8,9},{9,8},{10,11... | collective-permute-start | bytes 638984 | tf_op jit(solution)/shard_map/ppermute | solution.py:730
  58.9 19.2 %collective-permute-start.15 = (f32[1088,128]{1,0:T(8,128)S(1)}, f32[1088,128]{1,0:T(8,128)S(1)}, u32[]{:S(2)}, u32[]{:S(2)}) collective-permute-start(f32[1088,128]{1,0:T(8,128)S(1)} %dynamic-slice_bitcast_fusion), channel_id=1, source_target_pairs={{0,2},{1,3},{2,0},{3,1},{4,6},{5,7},{6,4},{7,5},{8,10},{9,11},{10,... | collective-permute-start | bytes 1671176 | tf_op jit(solution)/shard_map/ppermute | solution.py:730
  66.8 6.6 %copy-start.8 = (f32[4,4,3328]{2,1,0:T(4,128)}, f32[4,4,3328]{2,1,0:T(4,128)S(1)}, u32[]{:S(2)}) copy-start(f32[4,4,3328]{2,1,0:T(4,128)S(1)} %collective-permute-done.13.rest_2_) | copy-start | bytes 638980
  66.8 6.6 %collective-permute-start.14 = (f32[4,4,3328]{2,1,0:T(4,128)S(1)}, f32[4,4,3328]{2,1,0:T(4,128)S(1)}, u32[]{:S(2)}, u32[]{:S(2)}) collective-permute-start(f32[4,4,3328]{2,1,0:T(4,128)S(1)} %collective-permute-done.13.rest_2_), channel_id=1, source_target_pairs={{0,1},{1,0},{2,3},{3,2},{4,5},{5,4},{6,7},{7,6},{8,9},{9,8},{10,11... | collective-permute-start | bytes 638984 | tf_op jit(solution)/shard_map/ppermute | solution.py:730
  67.1 15.1 %all-to-all-start.1 = ((f32[4,4,3328]{2,1,0:T(4,128)}), f32[4,4,3328]{2,1,0:T(4,128)S(1)}, u32[]{:S(2)}, u32[]{:S(2)}) async-start(f32[4,4,3328]{2,1,0:T(4,128)} %shard_map.226), calls=%async_computation.1 | async-start | bytes 425984 | tf_op jit(solution)/shard_map/all_to_all | solution.py:813
  70.5 13.6 %collective-permute-start.17 = (f32[224,128]{1,0:T(8,128)S(1)}, f32[224,128]{1,0:T(8,128)}, u32[]{:S(2)}, u32[]{:S(2)}) collective-permute-start(f32[224,128]{1,0:T(8,128)S(1)} %dynamic-slice_bitcast_fusion.4), channel_id=1, source_target_pairs={{0,8},{4,12},{8,0},{12,4},{1,9},{5,13},{9,1},{13,5},{2,10},{6,14},... | collective-permute-start | bytes 344072 | tf_op jit(solution)/shard_map/ppermute | solution.py:730
  73.4 0.7 copy-start.9
  78.3 11.3 %collective-permute-start.16 = (f32[576,128]{1,0:T(8,128)S(1)}, f32[576,128]{1,0:T(8,128)S(1)}, u32[]{:S(2)}, u32[]{:S(2)}) collective-permute-start(f32[576,128]{1,0:T(8,128)S(1)} %dynamic-slice_bitcast_fusion.1), channel_id=1, source_target_pairs={{0,4},{4,0},{8,12},{12,8},{1,5},{5,1},{9,13},{13,9},{2,6},{6,2},{1... | collective-permute-start | bytes 884744 | tf_op jit(solution)/shard_map/ppermute | solution.py:730
  82.2 31.5 %copy-start.1 = (f32[4,4,3328]{2,1,0:T(4,128)}, f32[4,4,3328]{2,1,0:T(4,128)S(1)}, u32[]{:S(2)}) copy-start(f32[4,4,3328]{2,1,0:T(4,128)S(1)} %all-to-all-done.1.rest_0_) | copy-start | bytes 638980
  85.0 4.7 %collective-permute-start.19 = (f32[112,128]{1,0:T(8,128)S(1)}, f32[112,128]{1,0:T(8,128)S(1)}, u32[]{:S(2)}, u32[]{:S(2)}) collective-permute-start(f32[112,128]{1,0:T(8,128)S(1)} %dynamic-slice_bitcast_fusion.5), channel_id=1, source_target_pairs={{0,2},{1,3},{2,0},{3,1},{4,6},{5,7},{6,4},{7,5},{8,10},{9,11},{10,... | collective-permute-start | bytes 172040 | tf_op jit(solution)/shard_map/ppermute | solution.py:730
  89.7 9.1 %collective-permute-start.18 = (f32[288,128]{1,0:T(8,128)S(1)}, f32[288,128]{1,0:T(8,128)S(1)}, u32[]{:S(2)}, u32[]{:S(2)}) collective-permute-start(f32[288,128]{1,0:T(8,128)S(1)} %dynamic-slice_bitcast_fusion.3), channel_id=1, source_target_pairs={{0,8},{4,12},{8,0},{12,4},{1,9},{5,13},{9,1},{13,5},{2,10},{6,14},... | collective-permute-start | bytes 442376 | tf_op jit(solution)/shard_map/ppermute | solution.py:730
  98.8 6.9 %collective-permute-start.20 = (bf16[400,128]{1,0:T(8,128)(2,1)S(1)}, bf16[400,128]{1,0:T(8,128)(2,1)S(1)}, u32[]{:S(2)}, u32[]{:S(2)}) collective-permute-start(bf16[400,128]{1,0:T(8,128)(2,1)S(1)} %pad_maximum_fusion.4), channel_id=1, source_target_pairs={{0,8},{4,12},{8,0},{12,4},{1,9},{5,13},{9,1},{13,5},{2,10},{6,14},... | collective-permute-start | bytes 307208 | tf_op jit(solution)/shard_map/ppermute | solution.py:730
  105.8 7.1 %collective-permute-start.21 = (bf16[800,128]{1,0:T(8,128)(2,1)S(1)}, bf16[800,128]{1,0:T(8,128)(2,1)S(1)}, u32[]{:S(2)}, u32[]{:S(2)}) collective-permute-start(bf16[800,128]{1,0:T(8,128)(2,1)S(1)} %pad_maximum_fusion.3), channel_id=1, source_target_pairs={{0,4},{4,0},{8,12},{12,8},{1,5},{5,1},{9,13},{13,9},{2,6},{6,2},{1... | collective-permute-start | bytes 614408 | tf_op jit(solution)/shard_map/ppermute | solution.py:730
  105.9 7.8 %collective-permute-start.23 = (f32[4,4,3328]{2,1,0:T(4,128)S(1)}, f32[4,4,3328]{2,1,0:T(4,128)S(1)}, u32[]{:S(2)}, u32[]{:S(2)}) collective-permute-start(f32[4,4,3328]{2,1,0:T(4,128)S(1)} %all-to-all-done.1.rest_0_), channel_id=1, source_target_pairs={{0,2},{1,3},{2,0},{3,1},{4,6},{5,7},{6,4},{7,5},{8,10},{9,11},{10,... | collective-permute-start | bytes 638984 | tf_op jit(solution)/shard_map/ppermute | solution.py:730
  113.0 10.6 %collective-permute-start.25 = (bf16[1600,128]{1,0:T(8,128)(2,1)S(1)}, bf16[1600,128]{1,0:T(8,128)(2,1)S(1)}, u32[]{:S(2)}, u32[]{:S(2)}) collective-permute-start(bf16[1600,128]{1,0:T(8,128)(2,1)S(1)} %pad_maximum_fusion.2), channel_id=1, source_target_pairs={{0,2},{1,3},{2,0},{3,1},{4,6},{5,7},{6,4},{7,5},{8,10},{9,11},{10,... | collective-permute-start | bytes 1228808 | tf_op jit(solution)/shard_map/ppermute | solution.py:730
  113.7 1.5 %collective-permute-start.22 = (f32[4,4,3328]{2,1,0:T(4,128)S(1)}, f32[4,4,3328]{2,1,0:T(4,128)S(1)}, u32[]{:S(2)}, u32[]{:S(2)}) collective-permute-start(f32[4,4,3328]{2,1,0:T(4,128)S(1)} %all-to-all-done.1.rest_0_), channel_id=1, source_target_pairs={{0,1},{1,0},{2,3},{3,2},{4,5},{5,4},{6,7},{7,6},{8,9},{9,8},{10,11... | collective-permute-start | bytes 638984 | tf_op jit(solution)/shard_map/ppermute | solution.py:730
  113.7 1.8 %copy-start.5 = (f32[4,4,3328]{2,1,0:T(4,128)}, f32[4,4,3328]{2,1,0:T(4,128)S(1)}, u32[]{:S(2)}) copy-start(f32[4,4,3328]{2,1,0:T(4,128)S(1)} %collective-permute-done.23.rest_2_) | copy-start | bytes 638980
  113.7 1.7 %collective-permute-start.24 = (f32[4,4,3328]{2,1,0:T(4,128)S(1)}, f32[4,4,3328]{2,1,0:T(4,128)S(1)}, u32[]{:S(2)}, u32[]{:S(2)}) collective-permute-start(f32[4,4,3328]{2,1,0:T(4,128)S(1)} %collective-permute-done.23.rest_2_), channel_id=1, source_target_pairs={{0,1},{1,0},{2,3},{3,2},{4,5},{5,4},{6,7},{7,6},{8,9},{9,8},{10,11... | collective-permute-start | bytes 638984 | tf_op jit(solution)/shard_map/ppermute | solution.py:730
  115.1 0.7 copy-start.6
  115.8 0.7 copy-start.7
  123.9 2.4 %copy-start = (bf16[3200,128]{1,0:T(8,128)(2,1)}, bf16[3200,128]{1,0:T(8,128)(2,1)S(1)}, u32[]{:S(2)}) copy-start(bf16[3200,128]{1,0:T(8,128)(2,1)S(1)} %pad_maximum_fusion.mine) | copy-start | bytes 2457604
  123.9 2.4 %collective-permute-start.26 = (bf16[3200,128]{1,0:T(8,128)(2,1)S(1)}, bf16[3200,128]{1,0:T(8,128)(2,1)S(1)}, u32[]{:S(2)}, u32[]{:S(2)}) collective-permute-start(bf16[3200,128]{1,0:T(8,128)(2,1)S(1)} %pad_maximum_fusion.mine), channel_id=1, source_target_pairs={{0,1},{1,0},{2,3},{3,2},{4,5},{5,4},{6,7},{7,6},{8,9},{9,8},{10,11... | collective-permute-start | bytes 2457608 | tf_op jit(solution)/shard_map/ppermute | solution.py:730
  126.3 0.9 copy-start.3

commit v8 on v7

--- a/solution.py
+++ b/solution.py
@@ -594,8 +594,7 @@
         cols = lanes_total // 2
         col_bits = (cols - 1).bit_length()
         late = PROJ_ROWS // lanes_total
-        own_rows = CHUNKS[0][1] // cols
-        first_rows = (own_rows + late) // peers
+        first_rows = CHUNKS[0][1] // (cols * peers)
         share = first_rows + CHUNKS[1][1] // (cols * peers)
         main, zeros, tail = [], [], {}
         for core, value in enumerate(halves_of(mine, other)):
@@ -603,12 +602,12 @@
             for col in range(cols):
                 rows = []
                 for peer in range(peers):
-                    start = (col * peers + peer) * share
+                    start = col * (peers * share + late) + peer * share
                     rows.append(value[start : start + first_rows])
                     zero_parts[peer * cols + col] = value[start + first_rows : start + share]
-                rows = jnp.concatenate(rows, axis=0)
-                parts.append(rows[:own_rows])
-                tail[core * cols + reversed_bits(col, col_bits)] = rows[own_rows:]
+                parts += rows
+                end = (col + 1) * (peers * share + late)
+                tail[core * cols + reversed_bits(col, col_bits)] = value[end - late : end]
             main.append(jnp.concatenate(parts, axis=0))
             zeros.append(jnp.concatenate([zero_parts[n] for n in sorted(zero_parts)], axis=0))
         tail = jnp.concatenate([tail[n] for n in sorted(tail)], axis=0)
@@ -755,13 +754,11 @@
     return sorted(steps, key=lambda step: step[0] != first)
 
 
-def halve(kept, sent, first, order, late=None):
+def halve(kept, sent, first, order):
     other = swap(sent, "edge", 0)
     yield
     current = kept + order.hold(other)
-    for n, (axis, bit) in enumerate(share_steps(first)):
-        if late is not None and n == bits_of("edge") - 1:
-            current = jnp.concatenate([current, late[0]], axis=0)
+    for axis, bit in share_steps(first):
         mine = own_bit(axis, bit)
         parts = current.reshape(2, current.shape[0] // 2, -1)
         sent = order.mark(lax.dynamic_index_in_dim(parts, 1 - mine, 0, False))
@@ -771,8 +768,11 @@
     return order.mark(current.astype(bf16))
 
 
-def double(current, order):
+def double(current, late, order):
+    joined = False
     for axis, bit in reversed(share_steps("edge")):
+        if axis == "edge" and not joined:
+            current, joined = jnp.concatenate([current, late[0]], axis=0), True
         mine = own_bit(axis, bit)
         other = swap(current, axis, bit)
         yield
@@ -908,15 +908,12 @@
     total = lanes_total * slots
     order.mark(halves[0])
     messages = exchange(order.hold(sums))
-    late = []
-    rest_steps = halve(halves[0], halves[1], "edge", order, late)
+    rest_steps = halve(halves[0], halves[1], "edge", order)
     zero_steps = halve(halves[2], halves[3], "graph", order)
     next(rest_steps)
     next(zero_steps)
     next(rest_steps)
     next(zero_steps)
-    message_hops = gather_lanes(order.hold(messages), order)
-    next(message_hops)
     (source_sums,) = call(
         source_kernel,
         [((peers, cap, WIDE), f32)],
@@ -930,9 +927,16 @@
         conv_zero, conv_one, conv_two, alpha_in
     )
     order.mark(source_sums)
-    returned = exchange(source_sums)
     next(zero_steps)
+    returned = order.mark(order.hold(exchange(source_sums)))
+    for _ in range(bits_of("edge") - 1):
+        next(rest_steps)
+    message_hops = gather_lanes(order.hold(messages), order)
+    next(message_hops)
+    next(zero_steps)
+    next(rest_steps)
     message_rows = finish_steps(message_hops)
+    zero_share = finish_steps(zero_steps)
     out, proj = call(
         make_finish(lanes_total),
         [((COEFFS, atoms, CH), bf16), ((PROJ_ROWS, LANES), f32)],
@@ -943,20 +947,21 @@
     lane = lax.axis_index("edge")
     late_rows = PROJ_ROWS // lanes_total
     place = ((lane & 1) * (lanes_total // 2) + (lane >> 1)) * late_rows
-    late.append(lax.dynamic_slice_in_dim(proj, place, late_rows, 0))
-    for _ in range(bits_of("edge") - 1):
-        next(rest_steps)
-    source_hops = gather_lanes(order.mark(order.hold(returned)), order)
+    late = lax.dynamic_slice_in_dim(proj, place, late_rows, 0)
+    share = jnp.concatenate([finish_steps(rest_steps), zero_share], axis=0)
+    late_share = []
+    doubling = double(order.mark(share), late_share, order)
+    next(doubling)
+    source_hops = gather_lanes(order.hold(returned), order)
     next(source_hops)
-    next(zero_steps)
-    next(rest_steps)
-    zero_share = finish_steps(zero_steps)
+    for bit in range(bits_of("graph")):
+        late = order.mark(late + order.hold(swap(late, "graph", bit)))
+        if bit < bits_of("graph") - 1:
+            next(doubling)
+    late_share.append(late.astype(bf16))
+    for _ in share_steps("edge")[bits_of("graph") :]:
+        next(doubling)
     source_rows = finish_steps(source_hops)
-    share = jnp.concatenate([finish_steps(rest_steps), zero_share], axis=0)
-    doubling = double(order.mark(share), order)
-    next(doubling)
-    for _ in share_steps("edge")[1:]:
-        next(doubling)
     (embed,) = call(
         make_collect(lanes_total),
         [((COEFFS, atoms, CH), bf16)],

time: 131 us -> 131 us (level)
  starting transfers between devices: 31.7 us -> 38 us
  waiting for transfers between devices: 49.8 us -> 45.8 us
  other arithmetic: 5.57 us -> 3.41 us
    ppermute x18 -> x20, waiting for transfers between devices: 36.1 us -> 24.4 us  [swap(): return lax.ppermute(value, axis, [(i, i ^ 1 << bit) for i in range(size)])]
    all_to_all x2, waiting for transfers between devices: 5.04 us -> 12.7 us  [exchange(): lax.all_to_all(value, 'graph', split_axis=0, concat_axis=0, tiled=True)]
    ppermute x18 -> x20, starting transfers between devices: 12.1 us -> 18 us  [swap(): return lax.ppermute(value, axis, [(i, i ^ 1 << bit) for i in range(size)])]
    add x4, other arithmetic: 1.97 us -> 0.13 us  [halve(): lax.dynamic_index_in_dim(parts, mine, 0, False) + order.hold(other)]
    unnamed x35 -> x37, local copies, waits for them, and re-layouts: 6.46 us -> 6.11 us
  transfers between devices with their start and end apart: 29 -> 31, of which waited for: 17 -> 20; matrix products, arithmetic and copies ran while one was open for 6% -> 4% of each run, Pallas kernels for 9% -> 9%
where the time goes in v8:
time: 131 us; the launch traced here: 130 us
  waiting for transfers between devices  45.8 us (35%)
  starting transfers between devices  38 us (29%)
  Pallas kernels  33.6 us (26%)
  local copies, waits for them, and re-layouts  8.23 us (6%)
  other arithmetic  3.41 us (3%)
    pallas_call x7, Pallas kernels, call(): pl.pallas_call(kernel, out_shape=[jax.ShapeDtypeStruct(shape, kind) for s...  33.6 us
    ppermute x20, waiting for transfers between devices, swap(): return lax.ppermute(value, axis, [(i, i ^ 1 << bit) for i in range(size)])  24.4 us
    ppermute x20, starting transfers between devices, swap(): return lax.ppermute(value, axis, [(i, i ^ 1 << bit) for i in range(size)])  18 us
    all_to_all x2, waiting for transfers between devices, exchange(): lax.all_to_all(value, 'graph', split_axis=0, concat_axis=0, tiled=True)  12.7 us
    all_to_all x2, starting transfers between devices, exchange(): lax.all_to_all(value, 'graph', split_axis=0, concat_axis=0, tiled=True)  8.01 us
    unnamed x37, local copies, waits for them, and re-layouts  6.11 us
    ppermute x3, starting transfers between devices, shards(): lax.ppermute(outgoing[k], 'graph', [(i, i ^ k) for i in range(peers)])  5.62 us
    ppermute x3, starting transfers between devices, shards(): lax.ppermute(graph_stats, 'graph', [(i, i ^ k) for i in range(peers)])  4.44 us
  transfers between devices with their start and end apart: 31, of which 20 were waited for; matrix products, arithmetic and copies ran while one was open for 4% of the time, Pallas kernels for 9%

profile of v8, /device:TPU:0, one launch (start us, length us, event | category | flops | bytes accessed | tf_op | source)
XLA Modules:
  0.0 130.0 jit_solution(13645265167086787704)
XLA Ops:
  0.6 2.2 %shard_map.223 = (bf16[4,6528]{1,0:T(4,128)(2,1)}, bf16[4,6528]{1,0:T(4,128)(2,1)}, bf16[4,6528]{1,0:T(4,128)(2,1)}, bf16[4,6528]{1,0:T(4,128)(2,1)}) custom-call(s32[1,4,1,4]{3,2,1,0:T(1,128)} %send.1, s32[1,4,1,4]{3,2,1,0:T(1,128)} %recv.1, bf16[49,32,64]{2,1,0:T(8,128)(2,1)} %bitcast.57, bf16[49,32,64]{2,1,0:T(8,128)(2,1)} %bitcast.48), custom_call_target="tpu_custom_call" | custom-call | flops 1 | bytes 1 | tf_op jit(solution)/shard_map/pallas_call | solution.py:698
  2.9 3.0 %collective-permute-start = (bf16[4,6528]{1,0:T(4,128)(2,1)}, bf16[4,6528]{1,0:T(4,128)(2,1)S(1)}, u32[]{:S(2)}, u32[]{:S(2)}) collective-permute-start(bf16[4,6528]{1,0:T(4,128)(2,1)} %get-tuple-element.67), channel_id=1, source_target_pairs={{0,4},{4,0},{8,12},{12,8},{1,5},{5,1},{9,13},{13,9},{2,6},{6,2},{1... | collective-permute-start | bytes 156680 | tf_op jit(solution)/shard_map/ppermute | solution.py:823
  5.9 2.6 %collective-permute-start.1 = (bf16[4,6528]{1,0:T(4,128)(2,1)}, bf16[4,6528]{1,0:T(4,128)(2,1)S(1)}, u32[]{:S(2)}, u32[]{:S(2)}) collective-permute-start(bf16[4,6528]{1,0:T(4,128)(2,1)} %get-tuple-element.68), channel_id=1, source_target_pairs={{0,8},{4,12},{8,0},{12,4},{1,9},{5,13},{9,1},{13,5},{2,10},{6,14},... | collective-permute-start | bytes 156680 | tf_op jit(solution)/shard_map/ppermute | solution.py:823
  8.5 1.2 reshape.50.adot.refs_17_
  9.7 1.7 %copy.25.rotation = bf16[256,235]{1,0:T(8,128)(2,1)} copy(bf16[256,235]{0,1:T(8,128)(2,1)} %param.22) | data formatting | bytes 240640 | tf_op args[6]
  11.4 0.8 collective-permute-done.1.rest_2_
  12.2 2.5 %collective-permute-done.2.rest_3_ = bf16[4,6528]{1,0:T(4,128)(2,1)S(1)} collective-permute-done((bf16[4,6528]{1,0:T(4,128)(2,1)}, bf16[4,6528]{1,0:T(4,128)(2,1)S(1)}, u32[]{:S(2)}, u32[]{:S(2)}) %collective-permute-start.2) | collective-permute-done | bytes 52256 | tf_op jit(solution)/shard_map/ppermute | solution.py:823
  14.6 0.6 copy-done.13
  15.3 8.5 %shard_map.224 = (f32[4,4,3328]{2,1,0:T(4,128)}, f32[2,128]{1,0:T(2,128)}, bf16[448,256]{1,0:T(8,128)(2,1)}, bf16[384,512]{1,0:T(8,128)(2,1)}, bf16[320,512]{1,0...) custom-call(s32[1,256]{1,0:T(1,128)} %bitcast.61, ...), custom_call_target="tpu_custom_call" | custom-call | flops 1 | bytes 1 | tf_op jit(solution)/shard_map/pallas_call | solution.py:698
  23.9 1.6 %collective-permute-start.4 = (f32[2,128]{1,0:T(2,128)}, f32[2,128]{1,0:T(2,128)S(1)}, u32[]{:S(2)}, u32[]{:S(2)}) collective-permute-start(f32[2,128]{1,0:T(2,128)} %get-tuple-element.70), channel_id=1, source_target_pairs={{0,2},{1,3},{2,0},{3,1},{4,6},{5,7},{6,4},{7,5},{8,10},{9,11},{10,... | collective-permute-start | bytes 3080 | tf_op jit(solution)/shard_map/ppermute | solution.py:872
  25.4 0.3 collective-permute-start.5
  25.7 2.0 %collective-permute-done.4 = f32[2,128]{1,0:T(2,128)S(1)} collective-permute-done((f32[2,128]{1,0:T(2,128)}, f32[2,128]{1,0:T(2,128)S(1)}, u32[]{:S(2)}, u32[]{:S(2)}) %collective-permute-start.4) | collective-permute-done | bytes 1056 | tf_op jit(solution)/shard_map/ppermute | solution.py:872
  27.7 0.9 collective-permute-done.5
  28.6 0.7 pad_maximum_fusion.5.refs_0_
  29.3 0.1 collective-permute-start.6
  29.4 1.5 %collective-permute-start.7 = (f32[8,128]{1,0:T(8,128)S(1)}, f32[8,128]{1,0:T(8,128)S(1)}, u32[]{:S(2)}, u32[]{:S(2)}) collective-permute-start(f32[8,128]{1,0:T(8,128)S(1)} %pad_maximum_fusion.5.refs_0_), channel_id=1, source_target_pairs={{0,8},{4,12},{8,0},{12,4},{1,9},{5,13},{9,1},{13,5},{2,10},{6,14},... | collective-permute-start | bytes 12296 | tf_op jit(solution)/shard_map/ppermute | solution.py:877
  30.9 2.9 %collective-permute-start.8 = (f32[8,128]{1,0:T(8,128)S(1)}, f32[8,128]{1,0:T(8,128)S(1)}, u32[]{:S(2)}, u32[]{:S(2)}) collective-permute-start(f32[8,128]{1,0:T(8,128)S(1)} %pad_maximum_fusion.5.refs_0_), channel_id=1, source_target_pairs={{0,12},{4,8},{8,4},{12,0},{1,13},{5,9},{9,5},{13,1},{2,14},{6,10},... | collective-permute-start | bytes 12296 | tf_op jit(solution)/shard_map/ppermute | solution.py:877
  33.8 0.2 collective-permute-done.7.refs_2_
  34.0 2.3 %collective-permute-done.8.refs_3_ = f32[8,128]{1,0:T(8,128)S(1)} collective-permute-done((f32[8,128]{1,0:T(8,128)S(1)}, f32[8,128]{1,0:T(8,128)S(1)}, u32[]{:S(2)}, u32[]{:S(2)}) %collective-permute-start.8) | collective-permute-done | bytes 4128 | tf_op jit(solution)/shard_map/ppermute | solution.py:877
  36.3 0.6 copy-done.17
  36.9 8.5 %shard_map.225 = (bf16[448,256]{1,0:T(8,128)(2,1)}, bf16[384,512]{1,0:T(8,128)(2,1)}, bf16[320,512]{1,0:T(8,128)(2,1)}, bf16[256,256]{1,0:T(8,128)(2,1)}, f32[21...) custom-call(f32[8,128]{1,0:T(8,128)} %copy-done.14, f32[8,128]{1,0:T(8,128)} %copy-done.15, ...), custom_call_target="tpu_custom_call" | custom-call | flops 1 | bytes 1 | tf_op jit(solution)/shard_map/pallas_call | solution.py:698
  45.4 0.5 collective-permute-start.9
  45.9 2.5 %collective-permute-done.10 = f32[2176,128]{1,0:T(8,128)S(1)} collective-permute-done((f32[2176,128]{1,0:T(8,128)}, f32[2176,128]{1,0:T(8,128)S(1)}, u32[]{:S(2)}, u32[]{:S(2)}) %collective-permute-start.10) | collective-permute-done | bytes 1114144 | tf_op jit(solution)/shard_map/ppermute | solution.py:729
  48.4 1.4 %add.69 = f32[2176,128]{1,0:T(8,128)S(1)} add(f32[2176,128]{1,0:T(8,128)} %get-tuple-element.84, f32[2176,128]{1,0:T(8,128)S(1)} %collective-permute-done.10) | non-fusion elementwise | flops 278528 | bytes 3342336 | tf_op jit(solution)/shard_map/add | solution.py:760
  49.8 0.9 copy-done.4
  50.9 0.6 collective-permute-start.13
  51.6 5.6 %shard_map.226 = f32[4,4,3328]{2,1,0:T(4,128)} custom-call(s32[1,256]{1,0:T(1,128)} %bitcast.62, f32[16,128]{1,0:T(8,128)} %get-tuple-element.88.lists, f32[235,256]{1,0:T(8,128)} %get-tuple-element.73.refs_7_.rot, bf16[448,256]{1,0:T(8,128)(2,1)} %get-tuple-element.89.g0, bf16[384,512]{1,0:T(8,128)(2,1)} %get-tuple-element.90.g1, ...), custom_call_target="tpu_custom_call" | custom-call | flops 1 | bytes 1 | tf_op jit(solution)/shard_map/pallas_call | solution.py:698
  57.1 4.6 %all-to-all-start = ((f32[4,4,3328]{2,1,0:T(4,128)}), f32[4,4,3328]{2,1,0:T(4,128)S(1)}, u32[]{:S(2)}, u32[]{:S(2)}) async-start(f32[4,4,3328]{2,1,0:T(4,128)} %shard_map.226), calls=%async_computation | async-start | bytes 425984 | tf_op jit(solution)/shard_map/all_to_all | solution.py:813
  61.8 3.0 %collective-permute-start.12 = (f32[224,128]{1,0:T(8,128)S(1)}, f32[224,128]{1,0:T(8,128)S(1)}, u32[]{:S(2)}, u32[]{:S(2)}) collective-permute-start(f32[224,128]{1,0:T(8,128)S(1)} %dynamic-slice_bitcast_fusion.4), channel_id=1, source_target_pairs={{0,8},{4,12},{8,0},{12,4},{1,9},{5,13},{9,1},{13,5},{2,10},{6,14},... | collective-permute-start | bytes 344072 | tf_op jit(solution)/shard_map/ppermute | solution.py:729
  64.8 8.1 %all-to-all-done.rest_0_ = f32[4,4,3328]{2,1,0:T(4,128)S(1)} async-done(((f32[4,4,3328]{2,1,0:T(4,128)}), f32[4,4,3328]{2,1,0:T(4,128)S(1)}, u32[]{:S(2)}, u32[]{:S(2)}) %all-to-all-start) | async-done | bytes 213024 | tf_op jit(solution)/shard_map/all_to_all | solution.py:813
  73.0 3.4 %all-to-all-start.1 = ((f32[4,4,3328]{2,1,0:T(4,128)}), f32[4,4,3328]{2,1,0:T(4,128)S(1)}, u32[]{:S(2)}, u32[]{:S(2)}) async-start(f32[4,4,3328]{2,1,0:T(4,128)} %get-tuple-element.102), calls=%async_computation.1 | async-start | bytes 425984 | tf_op jit(solution)/shard_map/all_to_all | solution.py:813
  76.5 2.0 %collective-permute-start.15 = (f32[544,128]{1,0:T(8,128)S(1)}, f32[544,128]{1,0:T(8,128)S(1)}, u32[]{:S(2)}, u32[]{:S(2)}) collective-permute-start(f32[544,128]{1,0:T(8,128)S(1)} %dynamic-slice_bitcast_fusion.1), channel_id=1, source_target_pairs={{0,4},{4,0},{8,12},{12,8},{1,5},{5,1},{9,13},{13,9},{2,6},{6,2},{1... | collective-permute-start | bytes 835592 | tf_op jit(solution)/shard_map/ppermute | solution.py:729
  78.5 4.6 %all-to-all-done.1.rest_0_ = f32[4,4,3328]{2,1,0:T(4,128)S(1)} async-done(((f32[4,4,3328]{2,1,0:T(4,128)}), f32[4,4,3328]{2,1,0:T(4,128)S(1)}, u32[]{:S(2)}, u32[]{:S(2)}) %all-to-all-start.1) | async-done | bytes 213024 | tf_op jit(solution)/shard_map/all_to_all | solution.py:813
  83.1 1.4 %collective-permute-start.17 = (f32[4,4,3328]{2,1,0:T(4,128)S(1)}, f32[4,4,3328]{2,1,0:T(4,128)S(1)}, u32[]{:S(2)}, u32[]{:S(2)}) collective-permute-start(f32[4,4,3328]{2,1,0:T(4,128)S(1)} %all-to-all-done.1.rest_0_), channel_id=1, source_target_pairs={{0,2},{1,3},{2,0},{3,1},{4,6},{5,7},{6,4},{7,5},{8,10},{9,11},{10,... | collective-permute-start | bytes 638984 | tf_op jit(solution)/shard_map/ppermute | solution.py:729
  84.6 0.6 collective-permute-start.14
  85.2 0.4 collective-permute-done.15
  85.7 2.4 %collective-permute-start.19 = (f32[272,128]{1,0:T(8,128)S(1)}, f32[272,128]{1,0:T(8,128)S(1)}, u32[]{:S(2)}, u32[]{:S(2)}) collective-permute-start(f32[272,128]{1,0:T(8,128)S(1)} %dynamic-slice_bitcast_fusion.3), channel_id=1, source_target_pairs={{0,8},{4,12},{8,0},{12,4},{1,9},{5,13},{9,1},{13,5},{2,10},{6,14},... | collective-permute-start | bytes 417800 | tf_op jit(solution)/shard_map/ppermute | solution.py:729
  88.1 1.4 %collective-permute-done.17.rest_2_ = f32[4,4,3328]{2,1,0:T(4,128)S(1)} collective-permute-done((f32[4,4,3328]{2,1,0:T(4,128)S(1)}, f32[4,4,3328]{2,1,0:T(4,128)S(1)}, u32[]{:S(2)}, u32[]{:S(2)}) %collective-permute-start.17) | collective-permute-done | bytes 213024 | tf_op jit(solution)/shard_map/ppermute | solution.py:729
  89.6 0.6 collective-permute-done.14
  90.2 0.8 collective-permute-done.18.rest_3_
  91.0 0.7 copy-done.10
  91.7 3.3 %shard_map.227 = (bf16[49,32,64]{2,1,0:T(8,128)(2,1)}, f32[256,128]{1,0:T(8,128)}) custom-call(bf16[49,32,64]{2,1,0:T(8,128)(2,1)} %bitcast.49, bf16[7,64,64]{2,1,0:T(8,128)(2,1)} %out_proj.3, f32[4,4,3328]{2,1,0:T(4,128)} %copy-done.2, f32[4,4,3328]{2,1,0:T(4,128)} %copy-done.9, f32[4,4,3328]{2,1,0:T(4,128)} %copy-done.8, f32[4,4,3328]{2,1,0:T(4,128)} %copy-done.10), custom_call_target="tpu_custom_call" | custom-call | flops 1 | bytes 1 | tf_op jit(solution)/shard_map/pallas_call | solution.py:698
  95.1 0.8 constant_dynamic-slice_fusion
  95.8 1.9 %collective-permute-start.21 = (f32[64,128]{1,0:T(8,128)S(1)}, f32[64,128]{1,0:T(8,128)S(1)}, u32[]{:S(2)}, u32[]{:S(2)}) collective-permute-start(f32[64,128]{1,0:T(8,128)S(1)} %constant_dynamic-slice_fusion), channel_id=1, source_target_pairs={{0,4},{4,0},{8,12},{12,8},{1,5},{5,1},{9,13},{13,9},{2,6},{6,2},{1... | collective-permute-start | bytes 98312 | tf_op jit(solution)/shard_map/ppermute | solution.py:729
  97.8 0.4 collective-permute-start.20
  98.2 1.6 %collective-permute-done.21 = f32[64,128]{1,0:T(8,128)S(1)} collective-permute-done((f32[64,128]{1,0:T(8,128)S(1)}, f32[64,128]{1,0:T(8,128)S(1)}, u32[]{:S(2)}, u32[]{:S(2)}) %collective-permute-start.21) | collective-permute-done | bytes 32800 | tf_op jit(solution)/shard_map/ppermute | solution.py:729
  99.8 0.8 fusion.2
  100.5 4.6 %collective-permute-done.20 = bf16[384,128]{1,0:T(8,128)(2,1)S(1)} collective-permute-done((bf16[384,128]{1,0:T(8,128)(2,1)S(1)}, bf16[384,128]{1,0:T(8,128)(2,1)S(1)}, u32[]{:S(2)}, u32[]{:S(2)}) %collective-permute-start.20) | collective-permute-done | bytes 98336 | tf_op jit(solution)/shard_map/ppermute | solution.py:729
  105.2 0.1 collective-permute-start.22
  105.3 1.7 %collective-permute-start.23 = (f32[64,128]{1,0:T(8,128)S(1)}, f32[64,128]{1,0:T(8,128)S(1)}, u32[]{:S(2)}, u32[]{:S(2)}) collective-permute-start(f32[64,128]{1,0:T(8,128)S(1)} %fusion.2), channel_id=1, source_target_pairs={{0,8},{4,12},{8,0},{12,4},{1,9},{5,13},{9,1},{13,5},{2,10},{6,14},... | collective-permute-start | bytes 98312 | tf_op jit(solution)/shard_map/ppermute | solution.py:729
  107.0 1.4 %collective-permute-start.25 = (f32[4,4,3328]{2,1,0:T(4,128)S(1)}, f32[4,4,3328]{2,1,0:T(4,128)S(1)}, u32[]{:S(2)}, u32[]{:S(2)}) collective-permute-start(f32[4,4,3328]{2,1,0:T(4,128)S(1)} %all-to-all-done.rest_0_), channel_id=1, source_target_pairs={{0,2},{1,3},{2,0},{3,1},{4,6},{5,7},{6,4},{7,5},{8,10},{9,11},{10,... | collective-permute-start | bytes 638984 | tf_op jit(solution)/shard_map/ppermute | solution.py:729
  108.4 2.1 %collective-permute-done.23 = f32[64,128]{1,0:T(8,128)S(1)} collective-permute-done((f32[64,128]{1,0:T(8,128)S(1)}, f32[64,128]{1,0:T(8,128)S(1)}, u32[]{:S(2)}, u32[]{:S(2)}) %collective-permute-start.23) | collective-permute-done | bytes 32800 | tf_op jit(solution)/shard_map/ppermute | solution.py:729
  110.6 2.2 %collective-permute-done.22 = bf16[768,128]{1,0:T(8,128)(2,1)S(1)} collective-permute-done((bf16[768,128]{1,0:T(8,128)(2,1)S(1)}, bf16[768,128]{1,0:T(8,128)(2,1)S(1)}, u32[]{:S(2)}, u32[]{:S(2)}) %collective-permute-start.22) | collective-permute-done | bytes 196640 | tf_op jit(solution)/shard_map/ppermute | solution.py:729
  112.8 0.1 broadcast_select_fusion.3
  112.9 1.5 %collective-permute-start.27 = (bf16[1600,128]{1,0:T(8,128)(2,1)S(1)}, bf16[1600,128]{1,0:T(8,128)(2,1)S(1)}, u32[]{:S(2)}, u32[]{:S(2)}) collective-permute-start(bf16[1600,128]{1,0:T(8,128)(2,1)S(1)} %pad_maximum_fusion.1), channel_id=1, source_target_pairs={{0,2},{1,3},{2,0},{3,1},{4,6},{5,7},{6,4},{7,5},{8,10},{9,11},{10,... | collective-permute-start | bytes 1228808 | tf_op jit(solution)/shard_map/ppermute | solution.py:729
  114.4 1.4 %collective-permute-done.26.rest_3_ = f32[4,4,3328]{2,1,0:T(4,128)S(1)} collective-permute-done((f32[4,4,3328]{2,1,0:T(4,128)S(1)}, f32[4,4,3328]{2,1,0:T(4,128)S(1)}, u32[]{:S(2)}, u32[]{:S(2)}) %collective-permute-start.26) | collective-permute-done | bytes 213024 | tf_op jit(solution)/shard_map/ppermute | solution.py:729
  115.9 0.7 copy-done.7
  116.6 2.6 %shard_map.228 = bf16[49,32,64]{2,1,0:T(8,128)(2,1)} custom-call(f32[4,4,3328]{2,1,0:T(4,128)} %copy-done.1, f32[4,4,3328]{2,1,0:T(4,128)} %copy-done.6, f32[4,4,3328]{2,1,0:T(4,128)} %copy-done.5, f32[4,4,3328]{2,1,0:T(4,128)} %copy-done.7), custom_call_target="tpu_custom_call" | custom-call | flops 1 | bytes 1 | tf_op jit(solution)/shard_map/pallas_call | solution.py:698
  119.1 4.4 %collective-permute-done.27 = bf16[1600,128]{1,0:T(8,128)(2,1)S(1)} collective-permute-done((bf16[1600,128]{1,0:T(8,128)(2,1)S(1)}, bf16[1600,128]{1,0:T(8,128)(2,1)S(1)}, u32[]{:S(2)}, u32[]{:S(2)}) %collective-permute-start.27) | collective-permute-done | bytes 409632 | tf_op jit(solution)/shard_map/ppermute | solution.py:729
  123.5 0.2 broadcast_select_fusion.1
  123.7 0.1 collective-permute-start.28
  123.8 2.3 %collective-permute-done.28.other = bf16[3200,128]{1,0:T(8,128)(2,1)S(1)} collective-permute-done((bf16[3200,128]{1,0:T(8,128)(2,1)S(1)}, bf16[3200,128]{1,0:T(8,128)(2,1)S(1)}, u32[]{:S(2)}, u32[]{:S(2)}) %collective-permute-start.28) | collective-permute-done | bytes 819232 | tf_op jit(solution)/shard_map/ppermute | solution.py:729
  126.1 0.9 copy-done.3
  127.0 3.0 %shard_map.229 = (bf16[448,448]{1,0:T(8,128)(2,1)}, bf16[2,384,384]{2,1,0:T(8,128)(2,1)}, bf16[2,320,320]{2,1,0:T(8,128)(2,1)}, bf16[64,256]{1,0:T(8,128)(2,1)},...) custom-call(bf16[3200,128]{1,0:T(8,128)(2,1)} %copy-done, bf16[3200,128]{1,0:T(8,128)(2,1)} %copy-done.3), custom_call_target="tpu_custom_call" | custom-call | flops 1 | bytes 1 | tf_op jit(solution)/shard_map/pallas_call | solution.py:698
  (68 shorter events, 0.9 us)
Async XLA Ops:
  2.9 8.5 %collective-permute-start = (bf16[4,6528]{1,0:T(4,128)(2,1)}, bf16[4,6528]{1,0:T(4,128)(2,1)S(1)}, u32[]{:S(2)}, u32[]{:S(2)}) collective-permute-start(bf16[4,6528]{1,0:T(4,128)(2,1)} %get-tuple-element.67), channel_id=1, source_target_pairs={{0,4},{4,0},{8,12},{12,8},{1,5},{5,1},{9,13},{13,9},{2,6},{6,2},{1... | collective-permute-start | bytes 156680 | tf_op jit(solution)/shard_map/ppermute | solution.py:823
  5.9 6.2 %collective-permute-start.1 = (bf16[4,6528]{1,0:T(4,128)(2,1)}, bf16[4,6528]{1,0:T(4,128)(2,1)S(1)}, u32[]{:S(2)}, u32[]{:S(2)}) collective-permute-start(bf16[4,6528]{1,0:T(4,128)(2,1)} %get-tuple-element.68), channel_id=1, source_target_pairs={{0,8},{4,12},{8,0},{12,4},{1,9},{5,13},{9,1},{13,5},{2,10},{6,14},... | collective-permute-start | bytes 156680 | tf_op jit(solution)/shard_map/ppermute | solution.py:823
  8.5 6.1 %collective-permute-start.2 = (bf16[4,6528]{1,0:T(4,128)(2,1)}, bf16[4,6528]{1,0:T(4,128)(2,1)S(1)}, u32[]{:S(2)}, u32[]{:S(2)}) collective-permute-start(bf16[4,6528]{1,0:T(4,128)(2,1)} %get-tuple-element.69), channel_id=1, source_target_pairs={{0,12},{4,8},{8,4},{12,0},{1,13},{5,9},{9,5},{13,1},{2,14},{6,10},... | collective-permute-start | bytes 156680 | tf_op jit(solution)/shard_map/ppermute | solution.py:823
  11.4 3.3 %copy-start.11 = (bf16[4,6528]{1,0:T(4,128)(2,1)}, bf16[4,6528]{1,0:T(4,128)(2,1)S(1)}, u32[]{:S(2)}) copy-start(bf16[4,6528]{1,0:T(4,128)(2,1)S(1)} %collective-permute-done.rest_1_) | copy-start | bytes 156676
  12.2 2.5 %copy-start.12 = (bf16[4,6528]{1,0:T(4,128)(2,1)}, bf16[4,6528]{1,0:T(4,128)(2,1)S(1)}, u32[]{:S(2)}) copy-start(bf16[4,6528]{1,0:T(4,128)(2,1)S(1)} %collective-permute-done.1.rest_2_) | copy-start | bytes 156676
  14.6 0.6 copy-start.13
  23.8 1.9 %collective-permute-start.3 = (f32[2,128]{1,0:T(2,128)}, f32[2,128]{1,0:T(2,128)S(1)}, u32[]{:S(2)}, u32[]{:S(2)}) collective-permute-start(f32[2,128]{1,0:T(2,128)} %get-tuple-element.70), channel_id=1, source_target_pairs={{0,1},{1,0},{2,3},{3,2},{4,5},{5,4},{6,7},{7,6},{8,9},{9,8},{10,11... | collective-permute-start | bytes 3080 | tf_op jit(solution)/shard_map/ppermute | solution.py:872
  23.9 3.8 %collective-permute-start.4 = (f32[2,128]{1,0:T(2,128)}, f32[2,128]{1,0:T(2,128)S(1)}, u32[]{:S(2)}, u32[]{:S(2)}) collective-permute-start(f32[2,128]{1,0:T(2,128)} %get-tuple-element.70), channel_id=1, source_target_pairs={{0,2},{1,3},{2,0},{3,1},{4,6},{5,7},{6,4},{7,5},{8,10},{9,11},{10,... | collective-permute-start | bytes 3080 | tf_op jit(solution)/shard_map/ppermute | solution.py:872
  25.4 3.2 %collective-permute-start.5 = (f32[2,128]{1,0:T(2,128)}, f32[2,128]{1,0:T(2,128)S(1)}, u32[]{:S(2)}, u32[]{:S(2)}) collective-permute-start(f32[2,128]{1,0:T(2,128)} %get-tuple-element.70), channel_id=1, source_target_pairs={{0,3},{1,2},{2,1},{3,0},{4,7},{5,6},{6,5},{7,4},{8,11},{9,10},{10,... | collective-permute-start | bytes 3080 | tf_op jit(solution)/shard_map/ppermute | solution.py:872
  29.3 7.0 %copy-start.14 = (f32[8,128]{1,0:T(8,128)}, f32[8,128]{1,0:T(8,128)S(1)}, u32[]{:S(2)}) copy-start(f32[8,128]{1,0:T(8,128)S(1)} %pad_maximum_fusion.5.refs_0_) | copy-start | bytes 12292
  29.3 4.5 %collective-permute-start.6 = (f32[8,128]{1,0:T(8,128)S(1)}, f32[8,128]{1,0:T(8,128)S(1)}, u32[]{:S(2)}, u32[]{:S(2)}) collective-permute-start(f32[8,128]{1,0:T(8,128)S(1)} %pad_maximum_fusion.5.refs_0_), channel_id=1, source_target_pairs={{0,4},{4,0},{8,12},{12,8},{1,5},{5,1},{9,13},{13,9},{2,6},{6,2},{1... | collective-permute-start | bytes 12296 | tf_op jit(solution)/shard_map/ppermute | solution.py:877
  29.4 4.6 %collective-permute-start.7 = (f32[8,128]{1,0:T(8,128)S(1)}, f32[8,128]{1,0:T(8,128)S(1)}, u32[]{:S(2)}, u32[]{:S(2)}) collective-permute-start(f32[8,128]{1,0:T(8,128)S(1)} %pad_maximum_fusion.5.refs_0_), channel_id=1, source_target_pairs={{0,8},{4,12},{8,0},{12,4},{1,9},{5,13},{9,1},{13,5},{2,10},{6,14},... | collective-permute-start | bytes 12296 | tf_op jit(solution)/shard_map/ppermute | solution.py:877
  30.9 5.4 %collective-permute-start.8 = (f32[8,128]{1,0:T(8,128)S(1)}, f32[8,128]{1,0:T(8,128)S(1)}, u32[]{:S(2)}, u32[]{:S(2)}) collective-permute-start(f32[8,128]{1,0:T(8,128)S(1)} %pad_maximum_fusion.5.refs_0_), channel_id=1, source_target_pairs={{0,12},{4,8},{8,4},{12,0},{1,13},{5,9},{9,5},{13,1},{2,14},{6,10},... | collective-permute-start | bytes 12296 | tf_op jit(solution)/shard_map/ppermute | solution.py:877
  33.8 2.5 %copy-start.15 = (f32[8,128]{1,0:T(8,128)}, f32[8,128]{1,0:T(8,128)S(1)}, u32[]{:S(2)}) copy-start(f32[8,128]{1,0:T(8,128)S(1)} %collective-permute-done.6.refs_1_) | copy-start | bytes 12292
  34.0 2.3 %copy-start.16 = (f32[8,128]{1,0:T(8,128)}, f32[8,128]{1,0:T(8,128)S(1)}, u32[]{:S(2)}) copy-start(f32[8,128]{1,0:T(8,128)S(1)} %collective-permute-done.7.refs_2_) | copy-start | bytes 12292
  36.3 0.6 copy-start.17
  45.4 3.0 %collective-permute-start.10 = (f32[2176,128]{1,0:T(8,128)}, f32[2176,128]{1,0:T(8,128)S(1)}, u32[]{:S(2)}, u32[]{:S(2)}) collective-permute-start(f32[2176,128]{1,0:T(8,128)} %get-tuple-element.85), channel_id=1, source_target_pairs={{0,1},{1,0},{2,3},{3,2},{4,5},{5,4},{6,7},{7,6},{8,9},{9,8},{10,11... | collective-permute-start | bytes 3342344 | tf_op jit(solution)/shard_map/ppermute | solution.py:729
  45.4 4.4 %collective-permute-start.9 = (f32[896,128]{1,0:T(8,128)}, f32[896,128]{1,0:T(8,128)S(1)}, u32[]{:S(2)}, u32[]{:S(2)}) collective-permute-start(f32[896,128]{1,0:T(8,128)} %get-tuple-element.83), channel_id=1, source_target_pairs={{0,1},{1,0},{2,3},{3,2},{4,5},{5,4},{6,7},{7,6},{8,9},{9,8},{10,11... | collective-permute-start | bytes 1376264 | tf_op jit(solution)/shard_map/ppermute | solution.py:729
  49.8 1.0 copy-start.4
  50.9 10.9 %collective-permute-start.11 = (f32[448,128]{1,0:T(8,128)S(1)}, f32[448,128]{1,0:T(8,128)S(1)}, u32[]{:S(2)}, u32[]{:S(2)}) collective-permute-start(f32[448,128]{1,0:T(8,128)S(1)} %dynamic-slice_bitcast_fusion.2), channel_id=1, source_target_pairs={{0,4},{4,0},{8,12},{12,8},{1,5},{5,1},{9,13},{13,9},{2,6},{6,2},{1... | collective-permute-start | bytes 688136 | tf_op jit(solution)/shard_map/ppermute | solution.py:729
  50.9 25.4 %collective-permute-start.13 = (f32[1088,128]{1,0:T(8,128)S(1)}, f32[1088,128]{1,0:T(8,128)S(1)}, u32[]{:S(2)}, u32[]{:S(2)}) collective-permute-start(f32[1088,128]{1,0:T(8,128)S(1)} %dynamic-slice_bitcast_fusion), channel_id=1, source_target_pairs={{0,2},{1,3},{2,0},{3,1},{4,6},{5,7},{6,4},{7,5},{8,10},{9,11},{10,... | collective-permute-start | bytes 1671176 | tf_op jit(solution)/shard_map/ppermute | solution.py:729
  57.1 15.8 %all-to-all-start = ((f32[4,4,3328]{2,1,0:T(4,128)}), f32[4,4,3328]{2,1,0:T(4,128)S(1)}, u32[]{:S(2)}, u32[]{:S(2)}) async-start(f32[4,4,3328]{2,1,0:T(4,128)} %shard_map.226), calls=%async_computation | async-start | bytes 425984 | tf_op jit(solution)/shard_map/all_to_all | solution.py:813
  61.8 22.7 %collective-permute-start.12 = (f32[224,128]{1,0:T(8,128)S(1)}, f32[224,128]{1,0:T(8,128)S(1)}, u32[]{:S(2)}, u32[]{:S(2)}) collective-permute-start(f32[224,128]{1,0:T(8,128)S(1)} %dynamic-slice_bitcast_fusion.4), channel_id=1, source_target_pairs={{0,8},{4,12},{8,0},{12,4},{1,9},{5,13},{9,1},{13,5},{2,10},{6,14},... | collective-permute-start | bytes 344072 | tf_op jit(solution)/shard_map/ppermute | solution.py:729
  73.0 35.5 %copy-start.1 = (f32[4,4,3328]{2,1,0:T(4,128)}, f32[4,4,3328]{2,1,0:T(4,128)S(1)}, u32[]{:S(2)}) copy-start(f32[4,4,3328]{2,1,0:T(4,128)S(1)} %all-to-all-done.rest_0_) | copy-start | bytes 638980
  73.0 10.1 %all-to-all-start.1 = ((f32[4,4,3328]{2,1,0:T(4,128)}), f32[4,4,3328]{2,1,0:T(4,128)S(1)}, u32[]{:S(2)}, u32[]{:S(2)}) async-start(f32[4,4,3328]{2,1,0:T(4,128)} %get-tuple-element.102), calls=%async_computation.1 | async-start | bytes 425984 | tf_op jit(solution)/shard_map/all_to_all | solution.py:813
  76.5 9.2 %collective-permute-start.15 = (f32[544,128]{1,0:T(8,128)S(1)}, f32[544,128]{1,0:T(8,128)S(1)}, u32[]{:S(2)}, u32[]{:S(2)}) collective-permute-start(f32[544,128]{1,0:T(8,128)S(1)} %dynamic-slice_bitcast_fusion.1), channel_id=1, source_target_pairs={{0,4},{4,0},{8,12},{12,8},{1,5},{5,1},{9,13},{13,9},{2,6},{6,2},{1... | collective-permute-start | bytes 835592 | tf_op jit(solution)/shard_map/ppermute | solution.py:729
  83.1 7.9 %copy-start.2 = (f32[4,4,3328]{2,1,0:T(4,128)}, f32[4,4,3328]{2,1,0:T(4,128)S(1)}, u32[]{:S(2)}) copy-start(f32[4,4,3328]{2,1,0:T(4,128)S(1)} %all-to-all-done.1.rest_0_) | copy-start | bytes 638980
  83.1 6.5 %collective-permute-start.17 = (f32[4,4,3328]{2,1,0:T(4,128)S(1)}, f32[4,4,3328]{2,1,0:T(4,128)S(1)}, u32[]{:S(2)}, u32[]{:S(2)}) collective-permute-start(f32[4,4,3328]{2,1,0:T(4,128)S(1)} %all-to-all-done.1.rest_0_), channel_id=1, source_target_pairs={{0,2},{1,3},{2,0},{3,1},{4,6},{5,7},{6,4},{7,5},{8,10},{9,11},{10,... | collective-permute-start | bytes 638984 | tf_op jit(solution)/shard_map/ppermute | solution.py:729
  84.5 5.6 %collective-permute-start.16 = (f32[4,4,3328]{2,1,0:T(4,128)S(1)}, f32[4,4,3328]{2,1,0:T(4,128)S(1)}, u32[]{:S(2)}, u32[]{:S(2)}) collective-permute-start(f32[4,4,3328]{2,1,0:T(4,128)S(1)} %all-to-all-done.1.rest_0_), channel_id=1, source_target_pairs={{0,1},{1,0},{2,3},{3,2},{4,5},{5,4},{6,7},{7,6},{8,9},{9,8},{10,11... | collective-permute-start | bytes 638984 | tf_op jit(solution)/shard_map/ppermute | solution.py:729
  84.6 5.6 %collective-permute-start.14 = (f32[112,128]{1,0:T(8,128)S(1)}, f32[112,128]{1,0:T(8,128)S(1)}, u32[]{:S(2)}, u32[]{:S(2)}) collective-permute-start(f32[112,128]{1,0:T(8,128)S(1)} %dynamic-slice_bitcast_fusion.5), channel_id=1, source_target_pairs={{0,2},{1,3},{2,0},{3,1},{4,6},{5,7},{6,4},{7,5},{8,10},{9,11},{10,... | collective-permute-start | bytes 172040 | tf_op jit(solution)/shard_map/ppermute | solution.py:729
  85.7 9.3 %collective-permute-start.19 = (f32[272,128]{1,0:T(8,128)S(1)}, f32[272,128]{1,0:T(8,128)S(1)}, u32[]{:S(2)}, u32[]{:S(2)}) collective-permute-start(f32[272,128]{1,0:T(8,128)S(1)} %dynamic-slice_bitcast_fusion.3), channel_id=1, source_target_pairs={{0,8},{4,12},{8,0},{12,4},{1,9},{5,13},{9,1},{13,5},{2,10},{6,14},... | collective-permute-start | bytes 417800 | tf_op jit(solution)/shard_map/ppermute | solution.py:729
  89.6 1.5 %copy-start.8 = (f32[4,4,3328]{2,1,0:T(4,128)}, f32[4,4,3328]{2,1,0:T(4,128)S(1)}, u32[]{:S(2)}) copy-start(f32[4,4,3328]{2,1,0:T(4,128)S(1)} %collective-permute-done.17.rest_2_) | copy-start | bytes 638980
  89.6 1.5 %collective-permute-start.18 = (f32[4,4,3328]{2,1,0:T(4,128)S(1)}, f32[4,4,3328]{2,1,0:T(4,128)S(1)}, u32[]{:S(2)}, u32[]{:S(2)}) collective-permute-start(f32[4,4,3328]{2,1,0:T(4,128)S(1)} %collective-permute-done.17.rest_2_), channel_id=1, source_target_pairs={{0,1},{1,0},{2,3},{3,2},{4,5},{5,4},{6,7},{7,6},{8,9},{9,8},{10,11... | collective-permute-start | bytes 638984 | tf_op jit(solution)/shard_map/ppermute | solution.py:729
  90.2 0.8 copy-start.9
  91.0 0.7 copy-start.10
  95.8 3.9 %collective-permute-start.21 = (f32[64,128]{1,0:T(8,128)S(1)}, f32[64,128]{1,0:T(8,128)S(1)}, u32[]{:S(2)}, u32[]{:S(2)}) collective-permute-start(f32[64,128]{1,0:T(8,128)S(1)} %constant_dynamic-slice_fusion), channel_id=1, source_target_pairs={{0,4},{4,0},{8,12},{12,8},{1,5},{5,1},{9,13},{13,9},{2,6},{6,2},{1... | collective-permute-start | bytes 98312 | tf_op jit(solution)/shard_map/ppermute | solution.py:729
  97.8 7.3 %collective-permute-start.20 = (bf16[384,128]{1,0:T(8,128)(2,1)S(1)}, bf16[384,128]{1,0:T(8,128)(2,1)S(1)}, u32[]{:S(2)}, u32[]{:S(2)}) collective-permute-start(bf16[384,128]{1,0:T(8,128)(2,1)S(1)} %pad_maximum_fusion.4), channel_id=1, source_target_pairs={{0,8},{4,12},{8,0},{12,4},{1,9},{5,13},{9,1},{13,5},{2,10},{6,14},... | collective-permute-start | bytes 294920 | tf_op jit(solution)/shard_map/ppermute | solution.py:729
  105.2 7.6 %collective-permute-start.22 = (bf16[768,128]{1,0:T(8,128)(2,1)S(1)}, bf16[768,128]{1,0:T(8,128)(2,1)S(1)}, u32[]{:S(2)}, u32[]{:S(2)}) collective-permute-start(bf16[768,128]{1,0:T(8,128)(2,1)S(1)} %pad_maximum_fusion.3), channel_id=1, source_target_pairs={{0,4},{4,0},{8,12},{12,8},{1,5},{5,1},{9,13},{13,9},{2,6},{6,2},{1... | collective-permute-start | bytes 589832 | tf_op jit(solution)/shard_map/ppermute | solution.py:729
  105.3 5.3 %collective-permute-start.23 = (f32[64,128]{1,0:T(8,128)S(1)}, f32[64,128]{1,0:T(8,128)S(1)}, u32[]{:S(2)}, u32[]{:S(2)}) collective-permute-start(f32[64,128]{1,0:T(8,128)S(1)} %fusion.2), channel_id=1, source_target_pairs={{0,8},{4,12},{8,0},{12,4},{1,9},{5,13},{9,1},{13,5},{2,10},{6,14},... | collective-permute-start | bytes 98312 | tf_op jit(solution)/shard_map/ppermute | solution.py:729
  107.0 7.4 %collective-permute-start.25 = (f32[4,4,3328]{2,1,0:T(4,128)S(1)}, f32[4,4,3328]{2,1,0:T(4,128)S(1)}, u32[]{:S(2)}, u32[]{:S(2)}) collective-permute-start(f32[4,4,3328]{2,1,0:T(4,128)S(1)} %all-to-all-done.rest_0_), channel_id=1, source_target_pairs={{0,2},{1,3},{2,0},{3,1},{4,6},{5,7},{6,4},{7,5},{8,10},{9,11},{10,... | collective-permute-start | bytes 638984 | tf_op jit(solution)/shard_map/ppermute | solution.py:729
  108.4 6.0 %collective-permute-start.24 = (f32[4,4,3328]{2,1,0:T(4,128)S(1)}, f32[4,4,3328]{2,1,0:T(4,128)S(1)}, u32[]{:S(2)}, u32[]{:S(2)}) collective-permute-start(f32[4,4,3328]{2,1,0:T(4,128)S(1)} %all-to-all-done.rest_0_), channel_id=1, source_target_pairs={{0,1},{1,0},{2,3},{3,2},{4,5},{5,4},{6,7},{7,6},{8,9},{9,8},{10,11... | collective-permute-start | bytes 638984 | tf_op jit(solution)/shard_map/ppermute | solution.py:729
  112.9 10.6 %collective-permute-start.27 = (bf16[1600,128]{1,0:T(8,128)(2,1)S(1)}, bf16[1600,128]{1,0:T(8,128)(2,1)S(1)}, u32[]{:S(2)}, u32[]{:S(2)}) collective-permute-start(bf16[1600,128]{1,0:T(8,128)(2,1)S(1)} %pad_maximum_fusion.1), channel_id=1, source_target_pairs={{0,2},{1,3},{2,0},{3,1},{4,6},{5,7},{6,4},{7,5},{8,10},{9,11},{10,... | collective-permute-start | bytes 1228808 | tf_op jit(solution)/shard_map/ppermute | solution.py:729
  114.4 1.5 %copy-start.5 = (f32[4,4,3328]{2,1,0:T(4,128)}, f32[4,4,3328]{2,1,0:T(4,128)S(1)}, u32[]{:S(2)}) copy-start(f32[4,4,3328]{2,1,0:T(4,128)S(1)} %collective-permute-done.25.rest_2_) | copy-start | bytes 638980
  114.4 1.5 %collective-permute-start.26 = (f32[4,4,3328]{2,1,0:T(4,128)S(1)}, f32[4,4,3328]{2,1,0:T(4,128)S(1)}, u32[]{:S(2)}, u32[]{:S(2)}) collective-permute-start(f32[4,4,3328]{2,1,0:T(4,128)S(1)} %collective-permute-done.25.rest_2_), channel_id=1, source_target_pairs={{0,1},{1,0},{2,3},{3,2},{4,5},{5,4},{6,7},{7,6},{8,9},{9,8},{10,11... | collective-permute-start | bytes 638984 | tf_op jit(solution)/shard_map/ppermute | solution.py:729
  114.4 1.4 %copy-start.6 = (f32[4,4,3328]{2,1,0:T(4,128)}, f32[4,4,3328]{2,1,0:T(4,128)S(1)}, u32[]{:S(2)}) copy-start(f32[4,4,3328]{2,1,0:T(4,128)S(1)} %collective-permute-done.24.rest_1_) | copy-start | bytes 638980
  115.9 0.7 copy-start.7
  123.7 2.4 %copy-start = (bf16[3200,128]{1,0:T(8,128)(2,1)}, bf16[3200,128]{1,0:T(8,128)(2,1)S(1)}, u32[]{:S(2)}) copy-start(bf16[3200,128]{1,0:T(8,128)(2,1)S(1)} %pad_maximum_fusion.mine) | copy-start | bytes 2457604
  123.7 2.4 %collective-permute-start.28 = (bf16[3200,128]{1,0:T(8,128)(2,1)S(1)}, bf16[3200,128]{1,0:T(8,128)(2,1)S(1)}, u32[]{:S(2)}, u32[]{:S(2)}) collective-permute-start(bf16[3200,128]{1,0:T(8,128)(2,1)S(1)} %pad_maximum_fusion.mine), channel_id=1, source_target_pairs={{0,1},{1,0},{2,3},{3,2},{4,5},{5,4},{6,7},{7,6},{8,9},{9,8},{10,11... | collective-permute-start | bytes 2457608 | tf_op jit(solution)/shard_map/ppermute | solution.py:729
  126.1 0.9 copy-start.3

commit v9 on v8

--- a/solution.py
+++ b/solution.py
@@ -143,10 +143,8 @@
 
 def put_rows(out_ref, cols, value):
     peers, cap = out_ref.shape[0], out_ref.shape[1]
-    flip = flip_of(peers)
     for n in range(peers):
-        place = jnp.bitwise_xor(flip, n) if is_direct(peers) else n
-        out_ref[place, :, cols] = value[n * cap : (n + 1) * cap].astype(out_ref.dtype)
+        out_ref[n, :, cols] = value[n * cap : (n + 1) * cap].astype(out_ref.dtype)
 
 
 def slot_sums(terms, one_hot, out_ref, factor=None):
@@ -809,7 +807,15 @@
     direct = is_direct(peers)
     order = Order()
 
+    def pairwise(pieces):
+        return [pieces[0]] + [
+            lax.ppermute(pieces[k], "graph", [(i, i ^ k) for i in range(peers)])
+            for k in range(1, peers)
+        ]
+
     def exchange(value):
+        if direct:
+            return jnp.stack(pairwise([value[k] for k in range(peers)]))
         return lax.all_to_all(value, "graph", split_axis=0, concat_axis=0, tiled=True)
 
     cot = jnp.transpose(out_cotangent, (1, 0, 2))
@@ -818,13 +824,7 @@
         send_rows, recv_rows, jnp.transpose(atom_embed, (1, 0, 2)), cot,
         scalars=2
     )
-    if direct:
-        tables = [outgoing[0]] + [
-            lax.ppermute(outgoing[k], "graph", [(i, i ^ k) for i in range(peers)])
-            for k in range(1, peers)
-        ]
-    else:
-        tables = list(exchange(jnp.stack(outgoing)))
+    tables = pairwise(outgoing) if direct else list(exchange(jnp.stack(outgoing)))
 
     source_row = source_slot.reshape(1, edges)
     target_row = target_slot.reshape(1, edges)
@@ -928,12 +928,12 @@
     )
     order.mark(source_sums)
     next(zero_steps)
-    returned = order.mark(order.hold(exchange(source_sums)))
     for _ in range(bits_of("edge") - 1):
         next(rest_steps)
     message_hops = gather_lanes(order.hold(messages), order)
     next(message_hops)
     next(zero_steps)
+    returned = order.hold(exchange(source_sums))
     next(rest_steps)
     message_rows = finish_steps(message_hops)
     zero_share = finish_steps(zero_steps)

time: 131 us -> 122 us (0.931)
  starting transfers between devices: 38 us -> 30.8 us
  waiting for transfers between devices: 45.8 us -> 44.1 us
    all_to_all x2 -> x0, waiting for transfers between devices: 12.7 us -> none  [exchange(): lax.all_to_all(value, 'graph', split_axis=0, concat_axis=0, tiled=True)]
    ppermute x3 -> x9, starting transfers between devices: 5.62 us -> 15.1 us  [pairwise(): lax.ppermute(pieces[k], 'graph', [(i, i ^ k) for i in range(peers)])]
    ppermute x20, starting transfers between devices: 18 us -> 9.31 us  [swap(): return lax.ppermute(value, axis, [(i, i ^ 1 << bit) for i in range(size)])]
    all_to_all x2 -> x0, starting transfers between devices: 8.01 us -> none  [exchange(): lax.all_to_all(value, 'graph', split_axis=0, concat_axis=0, tiled=True)]
    ppermute x20, waiting for transfers between devices: 24.4 us -> 30.5 us  [swap(): return lax.ppermute(value, axis, [(i, i ^ 1 << bit) for i in range(size)])]
    ppermute x3 -> x9, waiting for transfers between devices: 3.27 us -> 8.26 us  [pairwise(): lax.ppermute(pieces[k], 'graph', [(i, i ^ k) for i in range(peers)])]
    unnamed x37 -> x39, local copies, waits for them, and re-layouts: 6.11 us -> 5.33 us
  transfers between devices with their start and end apart: 31 -> 35, of which waited for: 20 -> 19; matrix products, arithmetic and copies ran while one was open for 4% -> 6% of each run, Pallas kernels for 9% -> 9%
where the time goes in v9:
time: 122 us
  waiting for transfers between devices  44.1 us (36%)
  Pallas kernels  33.7 us (28%)
  starting transfers between devices  30.8 us (25%)
  local copies, waits for them, and re-layouts  8.37 us (7%)
  other arithmetic  3.56 us (3%)
    pallas_call x7, Pallas kernels, call(): pl.pallas_call(kernel, out_shape=[jax.ShapeDtypeStruct(shape, kind) for s...  33.7 us
    ppermute x20, waiting for transfers between devices, swap(): return lax.ppermute(value, axis, [(i, i ^ 1 << bit) for i in range(size)])  30.5 us
    ppermute x9, starting transfers between devices, pairwise(): lax.ppermute(pieces[k], 'graph', [(i, i ^ k) for i in range(peers)])  15.1 us
    ppermute x20, starting transfers between devices, swap(): return lax.ppermute(value, axis, [(i, i ^ 1 << bit) for i in range(size)])  9.31 us
    ppermute x9, waiting for transfers between devices, pairwise(): lax.ppermute(pieces[k], 'graph', [(i, i ^ k) for i in range(peers)])  8.26 us
    unnamed x39, local copies, waits for them, and re-layouts  5.33 us
    ppermute x3, starting transfers between devices, shards(): lax.ppermute(graph_stats, 'graph', [(i, i ^ k) for i in range(peers)])  4.44 us
    ppermute x3, waiting for transfers between devices, shards(): lax.ppermute(stats, 'edge', [(i, i ^ k) for i in range(lanes_total)])  2.74 us
  transfers between devices with their start and end apart: 35, of which 19 were waited for; matrix products, arithmetic and copies ran while one was open for 6% of the time, Pallas kernels for 9%

profile of v9, /device:TPU:0, one launch (start us, length us, event | category | flops | bytes accessed | tf_op | source)
XLA Modules:
  0.0 121.6 jit_solution(12972931153542004060)
XLA Ops:
  0.6 2.2 %shard_map.223 = (bf16[4,6528]{1,0:T(4,128)(2,1)}, bf16[4,6528]{1,0:T(4,128)(2,1)}, bf16[4,6528]{1,0:T(4,128)(2,1)}, bf16[4,6528]{1,0:T(4,128)(2,1)}) custom-call(s32[1,4,1,4]{3,2,1,0:T(1,128)} %send.1, s32[1,4,1,4]{3,2,1,0:T(1,128)} %recv.1, bf16[49,32,64]{2,1,0:T(8,128)(2,1)} %bitcast.75, bf16[49,32,64]{2,1,0:T(8,128)(2,1)} %bitcast.66), custom_call_target="tpu_custom_call" | custom-call | flops 1 | bytes 1 | tf_op jit(solution)/shard_map/pallas_call | solution.py:696
  2.9 3.0 %collective-permute-start = (bf16[4,6528]{1,0:T(4,128)(2,1)}, bf16[4,6528]{1,0:T(4,128)(2,1)S(1)}, u32[]{:S(2)}, u32[]{:S(2)}) collective-permute-start(bf16[4,6528]{1,0:T(4,128)(2,1)} %get-tuple-element.67), channel_id=1, source_target_pairs={{0,4},{4,0},{8,12},{12,8},{1,5},{5,1},{9,13},{13,9},{2,6},{6,2},{1... | collective-permute-start | bytes 156680 | tf_op jit(solution)/shard_map/ppermute | solution.py:812
  5.9 2.6 %collective-permute-start.1 = (bf16[4,6528]{1,0:T(4,128)(2,1)}, bf16[4,6528]{1,0:T(4,128)(2,1)S(1)}, u32[]{:S(2)}, u32[]{:S(2)}) collective-permute-start(bf16[4,6528]{1,0:T(4,128)(2,1)} %get-tuple-element.68), channel_id=1, source_target_pairs={{0,8},{4,12},{8,0},{12,4},{1,9},{5,13},{9,1},{13,5},{2,10},{6,14},... | collective-permute-start | bytes 156680 | tf_op jit(solution)/shard_map/ppermute | solution.py:812
  8.5 1.2 reshape.50.adot.refs_17_
  9.7 1.7 %copy.25.rotation = bf16[256,235]{1,0:T(8,128)(2,1)} copy(bf16[256,235]{0,1:T(8,128)(2,1)} %param.22) | data formatting | bytes 240640 | tf_op args[6]
  11.4 0.8 collective-permute-done.1.rest_2_
  12.2 2.5 %collective-permute-done.2.rest_3_ = bf16[4,6528]{1,0:T(4,128)(2,1)S(1)} collective-permute-done((bf16[4,6528]{1,0:T(4,128)(2,1)}, bf16[4,6528]{1,0:T(4,128)(2,1)S(1)}, u32[]{:S(2)}, u32[]{:S(2)}) %collective-permute-start.2) | collective-permute-done | bytes 52256 | tf_op jit(solution)/shard_map/ppermute | solution.py:812
  14.6 0.6 copy-done.14
  15.3 8.6 %shard_map.224 = (f32[4,4,3328]{2,1,0:T(4,128)}, f32[2,128]{1,0:T(2,128)}, bf16[448,256]{1,0:T(8,128)(2,1)}, bf16[384,512]{1,0:T(8,128)(2,1)}, bf16[320,512]{1,0...) custom-call(s32[1,256]{1,0:T(1,128)} %bitcast.85, ...), custom_call_target="tpu_custom_call" | custom-call | flops 1 | bytes 1 | tf_op jit(solution)/shard_map/pallas_call | solution.py:696
  23.9 1.6 %collective-permute-start.4 = (f32[2,128]{1,0:T(2,128)}, f32[2,128]{1,0:T(2,128)S(1)}, u32[]{:S(2)}, u32[]{:S(2)}) collective-permute-start(f32[2,128]{1,0:T(2,128)} %get-tuple-element.70), channel_id=1, source_target_pairs={{0,2},{1,3},{2,0},{3,1},{4,6},{5,7},{6,4},{7,5},{8,10},{9,11},{10,... | collective-permute-start | bytes 3080 | tf_op jit(solution)/shard_map/ppermute | solution.py:872
  25.5 0.3 collective-permute-start.5
  25.8 2.0 %collective-permute-done.4 = f32[2,128]{1,0:T(2,128)S(1)} collective-permute-done((f32[2,128]{1,0:T(2,128)}, f32[2,128]{1,0:T(2,128)S(1)}, u32[]{:S(2)}, u32[]{:S(2)}) %collective-permute-start.4) | collective-permute-done | bytes 1056 | tf_op jit(solution)/shard_map/ppermute | solution.py:872
  27.7 0.8 collective-permute-done.5
  28.5 0.6 pad_maximum_fusion.7.refs_0_
  29.1 0.1 collective-permute-start.6
  29.2 1.5 %collective-permute-start.7 = (f32[8,128]{1,0:T(8,128)S(1)}, f32[8,128]{1,0:T(8,128)S(1)}, u32[]{:S(2)}, u32[]{:S(2)}) collective-permute-start(f32[8,128]{1,0:T(8,128)S(1)} %pad_maximum_fusion.7.refs_0_), channel_id=1, source_target_pairs={{0,8},{4,12},{8,0},{12,4},{1,9},{5,13},{9,1},{13,5},{2,10},{6,14},... | collective-permute-start | bytes 12296 | tf_op jit(solution)/shard_map/ppermute | solution.py:877
  30.7 2.9 %collective-permute-start.8 = (f32[8,128]{1,0:T(8,128)S(1)}, f32[8,128]{1,0:T(8,128)S(1)}, u32[]{:S(2)}, u32[]{:S(2)}) collective-permute-start(f32[8,128]{1,0:T(8,128)S(1)} %pad_maximum_fusion.7.refs_0_), channel_id=1, source_target_pairs={{0,12},{4,8},{8,4},{12,0},{1,13},{5,9},{9,5},{13,1},{2,14},{6,10},... | collective-permute-start | bytes 12296 | tf_op jit(solution)/shard_map/ppermute | solution.py:877
  33.6 0.2 collective-permute-done.7.refs_2_
  33.8 2.3 %collective-permute-done.8.refs_3_ = f32[8,128]{1,0:T(8,128)S(1)} collective-permute-done((f32[8,128]{1,0:T(8,128)S(1)}, f32[8,128]{1,0:T(8,128)S(1)}, u32[]{:S(2)}, u32[]{:S(2)}) %collective-permute-start.8) | collective-permute-done | bytes 4128 | tf_op jit(solution)/shard_map/ppermute | solution.py:877
  36.1 0.6 copy-done.18
  36.7 8.5 %shard_map.225 = (bf16[448,256]{1,0:T(8,128)(2,1)}, bf16[384,512]{1,0:T(8,128)(2,1)}, bf16[320,512]{1,0:T(8,128)(2,1)}, bf16[256,256]{1,0:T(8,128)(2,1)}, f32[21...) custom-call(f32[8,128]{1,0:T(8,128)} %copy-done.15, f32[8,128]{1,0:T(8,128)} %copy-done.16, ...), custom_call_target="tpu_custom_call" | custom-call | flops 1 | bytes 1 | tf_op jit(solution)/shard_map/pallas_call | solution.py:696
  45.3 0.1 collective-permute-start.16
  45.4 3.4 %collective-permute-start.17 = (f32[4,3328]{1,0:T(4,128)S(1)}, f32[4,3328]{1,0:T(4,128)S(1)}, u32[]{:S(2)}, u32[]{:S(2)}) collective-permute-start(f32[4,3328]{1,0:T(4,128)S(1)} %get-tuple-element.133), channel_id=1, source_target_pairs={{0,8},{4,12},{8,0},{12,4},{1,9},{5,13},{9,1},{13,5},{2,10},{6,14},... | collective-permute-start | bytes 159752 | tf_op jit(solution)/shard_map/ppermute | solution.py:812
  48.9 0.9 collective-permute-start.18
  49.8 2.7 %collective-permute-done.17 = f32[4,3328]{1,0:T(4,128)S(1)} collective-permute-done((f32[4,3328]{1,0:T(4,128)S(1)}, f32[4,3328]{1,0:T(4,128)S(1)}, u32[]{:S(2)}, u32[]{:S(2)}) %collective-permute-start.17) | collective-permute-done | bytes 53280 | tf_op jit(solution)/shard_map/ppermute | solution.py:812
  52.5 2.3 %collective-permute-done.18 = f32[4,3328]{1,0:T(4,128)S(1)} collective-permute-done((f32[4,3328]{1,0:T(4,128)S(1)}, f32[4,3328]{1,0:T(4,128)S(1)}, u32[]{:S(2)}, u32[]{:S(2)}) %collective-permute-start.18) | collective-permute-done | bytes 53280 | tf_op jit(solution)/shard_map/ppermute | solution.py:812
  54.9 1.4 %add.69 = f32[2176,128]{1,0:T(8,128)S(1)} add(f32[2176,128]{1,0:T(8,128)} %get-tuple-element.84, f32[2176,128]{1,0:T(8,128)S(1)} %collective-permute-done.10) | non-fusion elementwise | flops 278528 | bytes 3342336 | tf_op jit(solution)/shard_map/add | solution.py:758
  56.4 0.8 collective-permute-start.13
  57.2 0.2 copy-done.4
  57.4 0.1 collective-permute-start.11
  57.5 5.6 %shard_map.226 = f32[4,4,3328]{2,1,0:T(4,128)} custom-call(s32[1,256]{1,0:T(1,128)} %bitcast.86, f32[16,128]{1,0:T(8,128)} %get-tuple-element.88.lists, f32[235,256]{1,0:T(8,128)} %get-tuple-element.73.refs_7_.rot, bf16[448,256]{1,0:T(8,128)(2,1)} %get-tuple-element.89.g0, bf16[384,512]{1,0:T(8,128)(2,1)} %get-tuple-element.90.g1, ...), custom_call_target="tpu_custom_call" | custom-call | flops 1 | bytes 1 | tf_op jit(solution)/shard_map/pallas_call | solution.py:696
  63.1 0.9 fusion.2
  64.0 2.1 %collective-permute-start.22 = (f32[4,3328]{1,0:T(4,128)S(1)}, f32[4,3328]{1,0:T(4,128)S(1)}, u32[]{:S(2)}, u32[]{:S(2)}) collective-permute-start(f32[4,3328]{1,0:T(4,128)S(1)} %get-tuple-element.130), channel_id=1, source_target_pairs={{0,4},{4,0},{8,12},{12,8},{1,5},{5,1},{9,13},{13,9},{2,6},{6,2},{1... | collective-permute-start | bytes 159752 | tf_op jit(solution)/shard_map/ppermute | solution.py:812
  66.0 1.2 %collective-permute-start.23 = (f32[4,3328]{1,0:T(4,128)S(1)}, f32[4,3328]{1,0:T(4,128)S(1)}, u32[]{:S(2)}, u32[]{:S(2)}) collective-permute-start(f32[4,3328]{1,0:T(4,128)S(1)} %get-tuple-element.129), channel_id=1, source_target_pairs={{0,8},{4,12},{8,0},{12,4},{1,9},{5,13},{9,1},{13,5},{2,10},{6,14},... | collective-permute-start | bytes 159752 | tf_op jit(solution)/shard_map/ppermute | solution.py:812
  67.3 1.8 %collective-permute-start.12 = (f32[224,128]{1,0:T(8,128)S(1)}, f32[224,128]{1,0:T(8,128)S(1)}, u32[]{:S(2)}, u32[]{:S(2)}) collective-permute-start(f32[224,128]{1,0:T(8,128)S(1)} %dynamic-slice_bitcast_fusion.4), channel_id=1, source_target_pairs={{0,8},{4,12},{8,0},{12,4},{1,9},{5,13},{9,1},{13,5},{2,10},{6,14},... | collective-permute-start | bytes 344072 | tf_op jit(solution)/shard_map/ppermute | solution.py:727
  69.1 0.8 collective-permute-done.13
  69.9 0.1 collective-permute-start.15
  70.1 0.8 collective-permute-start.20
  70.8 4.9 %collective-permute-done.12 = f32[224,128]{1,0:T(8,128)S(1)} collective-permute-done((f32[224,128]{1,0:T(8,128)S(1)}, f32[224,128]{1,0:T(8,128)S(1)}, u32[]{:S(2)}, u32[]{:S(2)}) %collective-permute-start.12) | collective-permute-done | bytes 114720 | tf_op jit(solution)/shard_map/ppermute | solution.py:727
  75.7 3.7 %collective-permute-done.15 = f32[544,128]{1,0:T(8,128)S(1)} collective-permute-done((f32[544,128]{1,0:T(8,128)S(1)}, f32[544,128]{1,0:T(8,128)S(1)}, u32[]{:S(2)}, u32[]{:S(2)}) %collective-permute-start.15) | collective-permute-done | bytes 278560 | tf_op jit(solution)/shard_map/ppermute | solution.py:727
  79.5 0.5 collective-permute-start.14
  80.1 1.0 collective-permute-start.25
  81.1 2.6 %collective-permute-done.14 = f32[112,128]{1,0:T(8,128)S(1)} collective-permute-done((f32[112,128]{1,0:T(8,128)S(1)}, f32[112,128]{1,0:T(8,128)S(1)}, u32[]{:S(2)}, u32[]{:S(2)}) %collective-permute-start.14) | collective-permute-done | bytes 57376 | tf_op jit(solution)/shard_map/ppermute | solution.py:727
  83.7 1.8 %collective-permute-start.24 = (f32[4,3328]{1,0:T(4,128)S(1)}, f32[4,3328]{1,0:T(4,128)S(1)}, u32[]{:S(2)}, u32[]{:S(2)}) collective-permute-start(f32[4,3328]{1,0:T(4,128)S(1)} %get-tuple-element.128), channel_id=1, source_target_pairs={{0,12},{4,8},{8,4},{12,0},{1,13},{5,9},{9,5},{13,1},{2,14},{6,10},... | collective-permute-start | bytes 159752 | tf_op jit(solution)/shard_map/ppermute | solution.py:812
  85.5 0.7 copy-done.11
  86.2 3.3 %shard_map.227 = (bf16[49,32,64]{2,1,0:T(8,128)(2,1)}, f32[256,128]{1,0:T(8,128)}) custom-call(bf16[49,32,64]{2,1,0:T(8,128)(2,1)} %bitcast.67, bf16[7,64,64]{2,1,0:T(8,128)(2,1)} %out_proj.3, f32[4,4,3328]{2,1,0:T(4,128)} %copy-done.2, f32[4,4,3328]{2,1,0:T(4,128)} %copy-done.10, f32[4,4,3328]{2,1,0:T(4,128)} %copy-done.9, f32[4,4,3328]{2,1,0:T(4,128)} %copy-done.11), custom_call_target="tpu_custom_call" | custom-call | flops 1 | bytes 1 | tf_op jit(solution)/shard_map/pallas_call | solution.py:696
  89.5 0.8 constant_dynamic-slice_fusion
  90.3 2.7 %collective-permute-start.26 = (bf16[384,128]{1,0:T(8,128)(2,1)S(1)}, bf16[384,128]{1,0:T(8,128)(2,1)S(1)}, u32[]{:S(2)}, u32[]{:S(2)}) collective-permute-start(bf16[384,128]{1,0:T(8,128)(2,1)S(1)} %pad_maximum_fusion.6), channel_id=1, source_target_pairs={{0,8},{4,12},{8,0},{12,4},{1,9},{5,13},{9,1},{13,5},{2,10},{6,14},... | collective-permute-start | bytes 294920 | tf_op jit(solution)/shard_map/ppermute | solution.py:727
  93.0 2.4 %collective-permute-done.27 = f32[64,128]{1,0:T(8,128)S(1)} collective-permute-done((f32[64,128]{1,0:T(8,128)S(1)}, f32[64,128]{1,0:T(8,128)S(1)}, u32[]{:S(2)}, u32[]{:S(2)}) %collective-permute-start.27) | collective-permute-done | bytes 32800 | tf_op jit(solution)/shard_map/ppermute | solution.py:727
  95.4 0.8 fusion.4
  96.2 2.8 %collective-permute-done.26 = bf16[384,128]{1,0:T(8,128)(2,1)S(1)} collective-permute-done((bf16[384,128]{1,0:T(8,128)(2,1)S(1)}, bf16[384,128]{1,0:T(8,128)(2,1)S(1)}, u32[]{:S(2)}, u32[]{:S(2)}) %collective-permute-start.26) | collective-permute-done | bytes 98336 | tf_op jit(solution)/shard_map/ppermute | solution.py:727
  99.3 0.9 collective-permute-start.31
  100.1 0.9 collective-permute-done.29
  101.0 4.2 %collective-permute-done.28 = bf16[768,128]{1,0:T(8,128)(2,1)S(1)} collective-permute-done((bf16[768,128]{1,0:T(8,128)(2,1)S(1)}, bf16[768,128]{1,0:T(8,128)(2,1)S(1)}, u32[]{:S(2)}, u32[]{:S(2)}) %collective-permute-start.28) | collective-permute-done | bytes 196640 | tf_op jit(solution)/shard_map/ppermute | solution.py:727
  105.2 0.1 broadcast_select_fusion.3
  105.3 0.5 collective-permute-start.33
  105.8 1.4 %collective-permute-done.32.rest_3_ = f32[4,4,3328]{2,1,0:T(4,128)S(1)} collective-permute-done((f32[4,4,3328]{2,1,0:T(4,128)S(1)}, f32[4,4,3328]{2,1,0:T(4,128)S(1)}, u32[]{:S(2)}, u32[]{:S(2)}) %collective-permute-start.32) | collective-permute-done | bytes 213024 | tf_op jit(solution)/shard_map/ppermute | solution.py:727
  107.3 0.7 copy-done.7
  108.0 2.6 %shard_map.228 = bf16[49,32,64]{2,1,0:T(8,128)(2,1)} custom-call(f32[4,4,3328]{2,1,0:T(4,128)} %copy-done.1, f32[4,4,3328]{2,1,0:T(4,128)} %copy-done.6, f32[4,4,3328]{2,1,0:T(4,128)} %copy-done.5, f32[4,4,3328]{2,1,0:T(4,128)} %copy-done.7), custom_call_target="tpu_custom_call" | custom-call | flops 1 | bytes 1 | tf_op jit(solution)/shard_map/pallas_call | solution.py:696
  110.6 4.5 %collective-permute-done.33 = bf16[1600,128]{1,0:T(8,128)(2,1)S(1)} collective-permute-done((bf16[1600,128]{1,0:T(8,128)(2,1)S(1)}, bf16[1600,128]{1,0:T(8,128)(2,1)S(1)}, u32[]{:S(2)}, u32[]{:S(2)}) %collective-permute-start.33) | collective-permute-done | bytes 409632 | tf_op jit(solution)/shard_map/ppermute | solution.py:727
  115.1 0.2 broadcast_select_fusion.1
  115.4 2.3 %collective-permute-done.34.other = bf16[3200,128]{1,0:T(8,128)(2,1)S(1)} collective-permute-done((bf16[3200,128]{1,0:T(8,128)(2,1)S(1)}, bf16[3200,128]{1,0:T(8,128)(2,1)S(1)}, u32[]{:S(2)}, u32[]{:S(2)}) %collective-permute-start.34) | collective-permute-done | bytes 819232 | tf_op jit(solution)/shard_map/ppermute | solution.py:727
  117.7 0.9 copy-done.3
  118.6 3.0 %shard_map.229 = (bf16[448,448]{1,0:T(8,128)(2,1)}, bf16[2,384,384]{2,1,0:T(8,128)(2,1)}, bf16[2,320,320]{2,1,0:T(8,128)(2,1)}, bf16[64,256]{1,0:T(8,128)(2,1)},...) custom-call(bf16[3200,128]{1,0:T(8,128)(2,1)} %copy-done, bf16[3200,128]{1,0:T(8,128)(2,1)} %copy-done.3), custom_call_target="tpu_custom_call" | custom-call | flops 1 | bytes 1 | tf_op jit(solution)/shard_map/pallas_call | solution.py:696
  (82 shorter events, 1.1 us)
Async XLA Ops:
  2.9 8.5 %collective-permute-start = (bf16[4,6528]{1,0:T(4,128)(2,1)}, bf16[4,6528]{1,0:T(4,128)(2,1)S(1)}, u32[]{:S(2)}, u32[]{:S(2)}) collective-permute-start(bf16[4,6528]{1,0:T(4,128)(2,1)} %get-tuple-element.67), channel_id=1, source_target_pairs={{0,4},{4,0},{8,12},{12,8},{1,5},{5,1},{9,13},{13,9},{2,6},{6,2},{1... | collective-permute-start | bytes 156680 | tf_op jit(solution)/shard_map/ppermute | solution.py:812
  5.9 6.2 %collective-permute-start.1 = (bf16[4,6528]{1,0:T(4,128)(2,1)}, bf16[4,6528]{1,0:T(4,128)(2,1)S(1)}, u32[]{:S(2)}, u32[]{:S(2)}) collective-permute-start(bf16[4,6528]{1,0:T(4,128)(2,1)} %get-tuple-element.68), channel_id=1, source_target_pairs={{0,8},{4,12},{8,0},{12,4},{1,9},{5,13},{9,1},{13,5},{2,10},{6,14},... | collective-permute-start | bytes 156680 | tf_op jit(solution)/shard_map/ppermute | solution.py:812
  8.5 6.1 %collective-permute-start.2 = (bf16[4,6528]{1,0:T(4,128)(2,1)}, bf16[4,6528]{1,0:T(4,128)(2,1)S(1)}, u32[]{:S(2)}, u32[]{:S(2)}) collective-permute-start(bf16[4,6528]{1,0:T(4,128)(2,1)} %get-tuple-element.69), channel_id=1, source_target_pairs={{0,12},{4,8},{8,4},{12,0},{1,13},{5,9},{9,5},{13,1},{2,14},{6,10},... | collective-permute-start | bytes 156680 | tf_op jit(solution)/shard_map/ppermute | solution.py:812
  11.4 3.3 %copy-start.12 = (bf16[4,6528]{1,0:T(4,128)(2,1)}, bf16[4,6528]{1,0:T(4,128)(2,1)S(1)}, u32[]{:S(2)}) copy-start(bf16[4,6528]{1,0:T(4,128)(2,1)S(1)} %collective-permute-done.rest_1_) | copy-start | bytes 156676
  12.2 2.5 %copy-start.13 = (bf16[4,6528]{1,0:T(4,128)(2,1)}, bf16[4,6528]{1,0:T(4,128)(2,1)S(1)}, u32[]{:S(2)}) copy-start(bf16[4,6528]{1,0:T(4,128)(2,1)S(1)} %collective-permute-done.1.rest_2_) | copy-start | bytes 156676
  14.6 0.6 copy-start.14
  23.8 1.9 %collective-permute-start.3 = (f32[2,128]{1,0:T(2,128)}, f32[2,128]{1,0:T(2,128)S(1)}, u32[]{:S(2)}, u32[]{:S(2)}) collective-permute-start(f32[2,128]{1,0:T(2,128)} %get-tuple-element.70), channel_id=1, source_target_pairs={{0,1},{1,0},{2,3},{3,2},{4,5},{5,4},{6,7},{7,6},{8,9},{9,8},{10,11... | collective-permute-start | bytes 3080 | tf_op jit(solution)/shard_map/ppermute | solution.py:872
  23.9 3.8 %collective-permute-start.4 = (f32[2,128]{1,0:T(2,128)}, f32[2,128]{1,0:T(2,128)S(1)}, u32[]{:S(2)}, u32[]{:S(2)}) collective-permute-start(f32[2,128]{1,0:T(2,128)} %get-tuple-element.70), channel_id=1, source_target_pairs={{0,2},{1,3},{2,0},{3,1},{4,6},{5,7},{6,4},{7,5},{8,10},{9,11},{10,... | collective-permute-start | bytes 3080 | tf_op jit(solution)/shard_map/ppermute | solution.py:872
  25.5 3.1 %collective-permute-start.5 = (f32[2,128]{1,0:T(2,128)}, f32[2,128]{1,0:T(2,128)S(1)}, u32[]{:S(2)}, u32[]{:S(2)}) collective-permute-start(f32[2,128]{1,0:T(2,128)} %get-tuple-element.70), channel_id=1, source_target_pairs={{0,3},{1,2},{2,1},{3,0},{4,7},{5,6},{6,5},{7,4},{8,11},{9,10},{10,... | collective-permute-start | bytes 3080 | tf_op jit(solution)/shard_map/ppermute | solution.py:872
  29.1 7.0 %copy-start.15 = (f32[8,128]{1,0:T(8,128)}, f32[8,128]{1,0:T(8,128)S(1)}, u32[]{:S(2)}) copy-start(f32[8,128]{1,0:T(8,128)S(1)} %pad_maximum_fusion.7.refs_0_) | copy-start | bytes 12292
  29.1 4.5 %collective-permute-start.6 = (f32[8,128]{1,0:T(8,128)S(1)}, f32[8,128]{1,0:T(8,128)S(1)}, u32[]{:S(2)}, u32[]{:S(2)}) collective-permute-start(f32[8,128]{1,0:T(8,128)S(1)} %pad_maximum_fusion.7.refs_0_), channel_id=1, source_target_pairs={{0,4},{4,0},{8,12},{12,8},{1,5},{5,1},{9,13},{13,9},{2,6},{6,2},{1... | collective-permute-start | bytes 12296 | tf_op jit(solution)/shard_map/ppermute | solution.py:877
  29.2 4.6 %collective-permute-start.7 = (f32[8,128]{1,0:T(8,128)S(1)}, f32[8,128]{1,0:T(8,128)S(1)}, u32[]{:S(2)}, u32[]{:S(2)}) collective-permute-start(f32[8,128]{1,0:T(8,128)S(1)} %pad_maximum_fusion.7.refs_0_), channel_id=1, source_target_pairs={{0,8},{4,12},{8,0},{12,4},{1,9},{5,13},{9,1},{13,5},{2,10},{6,14},... | collective-permute-start | bytes 12296 | tf_op jit(solution)/shard_map/ppermute | solution.py:877
  30.7 5.4 %collective-permute-start.8 = (f32[8,128]{1,0:T(8,128)S(1)}, f32[8,128]{1,0:T(8,128)S(1)}, u32[]{:S(2)}, u32[]{:S(2)}) collective-permute-start(f32[8,128]{1,0:T(8,128)S(1)} %pad_maximum_fusion.7.refs_0_), channel_id=1, source_target_pairs={{0,12},{4,8},{8,4},{12,0},{1,13},{5,9},{9,5},{13,1},{2,14},{6,10},... | collective-permute-start | bytes 12296 | tf_op jit(solution)/shard_map/ppermute | solution.py:877
  33.6 2.5 %copy-start.16 = (f32[8,128]{1,0:T(8,128)}, f32[8,128]{1,0:T(8,128)S(1)}, u32[]{:S(2)}) copy-start(f32[8,128]{1,0:T(8,128)S(1)} %collective-permute-done.6.refs_1_) | copy-start | bytes 12292
  33.8 2.3 %copy-start.17 = (f32[8,128]{1,0:T(8,128)}, f32[8,128]{1,0:T(8,128)S(1)}, u32[]{:S(2)}) copy-start(f32[8,128]{1,0:T(8,128)S(1)} %collective-permute-done.7.refs_2_) | copy-start | bytes 12292
  36.1 0.6 copy-start.18
  36.7 8.6 %copy-start.8 = (f32[4,4,3328]{2,1,0:T(4,128)S(1)}, f32[4,4,3328]{2,1,0:T(4,128)}, u32[]{:S(2)}) copy-start(f32[4,4,3328]{2,1,0:T(4,128)} %get-tuple-element.101) | copy-start | bytes 638980
  45.2 9.6 %collective-permute-start.10 = (f32[2176,128]{1,0:T(8,128)}, f32[2176,128]{1,0:T(8,128)S(1)}, u32[]{:S(2)}, u32[]{:S(2)}) collective-permute-start(f32[2176,128]{1,0:T(8,128)} %get-tuple-element.85), channel_id=1, source_target_pairs={{0,1},{1,0},{2,3},{3,2},{4,5},{5,4},{6,7},{7,6},{8,9},{9,8},{10,11... | collective-permute-start | bytes 3342344 | tf_op jit(solution)/shard_map/ppermute | solution.py:727
  45.3 4.5 %collective-permute-start.16 = (f32[4,3328]{1,0:T(4,128)S(1)}, f32[4,3328]{1,0:T(4,128)S(1)}, u32[]{:S(2)}, u32[]{:S(2)}) collective-permute-start(f32[4,3328]{1,0:T(4,128)S(1)} %get-tuple-element.134), channel_id=1, source_target_pairs={{0,4},{4,0},{8,12},{12,8},{1,5},{5,1},{9,13},{13,9},{2,6},{6,2},{1... | collective-permute-start | bytes 159752 | tf_op jit(solution)/shard_map/ppermute | solution.py:812
  45.4 7.0 %collective-permute-start.17 = (f32[4,3328]{1,0:T(4,128)S(1)}, f32[4,3328]{1,0:T(4,128)S(1)}, u32[]{:S(2)}, u32[]{:S(2)}) collective-permute-start(f32[4,3328]{1,0:T(4,128)S(1)} %get-tuple-element.133), channel_id=1, source_target_pairs={{0,8},{4,12},{8,0},{12,4},{1,9},{5,13},{9,1},{13,5},{2,10},{6,14},... | collective-permute-start | bytes 159752 | tf_op jit(solution)/shard_map/ppermute | solution.py:812
  48.9 5.9 %collective-permute-start.18 = (f32[4,3328]{1,0:T(4,128)S(1)}, f32[4,3328]{1,0:T(4,128)S(1)}, u32[]{:S(2)}, u32[]{:S(2)}) collective-permute-start(f32[4,3328]{1,0:T(4,128)S(1)} %get-tuple-element.132), channel_id=1, source_target_pairs={{0,12},{4,8},{8,4},{12,0},{1,13},{5,9},{9,5},{13,1},{2,14},{6,10},... | collective-permute-start | bytes 159752 | tf_op jit(solution)/shard_map/ppermute | solution.py:812
  49.8 7.4 %collective-permute-start.9 = (f32[896,128]{1,0:T(8,128)}, f32[896,128]{1,0:T(8,128)S(1)}, u32[]{:S(2)}, u32[]{:S(2)}) collective-permute-start(f32[896,128]{1,0:T(8,128)} %get-tuple-element.83), channel_id=1, source_target_pairs={{0,1},{1,0},{2,3},{3,2},{4,5},{5,4},{6,7},{7,6},{8,9},{9,8},{10,11... | collective-permute-start | bytes 1376264 | tf_op jit(solution)/shard_map/ppermute | solution.py:727
  54.8 20.9 %copy-start.2 = (f32[4,4,3328]{2,1,0:T(4,128)}, f32[4,4,3328]{2,1,0:T(4,128)S(1)}, u32[]{:S(2)}) copy-start(f32[4,4,3328]{2,1,0:T(4,128)S(1)} %pad_maximum_fusion.3.rest_0_) | copy-start | bytes 638980
  56.3 1.0 copy-start.4
  56.4 13.5 %collective-permute-start.13 = (f32[1088,128]{1,0:T(8,128)S(1)}, f32[1088,128]{1,0:T(8,128)S(1)}, u32[]{:S(2)}, u32[]{:S(2)}) collective-permute-start(f32[1088,128]{1,0:T(8,128)S(1)} %dynamic-slice_bitcast_fusion), channel_id=1, source_target_pairs={{0,2},{1,3},{2,0},{3,1},{4,6},{5,7},{6,4},{7,5},{8,10},{9,11},{10,... | collective-permute-start | bytes 1671176 | tf_op jit(solution)/shard_map/ppermute | solution.py:727
  57.4 9.8 %collective-permute-start.11 = (f32[448,128]{1,0:T(8,128)S(1)}, f32[448,128]{1,0:T(8,128)S(1)}, u32[]{:S(2)}, u32[]{:S(2)}) collective-permute-start(f32[448,128]{1,0:T(8,128)S(1)} %dynamic-slice_bitcast_fusion.2), channel_id=1, source_target_pairs={{0,4},{4,0},{8,12},{12,8},{1,5},{5,1},{9,13},{13,9},{2,6},{6,2},{1... | collective-permute-start | bytes 688136 | tf_op jit(solution)/shard_map/ppermute | solution.py:727
  64.0 35.2 %collective-permute-start.22 = (f32[4,3328]{1,0:T(4,128)S(1)}, f32[4,3328]{1,0:T(4,128)S(1)}, u32[]{:S(2)}, u32[]{:S(2)}) collective-permute-start(f32[4,3328]{1,0:T(4,128)S(1)} %get-tuple-element.130), channel_id=1, source_target_pairs={{0,4},{4,0},{8,12},{12,8},{1,5},{5,1},{9,13},{13,9},{2,6},{6,2},{1... | collective-permute-start | bytes 159752 | tf_op jit(solution)/shard_map/ppermute | solution.py:812
  66.0 33.2 %collective-permute-start.23 = (f32[4,3328]{1,0:T(4,128)S(1)}, f32[4,3328]{1,0:T(4,128)S(1)}, u32[]{:S(2)}, u32[]{:S(2)}) collective-permute-start(f32[4,3328]{1,0:T(4,128)S(1)} %get-tuple-element.129), channel_id=1, source_target_pairs={{0,8},{4,12},{8,0},{12,4},{1,9},{5,13},{9,1},{13,5},{2,10},{6,14},... | collective-permute-start | bytes 159752 | tf_op jit(solution)/shard_map/ppermute | solution.py:812
  67.3 8.4 %collective-permute-start.12 = (f32[224,128]{1,0:T(8,128)S(1)}, f32[224,128]{1,0:T(8,128)S(1)}, u32[]{:S(2)}, u32[]{:S(2)}) collective-permute-start(f32[224,128]{1,0:T(8,128)S(1)} %dynamic-slice_bitcast_fusion.4), channel_id=1, source_target_pairs={{0,8},{4,12},{8,0},{12,4},{1,9},{5,13},{9,1},{13,5},{2,10},{6,14},... | collective-permute-start | bytes 344072 | tf_op jit(solution)/shard_map/ppermute | solution.py:727
  69.9 9.5 %collective-permute-start.15 = (f32[544,128]{1,0:T(8,128)S(1)}, f32[544,128]{1,0:T(8,128)S(1)}, u32[]{:S(2)}, u32[]{:S(2)}) collective-permute-start(f32[544,128]{1,0:T(8,128)S(1)} %dynamic-slice_bitcast_fusion.1), channel_id=1, source_target_pairs={{0,4},{4,0},{8,12},{12,8},{1,5},{5,1},{9,13},{13,9},{2,6},{6,2},{1... | collective-permute-start | bytes 835592 | tf_op jit(solution)/shard_map/ppermute | solution.py:727
  70.1 10.0 %collective-permute-start.20 = (f32[4,4,3328]{2,1,0:T(4,128)S(1)}, f32[4,4,3328]{2,1,0:T(4,128)S(1)}, u32[]{:S(2)}, u32[]{:S(2)}) collective-permute-start(f32[4,4,3328]{2,1,0:T(4,128)S(1)} %pad_maximum_fusion.3.rest_0_), channel_id=1, source_target_pairs={{0,2},{1,3},{2,0},{3,1},{4,6},{5,7},{6,4},{7,5},{8,10},{9,11},{10,... | collective-permute-start | bytes 638984 | tf_op jit(solution)/shard_map/ppermute | solution.py:727
  75.7 8.0 %collective-permute-start.19 = (f32[4,4,3328]{2,1,0:T(4,128)S(1)}, f32[4,4,3328]{2,1,0:T(4,128)S(1)}, u32[]{:S(2)}, u32[]{:S(2)}) collective-permute-start(f32[4,4,3328]{2,1,0:T(4,128)S(1)} %pad_maximum_fusion.3.rest_0_), channel_id=1, source_target_pairs={{0,1},{1,0},{2,3},{3,2},{4,5},{5,4},{6,7},{7,6},{8,9},{9,8},{10,11... | collective-permute-start | bytes 638984 | tf_op jit(solution)/shard_map/ppermute | solution.py:727
  79.5 4.2 %collective-permute-start.14 = (f32[112,128]{1,0:T(8,128)S(1)}, f32[112,128]{1,0:T(8,128)S(1)}, u32[]{:S(2)}, u32[]{:S(2)}) collective-permute-start(f32[112,128]{1,0:T(8,128)S(1)} %dynamic-slice_bitcast_fusion.5), channel_id=1, source_target_pairs={{0,2},{1,3},{2,0},{3,1},{4,6},{5,7},{6,4},{7,5},{8,10},{9,11},{10,... | collective-permute-start | bytes 172040 | tf_op jit(solution)/shard_map/ppermute | solution.py:727
  80.1 5.4 %copy-start.9 = (f32[4,4,3328]{2,1,0:T(4,128)}, f32[4,4,3328]{2,1,0:T(4,128)S(1)}, u32[]{:S(2)}) copy-start(f32[4,4,3328]{2,1,0:T(4,128)S(1)} %collective-permute-done.20.rest_2_) | copy-start | bytes 638980
  80.1 9.4 %collective-permute-start.25 = (f32[272,128]{1,0:T(8,128)S(1)}, f32[272,128]{1,0:T(8,128)S(1)}, u32[]{:S(2)}, u32[]{:S(2)}) collective-permute-start(f32[272,128]{1,0:T(8,128)S(1)} %dynamic-slice_bitcast_fusion.3), channel_id=1, source_target_pairs={{0,8},{4,12},{8,0},{12,4},{1,9},{5,13},{9,1},{13,5},{2,10},{6,14},... | collective-permute-start | bytes 417800 | tf_op jit(solution)/shard_map/ppermute | solution.py:727
  83.7 1.8 %collective-permute-start.21 = (f32[4,4,3328]{2,1,0:T(4,128)S(1)}, f32[4,4,3328]{2,1,0:T(4,128)S(1)}, u32[]{:S(2)}, u32[]{:S(2)}) collective-permute-start(f32[4,4,3328]{2,1,0:T(4,128)S(1)} %collective-permute-done.20.rest_2_), channel_id=1, source_target_pairs={{0,1},{1,0},{2,3},{3,2},{4,5},{5,4},{6,7},{7,6},{8,9},{9,8},{10,11... | collective-permute-start | bytes 638984 | tf_op jit(solution)/shard_map/ppermute | solution.py:727
  83.7 1.8 %copy-start.10 = (f32[4,4,3328]{2,1,0:T(4,128)}, f32[4,4,3328]{2,1,0:T(4,128)S(1)}, u32[]{:S(2)}) copy-start(f32[4,4,3328]{2,1,0:T(4,128)S(1)} %collective-permute-done.19.rest_1_) | copy-start | bytes 638980
  83.7 15.5 %collective-permute-start.24 = (f32[4,3328]{1,0:T(4,128)S(1)}, f32[4,3328]{1,0:T(4,128)S(1)}, u32[]{:S(2)}, u32[]{:S(2)}) collective-permute-start(f32[4,3328]{1,0:T(4,128)S(1)} %get-tuple-element.128), channel_id=1, source_target_pairs={{0,12},{4,8},{8,4},{12,0},{1,13},{5,9},{9,5},{13,1},{2,14},{6,10},... | collective-permute-start | bytes 159752 | tf_op jit(solution)/shard_map/ppermute | solution.py:812
  85.5 0.7 copy-start.11
  90.3 5.1 %collective-permute-start.27 = (f32[64,128]{1,0:T(8,128)S(1)}, f32[64,128]{1,0:T(8,128)S(1)}, u32[]{:S(2)}, u32[]{:S(2)}) collective-permute-start(f32[64,128]{1,0:T(8,128)S(1)} %constant_dynamic-slice_fusion), channel_id=1, source_target_pairs={{0,4},{4,0},{8,12},{12,8},{1,5},{5,1},{9,13},{13,9},{2,6},{6,2},{1... | collective-permute-start | bytes 98312 | tf_op jit(solution)/shard_map/ppermute | solution.py:727
  90.3 8.7 %collective-permute-start.26 = (bf16[384,128]{1,0:T(8,128)(2,1)S(1)}, bf16[384,128]{1,0:T(8,128)(2,1)S(1)}, u32[]{:S(2)}, u32[]{:S(2)}) collective-permute-start(bf16[384,128]{1,0:T(8,128)(2,1)S(1)} %pad_maximum_fusion.6), channel_id=1, source_target_pairs={{0,8},{4,12},{8,0},{12,4},{1,9},{5,13},{9,1},{13,5},{2,10},{6,14},... | collective-permute-start | bytes 294920 | tf_op jit(solution)/shard_map/ppermute | solution.py:727
  96.2 4.8 %collective-permute-start.29 = (f32[64,128]{1,0:T(8,128)S(1)}, f32[64,128]{1,0:T(8,128)S(1)}, u32[]{:S(2)}, u32[]{:S(2)}) collective-permute-start(f32[64,128]{1,0:T(8,128)S(1)} %fusion.4), channel_id=1, source_target_pairs={{0,8},{4,12},{8,0},{12,4},{1,9},{5,13},{9,1},{13,5},{2,10},{6,14},... | collective-permute-start | bytes 98312 | tf_op jit(solution)/shard_map/ppermute | solution.py:727
  99.1 6.1 %collective-permute-start.28 = (bf16[768,128]{1,0:T(8,128)(2,1)S(1)}, bf16[768,128]{1,0:T(8,128)(2,1)S(1)}, u32[]{:S(2)}, u32[]{:S(2)}) collective-permute-start(bf16[768,128]{1,0:T(8,128)(2,1)S(1)} %pad_maximum_fusion.5), channel_id=1, source_target_pairs={{0,4},{4,0},{8,12},{12,8},{1,5},{5,1},{9,13},{13,9},{2,6},{6,2},{1... | collective-permute-start | bytes 589832 | tf_op jit(solution)/shard_map/ppermute | solution.py:727
  99.3 8.0 %copy-start.1 = (f32[4,4,3328]{2,1,0:T(4,128)}, f32[4,4,3328]{2,1,0:T(4,128)S(1)}, u32[]{:S(2)}) copy-start(f32[4,4,3328]{2,1,0:T(4,128)S(1)} %pad_maximum_fusion.4.rest_0_) | copy-start | bytes 638980
  99.3 6.5 %collective-permute-start.31 = (f32[4,4,3328]{2,1,0:T(4,128)S(1)}, f32[4,4,3328]{2,1,0:T(4,128)S(1)}, u32[]{:S(2)}, u32[]{:S(2)}) collective-permute-start(f32[4,4,3328]{2,1,0:T(4,128)S(1)} %pad_maximum_fusion.4.rest_0_), channel_id=1, source_target_pairs={{0,2},{1,3},{2,0},{3,1},{4,6},{5,7},{6,4},{7,5},{8,10},{9,11},{10,... | collective-permute-start | bytes 638984 | tf_op jit(solution)/shard_map/ppermute | solution.py:727
  100.1 5.7 %collective-permute-start.30 = (f32[4,4,3328]{2,1,0:T(4,128)S(1)}, f32[4,4,3328]{2,1,0:T(4,128)S(1)}, u32[]{:S(2)}, u32[]{:S(2)}) collective-permute-start(f32[4,4,3328]{2,1,0:T(4,128)S(1)} %pad_maximum_fusion.4.rest_0_), channel_id=1, source_target_pairs={{0,1},{1,0},{2,3},{3,2},{4,5},{5,4},{6,7},{7,6},{8,9},{9,8},{10,11... | collective-permute-start | bytes 638984 | tf_op jit(solution)/shard_map/ppermute | solution.py:727
  105.3 9.7 %collective-permute-start.33 = (bf16[1600,128]{1,0:T(8,128)(2,1)S(1)}, bf16[1600,128]{1,0:T(8,128)(2,1)S(1)}, u32[]{:S(2)}, u32[]{:S(2)}) collective-permute-start(bf16[1600,128]{1,0:T(8,128)(2,1)S(1)} %pad_maximum_fusion.1), channel_id=1, source_target_pairs={{0,2},{1,3},{2,0},{3,1},{4,6},{5,7},{6,4},{7,5},{8,10},{9,11},{10,... | collective-permute-start | bytes 1228808 | tf_op jit(solution)/shard_map/ppermute | solution.py:727
  105.8 1.5 %copy-start.5 = (f32[4,4,3328]{2,1,0:T(4,128)}, f32[4,4,3328]{2,1,0:T(4,128)S(1)}, u32[]{:S(2)}) copy-start(f32[4,4,3328]{2,1,0:T(4,128)S(1)} %collective-permute-done.31.rest_2_) | copy-start | bytes 638980
  105.8 1.5 %collective-permute-start.32 = (f32[4,4,3328]{2,1,0:T(4,128)S(1)}, f32[4,4,3328]{2,1,0:T(4,128)S(1)}, u32[]{:S(2)}, u32[]{:S(2)}) collective-permute-start(f32[4,4,3328]{2,1,0:T(4,128)S(1)} %collective-permute-done.31.rest_2_), channel_id=1, source_target_pairs={{0,1},{1,0},{2,3},{3,2},{4,5},{5,4},{6,7},{7,6},{8,9},{9,8},{10,11... | collective-permute-start | bytes 638984 | tf_op jit(solution)/shard_map/ppermute | solution.py:727
  105.8 1.5 %copy-start.6 = (f32[4,4,3328]{2,1,0:T(4,128)}, f32[4,4,3328]{2,1,0:T(4,128)S(1)}, u32[]{:S(2)}) copy-start(f32[4,4,3328]{2,1,0:T(4,128)S(1)} %collective-permute-done.30.rest_1_) | copy-start | bytes 638980
  107.3 0.7 copy-start.7
  115.3 2.4 %copy-start = (bf16[3200,128]{1,0:T(8,128)(2,1)}, bf16[3200,128]{1,0:T(8,128)(2,1)S(1)}, u32[]{:S(2)}) copy-start(bf16[3200,128]{1,0:T(8,128)(2,1)S(1)} %pad_maximum_fusion.mine) | copy-start | bytes 2457604
  115.3 2.4 %collective-permute-start.34 = (bf16[3200,128]{1,0:T(8,128)(2,1)S(1)}, bf16[3200,128]{1,0:T(8,128)(2,1)S(1)}, u32[]{:S(2)}, u32[]{:S(2)}) collective-permute-start(bf16[3200,128]{1,0:T(8,128)(2,1)S(1)} %pad_maximum_fusion.mine), channel_id=1, source_target_pairs={{0,1},{1,0},{2,3},{3,2},{4,5},{5,4},{6,7},{7,6},{8,9},{9,8},{10,11... | collective-permute-start | bytes 2457608 | tf_op jit(solution)/shard_map/ppermute | solution.py:727
  117.7 0.9 copy-start.3

commit v10 on v9

--- a/solution.py
+++ b/solution.py
@@ -907,7 +907,8 @@
 
     total = lanes_total * slots
     order.mark(halves[0])
-    messages = exchange(order.hold(sums))
+    held_sums = order.hold(sums)
+    pieces = pairwise([held_sums[k] for k in range(peers)]) if direct else [exchange(held_sums)]
     rest_steps = halve(halves[0], halves[1], "edge", order)
     zero_steps = halve(halves[2], halves[3], "graph", order)
     next(rest_steps)
@@ -930,7 +931,8 @@
     next(zero_steps)
     for _ in range(bits_of("edge") - 1):
         next(rest_steps)
-    message_hops = gather_lanes(order.hold(messages), order)
+    pieces = [order.hold(piece) for piece in pieces]
+    message_hops = gather_lanes(jnp.stack(pieces) if direct else pieces[0], order)
     next(message_hops)
     next(zero_steps)
     returned = order.hold(exchange(source_sums))

time: 122 us -> 121 us (level)
  waiting for transfers between devices: 44.1 us -> 41.2 us
  starting transfers between devices: 30.8 us -> 33 us
    ppermute x9, waiting for transfers between devices: 8.26 us -> 3.28 us  [pairwise(): lax.ppermute(pieces[k], 'graph', [(i, i ^ k) for i in range(peers)])]
    ppermute x20, waiting for transfers between devices: 30.5 us -> 32.7 us  [swap(): return lax.ppermute(value, axis, [(i, i ^ 1 << bit) for i in range(size)])]
    ppermute x20, starting transfers between devices: 9.31 us -> 11.3 us  [swap(): return lax.ppermute(value, axis, [(i, i ^ 1 << bit) for i in range(size)])]
  transfers between devices with their start and end apart: 35 -> 35, of which waited for: 19 -> 18; matrix products, arithmetic and copies ran while one was open for 6% -> 6% of each run, Pallas kernels for 9% -> 9%
where the time goes in v10:
time: 121 us
  waiting for transfers between devices  41.2 us (34%)
  Pallas kernels  33.7 us (28%)
  starting transfers between devices  33 us (27%)
  local copies, waits for them, and re-layouts  8.37 us (7%)
  other arithmetic  3.48 us (3%)
    pallas_call x7, Pallas kernels, call(): pl.pallas_call(kernel, out_shape=[jax.ShapeDtypeStruct(shape, kind) for s...  33.7 us
    ppermute x20, waiting for transfers between devices, swap(): return lax.ppermute(value, axis, [(i, i ^ 1 << bit) for i in range(size)])  32.7 us
    ppermute x9, starting transfers between devices, pairwise(): lax.ppermute(pieces[k], 'graph', [(i, i ^ k) for i in range(peers)])  15.2 us
    ppermute x20, starting transfers between devices, swap(): return lax.ppermute(value, axis, [(i, i ^ 1 << bit) for i in range(size)])  11.3 us
    unnamed x39, local copies, waits for them, and re-layouts  5.33 us
    ppermute x3, starting transfers between devices, shards(): lax.ppermute(graph_stats, 'graph', [(i, i ^ k) for i in range(peers)])  4.44 us
    ppermute x9, waiting for transfers between devices, pairwise(): lax.ppermute(pieces[k], 'graph', [(i, i ^ k) for i in range(peers)])  3.28 us
    ppermute x3, waiting for transfers between devices, shards(): lax.ppermute(stats, 'edge', [(i, i ^ k) for i in range(lanes_total)])  2.74 us
  transfers between devices with their start and end apart: 35, of which 18 were waited for; matrix products, arithmetic and copies ran while one was open for 6% of the time, Pallas kernels for 9%

profile of v10, /device:TPU:0, one launch (start us, length us, event | category | flops | bytes accessed | tf_op | source)
XLA Modules:
  0.0 120.8 jit_solution(14039799267154893184)
XLA Ops:
  0.6 2.2 %shard_map.223 = (bf16[4,6528]{1,0:T(4,128)(2,1)}, bf16[4,6528]{1,0:T(4,128)(2,1)}, bf16[4,6528]{1,0:T(4,128)(2,1)}, bf16[4,6528]{1,0:T(4,128)(2,1)}) custom-call(s32[1,4,1,4]{3,2,1,0:T(1,128)} %send.1, s32[1,4,1,4]{3,2,1,0:T(1,128)} %recv.1, bf16[49,32,64]{2,1,0:T(8,128)(2,1)} %bitcast.78, bf16[49,32,64]{2,1,0:T(8,128)(2,1)} %bitcast.69), custom_call_target="tpu_custom_call" | custom-call | flops 1 | bytes 1 | tf_op jit(solution)/shard_map/pallas_call | solution.py:696
  2.9 3.0 %collective-permute-start = (bf16[4,6528]{1,0:T(4,128)(2,1)}, bf16[4,6528]{1,0:T(4,128)(2,1)S(1)}, u32[]{:S(2)}, u32[]{:S(2)}) collective-permute-start(bf16[4,6528]{1,0:T(4,128)(2,1)} %get-tuple-element.70), channel_id=1, source_target_pairs={{0,4},{4,0},{8,12},{12,8},{1,5},{5,1},{9,13},{13,9},{2,6},{6,2},{1... | collective-permute-start | bytes 156680 | tf_op jit(solution)/shard_map/ppermute | solution.py:812
  5.9 2.6 %collective-permute-start.1 = (bf16[4,6528]{1,0:T(4,128)(2,1)}, bf16[4,6528]{1,0:T(4,128)(2,1)S(1)}, u32[]{:S(2)}, u32[]{:S(2)}) collective-permute-start(bf16[4,6528]{1,0:T(4,128)(2,1)} %get-tuple-element.71), channel_id=1, source_target_pairs={{0,8},{4,12},{8,0},{12,4},{1,9},{5,13},{9,1},{13,5},{2,10},{6,14},... | collective-permute-start | bytes 156680 | tf_op jit(solution)/shard_map/ppermute | solution.py:812
  8.5 1.2 reshape.50.adot.refs_17_
  9.7 1.7 %copy.25.rotation = bf16[256,235]{1,0:T(8,128)(2,1)} copy(bf16[256,235]{0,1:T(8,128)(2,1)} %param.22) | data formatting | bytes 240640 | tf_op args[6]
  11.4 0.8 collective-permute-done.1.rest_2_
  12.2 2.5 %collective-permute-done.2.rest_3_ = bf16[4,6528]{1,0:T(4,128)(2,1)S(1)} collective-permute-done((bf16[4,6528]{1,0:T(4,128)(2,1)}, bf16[4,6528]{1,0:T(4,128)(2,1)S(1)}, u32[]{:S(2)}, u32[]{:S(2)}) %collective-permute-start.2) | collective-permute-done | bytes 52256 | tf_op jit(solution)/shard_map/ppermute | solution.py:812
  14.6 0.6 copy-done.14
  15.3 8.6 %shard_map.224 = (f32[4,4,3328]{2,1,0:T(4,128)}, f32[2,128]{1,0:T(2,128)}, bf16[448,256]{1,0:T(8,128)(2,1)}, bf16[384,512]{1,0:T(8,128)(2,1)}, bf16[320,512]{1,0...) custom-call(s32[1,256]{1,0:T(1,128)} %bitcast.89, ...), custom_call_target="tpu_custom_call" | custom-call | flops 1 | bytes 1 | tf_op jit(solution)/shard_map/pallas_call | solution.py:696
  23.9 1.6 %collective-permute-start.4 = (f32[2,128]{1,0:T(2,128)}, f32[2,128]{1,0:T(2,128)S(1)}, u32[]{:S(2)}, u32[]{:S(2)}) collective-permute-start(f32[2,128]{1,0:T(2,128)} %get-tuple-element.73), channel_id=1, source_target_pairs={{0,2},{1,3},{2,0},{3,1},{4,6},{5,7},{6,4},{7,5},{8,10},{9,11},{10,... | collective-permute-start | bytes 3080 | tf_op jit(solution)/shard_map/ppermute | solution.py:872
  25.5 0.3 collective-permute-start.5
  25.8 2.0 %collective-permute-done.4 = f32[2,128]{1,0:T(2,128)S(1)} collective-permute-done((f32[2,128]{1,0:T(2,128)}, f32[2,128]{1,0:T(2,128)S(1)}, u32[]{:S(2)}, u32[]{:S(2)}) %collective-permute-start.4) | collective-permute-done | bytes 1056 | tf_op jit(solution)/shard_map/ppermute | solution.py:872
  27.7 0.8 collective-permute-done.5
  28.5 0.6 pad_maximum_fusion.7.refs_0_
  29.1 0.1 collective-permute-start.6
  29.2 1.5 %collective-permute-start.7 = (f32[8,128]{1,0:T(8,128)S(1)}, f32[8,128]{1,0:T(8,128)S(1)}, u32[]{:S(2)}, u32[]{:S(2)}) collective-permute-start(f32[8,128]{1,0:T(8,128)S(1)} %pad_maximum_fusion.7.refs_0_), channel_id=1, source_target_pairs={{0,8},{4,12},{8,0},{12,4},{1,9},{5,13},{9,1},{13,5},{2,10},{6,14},... | collective-permute-start | bytes 12296 | tf_op jit(solution)/shard_map/ppermute | solution.py:877
  30.7 2.9 %collective-permute-start.8 = (f32[8,128]{1,0:T(8,128)S(1)}, f32[8,128]{1,0:T(8,128)S(1)}, u32[]{:S(2)}, u32[]{:S(2)}) collective-permute-start(f32[8,128]{1,0:T(8,128)S(1)} %pad_maximum_fusion.7.refs_0_), channel_id=1, source_target_pairs={{0,12},{4,8},{8,4},{12,0},{1,13},{5,9},{9,5},{13,1},{2,14},{6,10},... | collective-permute-start | bytes 12296 | tf_op jit(solution)/shard_map/ppermute | solution.py:877
  33.6 0.2 collective-permute-done.7.refs_2_
  33.8 2.3 %collective-permute-done.8.refs_3_ = f32[8,128]{1,0:T(8,128)S(1)} collective-permute-done((f32[8,128]{1,0:T(8,128)S(1)}, f32[8,128]{1,0:T(8,128)S(1)}, u32[]{:S(2)}, u32[]{:S(2)}) %collective-permute-start.8) | collective-permute-done | bytes 4128 | tf_op jit(solution)/shard_map/ppermute | solution.py:877
  36.1 0.6 copy-done.18
  36.7 8.5 %shard_map.225 = (bf16[448,256]{1,0:T(8,128)(2,1)}, bf16[384,512]{1,0:T(8,128)(2,1)}, bf16[320,512]{1,0:T(8,128)(2,1)}, bf16[256,256]{1,0:T(8,128)(2,1)}, f32[21...) custom-call(f32[8,128]{1,0:T(8,128)} %copy-done.15, f32[8,128]{1,0:T(8,128)} %copy-done.16, ...), custom_call_target="tpu_custom_call" | custom-call | flops 1 | bytes 1 | tf_op jit(solution)/shard_map/pallas_call | solution.py:696
  45.3 0.5 collective-permute-start.9
  45.9 3.4 %collective-permute-start.17 = (f32[4,3328]{1,0:T(4,128)S(1)}, f32[4,3328]{1,0:T(4,128)S(1)}, u32[]{:S(2)}, u32[]{:S(2)}) collective-permute-start(f32[4,3328]{1,0:T(4,128)S(1)} %get-tuple-element.139), channel_id=1, source_target_pairs={{0,8},{4,12},{8,0},{12,4},{1,9},{5,13},{9,1},{13,5},{2,10},{6,14},... | collective-permute-start | bytes 159752 | tf_op jit(solution)/shard_map/ppermute | solution.py:812
  49.3 0.9 collective-permute-start.18
  50.3 1.4 %add.69 = f32[2176,128]{1,0:T(8,128)S(1)} add(f32[2176,128]{1,0:T(8,128)} %get-tuple-element.87, f32[2176,128]{1,0:T(8,128)S(1)} %collective-permute-done.10) | non-fusion elementwise | flops 278528 | bytes 3342336 | tf_op jit(solution)/shard_map/add | solution.py:758
  51.7 0.8 collective-permute-start.13
  52.5 0.2 copy-done.4
  52.8 0.1 collective-permute-start.11
  52.8 5.6 %shard_map.226 = f32[4,4,3328]{2,1,0:T(4,128)} custom-call(s32[1,256]{1,0:T(1,128)} %bitcast.90, f32[16,128]{1,0:T(8,128)} %get-tuple-element.91.lists, f32[235,256]{1,0:T(8,128)} %get-tuple-element.76.refs_7_.rot, bf16[448,256]{1,0:T(8,128)(2,1)} %get-tuple-element.92.g0, bf16[384,512]{1,0:T(8,128)(2,1)} %get-tuple-element.93.g1, ...), custom_call_target="tpu_custom_call" | custom-call | flops 1 | bytes 1 | tf_op jit(solution)/shard_map/pallas_call | solution.py:696
  58.4 0.9 fusion.2
  59.3 0.9 collective-permute-done.11
  60.2 1.2 %collective-permute-start.22 = (f32[4,3328]{1,0:T(4,128)S(1)}, f32[4,3328]{1,0:T(4,128)S(1)}, u32[]{:S(2)}, u32[]{:S(2)}) collective-permute-start(f32[4,3328]{1,0:T(4,128)S(1)} %get-tuple-element.136), channel_id=1, source_target_pairs={{0,4},{4,0},{8,12},{12,8},{1,5},{5,1},{9,13},{13,9},{2,6},{6,2},{1... | collective-permute-start | bytes 159752 | tf_op jit(solution)/shard_map/ppermute | solution.py:812
  61.4 4.1 %collective-permute-done.13 = f32[1088,128]{1,0:T(8,128)S(1)} collective-permute-done((f32[1088,128]{1,0:T(8,128)S(1)}, f32[1088,128]{1,0:T(8,128)S(1)}, u32[]{:S(2)}, u32[]{:S(2)}) %collective-permute-start.13) | collective-permute-done | bytes 557088 | tf_op jit(solution)/shard_map/ppermute | solution.py:727
  65.6 0.9 collective-permute-start.23
  66.6 2.1 %collective-permute-start.12 = (f32[224,128]{1,0:T(8,128)S(1)}, f32[224,128]{1,0:T(8,128)S(1)}, u32[]{:S(2)}, u32[]{:S(2)}) collective-permute-start(f32[224,128]{1,0:T(8,128)S(1)} %dynamic-slice_bitcast_fusion.4), channel_id=1, source_target_pairs={{0,8},{4,12},{8,0},{12,4},{1,9},{5,13},{9,1},{13,5},{2,10},{6,14},... | collective-permute-start | bytes 344072 | tf_op jit(solution)/shard_map/ppermute | solution.py:727
  68.7 0.6 collective-permute-start.15
  69.3 0.8 collective-permute-start.20
  70.1 4.0 %collective-permute-done.12 = f32[224,128]{1,0:T(8,128)S(1)} collective-permute-done((f32[224,128]{1,0:T(8,128)S(1)}, f32[224,128]{1,0:T(8,128)S(1)}, u32[]{:S(2)}, u32[]{:S(2)}) %collective-permute-start.12) | collective-permute-done | bytes 114720 | tf_op jit(solution)/shard_map/ppermute | solution.py:727
  74.2 3.4 %collective-permute-done.15 = f32[544,128]{1,0:T(8,128)S(1)} collective-permute-done((f32[544,128]{1,0:T(8,128)S(1)}, f32[544,128]{1,0:T(8,128)S(1)}, u32[]{:S(2)}, u32[]{:S(2)}) %collective-permute-start.15) | collective-permute-done | bytes 278560 | tf_op jit(solution)/shard_map/ppermute | solution.py:727
  77.5 0.7 collective-permute-start.14
  78.4 2.1 %collective-permute-start.25 = (f32[272,128]{1,0:T(8,128)S(1)}, f32[272,128]{1,0:T(8,128)S(1)}, u32[]{:S(2)}, u32[]{:S(2)}) collective-permute-start(f32[272,128]{1,0:T(8,128)S(1)} %dynamic-slice_bitcast_fusion.3), channel_id=1, source_target_pairs={{0,8},{4,12},{8,0},{12,4},{1,9},{5,13},{9,1},{13,5},{2,10},{6,14},... | collective-permute-start | bytes 417800 | tf_op jit(solution)/shard_map/ppermute | solution.py:727
  80.5 1.2 %collective-permute-done.14 = f32[112,128]{1,0:T(8,128)S(1)} collective-permute-done((f32[112,128]{1,0:T(8,128)S(1)}, f32[112,128]{1,0:T(8,128)S(1)}, u32[]{:S(2)}, u32[]{:S(2)}) %collective-permute-start.14) | collective-permute-done | bytes 57376 | tf_op jit(solution)/shard_map/ppermute | solution.py:727
  81.7 3.1 %collective-permute-start.24 = (f32[4,3328]{1,0:T(4,128)S(1)}, f32[4,3328]{1,0:T(4,128)S(1)}, u32[]{:S(2)}, u32[]{:S(2)}) collective-permute-start(f32[4,3328]{1,0:T(4,128)S(1)} %get-tuple-element.134), channel_id=1, source_target_pairs={{0,12},{4,8},{8,4},{12,0},{1,13},{5,9},{9,5},{13,1},{2,14},{6,10},... | collective-permute-start | bytes 159752 | tf_op jit(solution)/shard_map/ppermute | solution.py:812
  84.9 0.7 copy-done.11
  85.5 3.3 %shard_map.227 = (bf16[49,32,64]{2,1,0:T(8,128)(2,1)}, f32[256,128]{1,0:T(8,128)}) custom-call(bf16[49,32,64]{2,1,0:T(8,128)(2,1)} %bitcast.70, bf16[7,64,64]{2,1,0:T(8,128)(2,1)} %out_proj.3, f32[4,4,3328]{2,1,0:T(4,128)} %copy-done.2, f32[4,4,3328]{2,1,0:T(4,128)} %copy-done.10, f32[4,4,3328]{2,1,0:T(4,128)} %copy-done.9, f32[4,4,3328]{2,1,0:T(4,128)} %copy-done.11), custom_call_target="tpu_custom_call" | custom-call | flops 1 | bytes 1 | tf_op jit(solution)/shard_map/pallas_call | solution.py:696
  88.9 0.8 constant_dynamic-slice_fusion
  89.6 2.0 %collective-permute-start.26 = (bf16[384,128]{1,0:T(8,128)(2,1)S(1)}, bf16[384,128]{1,0:T(8,128)(2,1)S(1)}, u32[]{:S(2)}, u32[]{:S(2)}) collective-permute-start(bf16[384,128]{1,0:T(8,128)(2,1)S(1)} %pad_maximum_fusion.6), channel_id=1, source_target_pairs={{0,8},{4,12},{8,0},{12,4},{1,9},{5,13},{9,1},{13,5},{2,10},{6,14},... | collective-permute-start | bytes 294920 | tf_op jit(solution)/shard_map/ppermute | solution.py:727
  91.6 3.2 %collective-permute-done.27 = f32[64,128]{1,0:T(8,128)S(1)} collective-permute-done((f32[64,128]{1,0:T(8,128)S(1)}, f32[64,128]{1,0:T(8,128)S(1)}, u32[]{:S(2)}, u32[]{:S(2)}) %collective-permute-start.27) | collective-permute-done | bytes 32800 | tf_op jit(solution)/shard_map/ppermute | solution.py:727
  94.8 0.8 fusion.3
  95.5 3.0 %collective-permute-done.26 = bf16[384,128]{1,0:T(8,128)(2,1)S(1)} collective-permute-done((bf16[384,128]{1,0:T(8,128)(2,1)S(1)}, bf16[384,128]{1,0:T(8,128)(2,1)S(1)}, u32[]{:S(2)}, u32[]{:S(2)}) %collective-permute-start.26) | collective-permute-done | bytes 98336 | tf_op jit(solution)/shard_map/ppermute | solution.py:727
  98.6 0.1 collective-permute-start.28
  98.8 0.6 collective-permute-start.31
  99.4 0.9 collective-permute-done.29
  100.4 4.2 %collective-permute-done.28 = bf16[768,128]{1,0:T(8,128)(2,1)S(1)} collective-permute-done((bf16[768,128]{1,0:T(8,128)(2,1)S(1)}, bf16[768,128]{1,0:T(8,128)(2,1)S(1)}, u32[]{:S(2)}, u32[]{:S(2)}) %collective-permute-start.28) | collective-permute-done | bytes 196640 | tf_op jit(solution)/shard_map/ppermute | solution.py:727
  104.6 0.1 broadcast_select_fusion.3
  104.7 0.8 collective-permute-start.33
  105.5 1.4 %collective-permute-done.32.rest_3_ = f32[4,4,3328]{2,1,0:T(4,128)S(1)} collective-permute-done((f32[4,4,3328]{2,1,0:T(4,128)S(1)}, f32[4,4,3328]{2,1,0:T(4,128)S(1)}, u32[]{:S(2)}, u32[]{:S(2)}) %collective-permute-start.32) | collective-permute-done | bytes 213024 | tf_op jit(solution)/shard_map/ppermute | solution.py:727
  107.0 0.7 copy-done.7
  107.7 2.6 %shard_map.228 = bf16[49,32,64]{2,1,0:T(8,128)(2,1)} custom-call(f32[4,4,3328]{2,1,0:T(4,128)} %copy-done.1, f32[4,4,3328]{2,1,0:T(4,128)} %copy-done.6, f32[4,4,3328]{2,1,0:T(4,128)} %copy-done.5, f32[4,4,3328]{2,1,0:T(4,128)} %copy-done.7), custom_call_target="tpu_custom_call" | custom-call | flops 1 | bytes 1 | tf_op jit(solution)/shard_map/pallas_call | solution.py:696
  110.2 4.0 %collective-permute-done.33 = bf16[1600,128]{1,0:T(8,128)(2,1)S(1)} collective-permute-done((bf16[1600,128]{1,0:T(8,128)(2,1)S(1)}, bf16[1600,128]{1,0:T(8,128)(2,1)S(1)}, u32[]{:S(2)}, u32[]{:S(2)}) %collective-permute-start.33) | collective-permute-done | bytes 409632 | tf_op jit(solution)/shard_map/ppermute | solution.py:727
  114.3 0.2 broadcast_select_fusion.1
  114.6 2.3 %collective-permute-done.34.other = bf16[3200,128]{1,0:T(8,128)(2,1)S(1)} collective-permute-done((bf16[3200,128]{1,0:T(8,128)(2,1)S(1)}, bf16[3200,128]{1,0:T(8,128)(2,1)S(1)}, u32[]{:S(2)}, u32[]{:S(2)}) %collective-permute-start.34) | collective-permute-done | bytes 819232 | tf_op jit(solution)/shard_map/ppermute | solution.py:727
  116.9 0.9 copy-done.3
  117.8 3.0 %shard_map.229 = (bf16[448,448]{1,0:T(8,128)(2,1)}, bf16[2,384,384]{2,1,0:T(8,128)(2,1)}, bf16[2,320,320]{2,1,0:T(8,128)(2,1)}, bf16[64,256]{1,0:T(8,128)(2,1)},...) custom-call(bf16[3200,128]{1,0:T(8,128)(2,1)} %copy-done, bf16[3200,128]{1,0:T(8,128)(2,1)} %copy-done.3), custom_call_target="tpu_custom_call" | custom-call | flops 1 | bytes 1 | tf_op jit(solution)/shard_map/pallas_call | solution.py:696
  (82 shorter events, 1.1 us)
Async XLA Ops:
  2.9 8.5 %collective-permute-start = (bf16[4,6528]{1,0:T(4,128)(2,1)}, bf16[4,6528]{1,0:T(4,128)(2,1)S(1)}, u32[]{:S(2)}, u32[]{:S(2)}) collective-permute-start(bf16[4,6528]{1,0:T(4,128)(2,1)} %get-tuple-element.70), channel_id=1, source_target_pairs={{0,4},{4,0},{8,12},{12,8},{1,5},{5,1},{9,13},{13,9},{2,6},{6,2},{1... | collective-permute-start | bytes 156680 | tf_op jit(solution)/shard_map/ppermute | solution.py:812
  5.9 6.2 %collective-permute-start.1 = (bf16[4,6528]{1,0:T(4,128)(2,1)}, bf16[4,6528]{1,0:T(4,128)(2,1)S(1)}, u32[]{:S(2)}, u32[]{:S(2)}) collective-permute-start(bf16[4,6528]{1,0:T(4,128)(2,1)} %get-tuple-element.71), channel_id=1, source_target_pairs={{0,8},{4,12},{8,0},{12,4},{1,9},{5,13},{9,1},{13,5},{2,10},{6,14},... | collective-permute-start | bytes 156680 | tf_op jit(solution)/shard_map/ppermute | solution.py:812
  8.5 6.1 %collective-permute-start.2 = (bf16[4,6528]{1,0:T(4,128)(2,1)}, bf16[4,6528]{1,0:T(4,128)(2,1)S(1)}, u32[]{:S(2)}, u32[]{:S(2)}) collective-permute-start(bf16[4,6528]{1,0:T(4,128)(2,1)} %get-tuple-element.72), channel_id=1, source_target_pairs={{0,12},{4,8},{8,4},{12,0},{1,13},{5,9},{9,5},{13,1},{2,14},{6,10},... | collective-permute-start | bytes 156680 | tf_op jit(solution)/shard_map/ppermute | solution.py:812
  11.4 3.3 %copy-start.12 = (bf16[4,6528]{1,0:T(4,128)(2,1)}, bf16[4,6528]{1,0:T(4,128)(2,1)S(1)}, u32[]{:S(2)}) copy-start(bf16[4,6528]{1,0:T(4,128)(2,1)S(1)} %collective-permute-done.rest_1_) | copy-start | bytes 156676
  12.2 2.5 %copy-start.13 = (bf16[4,6528]{1,0:T(4,128)(2,1)}, bf16[4,6528]{1,0:T(4,128)(2,1)S(1)}, u32[]{:S(2)}) copy-start(bf16[4,6528]{1,0:T(4,128)(2,1)S(1)} %collective-permute-done.1.rest_2_) | copy-start | bytes 156676
  14.6 0.6 copy-start.14
  23.8 1.9 %collective-permute-start.3 = (f32[2,128]{1,0:T(2,128)}, f32[2,128]{1,0:T(2,128)S(1)}, u32[]{:S(2)}, u32[]{:S(2)}) collective-permute-start(f32[2,128]{1,0:T(2,128)} %get-tuple-element.73), channel_id=1, source_target_pairs={{0,1},{1,0},{2,3},{3,2},{4,5},{5,4},{6,7},{7,6},{8,9},{9,8},{10,11... | collective-permute-start | bytes 3080 | tf_op jit(solution)/shard_map/ppermute | solution.py:872
  23.9 3.8 %collective-permute-start.4 = (f32[2,128]{1,0:T(2,128)}, f32[2,128]{1,0:T(2,128)S(1)}, u32[]{:S(2)}, u32[]{:S(2)}) collective-permute-start(f32[2,128]{1,0:T(2,128)} %get-tuple-element.73), channel_id=1, source_target_pairs={{0,2},{1,3},{2,0},{3,1},{4,6},{5,7},{6,4},{7,5},{8,10},{9,11},{10,... | collective-permute-start | bytes 3080 | tf_op jit(solution)/shard_map/ppermute | solution.py:872
  25.5 3.1 %collective-permute-start.5 = (f32[2,128]{1,0:T(2,128)}, f32[2,128]{1,0:T(2,128)S(1)}, u32[]{:S(2)}, u32[]{:S(2)}) collective-permute-start(f32[2,128]{1,0:T(2,128)} %get-tuple-element.73), channel_id=1, source_target_pairs={{0,3},{1,2},{2,1},{3,0},{4,7},{5,6},{6,5},{7,4},{8,11},{9,10},{10,... | collective-permute-start | bytes 3080 | tf_op jit(solution)/shard_map/ppermute | solution.py:872
  29.1 7.0 %copy-start.15 = (f32[8,128]{1,0:T(8,128)}, f32[8,128]{1,0:T(8,128)S(1)}, u32[]{:S(2)}) copy-start(f32[8,128]{1,0:T(8,128)S(1)} %pad_maximum_fusion.7.refs_0_) | copy-start | bytes 12292
  29.1 4.5 %collective-permute-start.6 = (f32[8,128]{1,0:T(8,128)S(1)}, f32[8,128]{1,0:T(8,128)S(1)}, u32[]{:S(2)}, u32[]{:S(2)}) collective-permute-start(f32[8,128]{1,0:T(8,128)S(1)} %pad_maximum_fusion.7.refs_0_), channel_id=1, source_target_pairs={{0,4},{4,0},{8,12},{12,8},{1,5},{5,1},{9,13},{13,9},{2,6},{6,2},{1... | collective-permute-start | bytes 12296 | tf_op jit(solution)/shard_map/ppermute | solution.py:877
  29.2 4.6 %collective-permute-start.7 = (f32[8,128]{1,0:T(8,128)S(1)}, f32[8,128]{1,0:T(8,128)S(1)}, u32[]{:S(2)}, u32[]{:S(2)}) collective-permute-start(f32[8,128]{1,0:T(8,128)S(1)} %pad_maximum_fusion.7.refs_0_), channel_id=1, source_target_pairs={{0,8},{4,12},{8,0},{12,4},{1,9},{5,13},{9,1},{13,5},{2,10},{6,14},... | collective-permute-start | bytes 12296 | tf_op jit(solution)/shard_map/ppermute | solution.py:877
  30.7 5.4 %collective-permute-start.8 = (f32[8,128]{1,0:T(8,128)S(1)}, f32[8,128]{1,0:T(8,128)S(1)}, u32[]{:S(2)}, u32[]{:S(2)}) collective-permute-start(f32[8,128]{1,0:T(8,128)S(1)} %pad_maximum_fusion.7.refs_0_), channel_id=1, source_target_pairs={{0,12},{4,8},{8,4},{12,0},{1,13},{5,9},{9,5},{13,1},{2,14},{6,10},... | collective-permute-start | bytes 12296 | tf_op jit(solution)/shard_map/ppermute | solution.py:877
  33.6 2.5 %copy-start.16 = (f32[8,128]{1,0:T(8,128)}, f32[8,128]{1,0:T(8,128)S(1)}, u32[]{:S(2)}) copy-start(f32[8,128]{1,0:T(8,128)S(1)} %collective-permute-done.6.refs_1_) | copy-start | bytes 12292
  33.8 2.3 %copy-start.17 = (f32[8,128]{1,0:T(8,128)}, f32[8,128]{1,0:T(8,128)S(1)}, u32[]{:S(2)}) copy-start(f32[8,128]{1,0:T(8,128)S(1)} %collective-permute-done.7.refs_2_) | copy-start | bytes 12292
  36.1 0.6 copy-start.18
  36.7 9.1 %copy-start.8 = (f32[4,4,3328]{2,1,0:T(4,128)S(1)}, f32[4,4,3328]{2,1,0:T(4,128)}, u32[]{:S(2)}) copy-start(f32[4,4,3328]{2,1,0:T(4,128)} %get-tuple-element.104) | copy-start | bytes 638980
  45.2 5.1 %collective-permute-start.10 = (f32[2176,128]{1,0:T(8,128)}, f32[2176,128]{1,0:T(8,128)S(1)}, u32[]{:S(2)}, u32[]{:S(2)}) collective-permute-start(f32[2176,128]{1,0:T(8,128)} %get-tuple-element.88), channel_id=1, source_target_pairs={{0,1},{1,0},{2,3},{3,2},{4,5},{5,4},{6,7},{7,6},{8,9},{9,8},{10,11... | collective-permute-start | bytes 3342344 | tf_op jit(solution)/shard_map/ppermute | solution.py:727
  45.3 7.2 %collective-permute-start.9 = (f32[896,128]{1,0:T(8,128)}, f32[896,128]{1,0:T(8,128)S(1)}, u32[]{:S(2)}, u32[]{:S(2)}) collective-permute-start(f32[896,128]{1,0:T(8,128)} %get-tuple-element.86), channel_id=1, source_target_pairs={{0,1},{1,0},{2,3},{3,2},{4,5},{5,4},{6,7},{7,6},{8,9},{9,8},{10,11... | collective-permute-start | bytes 1376264 | tf_op jit(solution)/shard_map/ppermute | solution.py:727
  45.8 20.7 %collective-permute-start.16 = (f32[4,3328]{1,0:T(4,128)S(1)}, f32[4,3328]{1,0:T(4,128)S(1)}, u32[]{:S(2)}, u32[]{:S(2)}) collective-permute-start(f32[4,3328]{1,0:T(4,128)S(1)} %get-tuple-element.140), channel_id=1, source_target_pairs={{0,4},{4,0},{8,12},{12,8},{1,5},{5,1},{9,13},{13,9},{2,6},{6,2},{1... | collective-permute-start | bytes 159752 | tf_op jit(solution)/shard_map/ppermute | solution.py:812
  45.9 22.8 %collective-permute-start.17 = (f32[4,3328]{1,0:T(4,128)S(1)}, f32[4,3328]{1,0:T(4,128)S(1)}, u32[]{:S(2)}, u32[]{:S(2)}) collective-permute-start(f32[4,3328]{1,0:T(4,128)S(1)} %get-tuple-element.139), channel_id=1, source_target_pairs={{0,8},{4,12},{8,0},{12,4},{1,9},{5,13},{9,1},{13,5},{2,10},{6,14},... | collective-permute-start | bytes 159752 | tf_op jit(solution)/shard_map/ppermute | solution.py:812
  49.3 19.9 %collective-permute-start.18 = (f32[4,3328]{1,0:T(4,128)S(1)}, f32[4,3328]{1,0:T(4,128)S(1)}, u32[]{:S(2)}, u32[]{:S(2)}) collective-permute-start(f32[4,3328]{1,0:T(4,128)S(1)} %get-tuple-element.138), channel_id=1, source_target_pairs={{0,12},{4,8},{8,4},{12,0},{1,13},{5,9},{9,5},{13,1},{2,14},{6,10},... | collective-permute-start | bytes 159752 | tf_op jit(solution)/shard_map/ppermute | solution.py:812
  51.6 1.0 copy-start.4
  51.7 13.9 %collective-permute-start.13 = (f32[1088,128]{1,0:T(8,128)S(1)}, f32[1088,128]{1,0:T(8,128)S(1)}, u32[]{:S(2)}, u32[]{:S(2)}) collective-permute-start(f32[1088,128]{1,0:T(8,128)S(1)} %dynamic-slice_bitcast_fusion), channel_id=1, source_target_pairs={{0,2},{1,3},{2,0},{3,1},{4,6},{5,7},{6,4},{7,5},{8,10},{9,11},{10,... | collective-permute-start | bytes 1671176 | tf_op jit(solution)/shard_map/ppermute | solution.py:727
  52.8 7.4 %collective-permute-start.11 = (f32[448,128]{1,0:T(8,128)S(1)}, f32[448,128]{1,0:T(8,128)S(1)}, u32[]{:S(2)}, u32[]{:S(2)}) collective-permute-start(f32[448,128]{1,0:T(8,128)S(1)} %dynamic-slice_bitcast_fusion.2), channel_id=1, source_target_pairs={{0,4},{4,0},{8,12},{12,8},{1,5},{5,1},{9,13},{13,9},{2,6},{6,2},{1... | collective-permute-start | bytes 688136 | tf_op jit(solution)/shard_map/ppermute | solution.py:727
  60.2 38.5 %collective-permute-start.22 = (f32[4,3328]{1,0:T(4,128)S(1)}, f32[4,3328]{1,0:T(4,128)S(1)}, u32[]{:S(2)}, u32[]{:S(2)}) collective-permute-start(f32[4,3328]{1,0:T(4,128)S(1)} %get-tuple-element.136), channel_id=1, source_target_pairs={{0,4},{4,0},{8,12},{12,8},{1,5},{5,1},{9,13},{13,9},{2,6},{6,2},{1... | collective-permute-start | bytes 159752 | tf_op jit(solution)/shard_map/ppermute | solution.py:812
  65.6 33.1 %collective-permute-start.23 = (f32[4,3328]{1,0:T(4,128)S(1)}, f32[4,3328]{1,0:T(4,128)S(1)}, u32[]{:S(2)}, u32[]{:S(2)}) collective-permute-start(f32[4,3328]{1,0:T(4,128)S(1)} %get-tuple-element.135), channel_id=1, source_target_pairs={{0,8},{4,12},{8,0},{12,4},{1,9},{5,13},{9,1},{13,5},{2,10},{6,14},... | collective-permute-start | bytes 159752 | tf_op jit(solution)/shard_map/ppermute | solution.py:812
  66.6 7.6 %collective-permute-start.12 = (f32[224,128]{1,0:T(8,128)S(1)}, f32[224,128]{1,0:T(8,128)S(1)}, u32[]{:S(2)}, u32[]{:S(2)}) collective-permute-start(f32[224,128]{1,0:T(8,128)S(1)} %dynamic-slice_bitcast_fusion.4), channel_id=1, source_target_pairs={{0,8},{4,12},{8,0},{12,4},{1,9},{5,13},{9,1},{13,5},{2,10},{6,14},... | collective-permute-start | bytes 344072 | tf_op jit(solution)/shard_map/ppermute | solution.py:727
  68.7 8.9 %collective-permute-start.15 = (f32[544,128]{1,0:T(8,128)S(1)}, f32[544,128]{1,0:T(8,128)S(1)}, u32[]{:S(2)}, u32[]{:S(2)}) collective-permute-start(f32[544,128]{1,0:T(8,128)S(1)} %dynamic-slice_bitcast_fusion.1), channel_id=1, source_target_pairs={{0,4},{4,0},{8,12},{12,8},{1,5},{5,1},{9,13},{13,9},{2,6},{6,2},{1... | collective-permute-start | bytes 835592 | tf_op jit(solution)/shard_map/ppermute | solution.py:727
  69.3 15.5 %copy-start.2 = (f32[4,4,3328]{2,1,0:T(4,128)}, f32[4,4,3328]{2,1,0:T(4,128)S(1)}, u32[]{:S(2)}) copy-start(f32[4,4,3328]{2,1,0:T(4,128)S(1)} %pad_maximum_fusion.3.rest_0_) | copy-start | bytes 638980
  69.3 9.0 %collective-permute-start.20 = (f32[4,4,3328]{2,1,0:T(4,128)S(1)}, f32[4,4,3328]{2,1,0:T(4,128)S(1)}, u32[]{:S(2)}, u32[]{:S(2)}) collective-permute-start(f32[4,4,3328]{2,1,0:T(4,128)S(1)} %pad_maximum_fusion.3.rest_0_), channel_id=1, source_target_pairs={{0,2},{1,3},{2,0},{3,1},{4,6},{5,7},{6,4},{7,5},{8,10},{9,11},{10,... | collective-permute-start | bytes 638984 | tf_op jit(solution)/shard_map/ppermute | solution.py:727
  74.1 7.6 %collective-permute-start.19 = (f32[4,4,3328]{2,1,0:T(4,128)S(1)}, f32[4,4,3328]{2,1,0:T(4,128)S(1)}, u32[]{:S(2)}, u32[]{:S(2)}) collective-permute-start(f32[4,4,3328]{2,1,0:T(4,128)S(1)} %pad_maximum_fusion.3.rest_0_), channel_id=1, source_target_pairs={{0,1},{1,0},{2,3},{3,2},{4,5},{5,4},{6,7},{7,6},{8,9},{9,8},{10,11... | collective-permute-start | bytes 638984 | tf_op jit(solution)/shard_map/ppermute | solution.py:727
  77.5 4.2 %collective-permute-start.14 = (f32[112,128]{1,0:T(8,128)S(1)}, f32[112,128]{1,0:T(8,128)S(1)}, u32[]{:S(2)}, u32[]{:S(2)}) collective-permute-start(f32[112,128]{1,0:T(8,128)S(1)} %dynamic-slice_bitcast_fusion.5), channel_id=1, source_target_pairs={{0,2},{1,3},{2,0},{3,1},{4,6},{5,7},{6,4},{7,5},{8,10},{9,11},{10,... | collective-permute-start | bytes 172040 | tf_op jit(solution)/shard_map/ppermute | solution.py:727
  78.3 6.5 %copy-start.9 = (f32[4,4,3328]{2,1,0:T(4,128)}, f32[4,4,3328]{2,1,0:T(4,128)S(1)}, u32[]{:S(2)}) copy-start(f32[4,4,3328]{2,1,0:T(4,128)S(1)} %collective-permute-done.20.rest_2_) | copy-start | bytes 638980
  78.4 10.5 %collective-permute-start.25 = (f32[272,128]{1,0:T(8,128)S(1)}, f32[272,128]{1,0:T(8,128)S(1)}, u32[]{:S(2)}, u32[]{:S(2)}) collective-permute-start(f32[272,128]{1,0:T(8,128)S(1)} %dynamic-slice_bitcast_fusion.3), channel_id=1, source_target_pairs={{0,8},{4,12},{8,0},{12,4},{1,9},{5,13},{9,1},{13,5},{2,10},{6,14},... | collective-permute-start | bytes 417800 | tf_op jit(solution)/shard_map/ppermute | solution.py:727
  81.7 3.1 %collective-permute-start.21 = (f32[4,4,3328]{2,1,0:T(4,128)S(1)}, f32[4,4,3328]{2,1,0:T(4,128)S(1)}, u32[]{:S(2)}, u32[]{:S(2)}) collective-permute-start(f32[4,4,3328]{2,1,0:T(4,128)S(1)} %collective-permute-done.20.rest_2_), channel_id=1, source_target_pairs={{0,1},{1,0},{2,3},{3,2},{4,5},{5,4},{6,7},{7,6},{8,9},{9,8},{10,11... | collective-permute-start | bytes 638984 | tf_op jit(solution)/shard_map/ppermute | solution.py:727
  81.7 3.1 %copy-start.10 = (f32[4,4,3328]{2,1,0:T(4,128)}, f32[4,4,3328]{2,1,0:T(4,128)S(1)}, u32[]{:S(2)}) copy-start(f32[4,4,3328]{2,1,0:T(4,128)S(1)} %collective-permute-done.19.rest_1_) | copy-start | bytes 638980
  81.7 17.0 %collective-permute-start.24 = (f32[4,3328]{1,0:T(4,128)S(1)}, f32[4,3328]{1,0:T(4,128)S(1)}, u32[]{:S(2)}, u32[]{:S(2)}) collective-permute-start(f32[4,3328]{1,0:T(4,128)S(1)} %get-tuple-element.134), channel_id=1, source_target_pairs={{0,12},{4,8},{8,4},{12,0},{1,13},{5,9},{9,5},{13,1},{2,14},{6,10},... | collective-permute-start | bytes 159752 | tf_op jit(solution)/shard_map/ppermute | solution.py:812
  84.9 0.7 copy-start.11
  89.6 5.1 %collective-permute-start.27 = (f32[64,128]{1,0:T(8,128)S(1)}, f32[64,128]{1,0:T(8,128)S(1)}, u32[]{:S(2)}, u32[]{:S(2)}) collective-permute-start(f32[64,128]{1,0:T(8,128)S(1)} %constant_dynamic-slice_fusion), channel_id=1, source_target_pairs={{0,4},{4,0},{8,12},{12,8},{1,5},{5,1},{9,13},{13,9},{2,6},{6,2},{1... | collective-permute-start | bytes 98312 | tf_op jit(solution)/shard_map/ppermute | solution.py:727
  89.6 8.9 %collective-permute-start.26 = (bf16[384,128]{1,0:T(8,128)(2,1)S(1)}, bf16[384,128]{1,0:T(8,128)(2,1)S(1)}, u32[]{:S(2)}, u32[]{:S(2)}) collective-permute-start(bf16[384,128]{1,0:T(8,128)(2,1)S(1)} %pad_maximum_fusion.6), channel_id=1, source_target_pairs={{0,8},{4,12},{8,0},{12,4},{1,9},{5,13},{9,1},{13,5},{2,10},{6,14},... | collective-permute-start | bytes 294920 | tf_op jit(solution)/shard_map/ppermute | solution.py:727
  95.5 4.8 %collective-permute-start.29 = (f32[64,128]{1,0:T(8,128)S(1)}, f32[64,128]{1,0:T(8,128)S(1)}, u32[]{:S(2)}, u32[]{:S(2)}) collective-permute-start(f32[64,128]{1,0:T(8,128)S(1)} %fusion.3), channel_id=1, source_target_pairs={{0,8},{4,12},{8,0},{12,4},{1,9},{5,13},{9,1},{13,5},{2,10},{6,14},... | collective-permute-start | bytes 98312 | tf_op jit(solution)/shard_map/ppermute | solution.py:727
  98.6 5.9 %collective-permute-start.28 = (bf16[768,128]{1,0:T(8,128)(2,1)S(1)}, bf16[768,128]{1,0:T(8,128)(2,1)S(1)}, u32[]{:S(2)}, u32[]{:S(2)}) collective-permute-start(bf16[768,128]{1,0:T(8,128)(2,1)S(1)} %pad_maximum_fusion.5), channel_id=1, source_target_pairs={{0,4},{4,0},{8,12},{12,8},{1,5},{5,1},{9,13},{13,9},{2,6},{6,2},{1... | collective-permute-start | bytes 589832 | tf_op jit(solution)/shard_map/ppermute | solution.py:727
  98.8 8.2 %copy-start.1 = (f32[4,4,3328]{2,1,0:T(4,128)}, f32[4,4,3328]{2,1,0:T(4,128)S(1)}, u32[]{:S(2)}) copy-start(f32[4,4,3328]{2,1,0:T(4,128)S(1)} %pad_maximum_fusion.4.rest_0_) | copy-start | bytes 638980
  98.8 6.7 %collective-permute-start.31 = (f32[4,4,3328]{2,1,0:T(4,128)S(1)}, f32[4,4,3328]{2,1,0:T(4,128)S(1)}, u32[]{:S(2)}, u32[]{:S(2)}) collective-permute-start(f32[4,4,3328]{2,1,0:T(4,128)S(1)} %pad_maximum_fusion.4.rest_0_), channel_id=1, source_target_pairs={{0,2},{1,3},{2,0},{3,1},{4,6},{5,7},{6,4},{7,5},{8,10},{9,11},{10,... | collective-permute-start | bytes 638984 | tf_op jit(solution)/shard_map/ppermute | solution.py:727
  99.4 6.1 %collective-permute-start.30 = (f32[4,4,3328]{2,1,0:T(4,128)S(1)}, f32[4,4,3328]{2,1,0:T(4,128)S(1)}, u32[]{:S(2)}, u32[]{:S(2)}) collective-permute-start(f32[4,4,3328]{2,1,0:T(4,128)S(1)} %pad_maximum_fusion.4.rest_0_), channel_id=1, source_target_pairs={{0,1},{1,0},{2,3},{3,2},{4,5},{5,4},{6,7},{7,6},{8,9},{9,8},{10,11... | collective-permute-start | bytes 638984 | tf_op jit(solution)/shard_map/ppermute | solution.py:727
  104.7 9.6 %collective-permute-start.33 = (bf16[1600,128]{1,0:T(8,128)(2,1)S(1)}, bf16[1600,128]{1,0:T(8,128)(2,1)S(1)}, u32[]{:S(2)}, u32[]{:S(2)}) collective-permute-start(bf16[1600,128]{1,0:T(8,128)(2,1)S(1)} %pad_maximum_fusion.1), channel_id=1, source_target_pairs={{0,2},{1,3},{2,0},{3,1},{4,6},{5,7},{6,4},{7,5},{8,10},{9,11},{10,... | collective-permute-start | bytes 1228808 | tf_op jit(solution)/shard_map/ppermute | solution.py:727
  105.5 1.5 %copy-start.5 = (f32[4,4,3328]{2,1,0:T(4,128)}, f32[4,4,3328]{2,1,0:T(4,128)S(1)}, u32[]{:S(2)}) copy-start(f32[4,4,3328]{2,1,0:T(4,128)S(1)} %collective-permute-done.31.rest_2_) | copy-start | bytes 638980
  105.5 1.5 %collective-permute-start.32 = (f32[4,4,3328]{2,1,0:T(4,128)S(1)}, f32[4,4,3328]{2,1,0:T(4,128)S(1)}, u32[]{:S(2)}, u32[]{:S(2)}) collective-permute-start(f32[4,4,3328]{2,1,0:T(4,128)S(1)} %collective-permute-done.31.rest_2_), channel_id=1, source_target_pairs={{0,1},{1,0},{2,3},{3,2},{4,5},{5,4},{6,7},{7,6},{8,9},{9,8},{10,11... | collective-permute-start | bytes 638984 | tf_op jit(solution)/shard_map/ppermute | solution.py:727
  105.5 1.5 %copy-start.6 = (f32[4,4,3328]{2,1,0:T(4,128)}, f32[4,4,3328]{2,1,0:T(4,128)S(1)}, u32[]{:S(2)}) copy-start(f32[4,4,3328]{2,1,0:T(4,128)S(1)} %collective-permute-done.30.rest_1_) | copy-start | bytes 638980
  107.0 0.7 copy-start.7
  114.5 2.4 %copy-start = (bf16[3200,128]{1,0:T(8,128)(2,1)}, bf16[3200,128]{1,0:T(8,128)(2,1)S(1)}, u32[]{:S(2)}) copy-start(bf16[3200,128]{1,0:T(8,128)(2,1)S(1)} %pad_maximum_fusion.mine) | copy-start | bytes 2457604
  114.5 2.4 %collective-permute-start.34 = (bf16[3200,128]{1,0:T(8,128)(2,1)S(1)}, bf16[3200,128]{1,0:T(8,128)(2,1)S(1)}, u32[]{:S(2)}, u32[]{:S(2)}) collective-permute-start(bf16[3200,128]{1,0:T(8,128)(2,1)S(1)} %pad_maximum_fusion.mine), channel_id=1, source_target_pairs={{0,1},{1,0},{2,3},{3,2},{4,5},{5,4},{6,7},{7,6},{8,9},{9,8},{10,11... | collective-permute-start | bytes 2457608 | tf_op jit(solution)/shard_map/ppermute | solution.py:727
  116.9 0.9 copy-start.3
